TPU v7x, 32 devices: a whole 2x2x4 slice. The times are simulated.
32 devices in a mesh: groups: 2 (over y), seq: 4 (over z), tp: 4 (over x, core).
Axes of the slice: x: 2, y: 2, z: 4, core: 2. Of those that a mesh axis runs over, the one named last changes fastest.
Arguments:
- lengths: int32 [8], P('groups'), parts along dimension 0, may hold values from 1 to 4096, 8192 in all
- owner_map: int32 [1024], P(('groups', 'seq')), parts along dimension 0, may hold values from 0 to 3, as said below
- row_request: int32 [128], P('groups'), parts along dimension 0, may hold values from 0 to 3
- deltas: bfloat16 [16384, 2, 512], P(('groups', 'seq'), None, 'tp'), parts along dimension 0, may hold values from -6 to 6
- anchors: float32 [1024, 2, 512], P(('groups', 'seq'), None, 'tp'), parts along dimension 0, may hold values from -6 to 6
- scales: float32 [4, 512], P('groups', 'tp'), parts along dimension 0, may hold values from 0.1 to 0.8
- queries: bfloat16 [128, 2, 4096], P('groups', None, 'tp'), parts along dimension 0, may hold values from -200 to 200
- new_kv: bfloat16 [128, 2, 2, 512], P(('groups', 'seq'), None, None, 'tp'), parts along dimension 0, may hold values from -8 to 8
Outputs:
- pages: bfloat16 [1024, 16, 2, 512], P(('groups', 'seq'), None, None, 'tp'), parts along dimension 0
- attended: bfloat16 [128, 2, 4096], P(('groups', 'seq'), None, 'tp'), parts along dimension 0
There are 2 independent parts, one for each index of `groups`. A program takes and returns all parts, laid end to end along the dimension named above; each array names one. Nothing has to cross between parts.
Inputs may be any that keep to these rules, and one draw needn't show every extreme that they name: `owner_map`: the 128 blocks of each prefill owner name every decode owner exactly 32 times.
All inputs are finite; a program needn't handle non-finite values.
Results may differ from a plain program's by a relative error of at most 0.0055.
Values may be sent and summed in bfloat16 or wider, within the bound.
No kernel may reach another device: no remote copies, remote signals or barrier semaphores. Data moves between devices by JAX's collectives and lax.ppermute only.
A program may use at most 128 MiB of HBM per device.

v0:
```python
import jax
import jax.numpy as jnp
from jax import lax
from jax.sharding import PartitionSpec as P

HD = 128
GQ = 8


neg_big = -1e30


def combined_all(array, axis, combine):
    everything = jax.tree.map(lambda part: lax.all_gather(part, axis), array)
    first = jax.tree.map(lambda part: part[0], everything)

    def lap(k, so_far):
        return combine(so_far, jax.tree.map(lambda part: part[k], everything))

    return lax.fori_loop(1, lax.axis_size(axis), lap, first)


def request_of(positions, request_ends):
    return jnp.sum((positions[:, None] >= request_ends[None, :]).astype(jnp.int32), axis=1)


def join_partials(earlier, latter):
    top_all = jnp.maximum(earlier[0], latter[0])
    scale_a = jnp.exp(earlier[0] - top_all)
    scale_b = jnp.exp(latter[0] - top_all)
    return (
        top_all,
        earlier[1] * scale_a + latter[1] * scale_b,
        earlier[2] * scale_a[..., None] + latter[2] * scale_b[..., None],
    )


def per_device(lengths, owner_map, row_request, deltas, anchors, scales, queries, new_kv):
    blk_dev = anchors.shape[0]
    width = anchors.shape[2]
    block_len = deltas.shape[0] // blk_dev
    heads_kv = width // HD
    nseq = lax.axis_size("seq")
    me_index = lax.axis_index("seq")
    capacity = blk_dev // nseq
    factor = HD ** (-0.5)
    decoded = (
        anchors[:, None] + scales * deltas.reshape(blk_dev, block_len, 2, width).astype(jnp.float32)
    ).astype(jnp.bfloat16)
    matches = (owner_map[:, None] == jnp.arange(nseq, dtype=jnp.int32)[None, :]).astype(jnp.int32)
    ranking = jnp.sum((jnp.cumsum(matches, axis=0) - 1) * matches, axis=1)
    slot_index = owner_map * capacity + ranking
    source_rows = (
        jnp.zeros((blk_dev,), jnp.int32).at[slot_index].set(jnp.arange(blk_dev, dtype=jnp.int32))
    )
    outgoing = jnp.take(decoded, source_rows, axis=0)
    pages = lax.all_to_all(outgoing, "seq", split_axis=0, concat_axis=0, tiled=True)
    request_ends = jnp.cumsum(lengths)
    owner_table = lax.all_gather(owner_map, "seq", axis=0, tiled=True).reshape(nseq, blk_dev)
    is_mine = (owner_table == me_index).astype(jnp.int32)
    mine_rank = (jnp.cumsum(is_mine, axis=1) - 1) * is_mine
    picked = is_mine[:, :, None] * (
        mine_rank[:, :, None] == jnp.arange(capacity, dtype=jnp.int32)[None, None, :]
    ).astype(jnp.int32)
    local_ids = jnp.sum(picked * jnp.arange(blk_dev, dtype=jnp.int32)[None, :, None], axis=1)
    block_ids = (local_ids + jnp.arange(nseq, dtype=jnp.int32)[:, None] * blk_dev).reshape(-1)
    positions = (
        block_ids[:, None] * block_len + jnp.arange(block_len, dtype=jnp.int32)[None, :]
    ).reshape(-1)
    key_req = request_of(positions, request_ends)
    num_keys = blk_dev * block_len
    key_block = 512
    num_blocks = num_keys // key_block
    key_rows = pages[:, :, 0].reshape(num_blocks, key_block, heads_kv, HD)
    value_rows = pages[:, :, 1].reshape(num_blocks, key_block, heads_kv, HD)
    req_blocks = key_req.reshape(num_blocks, key_block)
    all_rows = queries.shape[0]
    queried = queries.reshape(all_rows, 2, heads_kv, GQ, HD)

    def attend_block(carry, items):
        top_run, total_run, summed_run = carry
        key_blk, value_blk, req_blk = items
        scored = (
            jnp.einsum("rsagd,kad->rsagk", queried, key_blk, preferred_element_type=jnp.float32)
            * factor
        )
        mask = (row_request[:, None] == req_blk[None, :])[:, None, None, None, :]
        block_top = jnp.max(jnp.where(mask, scored, neg_big), axis=-1)
        top_new = jnp.maximum(top_run, block_top)
        weights = jnp.where(mask, jnp.exp(scored - top_new[..., None]), 0.0)
        shrink = jnp.exp(top_run - top_new)
        total_new = total_run * shrink + jnp.sum(weights, axis=-1)
        summed_new = summed_run * shrink[..., None] + jnp.einsum(
            "rsagk,kad->rsagd",
            weights.astype(jnp.bfloat16),
            value_blk,
            preferred_element_type=jnp.float32,
        )
        return ((top_new, total_new, summed_new), None)

    start_top = jnp.full((all_rows, 2, heads_kv, GQ), neg_big, jnp.float32)
    start_total = jnp.zeros((all_rows, 2, heads_kv, GQ), jnp.float32)
    start_summed = jnp.zeros((all_rows, 2, heads_kv, GQ, HD), jnp.float32)
    (top_local, total_local, summed_local), _ = lax.scan(
        attend_block, (start_top, start_total, start_summed), (key_rows, value_rows, req_blocks)
    )
    rows_dev = new_kv.shape[0]
    row_start = me_index * rows_dev
    top_glob, total_glob, summed_glob = combined_all(
        (top_local, total_local, summed_local), "seq", join_partials
    )
    cache_top = lax.dynamic_slice_in_dim(top_glob, row_start, rows_dev, 0)
    cache_total = lax.dynamic_slice_in_dim(total_glob, row_start, rows_dev, 0)
    cache_summed = lax.dynamic_slice_in_dim(summed_glob, row_start, rows_dev, 0)
    own_rows = new_kv.reshape(rows_dev, 2, 2, heads_kv, HD)
    query_mine = lax.dynamic_slice_in_dim(queried, row_start, rows_dev, 0)
    own_scored = (
        jnp.einsum(
            "rsagd,rtad->rsagt", query_mine, own_rows[:, :, 0], preferred_element_type=jnp.float32
        )
        * factor
    )
    causal = (jnp.arange(2)[None, :] <= jnp.arange(2)[:, None])[None, :, None, None, :]
    top_final = jnp.maximum(cache_top, jnp.max(jnp.where(causal, own_scored, neg_big), axis=-1))
    cache_scale = jnp.exp(cache_top - top_final)
    own_weights = jnp.where(causal, jnp.exp(own_scored - top_final[..., None]), 0.0)
    total_all = cache_total * cache_scale + jnp.sum(own_weights, axis=-1)
    summed_all = cache_summed * cache_scale[..., None] + jnp.einsum(
        "rsagt,rtad->rsagd",
        own_weights.astype(jnp.bfloat16),
        own_rows[:, :, 1],
        preferred_element_type=jnp.float32,
    )
    attended = (
        (summed_all / total_all[..., None])
        .astype(jnp.bfloat16)
        .reshape(rows_dev, 2, heads_kv * GQ * HD)
    )
    return (pages, attended)


def solution(mesh):
    placed = (
        P("groups"),
        P(("groups", "seq")),
        P("groups"),
        P(("groups", "seq"), None, "tp"),
        P(("groups", "seq"), None, "tp"),
        P("groups", "tp"),
        P("groups", None, "tp"),
        P(("groups", "seq"), None, None, "tp"),
    )
    return jax.shard_map(
        per_device,
        mesh=mesh,
        in_specs=placed,
        out_specs=(P(("groups", "seq"), None, None, "tp"), P(("groups", "seq"), None, "tp")),
        check_vma=False,
    )
```

profile of v0, /device:TPU:0, one launch (start us, length us, event | category | flops | bytes accessed | tf_op | source)
XLA Modules:
  0.0 125.1 jit_solution(15690844090015983437)
XLA Ops:
  7.2 0.8 fusion.37
  8.1 0.8 select_reduce_fusion
  9.0 0.7 compare_select_fusion.1
  9.6 1.0 scatter_custom_fusion
  10.7 1.4 %copy.94 = bf16[2048,2,128]{2,0,1:T(8,128)(2,1)S(1)} copy(bf16[2048,2,128]{2,1,0:T(2,128)(2,1)} %param.15) | data formatting | bytes 2097152 | tf_op args[3]
  12.3 0.8 gather_fusion
  13.1 1.2 broadcast_select_fusion
  14.3 6.3 %all-to-all-start = ((bf16[128,16,2,128]{3,1,2,0:T(8,128)(2,1)}), bf16[128,16,2,128]{3,1,2,0:T(8,128)(2,1)S(1)}, u32[]{:S(2)}, u32[]{:S(2)}) async-start(bf16[128,16,2,128]{3,1,2,0:T(8,128)(2,1)} %broadcast_select_fusion), calls=%async_computation | async-start | bytes 2097152 | tf_op jit(solution)/shard_map/all_to_all | solution.py:57
  20.9 22.7 %all-gather.3 = s32[4,1,128]{2,1,0:T(1,128)S(1)} all-gather(s32[1,1,128]{2,1,0:T(1,128)S(1)} %bitcast.215), channel_id=1, replica_groups=mesh['groups'=2,'seq'=4,'tp'=4] {'seq'}, dimensions={0}, use_global_device_ids=true | all-gather | bytes 2560 | tf_op jit(solution)/shard_map/all_gather | solution.py:59
  44.7 1.7 %all-to-all-done = bf16[128,16,2,128]{3,1,2,0:T(8,128)(2,1)S(1)} async-done(((bf16[128,16,2,128]{3,1,2,0:T(8,128)(2,1)}), bf16[128,16,2,128]{3,1,2,0:T(8,128)(2,1)S(1)}, u32[]{:S(2)}, u32[]{:S(2)}) %all-to-all-start) | async-done | bytes 1048608 | tf_op jit(solution)/shard_map/all_to_all | solution.py:57
  46.6 8.9 %while.35 = (s32[]{:T(128)}, f32[64,2,1,8]{0,3,1,2:T(8,128)S(1)}, f32[64,2,1,8]{0,3,1,2:T(8,128)S(1)}, f32[64,2,1,8,128]{4,0,3,1,2:T(8,128)S(1)}, s32[64]{0:T(12...) while((s32[]{:T(128)}, f32[64,2,1,8]{0,3,1,2:T(8,128)S(1)}, ...), condition=%wide.region_10.11_spmd.clone, body=%wide.region_7.10_spmd.clone.sunk | while | flops 274634752 | bytes 8075661 | solution.py:104
  47.3 0.7 fusion.66
  47.9 0.8 fusion.67
  49.5 0.7 fusion.66
  50.2 0.8 fusion.67
  51.7 0.7 fusion.66
  52.4 0.8 fusion.67
  53.9 0.7 fusion.66
  54.6 0.8 fusion.67
  55.5 0.8 copy-done
  57.0 17.6 %all-gather.1 = f32[256,2,1,8]{3,1,2,0:T(2,128)S(1)} all-gather(f32[64,2,1,8]{3,1,2,0:T(2,128)S(1)} %copy.102), channel_id=3, replica_groups=mesh['groups'=2,'seq'=4,'tp'=4] {'seq'}, dimensions={0}, use_global_device_ids=true | all-gather | bytes 20480 | tf_op jit(solution)/shard_map/all_gather | solution.py:14
  74.7 16.1 %all-gather = f32[256,2,1,8]{3,1,2,0:T(2,128)S(1)} all-gather(f32[64,2,1,8]{3,1,2,0:T(2,128)S(1)} %copy.101), channel_id=2, replica_groups=mesh['groups'=2,'seq'=4,'tp'=4] {'seq'}, dimensions={0}, use_global_device_ids=true | all-gather | bytes 20480 | tf_op jit(solution)/shard_map/all_gather | solution.py:14
  91.0 1.8 %copy.114 = bf16[128,16,2,128]{3,2,1,0:T(2,128)(2,1)} copy(bf16[128,16,2,128]{3,1,2,0:T(8,128)(2,1)S(1)} %all-to-all-done) | data formatting | bytes 2097152
  92.8 16.7 %all-gather.6.cloned.1.call-done = f32[256,2,1,8,128]{4,0,3,1,2:T(8,128)} async-done(((f32[64,2,1,8,128]{4,0,3,1,2:T(8,128)}), f32[256,2,1,8,128]{4,0,3,1,2:T(8,128)}) %all-gather.6.cloned.1.call-update) | async-done | bytes 2097168 | tf_op jit(solution)/shard_map/all_gather | solution.py:14
  109.6 1.1 slice.37
  110.9 5.9 %while.34 = (s32[]{:T(128)}, f32[64,2,1,8]{0,3,2,1:T(8,128)S(1)}, f32[64,2,1,8]{0,3,2,1:T(8,128)S(1)}, f32[64,2,1,8,128]{4,3,2,1,0:T(8,128)S(1)}, f32[4,64,2,1,8...) while((s32[]{:T(128)}, f32[64,2,1,8]{0,3,2,1:T(8,128)S(1)}, ...), condition=%wide.region_12.13_spmd, body=%wide.region_11.12_spmd.sunk | while | flops 400389 | bytes 2699411 | solution.py:20
  111.2 1.1 constant_dynamic-slice_fusion.4
  112.3 0.6 fusion.61
  113.2 1.1 constant_dynamic-slice_fusion.4
  115.2 1.1 constant_dynamic-slice_fusion.4
  116.3 0.6 fusion.61
  117.6 0.7 reshape.249
  (99 shorter events, 8.0 us)
Async XLA Ops:
  7.2 4.9 %copy-start.6 = (f32[2,128]{1,0:T(2,128)S(1)}, f32[2,128]{1,0:T(2,128)}, u32[]{:S(2)}) copy-start(f32[2,128]{1,0:T(2,128)} %param.17) | copy-start | bytes 3076
  7.2 4.9 %copy-start.2 = (f32[128,2,128]{2,1,0:T(2,128)S(1)}, f32[128,2,128]{2,1,0:T(2,128)}, u32[]{:S(2)}) copy-start(f32[128,2,128]{2,1,0:T(2,128)} %param.16) | copy-start | bytes 393220
  13.1 7.6 %copy-start.7 = (s32[4]{0:T(128)S(1)}, s32[4]{0:T(128)}, u32[]{:S(2)}) copy-start(s32[4]{0:T(128)} %param.12) | copy-start | bytes 52
  13.1 7.7 %copy-start.5 = (s32[128]{0:T(128)S(1)}, s32[128]{0:T(128)}, u32[]{:S(2)}) copy-start(s32[128]{0:T(128)} %param.13) | copy-start | bytes 1540
  13.1 31.3 %copy-start.1 = (bf16[64,2,1024]{2,1,0:T(2,128)(2,1)S(1)}, bf16[64,2,1024]{2,1,0:T(2,128)(2,1)}, u32[]{:S(2)}) copy-start(bf16[64,2,1024]{2,1,0:T(2,128)(2,1)} %param.18) | copy-start | bytes 786436
  14.3 32.1 %all-to-all-start = ((bf16[128,16,2,128]{3,1,2,0:T(8,128)(2,1)}), bf16[128,16,2,128]{3,1,2,0:T(8,128)(2,1)S(1)}, u32[]{:S(2)}, u32[]{:S(2)}) async-start(bf16[128,16,2,128]{3,1,2,0:T(8,128)(2,1)} %broadcast_select_fusion), calls=%async_computation | async-start | bytes 2097152 | tf_op jit(solution)/shard_map/all_to_all | solution.py:57
  20.6 25.9 %copy-start.4 = (s32[64]{0:T(128)S(1)}, s32[64]{0:T(128)}, u32[]{:S(2)}) copy-start(s32[64]{0:T(128)} %param.14) | copy-start | bytes 772
  20.6 88.9 %all-gather.6.cloned.1.call-start = ((), (), s32[]{:S(2)}) async-start(), calls=%async_computation.1 | async-start | bytes 2621440 | tf_op jit(solution)/shard_map/all_gather | solution.py:14
  46.6 9.7 %copy-start.3 = (bf16[16,2,2,128]{3,2,1,0:T(2,128)(2,1)S(1)}, bf16[16,2,2,128]{3,2,1,0:T(2,128)(2,1)}, u32[]{:S(2)}) copy-start(bf16[16,2,2,128]{3,2,1,0:T(2,128)(2,1)} %param.19) | copy-start | bytes 49156
  55.5 0.8 copy-start
Sparse Core Ops, SparseCore 0:
  56.4 53.1 all-gather.5
where the time goes:
time: 126 us; the launch traced here: 125 us
  blocking collectives  56.3 us (45%)
  waiting for transfers between devices  18.4 us (15%)
  between operations  14.4 us (11%)
  local copies, waits for them, and re-layouts  13.2 us (10%)
  other arithmetic  9.93 us (8%)
  starting transfers between devices  6.32 us (5%)
  matrix products  6.15 us (5%)
    all_gather x2, blocking collectives, combined_all(): everything = jax.tree.map(lambda part: lax.all_gather(part, axis), array)  33.6 us
    all_gather x1, blocking collectives, per_device(): lax.all_gather(owner_map, 'seq', axis=0, tiled=True).reshape(nseq, blk_dev)  22.7 us
    all_gather x1, waiting for transfers between devices, combined_all(): everything = jax.tree.map(lambda part: lax.all_gather(part, axis), array)  16.7 us
    all_to_all x1, starting transfers between devices, per_device(): lax.all_to_all(outgoing, 'seq', split_axis=0, concat_axis=0, tiled=True)  6.32 us
    unnamed x20, local copies, waits for them, and re-layouts  4.1 us
    dot_general x4, matrix products, attend_block(): jnp.einsum('rsagk,kad->rsagd', weights.astype(jnp.bfloat16), value_blk, p...  3.3 us
    dynamic_slice x3, local copies, waits for them, and re-layouts, lap(): return combine(so_far, jax.tree.map(lambda part: part[k], everything))  3.29 us
    reduce_sum x4, other arithmetic, attend_block(): total_new = total_run * shrink + jnp.sum(weights, axis=-1)  2.67 us
  transfers between devices with their start and end apart: 2, of which 2 were waited for; matrix products, arithmetic and copies ran while one was open for 3% of the time, Pallas kernels for 0%

commit v1 on v0

v1 whole, which is shorter than its diff:
```python
import functools

import jax
import jax.numpy as jnp
from jax import lax
from jax.experimental import pallas as pl
from jax.experimental.pallas import tpu as pltpu
from jax.sharding import PartitionSpec as P

HD = 128
GQ = 8
STEPS = 2
STAT_ROWS = 16
FAR = -1e30
RATE = HD ** (-0.5) * 1.4426950408889634

VMEM = pl.BlockSpec(memory_space=pltpu.VMEM)
SMEM = pl.BlockSpec(memory_space=pltpu.SMEM)


def place_kernel(capacity, owner_ref, deltas_ref, anchors_ref, scales_ref, out_ref, count_ref):
    blocks = owner_ref.shape[0]
    rows = deltas_ref.shape[0] // blocks
    for owner in range(count_ref.shape[0]):
        count_ref[owner] = owner * capacity
    odd = lax.broadcasted_iota(jnp.int32, (8, HD), 0) % 2 == 1
    scale = jnp.where(odd, scales_ref[1:2, :], scales_ref[0:1, :])[None]

    def one_block(block, carry):
        owner = owner_ref[block]
        slot = count_ref[owner]
        count_ref[owner] = slot + 1
        anchor = jnp.where(
            odd, anchors_ref[pl.ds(2 * block + 1, 1), :], anchors_ref[pl.ds(2 * block, 1), :]
        )[None]
        delta = deltas_ref[pl.ds(block * rows, rows), :].astype(jnp.float32)
        decoded = anchor + scale * delta.reshape(rows // 8, 8, HD)
        out_ref[pl.ds(pl.multiple_of(slot * rows, rows), rows), :] = decoded.reshape(rows, HD).astype(
            jnp.bfloat16
        )
        return carry

    lax.fori_loop(0, blocks, one_block, 0, unroll=4)


def pieces(values):
    high = values.astype(jnp.bfloat16)
    rest = values - high.astype(jnp.float32)
    middle = rest.astype(jnp.bfloat16)
    low = (rest - middle.astype(jnp.float32)).astype(jnp.bfloat16)
    return [high, middle, low]


def attend_kernel(
    position_ref,
    lengths_ref,
    request_ref,
    deltas_ref,
    anchors_ref,
    scales_ref,
    queries_ref,
    mine_ref,
    new_ref,
    out_ref,
    own_ref,
    wide_ref,
    keys_ref,
    values_ref,
    asked_ref,
):
    blocks = anchors_ref.shape[0] // 2
    rows = deltas_ref.shape[0] // blocks
    tokens = rows // 2
    requests = lengths_ref.shape[0]
    asked = queries_ref.shape[0]
    per_row = asked // request_ref.shape[0]
    receivers, _, width = out_ref.shape

    wide_ref[...] = deltas_ref[...].astype(jnp.float32)
    scale_key = scales_ref[0:1, :]
    scale_value = scales_ref[1:2, :]

    def one_block(block, carry):
        here = pl.ds(pl.multiple_of(block * tokens, tokens), tokens)
        key = wide_ref[pl.ds(block * rows, tokens, stride=2), :]
        value = wide_ref[pl.ds(block * rows + 1, tokens, stride=2), :]
        keys_ref[here, 0:HD] = (anchors_ref[pl.ds(2 * block, 1), :] + scale_key * key).astype(jnp.bfloat16)
        values_ref[here, :] = (anchors_ref[pl.ds(2 * block + 1, 1), :] + scale_value * value).astype(
            jnp.bfloat16
        )
        return carry

    lax.fori_loop(0, blocks, one_block, 0, unroll=4)

    lane = lax.broadcasted_iota(jnp.int32, (1, HD), 1)
    first = jnp.zeros((1, HD), jnp.int32)
    last = jnp.zeros((1, HD), jnp.int32)
    end = 0 - position_ref[0]
    for request in range(requests):
        start = end
        end = end + lengths_ref[request]
        first = jnp.where(lane == request, start, first)
        last = jnp.where(lane == request, end, last)
    place = lax.broadcasted_iota(jnp.int32, (blocks * tokens, HD), 0)
    keys_ref[:, HD:] = jnp.where((place >= first) & (place < last), 1.0, 0.0).astype(jnp.bfloat16)

    asked_ref[:, 0:HD] = queries_ref[...]
    wide_lane = lax.broadcasted_iota(jnp.int32, (per_row, HD), 1)

    def one_row(row, carry):
        asked_ref[pl.ds(pl.multiple_of(row * per_row, per_row), per_row), HD:] = jnp.where(
            (wide_lane == request_ref[row]) | (wide_lane >= requests), 0.0, FAR
        ).astype(jnp.bfloat16)
        return carry

    lax.fori_loop(0, request_ref.shape[0], one_row, 0, unroll=4)

    tile = min(256, asked)
    parts = max(1, tile // width)

    def one_tile(index, carry):
        here = asked_ref[pl.ds(pl.multiple_of(index * tile, tile), tile), :]
        scores = lax.dot_general(
            keys_ref[...], here, (((1,), (1,)), ((), ())), preferred_element_type=jnp.float32
        )
        top = jnp.max(scores, axis=0, keepdims=True)
        weights = jnp.exp2((scores - top) * RATE)
        total = jnp.sum(weights, axis=0, keepdims=True)
        summed = lax.dot_general(
            values_ref[...],
            weights.astype(jnp.bfloat16),
            (((0,), (0,)), ((), ())),
            preferred_element_type=jnp.float32,
        )
        stats = pieces(top) + pieces(total)
        stats = jnp.concatenate(
            stats + [jnp.zeros((STAT_ROWS - len(stats), tile), jnp.bfloat16)], axis=0
        )
        both = jnp.concatenate([summed.astype(jnp.bfloat16), stats], axis=0)
        for part in range(parts):
            out_ref[index * parts + part] = both[:, part * width : (part + 1) * width]
        return carry

    lax.fori_loop(0, asked // tile, one_tile, 0)

    fresh = new_ref.shape[0] // 4
    new = new_ref[...].astype(jnp.float32).reshape(fresh, 4, HD)
    mine = mine_ref[...]
    of_row = lax.broadcasted_iota(jnp.int32, (fresh, width), 1) // (GQ * STEPS)
    same = of_row == lax.broadcasted_iota(jnp.int32, (fresh, width), 0)
    step = lax.broadcasted_iota(jnp.int32, (1, width), 1) % STEPS
    own_scores = []
    for which in range(STEPS):
        scored = lax.dot_general(
            new[:, 2 * which, :].astype(jnp.bfloat16),
            mine,
            (((1,), (1,)), ((), ())),
            preferred_element_type=jnp.float32,
        )
        picked = jnp.sum(jnp.where(same, scored, 0.0), axis=0, keepdims=True)
        own_scores.append(jnp.where(step >= which, picked, FAR))
    own_top = jnp.maximum(own_scores[0], own_scores[1])
    own_total = jnp.zeros((1, width), jnp.float32)
    own_summed = jnp.zeros((HD, width), jnp.float32)
    for which in range(STEPS):
        weight = jnp.exp2((own_scores[which] - own_top) * RATE)
        own_total = own_total + weight
        spread = jnp.where(same, weight, 0.0).astype(jnp.bfloat16)
        own_summed = own_summed + lax.dot_general(
            new[:, 2 * which + 1, :].astype(jnp.bfloat16),
            spread,
            (((0,), (0,)), ((), ())),
            preferred_element_type=jnp.float32,
        )
    own_ref[0:HD, :] = own_summed
    own_ref[HD:, :] = jnp.concatenate(
        [own_top, own_total, jnp.zeros((6, width), jnp.float32)], axis=0
    )


def join_kernel(partial_ref, own_ref, out_ref):
    senders = partial_ref.shape[0]
    tops = [own_ref[HD : HD + 1, :]]
    totals = [own_ref[HD + 1 : HD + 2, :]]
    for sender in range(senders):
        stats = partial_ref[sender, HD:, :].astype(jnp.float32)
        tops.append(stats[0:1] + stats[1:2] + stats[2:3])
        totals.append(stats[3:4] + stats[4:5] + stats[5:6])
    top = functools.reduce(jnp.maximum, tops)
    scale = jnp.exp2((tops[0] - top) * RATE)
    total = totals[0] * scale
    summed = own_ref[0:HD, :] * scale
    for sender in range(senders):
        scale = jnp.exp2((tops[sender + 1] - top) * RATE)
        total = total + totals[sender + 1] * scale
        summed = summed + partial_ref[sender, 0:HD, :].astype(jnp.float32) * scale
    out_ref[...] = (summed / total).T.astype(jnp.bfloat16)


def per_device(lengths, owner_map, row_request, deltas, anchors, scales, queries, new_kv):
    blocks = anchors.shape[0]
    tokens = deltas.shape[0]
    senders = lax.axis_size("seq")
    me = lax.axis_index("seq")
    rows, steps, _ = queries.shape
    rows_dev = new_kv.shape[0]
    width = rows_dev * GQ * steps
    limit = pltpu.CompilerParams(vmem_limit_bytes=48 * 1024 * 1024)

    flat_deltas = deltas.reshape(tokens * 2, HD)
    flat_anchors = anchors.reshape(blocks * 2, HD)
    flat_queries = queries.reshape(rows, steps, GQ, HD).transpose(0, 2, 1, 3).reshape(-1, HD)
    flat_new = new_kv.reshape(rows_dev * 4, HD)

    outgoing = pl.pallas_call(
        functools.partial(place_kernel, blocks // senders),
        out_shape=jax.ShapeDtypeStruct(flat_deltas.shape, jnp.bfloat16),
        in_specs=[SMEM, VMEM, VMEM, VMEM],
        out_specs=VMEM,
        scratch_shapes=[pltpu.SMEM((senders,), jnp.int32)],
        compiler_params=limit,
        name="place",
    )(owner_map, flat_deltas, flat_anchors, scales)
    pages = lax.all_to_all(
        outgoing.reshape(blocks, tokens // blocks, 2, HD), "seq", split_axis=0, concat_axis=0, tiled=True
    )

    mine = lax.dynamic_slice_in_dim(flat_queries, me * width, width, 0)
    partial, own = pl.pallas_call(
        attend_kernel,
        out_shape=(
            jax.ShapeDtypeStruct((senders, HD + STAT_ROWS, width), jnp.bfloat16),
            jax.ShapeDtypeStruct((HD + 8, width), jnp.float32),
        ),
        in_specs=[SMEM, SMEM, SMEM] + [VMEM] * 6,
        out_specs=(VMEM, VMEM),
        scratch_shapes=[
            pltpu.VMEM((tokens * 2, HD), jnp.float32),
            pltpu.VMEM((tokens, 2 * HD), jnp.bfloat16),
            pltpu.VMEM((tokens, HD), jnp.bfloat16),
            pltpu.VMEM((rows * GQ * steps, 2 * HD), jnp.bfloat16),
        ],
        compiler_params=limit,
        name="attend",
    )(
        (me * tokens).astype(jnp.int32).reshape(1),
        lengths,
        row_request,
        flat_deltas,
        flat_anchors,
        scales,
        flat_queries,
        mine,
        flat_new,
    )
    received = lax.all_to_all(partial, "seq", split_axis=0, concat_axis=0, tiled=True)
    attended = pl.pallas_call(
        join_kernel,
        out_shape=jax.ShapeDtypeStruct((width, HD), jnp.bfloat16),
        in_specs=[VMEM, VMEM],
        out_specs=VMEM,
        compiler_params=limit,
        name="join",
    )(received, own)
    attended = (
        attended.reshape(rows_dev, GQ, steps, HD).transpose(0, 2, 1, 3).reshape(rows_dev, steps, GQ * HD)
    )
    return pages, attended


def solution(mesh):
    placed = (
        P("groups"),
        P(("groups", "seq")),
        P("groups"),
        P(("groups", "seq"), None, "tp"),
        P(("groups", "seq"), None, "tp"),
        P("groups", "tp"),
        P("groups", None, "tp"),
        P(("groups", "seq"), None, None, "tp"),
    )
    return jax.shard_map(
        per_device,
        mesh=mesh,
        in_specs=placed,
        out_specs=(P(("groups", "seq"), None, None, "tp"), P(("groups", "seq"), None, "tp")),
        check_vma=False,
    )
```

time: 126 us -> 57 us (0.45)
  blocking collectives: 56.3 us -> 0 us
  between operations: 14.4 us -> 0.7 us
  waiting for transfers between devices: 18.4 us -> 30.7 us
  Pallas kernels: 0 us -> 10.5 us
  other arithmetic: 9.93 us -> 0 us
  local copies, waits for them, and re-layouts: 13.2 us -> 4.72 us
  matrix products: 6.15 us -> 0 us
  starting transfers between devices: 6.32 us -> 9.97 us
    all_gather x3 -> x0, blocking collectives: 56.3 us -> none  [the longest x2 33.6 us: combined_all(): everything = jax.tree.map(lambda part: lax.all_gather(part, axis), array)]
    all_to_all x1 -> x2, waiting for transfers between devices: 1.68 us -> 30.7 us  [the longest x1 23.3 us: per_device(): lax.all_to_all(outgoing.reshape(blocks, tokens // blocks, 2, HD), 'seq',...]
    all_gather x1 -> x0, waiting for transfers between devices: 16.7 us -> none  [combined_all(): everything = jax.tree.map(lambda part: lax.all_gather(part, axis), array)]
    pallas_call x0 -> x3, Pallas kernels: none -> 10.5 us  [the longest x1 7.53 us: per_device(): pl.pallas_call(attend_kernel, out_shape=(jax.ShapeDtypeStruct((senders, H...]
    dot_general x10 -> x0, matrix products: 6.15 us -> none  [the longest x4 3.3 us: attend_block(): jnp.einsum('rsagk,kad->rsagd', weights.astype(jnp.bfloat16), value_blk, p...]
    reduce_sum x8 -> x0, other arithmetic: 3.86 us -> none  [the longest x4 2.67 us: attend_block(): total_new = total_run * shrink + jnp.sum(weights, axis=-1)]
    all_to_all x1 -> x2, starting transfers between devices: 6.32 us -> 9.97 us  [the longest x1 6.45 us: per_device(): lax.all_to_all(partial, 'seq', split_axis=0, concat_axis=0, tiled=True)]
    dynamic_slice x7 -> x1, local copies, waits for them, and re-layouts: 3.33 us -> 0.9 us  [per_device(): mine = lax.dynamic_slice_in_dim(flat_queries, me * width, width, 0)]
  transfers between devices with their start and end apart: 2 -> 2, of which waited for: 2 -> 2; matrix products, arithmetic and copies ran while one was open for 3% -> 0% of each run, Pallas kernels for 0% -> 5%
where the time goes in v1:
time: 57 us; the launch traced here: 56.6 us
  waiting for transfers between devices  30.7 us (54%)
  Pallas kernels  10.5 us (18%)
  starting transfers between devices  9.97 us (17%)
  local copies, waits for them, and re-layouts  4.72 us (8%)
  between operations  0.7 us (1%)
    all_to_all x1, waiting for transfers between devices, per_device(): lax.all_to_all(outgoing.reshape(blocks, tokens // blocks, 2, HD), 'seq',...  23.3 us
    pallas_call x1, Pallas kernels, per_device(): pl.pallas_call(attend_kernel, out_shape=(jax.ShapeDtypeStruct((senders, H...  7.53 us
    all_to_all x1, waiting for transfers between devices, per_device(): lax.all_to_all(partial, 'seq', split_axis=0, concat_axis=0, tiled=True)  7.41 us
    all_to_all x1, starting transfers between devices, per_device(): lax.all_to_all(partial, 'seq', split_axis=0, concat_axis=0, tiled=True)  6.45 us
    unnamed x19, local copies, waits for them, and re-layouts  3.82 us
    all_to_all x1, starting transfers between devices, per_device(): lax.all_to_all(outgoing.reshape(blocks, tokens // blocks, 2, HD), 'seq',...  3.52 us
    pallas_call x1, Pallas kernels, per_device(): pl.pallas_call(functools.partial(place_kernel, blocks // senders), out_sh...  2.2 us
  transfers between devices with their start and end apart: 2, of which 2 were waited for; matrix products, arithmetic and copies ran while one was open for 0% of the time, Pallas kernels for 5%

profile of v1, /device:TPU:0, one launch (start us, length us, event | category | flops | bytes accessed | tf_op | source)
XLA Modules:
  0.0 56.6 jit_solution(10578186502515406639)
XLA Ops:
  0.6 0.0 copy-start.2
  0.6 0.0 copy-start.4
  0.7 0.9 %constant_dynamic-slice_fusion.mine_ref = bf16[256,128]{1,0:T(8,128)(2,1)S(1)} fusion(bf16[1024,128]{1,0:T(8,128)(2,1)} %bitcast.19, s32[]{:T(128)S(6)} %select_n.3), kind=kLoop, calls=%fused_computation | loop fusion | bytes 131076 | tf_op jit(solution)/shard_map/dynamic_slice | solution.py:228
  1.6 0.0 copy-start.7
  1.6 0.0 copy-start.5
  1.6 0.0 copy-start.6
  1.6 0.0 copy-done.2
  1.6 0.0 copy-done.4
  1.6 0.6 %copy-done.7 = s32[64]{0:T(128)S(1)} copy-done((s32[64]{0:T(128)S(1)}, s32[64]{0:T(128)}, u32[]{:S(2)}) %copy-start.7) | copy-done | bytes 280
  2.2 0.0 copy-done.5
  2.2 0.0 copy-done.6
  2.3 0.0 copy-start
  2.3 1.2 %copy-done = bf16[2048,2,128]{2,1,0:T(2,128)(2,1)S(1)} copy-done((bf16[2048,2,128]{2,1,0:T(2,128)(2,1)S(1)}, bf16[2048,2,128]{2,1,0:T(2,128)(2,1)}, u32[]{:S(2)}) %copy-start) | copy-done | bytes 1048600
  3.5 0.0 copy-start.3
  3.5 0.9 %copy-done.3 = bf16[64,2,1024]{2,1,0:T(2,128)(2,1)S(1)} copy-done((bf16[64,2,1024]{2,1,0:T(2,128)(2,1)S(1)}, bf16[64,2,1024]{2,1,0:T(2,128)(2,1)}, u32[]{:S(2)}) %copy-start.3) | copy-done | bytes 262168
  4.4 0.0 copy-start.1
  4.4 7.5 %attend.1 = (bf16[4,144,256]{2,1,0:T(8,128)(2,1)}, f32[136,256]{1,0:T(8,128)S(1)}) custom-call(s32[1]{0:T(128)} %bitcast.3.position_ref, s32[4]{0:T(128)S(1)} %copy-done.6, s32[64]{0:T(128)S(1)} %copy-done.7, bf16[4096,128]{1,0:T(8,128)(2,1)S(1)} %bitcast.15, f32[256,128]{1,0:T(8,128)S(1)} %bitcast.17, f32[2,128]{1,0:T(2,128)S(1)} %copy-done.5, ...), custom_call_target="tpu_custom_call" | custom-call | tf_op jit(solution)/shard_map/attend/pallas_call | solution.py:229
  12.0 0.0 copy-start.8
  12.0 6.5 %all-to-all-start.1 = ((bf16[4,144,256]{2,1,0:T(8,128)(2,1)}), bf16[4,144,256]{2,1,0:T(8,128)(2,1)S(1)}, u32[]{:S(2)}, u32[]{:S(2)}) async-start(bf16[4,144,256]{2,1,0:T(8,128)(2,1)} %get-tuple-element.4), calls=%async_computation.1 | async-start | bytes 589824 | tf_op jit(solution)/shard_map/all_to_all | solution.py:256
  18.4 0.0 copy-done.1
  18.4 0.0 copy-done.8
  18.4 2.2 %place.1 = bf16[4096,128]{1,0:T(8,128)(2,1)} custom-call(s32[128]{0:T(128)S(1)} %copy-done.8, bf16[4096,128]{1,0:T(8,128)(2,1)S(1)} %bitcast.16, f32[256,128]{1,0:T(8,128)S(1)} %bitcast.18, f32[2,128]{1,0:T(2,128)S(1)} %copy-done.5), custom_call_target="tpu_custom_call" | custom-call | tf_op jit(solution)/shard_map/place/pallas_call | solution.py:215
  20.6 7.4 %all-to-all-done.1.partial_ref = bf16[4,144,256]{2,1,0:T(8,128)(2,1)S(1)} async-done(((bf16[4,144,256]{2,1,0:T(8,128)(2,1)}), bf16[4,144,256]{2,1,0:T(8,128)(2,1)S(1)}, u32[]{:S(2)}, u32[]{:S(2)}) %all-to-all-start.1) | async-done | bytes 294944 | tf_op jit(solution)/shard_map/all_to_all | solution.py:256
  28.0 3.5 %all-to-all-start = ((bf16[128,16,2,128]{3,2,1,0:T(2,128)(2,1)}), bf16[128,16,2,128]{3,2,1,0:T(2,128)(2,1)S(1)}, u32[]{:S(2)}, u32[]{:S(2)}) async-start(bf16[128,16,2,128]{3,2,1,0:T(2,128)(2,1)} %bitcast.2), calls=%async_computation | async-start | bytes 2097152 | tf_op jit(solution)/shard_map/all_to_all | solution.py:224
  31.6 0.8 %join.1 = bf16[256,128]{1,0:T(8,128)(2,1)} custom-call(bf16[4,144,256]{2,1,0:T(8,128)(2,1)S(1)} %all-to-all-done.1.partial_ref, f32[136,256]{1,0:T(8,128)S(1)} %get-tuple-element.5.own_ref), custom_call_target="tpu_custom_call" | custom-call | tf_op jit(solution)/shard_map/join/pallas_call | solution.py:257
  32.4 23.3 %all-to-all-done = bf16[128,16,2,128]{3,2,1,0:T(2,128)(2,1)S(1)} async-done(((bf16[128,16,2,128]{3,2,1,0:T(2,128)(2,1)}), bf16[128,16,2,128]{3,2,1,0:T(2,128)(2,1)S(1)}, u32[]{:S(2)}, u32[]{:S(2)}) %all-to-all-start) | async-done | bytes 1048608 | tf_op jit(solution)/shard_map/all_to_all | solution.py:224
  55.7 1.0 %copy.13 = bf16[128,16,2,128]{3,2,1,0:T(2,128)(2,1)} copy(bf16[128,16,2,128]{3,2,1,0:T(2,128)(2,1)S(1)} %all-to-all-done) | data formatting | bytes 2097152
Async XLA Ops:
  0.6 0.9 %copy-start.2 = (f32[128,2,128]{2,1,0:T(2,128)S(1)}, f32[128,2,128]{2,1,0:T(2,128)}, u32[]{:S(2)}) copy-start(f32[128,2,128]{2,1,0:T(2,128)} %param.12) | copy-start | bytes 393220
  0.6 0.9 %copy-start.4 = (bf16[16,2,2,128]{3,2,1,0:T(2,128)(2,1)S(1)}, bf16[16,2,2,128]{3,2,1,0:T(2,128)(2,1)}, u32[]{:S(2)}) copy-start(bf16[16,2,2,128]{3,2,1,0:T(2,128)(2,1)} %param.15) | copy-start | bytes 49156
  1.6 0.7 %copy-start.7 = (s32[64]{0:T(128)S(1)}, s32[64]{0:T(128)}, u32[]{:S(2)}) copy-start(s32[64]{0:T(128)} %request_ref.1) | copy-start | bytes 772
  1.6 0.7 %copy-start.5 = (f32[2,128]{1,0:T(2,128)S(1)}, f32[2,128]{1,0:T(2,128)}, u32[]{:S(2)}) copy-start(f32[2,128]{1,0:T(2,128)} %scales_ref.3) | copy-start | bytes 3076
  1.6 0.7 %copy-start.6 = (s32[4]{0:T(128)S(1)}, s32[4]{0:T(128)}, u32[]{:S(2)}) copy-start(s32[4]{0:T(128)} %lengths_ref.1) | copy-start | bytes 52
  2.3 1.2 %copy-start = (bf16[2048,2,128]{2,1,0:T(2,128)(2,1)S(1)}, bf16[2048,2,128]{2,1,0:T(2,128)(2,1)}, u32[]{:S(2)}) copy-start(bf16[2048,2,128]{2,1,0:T(2,128)(2,1)} %param.11) | copy-start | bytes 3145732
  3.5 0.9 %copy-start.3 = (bf16[64,2,1024]{2,1,0:T(2,128)(2,1)S(1)}, bf16[64,2,1024]{2,1,0:T(2,128)(2,1)}, u32[]{:S(2)}) copy-start(bf16[64,2,1024]{2,1,0:T(2,128)(2,1)} %param.14) | copy-start | bytes 786436
  4.4 14.0 %copy-start.1 = (bf16[2048,2,128]{2,1,0:T(2,128)(2,1)S(1)}, bf16[2048,2,128]{2,1,0:T(2,128)(2,1)}, u32[]{:S(2)}) copy-start(bf16[2048,2,128]{2,1,0:T(2,128)(2,1)} %param.11) | copy-start | bytes 3145732
  12.0 6.5 %copy-start.8 = (s32[128]{0:T(128)S(1)}, s32[128]{0:T(128)}, u32[]{:S(2)}) copy-start(s32[128]{0:T(128)} %owner_ref.1) | copy-start | bytes 1540
  12.0 16.1 %all-to-all-start.1 = ((bf16[4,144,256]{2,1,0:T(8,128)(2,1)}), bf16[4,144,256]{2,1,0:T(8,128)(2,1)S(1)}, u32[]{:S(2)}, u32[]{:S(2)}) async-start(bf16[4,144,256]{2,1,0:T(8,128)(2,1)} %get-tuple-element.4), calls=%async_computation.1 | async-start | bytes 589824 | tf_op jit(solution)/shard_map/all_to_all | solution.py:256
  28.0 27.6 %all-to-all-start = ((bf16[128,16,2,128]{3,2,1,0:T(2,128)(2,1)}), bf16[128,16,2,128]{3,2,1,0:T(2,128)(2,1)S(1)}, u32[]{:S(2)}, u32[]{:S(2)}) async-start(bf16[128,16,2,128]{3,2,1,0:T(2,128)(2,1)} %bitcast.2), calls=%async_computation | async-start | bytes 2097152 | tf_op jit(solution)/shard_map/all_to_all | solution.py:224

commit v2 on v1

--- a/solution.py
+++ b/solution.py
@@ -52,14 +52,13 @@
 
 
 def attend_kernel(
-    position_ref,
+    me_ref,
     lengths_ref,
     request_ref,
     deltas_ref,
     anchors_ref,
     scales_ref,
     queries_ref,
-    mine_ref,
     new_ref,
     out_ref,
     own_ref,
@@ -95,7 +94,7 @@
     lane = lax.broadcasted_iota(jnp.int32, (1, HD), 1)
     first = jnp.zeros((1, HD), jnp.int32)
     last = jnp.zeros((1, HD), jnp.int32)
-    end = 0 - position_ref[0]
+    end = 0 - me_ref[0] * (blocks * tokens)
     for request in range(requests):
         start = end
         end = end + lengths_ref[request]
@@ -145,7 +144,7 @@
 
     fresh = new_ref.shape[0] // 4
     new = new_ref[...].astype(jnp.float32).reshape(fresh, 4, HD)
-    mine = mine_ref[...]
+    mine = queries_ref[pl.ds(pl.multiple_of(me_ref[0] * width, width), width), :]
     of_row = lax.broadcasted_iota(jnp.int32, (fresh, width), 1) // (GQ * STEPS)
     same = of_row == lax.broadcasted_iota(jnp.int32, (fresh, width), 0)
     step = lax.broadcasted_iota(jnp.int32, (1, width), 1) % STEPS
@@ -221,18 +220,17 @@
         compiler_params=limit,
         name="place",
     )(owner_map, flat_deltas, flat_anchors, scales)
+    outgoing, late_deltas = lax.optimization_barrier((outgoing, flat_deltas))
     pages = lax.all_to_all(
         outgoing.reshape(blocks, tokens // blocks, 2, HD), "seq", split_axis=0, concat_axis=0, tiled=True
     )
-
-    mine = lax.dynamic_slice_in_dim(flat_queries, me * width, width, 0)
     partial, own = pl.pallas_call(
         attend_kernel,
         out_shape=(
             jax.ShapeDtypeStruct((senders, HD + STAT_ROWS, width), jnp.bfloat16),
             jax.ShapeDtypeStruct((HD + 8, width), jnp.float32),
         ),
-        in_specs=[SMEM, SMEM, SMEM] + [VMEM] * 6,
+        in_specs=[SMEM, SMEM, SMEM] + [VMEM] * 5,
         out_specs=(VMEM, VMEM),
         scratch_shapes=[
             pltpu.VMEM((tokens * 2, HD), jnp.float32),
@@ -243,14 +241,13 @@
         compiler_params=limit,
         name="attend",
     )(
-        (me * tokens).astype(jnp.int32).reshape(1),
+        me.astype(jnp.int32).reshape(1),
         lengths,
         row_request,
-        flat_deltas,
+        late_deltas,
         flat_anchors,
         scales,
         flat_queries,
-        mine,
         flat_new,
     )
     received = lax.all_to_all(partial, "seq", split_axis=0, concat_axis=0, tiled=True)

time: 57 us -> 58.2 us (1.021)
  blocking collectives: 0 us -> 15.7 us
  waiting for transfers between devices: 30.7 us -> 23.4 us
  starting transfers between devices: 9.97 us -> 3.52 us
    all_to_all x0 -> x1, blocking collectives: none -> 15.7 us  [per_device(): lax.all_to_all(partial, 'seq', split_axis=0, concat_axis=0, tiled=True)]
    all_to_all x1 -> x0, waiting for transfers between devices: 7.41 us -> none  [per_device(): lax.all_to_all(partial, 'seq', split_axis=0, concat_axis=0, tiled=True)]
    all_to_all x1 -> x0, starting transfers between devices: 6.45 us -> none  [per_device(): lax.all_to_all(partial, 'seq', split_axis=0, concat_axis=0, tiled=True)]
    dynamic_slice x1 -> x0, local copies, waits for them, and re-layouts: 0.9 us -> none  [per_device(): mine = lax.dynamic_slice_in_dim(flat_queries, me * width, width, 0)]
    unnamed x19 -> x21, local copies, waits for them, and re-layouts: 3.82 us -> 4.42 us
  transfers between devices with their start and end apart: 2 -> 1, of which waited for: 2 -> 1; matrix products, arithmetic and copies ran while one was open for 0% -> 0% of each run, Pallas kernels for 5% -> 1%
where the time goes in v2:
time: 58.2 us; the launch traced here: 57.9 us
  waiting for transfers between devices  23.4 us (40%)
  blocking collectives  15.7 us (27%)
  Pallas kernels  10.2 us (18%)
  local copies, waits for them, and re-layouts  4.42 us (8%)
  starting transfers between devices  3.52 us (6%)
  between operations  0.7 us (1%)
    all_to_all x1, waiting for transfers between devices, per_device(): lax.all_to_all(outgoing.reshape(blocks, tokens // blocks, 2, HD), 'seq',...  23.4 us
    all_to_all x1, blocking collectives, per_device(): lax.all_to_all(partial, 'seq', split_axis=0, concat_axis=0, tiled=True)  15.7 us
    pallas_call x1, Pallas kernels, per_device(): pl.pallas_call(attend_kernel, out_shape=(jax.ShapeDtypeStruct((senders, H...  7.18 us
    unnamed x21, local copies, waits for them, and re-layouts  4.42 us
    all_to_all x1, starting transfers between devices, per_device(): lax.all_to_all(outgoing.reshape(blocks, tokens // blocks, 2, HD), 'seq',...  3.52 us
    pallas_call x1, Pallas kernels, per_device(): pl.pallas_call(functools.partial(place_kernel, blocks // senders), out_sh...  2.21 us
  transfers between devices with their start and end apart: 1, of which 1 were waited for; matrix products, arithmetic and copies ran while one was open for 0% of the time, Pallas kernels for 1%

profile of v2, /device:TPU:0, one launch (start us, length us, event | category | flops | bytes accessed | tf_op | source)
XLA Modules:
  0.0 57.9 jit_solution(566685546372403083)
XLA Ops:
  0.6 0.0 copy-start.6
  0.6 0.0 copy-start.7
  0.7 0.7 %copy-done.6 = f32[2,128]{1,0:T(2,128)S(1)} copy-done((f32[2,128]{1,0:T(2,128)S(1)}, f32[2,128]{1,0:T(2,128)}, u32[]{:S(2)}) %copy-start.6) | copy-done | bytes 1048
  1.3 0.0 copy-done.7
  1.3 0.0 copy-start
  1.3 1.2 %copy-done = bf16[2048,2,128]{2,1,0:T(2,128)(2,1)S(1)} copy-done((bf16[2048,2,128]{2,1,0:T(2,128)(2,1)S(1)}, bf16[2048,2,128]{2,1,0:T(2,128)(2,1)}, u32[]{:S(2)}) %copy-start) | copy-done | bytes 1048600
  2.5 0.0 copy-start.2
  2.5 0.9 %copy-done.2 = f32[128,2,128]{2,1,0:T(2,128)S(1)} copy-done((f32[128,2,128]{2,1,0:T(2,128)S(1)}, f32[128,2,128]{2,1,0:T(2,128)}, u32[]{:S(2)}) %copy-start.2) | copy-done | bytes 131096
  3.4 0.0 copy-start.1
  3.5 0.0 copy-start.3
  3.5 0.0 copy-start.4
  3.5 0.0 copy-start.5
  3.5 2.2 %place.1 = bf16[4096,128]{1,0:T(8,128)(2,1)} custom-call(s32[128]{0:T(128)S(1)} %copy-done.7, bf16[4096,128]{1,0:T(8,128)(2,1)S(1)} %bitcast.15, f32[256,128]{1,0:T(8,128)S(1)} %bitcast.17, f32[2,128]{1,0:T(2,128)S(1)} %copy-done.6), custom_call_target="tpu_custom_call" | custom-call | tf_op jit(solution)/shard_map/place/pallas_call | solution.py:214
  5.7 0.0 copy-start.8
  5.7 0.0 copy-start.9
  5.7 0.0 copy-done.1
  5.7 0.0 copy-done.3
  5.7 0.0 copy-done.4
  5.7 0.0 copy-done.5
  5.7 0.6 %copy-done.8 = s32[4]{0:T(128)S(1)} copy-done((s32[4]{0:T(128)S(1)}, s32[4]{0:T(128)}, u32[]{:S(2)}) %copy-start.8) | copy-done | bytes 40
  6.3 0.0 copy-done.9
  6.3 7.2 %attend.1 = (bf16[4,144,256]{2,1,0:T(8,128)(2,1)S(1)}, f32[136,256]{1,0:T(8,128)S(1)}) custom-call(s32[1]{0:T(128)} %bitcast.3.me_ref, s32[4]{0:T(128)S(1)} %copy-done.8, s32[64]{0:T(128)S(1)} %copy-done.9, bf16[4096,128]{1,0:T(8,128)(2,1)S(1)} %bitcast.16, f32[256,128]{1,0:T(8,128)S(1)} %bitcast.18, f32[2,128]{1,0:T(2,128)S(1)} %copy-done.6, ...), custom_call_target="tpu_custom_call" | custom-call | tf_op jit(solution)/shard_map/attend/pallas_call | solution.py:227
  13.5 15.7 %all_to_all.10.partial_ref = bf16[4,144,256]{2,1,0:T(8,128)(2,1)S(1)} all-to-all(bf16[4,144,256]{2,1,0:T(8,128)(2,1)S(1)} %get-tuple-element.8), channel_id=1, replica_groups=mesh['groups'=2,'seq'=4,'tp'=4] {'seq'}, dimensions={0} | all-to-all | bytes 589824 | tf_op jit(solution)/shard_map/all_to_all | solution.py:253
  29.2 3.5 %all-to-all-start = ((bf16[128,16,2,128]{3,2,1,0:T(2,128)(2,1)}), bf16[128,16,2,128]{3,2,1,0:T(2,128)(2,1)S(1)}, u32[]{:S(2)}, u32[]{:S(2)}) async-start(bf16[128,16,2,128]{3,2,1,0:T(2,128)(2,1)} %bitcast.2), calls=%async_computation | async-start | bytes 2097152 | tf_op jit(solution)/shard_map/all_to_all | solution.py:224
  32.7 0.8 %join.1 = bf16[256,128]{1,0:T(8,128)(2,1)} custom-call(bf16[4,144,256]{2,1,0:T(8,128)(2,1)S(1)} %all_to_all.10.partial_ref, f32[136,256]{1,0:T(8,128)S(1)} %get-tuple-element.9.own_ref), custom_call_target="tpu_custom_call" | custom-call | tf_op jit(solution)/shard_map/join/pallas_call | solution.py:254
  33.5 23.4 %all-to-all-done = bf16[128,16,2,128]{3,2,1,0:T(2,128)(2,1)S(1)} async-done(((bf16[128,16,2,128]{3,2,1,0:T(2,128)(2,1)}), bf16[128,16,2,128]{3,2,1,0:T(2,128)(2,1)S(1)}, u32[]{:S(2)}, u32[]{:S(2)}) %all-to-all-start) | async-done | bytes 1048608 | tf_op jit(solution)/shard_map/all_to_all | solution.py:224
  56.9 1.0 %copy.13 = bf16[128,16,2,128]{3,2,1,0:T(2,128)(2,1)} copy(bf16[128,16,2,128]{3,2,1,0:T(2,128)(2,1)S(1)} %all-to-all-done) | data formatting | bytes 2097152
Async XLA Ops:
  0.6 0.7 %copy-start.6 = (f32[2,128]{1,0:T(2,128)S(1)}, f32[2,128]{1,0:T(2,128)}, u32[]{:S(2)}) copy-start(f32[2,128]{1,0:T(2,128)} %scales_ref.3) | copy-start | bytes 3076
  0.6 0.7 %copy-start.7 = (s32[128]{0:T(128)S(1)}, s32[128]{0:T(128)}, u32[]{:S(2)}) copy-start(s32[128]{0:T(128)} %owner_ref.1) | copy-start | bytes 1540
  1.3 1.2 %copy-start = (bf16[2048,2,128]{2,1,0:T(2,128)(2,1)S(1)}, bf16[2048,2,128]{2,1,0:T(2,128)(2,1)}, u32[]{:S(2)}) copy-start(bf16[2048,2,128]{2,1,0:T(2,128)(2,1)} %param.11) | copy-start | bytes 3145732
  2.5 0.9 %copy-start.2 = (f32[128,2,128]{2,1,0:T(2,128)S(1)}, f32[128,2,128]{2,1,0:T(2,128)}, u32[]{:S(2)}) copy-start(f32[128,2,128]{2,1,0:T(2,128)} %param.12) | copy-start | bytes 393220
  3.4 2.2 %copy-start.1 = (bf16[2048,2,128]{2,1,0:T(2,128)(2,1)S(1)}, bf16[2048,2,128]{2,1,0:T(2,128)(2,1)}, u32[]{:S(2)}) copy-start(bf16[2048,2,128]{2,1,0:T(2,128)(2,1)} %param.11) | copy-start | bytes 3145732
  3.5 2.2 %copy-start.3 = (f32[128,2,128]{2,1,0:T(2,128)S(1)}, f32[128,2,128]{2,1,0:T(2,128)}, u32[]{:S(2)}) copy-start(f32[128,2,128]{2,1,0:T(2,128)} %param.12) | copy-start | bytes 393220
  3.5 2.2 %copy-start.4 = (bf16[64,2,1024]{2,1,0:T(2,128)(2,1)S(1)}, bf16[64,2,1024]{2,1,0:T(2,128)(2,1)}, u32[]{:S(2)}) copy-start(bf16[64,2,1024]{2,1,0:T(2,128)(2,1)} %param.14) | copy-start | bytes 786436
  3.5 2.2 %copy-start.5 = (bf16[16,2,2,128]{3,2,1,0:T(2,128)(2,1)S(1)}, bf16[16,2,2,128]{3,2,1,0:T(2,128)(2,1)}, u32[]{:S(2)}) copy-start(bf16[16,2,2,128]{3,2,1,0:T(2,128)(2,1)} %param.15) | copy-start | bytes 49156
  5.7 0.7 %copy-start.8 = (s32[4]{0:T(128)S(1)}, s32[4]{0:T(128)}, u32[]{:S(2)}) copy-start(s32[4]{0:T(128)} %lengths_ref.1) | copy-start | bytes 52
  5.7 0.7 %copy-start.9 = (s32[64]{0:T(128)S(1)}, s32[64]{0:T(128)}, u32[]{:S(2)}) copy-start(s32[64]{0:T(128)} %request_ref.1) | copy-start | bytes 772
  29.2 27.7 %all-to-all-start = ((bf16[128,16,2,128]{3,2,1,0:T(2,128)(2,1)}), bf16[128,16,2,128]{3,2,1,0:T(2,128)(2,1)S(1)}, u32[]{:S(2)}, u32[]{:S(2)}) async-start(bf16[128,16,2,128]{3,2,1,0:T(2,128)(2,1)} %bitcast.2), calls=%async_computation | async-start | bytes 2097152 | tf_op jit(solution)/shard_map/all_to_all | solution.py:224

commit v3 on v2

--- a/solution.py
+++ b/solution.py
@@ -15,32 +15,107 @@
 RATE = HD ** (-0.5) * 1.4426950408889634
 
 VMEM = pl.BlockSpec(memory_space=pltpu.VMEM)
+ANY = pl.BlockSpec(memory_space=pl.ANY)
 SMEM = pl.BlockSpec(memory_space=pltpu.SMEM)
 
 
-def place_kernel(capacity, owner_ref, deltas_ref, anchors_ref, scales_ref, out_ref, count_ref):
+def partner(me, k, count):
+    if count & (count - 1) == 0:
+        return me ^ k
+    return lax.rem(me + k, count)
+
+
+def source_of(me, k, count):
+    if count & (count - 1) == 0:
+        return me ^ k
+    return lax.rem(me + count - k, count)
+
+
+def exchange(sent, count):
+    got = []
+    for k, message in enumerate(sent, start=1):
+        power = count & (count - 1) == 0
+        pairs = [(i, i ^ k if power else (i + k) % count) for i in range(count)]
+        got.append(lax.ppermute(message, "seq", pairs))
+    return got
+
+
+def place_kernel(owner_any, deltas_any, anchors_any, scales_any, *refs):
+    receivers = lax.axis_size("seq")
+    me = lax.axis_index("seq")
+    sent, pages = refs[: receivers - 1], refs[receivers - 1]
+    owner_ref, source_ref, count_ref, deltas_ref, anchors_ref, scales_ref, placed_ref, sems = refs[receivers:]
     blocks = owner_ref.shape[0]
     rows = deltas_ref.shape[0] // blocks
-    for owner in range(count_ref.shape[0]):
+    capacity = blocks // receivers
+    loads = [
+        pltpu.make_async_copy(source, target, sems.at[index])
+        for index, (source, target) in enumerate(
+            [
+                (owner_any, owner_ref),
+                (scales_any, scales_ref),
+                (anchors_any, anchors_ref),
+                (deltas_any, deltas_ref),
+            ]
+        )
+    ]
+    for load in loads:
+        load.start()
+    for owner in range(receivers):
         count_ref[owner] = owner * capacity
-    odd = lax.broadcasted_iota(jnp.int32, (8, HD), 0) % 2 == 1
-    scale = jnp.where(odd, scales_ref[1:2, :], scales_ref[0:1, :])[None]
-
-    def one_block(block, carry):
+    loads[0].wait()
+
+    def find(block, carry):
         owner = owner_ref[block]
         slot = count_ref[owner]
         count_ref[owner] = slot + 1
-        anchor = jnp.where(
-            odd, anchors_ref[pl.ds(2 * block + 1, 1), :], anchors_ref[pl.ds(2 * block, 1), :]
-        )[None]
-        delta = deltas_ref[pl.ds(block * rows, rows), :].astype(jnp.float32)
-        decoded = anchor + scale * delta.reshape(rows // 8, 8, HD)
-        out_ref[pl.ds(pl.multiple_of(slot * rows, rows), rows), :] = decoded.reshape(rows, HD).astype(
-            jnp.bfloat16
-        )
+        source_ref[slot] = block
         return carry
 
-    lax.fori_loop(0, blocks, one_block, 0, unroll=4)
+    lax.fori_loop(0, blocks, find, 0, unroll=8)
+    for load in loads[1:]:
+        load.wait()
+    odd = lax.broadcasted_iota(jnp.int32, (8, HD), 0) % 2 == 1
+    scale = jnp.where(odd, scales_ref[1:2, :], scales_ref[0:1, :])[None]
+    stores = []
+    for k in reversed(range(receivers)):
+        first = partner(me, k, receivers) * capacity
+
+        def one_slot(slot, carry, k=k, first=first):
+            block = source_ref[first + slot]
+            anchor = jnp.where(
+                odd, anchors_ref[pl.ds(2 * block + 1, 1), :], anchors_ref[pl.ds(2 * block, 1), :]
+            )[None]
+            here = pl.ds(pl.multiple_of(block * rows, rows), rows)
+            delta = deltas_ref[here, :].astype(jnp.float32)
+            decoded = anchor + scale * delta.reshape(rows // 8, 8, HD)
+            placed_ref[k, pl.ds(pl.multiple_of(slot * rows, rows), rows), :] = decoded.reshape(
+                rows, HD
+            ).astype(jnp.bfloat16)
+            return carry
+
+        lax.fori_loop(0, capacity, one_slot, 0, unroll=min(8, capacity))
+        own = pages.at[pl.ds(pl.multiple_of(me * capacity * rows, capacity * rows), capacity * rows), :]
+        store = pltpu.make_async_copy(placed_ref.at[k], sent[k - 1] if k else own, sems.at[4 + k])
+        store.start()
+        stores.append(store)
+    for store in stores:
+        store.wait()
+
+
+def settle_kernel(*refs):
+    receivers = lax.axis_size("seq")
+    me = lax.axis_index("seq")
+    got, pages, sems = refs[1:receivers], refs[receivers], refs[receivers + 1]
+    size = got[0].shape[0]
+    copies = []
+    for k in range(1, receivers):
+        first = pl.multiple_of(source_of(me, k, receivers) * size, size)
+        copy = pltpu.make_async_copy(got[k - 1], pages.at[pl.ds(first, size), :], sems.at[k - 1])
+        copy.start()
+        copies.append(copy)
+    for copy in copies:
+        copy.wait()
 
 
 def pieces(values):
@@ -52,7 +127,6 @@
 
 
 def attend_kernel(
-    me_ref,
     lengths_ref,
     request_ref,
     deltas_ref,
@@ -60,20 +134,19 @@
     scales_ref,
     queries_ref,
     new_ref,
-    out_ref,
-    own_ref,
-    wide_ref,
-    keys_ref,
-    values_ref,
-    asked_ref,
+    *refs,
 ):
+    receivers = lax.axis_size("seq")
+    me = lax.axis_index("seq")
+    outs = refs[:receivers]
+    own_ref, wide_ref, keys_ref, values_ref, asked_ref, out_ref, sems = refs[receivers:]
     blocks = anchors_ref.shape[0] // 2
     rows = deltas_ref.shape[0] // blocks
     tokens = rows // 2
     requests = lengths_ref.shape[0]
     asked = queries_ref.shape[0]
     per_row = asked // request_ref.shape[0]
-    receivers, _, width = out_ref.shape
+    width = out_ref.shape[2]
 
     wide_ref[...] = deltas_ref[...].astype(jnp.float32)
     scale_key = scales_ref[0:1, :]
@@ -94,7 +167,7 @@
     lane = lax.broadcasted_iota(jnp.int32, (1, HD), 1)
     first = jnp.zeros((1, HD), jnp.int32)
     last = jnp.zeros((1, HD), jnp.int32)
-    end = 0 - me_ref[0] * (blocks * tokens)
+    end = 0 - me * (blocks * tokens)
     for request in range(requests):
         start = end
         end = end + lengths_ref[request]
@@ -142,9 +215,15 @@
 
     lax.fori_loop(0, asked // tile, one_tile, 0)
 
+    stores = []
+    for k in range(receivers):
+        copy = pltpu.make_async_copy(out_ref.at[partner(me, k, receivers)], outs[k], sems.at[k])
+        copy.start()
+        stores.append(copy)
+
     fresh = new_ref.shape[0] // 4
     new = new_ref[...].astype(jnp.float32).reshape(fresh, 4, HD)
-    mine = queries_ref[pl.ds(pl.multiple_of(me_ref[0] * width, width), width), :]
+    mine = queries_ref[pl.ds(pl.multiple_of(me * width, width), width), :]
     of_row = lax.broadcasted_iota(jnp.int32, (fresh, width), 1) // (GQ * STEPS)
     same = of_row == lax.broadcasted_iota(jnp.int32, (fresh, width), 0)
     step = lax.broadcasted_iota(jnp.int32, (1, width), 1) % STEPS
@@ -175,24 +254,26 @@
     own_ref[HD:, :] = jnp.concatenate(
         [own_top, own_total, jnp.zeros((6, width), jnp.float32)], axis=0
     )
-
-
-def join_kernel(partial_ref, own_ref, out_ref):
-    senders = partial_ref.shape[0]
+    for copy in stores:
+        copy.wait()
+
+
+def join_kernel(own_ref, *refs):
+    partials, out_ref = refs[:-1], refs[-1]
     tops = [own_ref[HD : HD + 1, :]]
     totals = [own_ref[HD + 1 : HD + 2, :]]
-    for sender in range(senders):
-        stats = partial_ref[sender, HD:, :].astype(jnp.float32)
+    for partial_ref in partials:
+        stats = partial_ref[HD:, :].astype(jnp.float32)
         tops.append(stats[0:1] + stats[1:2] + stats[2:3])
         totals.append(stats[3:4] + stats[4:5] + stats[5:6])
     top = functools.reduce(jnp.maximum, tops)
     scale = jnp.exp2((tops[0] - top) * RATE)
     total = totals[0] * scale
     summed = own_ref[0:HD, :] * scale
-    for sender in range(senders):
-        scale = jnp.exp2((tops[sender + 1] - top) * RATE)
-        total = total + totals[sender + 1] * scale
-        summed = summed + partial_ref[sender, 0:HD, :].astype(jnp.float32) * scale
+    for index, partial_ref in enumerate(partials, start=1):
+        scale = jnp.exp2((tops[index] - top) * RATE)
+        total = total + totals[index] * scale
+        summed = summed + partial_ref[0:HD, :].astype(jnp.float32) * scale
     out_ref[...] = (summed / total).T.astype(jnp.bfloat16)
 
 
@@ -204,61 +285,78 @@
     rows, steps, _ = queries.shape
     rows_dev = new_kv.shape[0]
     width = rows_dev * GQ * steps
-    limit = pltpu.CompilerParams(vmem_limit_bytes=48 * 1024 * 1024)
+    limit = pltpu.CompilerParams(vmem_limit_bytes=60 * 1024 * 1024)
+    small = pltpu.CompilerParams(vmem_limit_bytes=8 * 1024 * 1024)
 
     flat_deltas = deltas.reshape(tokens * 2, HD)
     flat_anchors = anchors.reshape(blocks * 2, HD)
     flat_queries = queries.reshape(rows, steps, GQ, HD).transpose(0, 2, 1, 3).reshape(-1, HD)
     flat_new = new_kv.reshape(rows_dev * 4, HD)
 
-    outgoing = pl.pallas_call(
-        functools.partial(place_kernel, blocks // senders),
-        out_shape=jax.ShapeDtypeStruct(flat_deltas.shape, jnp.bfloat16),
-        in_specs=[SMEM, VMEM, VMEM, VMEM],
-        out_specs=VMEM,
-        scratch_shapes=[pltpu.SMEM((senders,), jnp.int32)],
+    hand = jax.ShapeDtypeStruct((tokens * 2 // senders, HD), jnp.bfloat16)
+    *sent, pages = pl.pallas_call(
+        place_kernel,
+        out_shape=[hand] * (senders - 1) + [jax.ShapeDtypeStruct((tokens * 2, HD), jnp.bfloat16)],
+        in_specs=[ANY] * 4,
+        out_specs=[ANY] * senders,
+        scratch_shapes=[
+            pltpu.SMEM((blocks,), jnp.int32),
+            pltpu.SMEM((blocks,), jnp.int32),
+            pltpu.SMEM((senders,), jnp.int32),
+            pltpu.VMEM((tokens * 2, HD), jnp.bfloat16),
+            pltpu.VMEM((blocks * 2, HD), jnp.float32),
+            pltpu.VMEM((2, HD), jnp.float32),
+            pltpu.VMEM((senders, tokens * 2 // senders, HD), jnp.bfloat16),
+            pltpu.SemaphoreType.DMA((4 + senders,)),
+        ],
         compiler_params=limit,
         name="place",
     )(owner_map, flat_deltas, flat_anchors, scales)
-    outgoing, late_deltas = lax.optimization_barrier((outgoing, flat_deltas))
-    pages = lax.all_to_all(
-        outgoing.reshape(blocks, tokens // blocks, 2, HD), "seq", split_axis=0, concat_axis=0, tiled=True
-    )
-    partial, own = pl.pallas_call(
+    sent, late_deltas = lax.optimization_barrier((sent, flat_deltas))
+    got = exchange(sent, senders)
+
+    *partials, own = pl.pallas_call(
         attend_kernel,
-        out_shape=(
-            jax.ShapeDtypeStruct((senders, HD + STAT_ROWS, width), jnp.bfloat16),
-            jax.ShapeDtypeStruct((HD + 8, width), jnp.float32),
-        ),
-        in_specs=[SMEM, SMEM, SMEM] + [VMEM] * 5,
-        out_specs=(VMEM, VMEM),
+        out_shape=[jax.ShapeDtypeStruct((HD + STAT_ROWS, width), jnp.bfloat16)] * senders
+        + [jax.ShapeDtypeStruct((HD + 8, width), jnp.float32)],
+        in_specs=[SMEM, SMEM] + [VMEM] * 5,
+        out_specs=[ANY] * senders + [VMEM],
         scratch_shapes=[
             pltpu.VMEM((tokens * 2, HD), jnp.float32),
             pltpu.VMEM((tokens, 2 * HD), jnp.bfloat16),
             pltpu.VMEM((tokens, HD), jnp.bfloat16),
             pltpu.VMEM((rows * GQ * steps, 2 * HD), jnp.bfloat16),
+            pltpu.VMEM((senders, HD + STAT_ROWS, width), jnp.bfloat16),
+            pltpu.SemaphoreType.DMA((senders,)),
         ],
         compiler_params=limit,
+        cost_estimate=pl.CostEstimate(
+            flops=6 * rows * GQ * steps * tokens * HD,
+            bytes_accessed=tokens * 4 * HD + rows * GQ * steps * 4 * HD,
+            transcendentals=rows * GQ * steps * tokens,
+        ),
         name="attend",
-    )(
-        me.astype(jnp.int32).reshape(1),
-        lengths,
-        row_request,
-        late_deltas,
-        flat_anchors,
-        scales,
-        flat_queries,
-        flat_new,
-    )
-    received = lax.all_to_all(partial, "seq", split_axis=0, concat_axis=0, tiled=True)
+    )(lengths, row_request, late_deltas, flat_anchors, scales, flat_queries, flat_new)
+    joined = [partials[0]] + exchange(partials[1:], senders)
     attended = pl.pallas_call(
         join_kernel,
         out_shape=jax.ShapeDtypeStruct((width, HD), jnp.bfloat16),
-        in_specs=[VMEM, VMEM],
+        in_specs=[VMEM] * (senders + 1),
         out_specs=VMEM,
-        compiler_params=limit,
+        compiler_params=small,
         name="join",
-    )(received, own)
+    )(own, *joined)
+    pages = pl.pallas_call(
+        settle_kernel,
+        out_shape=jax.ShapeDtypeStruct((tokens * 2, HD), jnp.bfloat16),
+        in_specs=[ANY] * senders,
+        out_specs=ANY,
+        scratch_shapes=[pltpu.SemaphoreType.DMA((senders - 1,))],
+        input_output_aliases={0: 0},
+        compiler_params=small,
+        name="settle",
+    )(pages, *got)
+    pages = pages.reshape(blocks, tokens // blocks, 2, HD)
     attended = (
         attended.reshape(rows_dev, GQ, steps, HD).transpose(0, 2, 1, 3).reshape(rows_dev, steps, GQ * HD)
     )

time: 58.2 us -> 41.4 us (0.71)
  blocking collectives: 15.7 us -> 0 us
  waiting for transfers between devices: 23.4 us -> 12.7 us
  starting transfers between devices: 3.52 us -> 12.7 us
  Pallas kernels: 10.2 us -> 13.4 us
  local copies, waits for them, and re-layouts: 4.42 us -> 1.79 us
    all_to_all x1 -> x0, waiting for transfers between devices: 23.4 us -> none  [per_device(): lax.all_to_all(outgoing.reshape(blocks, tokens // blocks, 2, HD), 'seq',...]
    all_to_all x1 -> x0, blocking collectives: 15.7 us -> none  [per_device(): lax.all_to_all(partial, 'seq', split_axis=0, concat_axis=0, tiled=True)]
    ppermute x0 -> x6, starting transfers between devices: none -> 12.7 us  [exchange(): got.append(lax.ppermute(message, 'seq', pairs))]
    ppermute x0 -> x6, waiting for transfers between devices: none -> 12.7 us  [exchange(): got.append(lax.ppermute(message, 'seq', pairs))]
    all_to_all x1 -> x0, starting transfers between devices: 3.52 us -> none  [per_device(): lax.all_to_all(outgoing.reshape(blocks, tokens // blocks, 2, HD), 'seq',...]
    pallas_call x2 -> x3, Pallas kernels: 9.38 us -> 12.6 us  [the longest x1 9.08 us: per_device(): pl.pallas_call(attend_kernel, out_shape=[jax.ShapeDtypeStruct((HD + STAT_...]
    unnamed x21 -> x4, local copies, waits for them, and re-layouts: 4.42 us -> 1.79 us
  transfers between devices with their start and end apart: 1 -> 6, of which waited for: 1 -> 2; matrix products, arithmetic and copies ran while one was open for 0% -> 0% of each run, Pallas kernels for 1% -> 24%
where the time goes in v3:
time: 41.4 us; the launch traced here: 41.2 us
  Pallas kernels  13.4 us (32%)
  starting transfers between devices  12.7 us (31%)
  waiting for transfers between devices  12.7 us (31%)
  local copies, waits for them, and re-layouts  1.79 us (4%)
  between operations  0.66 us (2%)
    ppermute x6, starting transfers between devices, exchange(): got.append(lax.ppermute(message, 'seq', pairs))  12.7 us
    ppermute x6, waiting for transfers between devices, exchange(): got.append(lax.ppermute(message, 'seq', pairs))  12.7 us
    pallas_call x1, Pallas kernels, per_device(): pl.pallas_call(attend_kernel, out_shape=[jax.ShapeDtypeStruct((HD + STAT_...  9.08 us
    pallas_call x1, Pallas kernels, per_device(): pl.pallas_call(place_kernel, out_shape=[hand] * (senders - 1) + [jax.Shap...  2.62 us
    unnamed x4, local copies, waits for them, and re-layouts  1.79 us
    pallas_call x1, Pallas kernels, per_device(): pl.pallas_call(settle_kernel, out_shape=jax.ShapeDtypeStruct((tokens * 2,...  0.92 us
  transfers between devices with their start and end apart: 6, of which 2 were waited for; matrix products, arithmetic and copies ran while one was open for 0% of the time, Pallas kernels for 24%

profile of v3, /device:TPU:0, one launch (start us, length us, event | category | flops | bytes accessed | tf_op | source)
XLA Modules:
  0.0 41.2 jit_solution(12395195741267935426)
XLA Ops:
  0.6 2.6 %place.1 = (bf16[1024,128]{1,0:T(8,128)(2,1)}, bf16[1024,128]{1,0:T(8,128)(2,1)}, bf16[1024,128]{1,0:T(8,128)(2,1)}, bf16[4096,128]{1,0:T(8,128)(2,1)}) custom-call(s32[128]{0:T(128)} %owner_any.1, bf16[4096,128]{1,0:T(8,128)(2,1)} %bitcast.14, f32[256,128]{1,0:T(8,128)} %bitcast.17, f32[2,128]{1,0:T(2,128)} %scales_ref.1), custom_call_target="tpu_custom_call" | custom-call | tf_op jit(solution)/shard_map/place/pallas_call | solution.py:297
  3.3 3.1 %collective-permute-start = (bf16[1024,128]{1,0:T(8,128)(2,1)}, bf16[1024,128]{1,0:T(8,128)(2,1)S(1)}, u32[]{:S(2)}, u32[]{:S(2)}) collective-permute-start(bf16[1024,128]{1,0:T(8,128)(2,1)} %get-tuple-element.19), channel_id=1, source_target_pairs={{0,4},{4,0},{8,12},{12,8},{1,5},{5,1},{9,13},{13,9},{2,6},{6,2},{1... | collective-permute-start | bytes 786440 | tf_op jit(solution)/shard_map/ppermute | solution.py:39
  6.3 2.6 %collective-permute-start.1 = (bf16[1024,128]{1,0:T(8,128)(2,1)}, bf16[1024,128]{1,0:T(8,128)(2,1)S(1)}, u32[]{:S(2)}, u32[]{:S(2)}) collective-permute-start(bf16[1024,128]{1,0:T(8,128)(2,1)} %get-tuple-element.20), channel_id=1, source_target_pairs={{0,8},{4,12},{8,0},{12,4},{1,9},{5,13},{9,1},{13,5},{2,10},{6,14},... | collective-permute-start | bytes 786440 | tf_op jit(solution)/shard_map/ppermute | solution.py:39
  8.9 0.0 collective-permute-start.2
  8.9 9.1 %attend.1 = (bf16[144,256]{1,0:T(8,128)(2,1)}, bf16[144,256]{1,0:T(8,128)(2,1)}, bf16[144,256]{1,0:T(8,128)(2,1)}, bf16[144,256]{1,0:T(8,128)(2,1)}, f32[136,256]{1,0:T(8,128)}) custom-call(s32[4]{0:T(128)} %lengths_ref.1, s32[64]{0:T(128)} %request_ref.1, bf16[4096,128]{1,0:T(8,128)(2,1)} %bitcast.15, f32[256,128]{1,0:T(8,128)} %bitcast.18, ...), custom_call_target="tpu_custom_call" | custom-call | flops 1610612736 | bytes 1572864 | tf_op jit(solution)/shard_map/attend/pallas_call | solution.py:318
  18.0 1.0 %collective-permute-start.3 = (bf16[144,256]{1,0:T(8,128)(2,1)}, bf16[144,256]{1,0:T(8,128)(2,1)S(1)}, u32[]{:S(2)}, u32[]{:S(2)}) collective-permute-start(bf16[144,256]{1,0:T(8,128)(2,1)} %get-tuple-element.25), channel_id=1, source_target_pairs={{0,4},{4,0},{8,12},{12,8},{1,5},{5,1},{9,13},{13,9},{2,6},{6,2},{1... | collective-permute-start | bytes 221192 | tf_op jit(solution)/shard_map/ppermute | solution.py:39
  19.0 3.5 %collective-permute-start.4 = (bf16[144,256]{1,0:T(8,128)(2,1)}, bf16[144,256]{1,0:T(8,128)(2,1)S(1)}, u32[]{:S(2)}, u32[]{:S(2)}) collective-permute-start(bf16[144,256]{1,0:T(8,128)(2,1)} %get-tuple-element.26), channel_id=1, source_target_pairs={{0,8},{4,12},{8,0},{12,4},{1,9},{5,13},{9,1},{13,5},{2,10},{6,14},... | collective-permute-start | bytes 221192 | tf_op jit(solution)/shard_map/ppermute | solution.py:39
  22.5 5.0 %collective-permute-done.3.refs_1_ = bf16[144,256]{1,0:T(8,128)(2,1)S(1)} collective-permute-done((bf16[144,256]{1,0:T(8,128)(2,1)}, bf16[144,256]{1,0:T(8,128)(2,1)S(1)}, u32[]{:S(2)}, u32[]{:S(2)}) %collective-permute-start.3) | collective-permute-done | bytes 73760 | tf_op jit(solution)/shard_map/ppermute | solution.py:39
  27.5 2.6 %collective-permute-start.5 = (bf16[144,256]{1,0:T(8,128)(2,1)}, bf16[144,256]{1,0:T(8,128)(2,1)S(1)}, u32[]{:S(2)}, u32[]{:S(2)}) collective-permute-start(bf16[144,256]{1,0:T(8,128)(2,1)} %get-tuple-element.27), channel_id=1, source_target_pairs={{0,12},{4,8},{8,4},{12,0},{1,13},{5,9},{9,5},{13,1},{2,14},{6,10},... | collective-permute-start | bytes 221192 | tf_op jit(solution)/shard_map/ppermute | solution.py:39
  30.1 7.6 %collective-permute-done.4.refs_2_ = bf16[144,256]{1,0:T(8,128)(2,1)S(1)} collective-permute-done((bf16[144,256]{1,0:T(8,128)(2,1)}, bf16[144,256]{1,0:T(8,128)(2,1)S(1)}, u32[]{:S(2)}, u32[]{:S(2)}) %collective-permute-start.4) | collective-permute-done | bytes 73760 | tf_op jit(solution)/shard_map/ppermute | solution.py:39
  37.7 0.0 collective-permute-done.5.refs_3_
  37.7 0.0 copy-start
  37.7 0.9 %copy-done = f32[136,256]{1,0:T(8,128)S(1)} copy-done((f32[136,256]{1,0:T(8,128)S(1)}, f32[136,256]{1,0:T(8,128)}, u32[]{:S(2)}) %copy-start) | copy-done | bytes 139288
  38.6 0.0 copy-start.1
  38.6 0.9 %copy-done.1 = bf16[144,256]{1,0:T(8,128)(2,1)S(1)} copy-done((bf16[144,256]{1,0:T(8,128)(2,1)S(1)}, bf16[144,256]{1,0:T(8,128)(2,1)}, u32[]{:S(2)}) %copy-start.1) | copy-done | bytes 73752
  39.5 0.8 %join.1 = bf16[256,128]{1,0:T(8,128)(2,1)} custom-call(f32[136,256]{1,0:T(8,128)S(1)} %copy-done, bf16[144,256]{1,0:T(8,128)(2,1)S(1)} %copy-done.1, bf16[144,256]{1,0:T(8,128)(2,1)S(1)} %collective-permute-done.3.refs_1_, bf16[144,256]{1,0:T(8,128)(2,1)S(1)} %collective-permute-done.4.refs_2_, bf16[144,256]{1,0:T(8,128)(2,1)S(1)} %collective-permute-done.5.refs_3_), custom_call_target="tpu_custom_call" | custom-call | tf_op jit(solution)/shard_map/join/pallas_call | solution.py:341
  40.3 0.0 collective-permute-done.refs_1_
  40.3 0.0 collective-permute-done.1.refs_2_
  40.3 0.0 collective-permute-done.2.refs_3_
  40.3 0.9 %settle.1 = bf16[4096,128]{1,0:T(8,128)(2,1)} custom-call(bf16[4096,128]{1,0:T(8,128)(2,1)} %get-tuple-element.15.refs_0_, bf16[1024,128]{1,0:T(8,128)(2,1)S(1)} %collective-permute-done.refs_1_, bf16[1024,128]{1,0:T(8,128)(2,1)S(1)} %collective-permute-done.1.refs_2_, ...), custom_call_target="tpu_custom_call", output_to_operand_aliasing={{}: (0, {})} | custom-call | tf_op jit(solution)/shard_map/settle/pallas_call | solution.py:349
Async XLA Ops:
  3.3 37.0 %collective-permute-start = (bf16[1024,128]{1,0:T(8,128)(2,1)}, bf16[1024,128]{1,0:T(8,128)(2,1)S(1)}, u32[]{:S(2)}, u32[]{:S(2)}) collective-permute-start(bf16[1024,128]{1,0:T(8,128)(2,1)} %get-tuple-element.19), channel_id=1, source_target_pairs={{0,4},{4,0},{8,12},{12,8},{1,5},{5,1},{9,13},{13,9},{2,6},{6,2},{1... | collective-permute-start | bytes 786440 | tf_op jit(solution)/shard_map/ppermute | solution.py:39
  6.3 33.9 %collective-permute-start.1 = (bf16[1024,128]{1,0:T(8,128)(2,1)}, bf16[1024,128]{1,0:T(8,128)(2,1)S(1)}, u32[]{:S(2)}, u32[]{:S(2)}) collective-permute-start(bf16[1024,128]{1,0:T(8,128)(2,1)} %get-tuple-element.20), channel_id=1, source_target_pairs={{0,8},{4,12},{8,0},{12,4},{1,9},{5,13},{9,1},{13,5},{2,10},{6,14},... | collective-permute-start | bytes 786440 | tf_op jit(solution)/shard_map/ppermute | solution.py:39
  8.9 31.4 %collective-permute-start.2 = (bf16[1024,128]{1,0:T(8,128)(2,1)}, bf16[1024,128]{1,0:T(8,128)(2,1)S(1)}, u32[]{:S(2)}, u32[]{:S(2)}) collective-permute-start(bf16[1024,128]{1,0:T(8,128)(2,1)} %get-tuple-element.21), channel_id=1, source_target_pairs={{0,12},{4,8},{8,4},{12,0},{1,13},{5,9},{9,5},{13,1},{2,14},{6,10},... | collective-permute-start | bytes 786440 | tf_op jit(solution)/shard_map/ppermute | solution.py:39
  18.0 9.5 %collective-permute-start.3 = (bf16[144,256]{1,0:T(8,128)(2,1)}, bf16[144,256]{1,0:T(8,128)(2,1)S(1)}, u32[]{:S(2)}, u32[]{:S(2)}) collective-permute-start(bf16[144,256]{1,0:T(8,128)(2,1)} %get-tuple-element.25), channel_id=1, source_target_pairs={{0,4},{4,0},{8,12},{12,8},{1,5},{5,1},{9,13},{13,9},{2,6},{6,2},{1... | collective-permute-start | bytes 221192 | tf_op jit(solution)/shard_map/ppermute | solution.py:39
  19.0 18.7 %collective-permute-start.4 = (bf16[144,256]{1,0:T(8,128)(2,1)}, bf16[144,256]{1,0:T(8,128)(2,1)S(1)}, u32[]{:S(2)}, u32[]{:S(2)}) collective-permute-start(bf16[144,256]{1,0:T(8,128)(2,1)} %get-tuple-element.26), channel_id=1, source_target_pairs={{0,8},{4,12},{8,0},{12,4},{1,9},{5,13},{9,1},{13,5},{2,10},{6,14},... | collective-permute-start | bytes 221192 | tf_op jit(solution)/shard_map/ppermute | solution.py:39
  27.5 10.2 %collective-permute-start.5 = (bf16[144,256]{1,0:T(8,128)(2,1)}, bf16[144,256]{1,0:T(8,128)(2,1)S(1)}, u32[]{:S(2)}, u32[]{:S(2)}) collective-permute-start(bf16[144,256]{1,0:T(8,128)(2,1)} %get-tuple-element.27), channel_id=1, source_target_pairs={{0,12},{4,8},{8,4},{12,0},{1,13},{5,9},{9,5},{13,1},{2,14},{6,10},... | collective-permute-start | bytes 221192 | tf_op jit(solution)/shard_map/ppermute | solution.py:39
  37.7 0.9 %copy-start = (f32[136,256]{1,0:T(8,128)S(1)}, f32[136,256]{1,0:T(8,128)}, u32[]{:S(2)}) copy-start(f32[136,256]{1,0:T(8,128)} %get-tuple-element.23.own_ref) | copy-start | bytes 417796
  38.6 0.9 %copy-start.1 = (bf16[144,256]{1,0:T(8,128)(2,1)S(1)}, bf16[144,256]{1,0:T(8,128)(2,1)}, u32[]{:S(2)}) copy-start(bf16[144,256]{1,0:T(8,128)(2,1)} %get-tuple-element.24.refs_0_) | copy-start | bytes 221188

commit v4 on v3

--- a/solution.py
+++ b/solution.py
@@ -11,6 +11,7 @@
 GQ = 8
 STEPS = 2
 STAT_ROWS = 16
+KEEP_ROWS = 8
 FAR = -1e30
 RATE = HD ** (-0.5) * 1.4426950408889634
 
@@ -19,32 +20,18 @@
 SMEM = pl.BlockSpec(memory_space=pltpu.SMEM)
 
 
-def partner(me, k, count):
-    if count & (count - 1) == 0:
-        return me ^ k
-    return lax.rem(me + k, count)
-
-
-def source_of(me, k, count):
-    if count & (count - 1) == 0:
-        return me ^ k
-    return lax.rem(me + count - k, count)
-
-
-def exchange(sent, count):
-    got = []
-    for k, message in enumerate(sent, start=1):
-        power = count & (count - 1) == 0
-        pairs = [(i, i ^ k if power else (i + k) % count) for i in range(count)]
-        got.append(lax.ppermute(message, "seq", pairs))
-    return got
-
-
-def place_kernel(owner_any, deltas_any, anchors_any, scales_any, *refs):
+def exchange(message, k):
+    count = lax.axis_size("seq")
+    return lax.ppermute(message, "seq", [(i, i ^ k) for i in range(count)])
+
+
+def place_kernel(partners, owner_any, deltas_any, anchors_any, scales_any, *refs):
     receivers = lax.axis_size("seq")
     me = lax.axis_index("seq")
-    sent, pages = refs[: receivers - 1], refs[receivers - 1]
-    owner_ref, source_ref, count_ref, deltas_ref, anchors_ref, scales_ref, placed_ref, sems = refs[receivers:]
+    outs = refs[: len(partners)]
+    owner_ref, source_ref, count_ref, deltas_ref, anchors_ref, scales_ref, placed_ref, sems = refs[
+        len(partners) :
+    ]
     blocks = owner_ref.shape[0]
     rows = deltas_ref.shape[0] // blocks
     capacity = blocks // receivers
@@ -61,8 +48,9 @@
     ]
     for load in loads:
         load.start()
-    for owner in range(receivers):
-        count_ref[owner] = owner * capacity
+    if len(partners) > 1:
+        for owner in range(receivers):
+            count_ref[owner] = owner * capacity
     loads[0].wait()
 
     def find(block, carry):
@@ -72,16 +60,23 @@
         source_ref[slot] = block
         return carry
 
-    lax.fori_loop(0, blocks, find, 0, unroll=8)
+    def find_one(block, slot):
+        source_ref[slot] = block
+        return slot + (owner_ref[block] == (me ^ partners[0])).astype(jnp.int32)
+
+    if len(partners) > 1:
+        lax.fori_loop(0, blocks, find, 0, unroll=8)
+    else:
+        lax.fori_loop(0, blocks, find_one, 0, unroll=8)
     for load in loads[1:]:
         load.wait()
     odd = lax.broadcasted_iota(jnp.int32, (8, HD), 0) % 2 == 1
     scale = jnp.where(odd, scales_ref[1:2, :], scales_ref[0:1, :])[None]
     stores = []
-    for k in reversed(range(receivers)):
-        first = partner(me, k, receivers) * capacity
-
-        def one_slot(slot, carry, k=k, first=first):
+    for index, k in enumerate(partners):
+        first = (me ^ k) * capacity if len(partners) > 1 else 0
+
+        def one_slot(slot, carry, index=index, first=first):
             block = source_ref[first + slot]
             anchor = jnp.where(
                 odd, anchors_ref[pl.ds(2 * block + 1, 1), :], anchors_ref[pl.ds(2 * block, 1), :]
@@ -89,14 +84,15 @@
             here = pl.ds(pl.multiple_of(block * rows, rows), rows)
             delta = deltas_ref[here, :].astype(jnp.float32)
             decoded = anchor + scale * delta.reshape(rows // 8, 8, HD)
-            placed_ref[k, pl.ds(pl.multiple_of(slot * rows, rows), rows), :] = decoded.reshape(
+            placed_ref[index, pl.ds(pl.multiple_of(slot * rows, rows), rows), :] = decoded.reshape(
                 rows, HD
             ).astype(jnp.bfloat16)
             return carry
 
         lax.fori_loop(0, capacity, one_slot, 0, unroll=min(8, capacity))
-        own = pages.at[pl.ds(pl.multiple_of(me * capacity * rows, capacity * rows), capacity * rows), :]
-        store = pltpu.make_async_copy(placed_ref.at[k], sent[k - 1] if k else own, sems.at[4 + k])
+        size = capacity * rows
+        target = outs[index] if k else outs[index].at[pl.ds(pl.multiple_of(me * size, size), size), :]
+        store = pltpu.make_async_copy(placed_ref.at[index], target, sems.at[4 + index])
         store.start()
         stores.append(store)
     for store in stores:
@@ -110,7 +106,7 @@
     size = got[0].shape[0]
     copies = []
     for k in range(1, receivers):
-        first = pl.multiple_of(source_of(me, k, receivers) * size, size)
+        first = pl.multiple_of((me ^ k) * size, size)
         copy = pltpu.make_async_copy(got[k - 1], pages.at[pl.ds(first, size), :], sems.at[k - 1])
         copy.start()
         copies.append(copy)
@@ -124,6 +120,41 @@
     middle = rest.astype(jnp.bfloat16)
     low = (rest - middle.astype(jnp.float32)).astype(jnp.bfloat16)
     return [high, middle, low]
+
+
+def packed(partial):
+    summed, top, total = partial
+    stats = pieces(top) + pieces(total)
+    rest = jnp.zeros((STAT_ROWS - len(stats), top.shape[1]), jnp.bfloat16)
+    return jnp.concatenate([summed.astype(jnp.bfloat16)] + stats + [rest], axis=0)
+
+
+def unpacked(block):
+    stats = block[HD:, :].astype(jnp.float32)
+    top = stats[0:1] + stats[1:2] + stats[2:3]
+    total = stats[3:4] + stats[4:5] + stats[5:6]
+    return block[0:HD, :].astype(jnp.float32), top, total
+
+
+def held(partial):
+    summed, top, total = partial
+    rest = jnp.zeros((KEEP_ROWS - 2, top.shape[1]), jnp.float32)
+    return jnp.concatenate([summed, top, total, rest], axis=0)
+
+
+def taken(block):
+    return block[0:HD, :], block[HD : HD + 1, :], block[HD + 1 : HD + 2, :]
+
+
+def joined(one, other):
+    top = jnp.maximum(one[1], other[1])
+    scale_one = jnp.exp2((one[1] - top) * RATE)
+    scale_other = jnp.exp2((other[1] - top) * RATE)
+    return (
+        one[0] * scale_one + other[0] * scale_other,
+        top,
+        one[2] * scale_one + other[2] * scale_other,
+    )
 
 
 def attend_kernel(
@@ -136,17 +167,15 @@
     new_ref,
     *refs,
 ):
-    receivers = lax.axis_size("seq")
     me = lax.axis_index("seq")
-    outs = refs[:receivers]
-    own_ref, wide_ref, keys_ref, values_ref, asked_ref, out_ref, sems = refs[receivers:]
+    send_ref, keep_ref, wide_ref, keys_ref, values_ref, asked_ref = refs
     blocks = anchors_ref.shape[0] // 2
     rows = deltas_ref.shape[0] // blocks
     tokens = rows // 2
     requests = lengths_ref.shape[0]
     asked = queries_ref.shape[0]
     per_row = asked // request_ref.shape[0]
-    width = out_ref.shape[2]
+    width = keep_ref.shape[2]
 
     wide_ref[...] = deltas_ref[...].astype(jnp.float32)
     scale_key = scales_ref[0:1, :]
@@ -204,22 +233,22 @@
             (((0,), (0,)), ((), ())),
             preferred_element_type=jnp.float32,
         )
-        stats = pieces(top) + pieces(total)
-        stats = jnp.concatenate(
-            stats + [jnp.zeros((STAT_ROWS - len(stats), tile), jnp.bfloat16)], axis=0
-        )
-        both = jnp.concatenate([summed.astype(jnp.bfloat16), stats], axis=0)
         for part in range(parts):
-            out_ref[index * parts + part] = both[:, part * width : (part + 1) * width]
+            lanes = slice(part * width, (part + 1) * width)
+            partial = summed[:, lanes], top[:, lanes], total[:, lanes]
+            apart = (index * parts + part) ^ me
+
+            @pl.when(apart % 2 == 1)
+            def _(partial=partial, apart=apart):
+                send_ref[apart // 2] = packed(partial)
+
+            @pl.when(apart % 2 == 0)
+            def _(partial=partial, apart=apart):
+                keep_ref[apart // 2] = held(partial)
+
         return carry
 
     lax.fori_loop(0, asked // tile, one_tile, 0)
-
-    stores = []
-    for k in range(receivers):
-        copy = pltpu.make_async_copy(out_ref.at[partner(me, k, receivers)], outs[k], sems.at[k])
-        copy.start()
-        stores.append(copy)
 
     fresh = new_ref.shape[0] // 4
     new = new_ref[...].astype(jnp.float32).reshape(fresh, 4, HD)
@@ -250,30 +279,20 @@
             (((0,), (0,)), ((), ())),
             preferred_element_type=jnp.float32,
         )
-    own_ref[0:HD, :] = own_summed
-    own_ref[HD:, :] = jnp.concatenate(
-        [own_top, own_total, jnp.zeros((6, width), jnp.float32)], axis=0
-    )
-    for copy in stores:
-        copy.wait()
-
-
-def join_kernel(own_ref, *refs):
-    partials, out_ref = refs[:-1], refs[-1]
-    tops = [own_ref[HD : HD + 1, :]]
-    totals = [own_ref[HD + 1 : HD + 2, :]]
-    for partial_ref in partials:
-        stats = partial_ref[HD:, :].astype(jnp.float32)
-        tops.append(stats[0:1] + stats[1:2] + stats[2:3])
-        totals.append(stats[3:4] + stats[4:5] + stats[5:6])
-    top = functools.reduce(jnp.maximum, tops)
-    scale = jnp.exp2((tops[0] - top) * RATE)
-    total = totals[0] * scale
-    summed = own_ref[0:HD, :] * scale
-    for index, partial_ref in enumerate(partials, start=1):
-        scale = jnp.exp2((tops[index] - top) * RATE)
-        total = total + totals[index] * scale
-        summed = summed + partial_ref[0:HD, :].astype(jnp.float32) * scale
+    keep_ref[0] = held(joined(taken(keep_ref[0]), (own_summed, own_top, own_total)))
+
+
+def join_kernel(keep_ref, got_ref, send_ref, next_ref):
+    for index in range(keep_ref.shape[0]):
+        partial = joined(taken(keep_ref[index]), unpacked(got_ref[index]))
+        if index % 2 == 1:
+            send_ref[index // 2] = packed(partial)
+        else:
+            next_ref[index // 2] = held(partial)
+
+
+def finish_kernel(keep_ref, got_ref, out_ref):
+    summed, _, total = joined(taken(keep_ref[0]), unpacked(got_ref[0]))
     out_ref[...] = (summed / total).T.astype(jnp.bfloat16)
 
 
@@ -294,42 +313,55 @@
     flat_new = new_kv.reshape(rows_dev * 4, HD)
 
     hand = jax.ShapeDtypeStruct((tokens * 2 // senders, HD), jnp.bfloat16)
-    *sent, pages = pl.pallas_call(
-        place_kernel,
-        out_shape=[hand] * (senders - 1) + [jax.ShapeDtypeStruct((tokens * 2, HD), jnp.bfloat16)],
-        in_specs=[ANY] * 4,
-        out_specs=[ANY] * senders,
-        scratch_shapes=[
-            pltpu.SMEM((blocks,), jnp.int32),
-            pltpu.SMEM((blocks,), jnp.int32),
-            pltpu.SMEM((senders,), jnp.int32),
-            pltpu.VMEM((tokens * 2, HD), jnp.bfloat16),
-            pltpu.VMEM((blocks * 2, HD), jnp.float32),
-            pltpu.VMEM((2, HD), jnp.float32),
-            pltpu.VMEM((senders, tokens * 2 // senders, HD), jnp.bfloat16),
-            pltpu.SemaphoreType.DMA((4 + senders,)),
-        ],
-        compiler_params=limit,
-        name="place",
-    )(owner_map, flat_deltas, flat_anchors, scales)
-    sent, late_deltas = lax.optimization_barrier((sent, flat_deltas))
-    got = exchange(sent, senders)
-
-    *partials, own = pl.pallas_call(
+    whole = jax.ShapeDtypeStruct((tokens * 2, HD), jnp.bfloat16)
+
+    def place(partners, deltas):
+        return pl.pallas_call(
+            functools.partial(place_kernel, partners),
+            out_shape=[hand if k else whole for k in partners],
+            in_specs=[ANY] * 4,
+            out_specs=[ANY] * len(partners),
+            scratch_shapes=[
+                pltpu.SMEM((blocks,), jnp.int32),
+                pltpu.SMEM((blocks,), jnp.int32),
+                pltpu.SMEM((senders,), jnp.int32),
+                pltpu.VMEM((tokens * 2, HD), jnp.bfloat16),
+                pltpu.VMEM((blocks * 2, HD), jnp.float32),
+                pltpu.VMEM((2, HD), jnp.float32),
+                pltpu.VMEM((len(partners),) + hand.shape, jnp.bfloat16),
+                pltpu.SemaphoreType.DMA((4 + len(partners),)),
+            ],
+            compiler_params=limit,
+            name="place",
+        )(owner_map, deltas, flat_anchors, scales)
+
+    (farthest,) = place([senders - 1], flat_deltas)
+    farthest, late_deltas = lax.optimization_barrier((farthest, flat_deltas))
+    got = [exchange(farthest, senders - 1)]
+    *sent, pages = place(list(reversed(range(senders - 1))), late_deltas)
+    sent, late_deltas = lax.optimization_barrier((sent, late_deltas))
+    for k, message in zip(reversed(range(1, senders - 1)), sent):
+        got.append(exchange(message, k))
+    got.reverse()
+
+    def parted(count):
+        return [
+            jax.ShapeDtypeStruct((count // 2, HD + STAT_ROWS, width), jnp.bfloat16),
+            jax.ShapeDtypeStruct((count // 2, HD + KEEP_ROWS, width), jnp.float32),
+        ]
+
+    send, keep = pl.pallas_call(
         attend_kernel,
-        out_shape=[jax.ShapeDtypeStruct((HD + STAT_ROWS, width), jnp.bfloat16)] * senders
-        + [jax.ShapeDtypeStruct((HD + 8, width), jnp.float32)],
+        out_shape=parted(senders),
         in_specs=[SMEM, SMEM] + [VMEM] * 5,
-        out_specs=[ANY] * senders + [VMEM],
+        out_specs=[VMEM] * 2,
         scratch_shapes=[
             pltpu.VMEM((tokens * 2, HD), jnp.float32),
             pltpu.VMEM((tokens, 2 * HD), jnp.bfloat16),
             pltpu.VMEM((tokens, HD), jnp.bfloat16),
             pltpu.VMEM((rows * GQ * steps, 2 * HD), jnp.bfloat16),
-            pltpu.VMEM((senders, HD + STAT_ROWS, width), jnp.bfloat16),
-            pltpu.SemaphoreType.DMA((senders,)),
         ],
-        compiler_params=limit,
+        compiler_params=pltpu.CompilerParams(vmem_limit_bytes=32 * 1024 * 1024),
         cost_estimate=pl.CostEstimate(
             flops=6 * rows * GQ * steps * tokens * HD,
             bytes_accessed=tokens * 4 * HD + rows * GQ * steps * 4 * HD,
@@ -337,18 +369,29 @@
         ),
         name="attend",
     )(lengths, row_request, late_deltas, flat_anchors, scales, flat_queries, flat_new)
-    joined = [partials[0]] + exchange(partials[1:], senders)
+
+    k, count = 1, senders // 2
+    while count > 1:
+        send, keep = pl.pallas_call(
+            join_kernel,
+            out_shape=parted(count),
+            in_specs=[VMEM] * 2,
+            out_specs=[VMEM] * 2,
+            compiler_params=small,
+            name="join",
+        )(keep, exchange(send, k))
+        k, count = 2 * k, count // 2
     attended = pl.pallas_call(
-        join_kernel,
+        finish_kernel,
         out_shape=jax.ShapeDtypeStruct((width, HD), jnp.bfloat16),
-        in_specs=[VMEM] * (senders + 1),
+        in_specs=[VMEM] * 2,
         out_specs=VMEM,
         compiler_params=small,
-        name="join",
-    )(own, *joined)
+        name="finish",
+    )(keep, exchange(send, k))
     pages = pl.pallas_call(
         settle_kernel,
-        out_shape=jax.ShapeDtypeStruct((tokens * 2, HD), jnp.bfloat16),
+        out_shape=whole,
         in_specs=[ANY] * senders,
         out_specs=ANY,
         scratch_shapes=[pltpu.SemaphoreType.DMA((senders - 1,))],

time: 41.4 us -> 36.4 us (0.88)
  starting transfers between devices: 12.7 us -> 8.6 us
  local copies, waits for them, and re-layouts: 1.79 us -> 0.67 us
    ppermute x6 -> x5, starting transfers between devices: 12.7 us -> 8.6 us  [exchange(): return lax.ppermute(message, 'seq', [(i, i ^ k) for i in range(count)])]
    unnamed x4 -> x14, local copies, waits for them, and re-layouts: 1.79 us -> 0.67 us
    ppermute x6 -> x5, waiting for transfers between devices: 12.7 us -> 12.8 us  [exchange(): return lax.ppermute(message, 'seq', [(i, i ^ k) for i in range(count)])]
    pallas_call x4 -> x6, Pallas kernels: 13.4 us -> 13.4 us  [the longest x1 6.79 us: per_device(): pl.pallas_call(attend_kernel, out_shape=parted(senders), in_specs=[SMEM,...]
  transfers between devices with their start and end apart: 6 -> 5, of which waited for: 2 -> 2; matrix products, arithmetic and copies ran while one was open for 0% -> 0% of each run, Pallas kernels for 24% -> 28%
where the time goes in v4:
time: 36.4 us; the launch traced here: 36.2 us
  Pallas kernels  13.4 us (37%)
  waiting for transfers between devices  12.8 us (35%)
  starting transfers between devices  8.6 us (24%)
  between operations  0.73 us (2%)
  local copies, waits for them, and re-layouts  0.67 us (2%)
    ppermute x5, waiting for transfers between devices, exchange(): return lax.ppermute(message, 'seq', [(i, i ^ k) for i in range(count)])  12.8 us
    ppermute x5, starting transfers between devices, exchange(): return lax.ppermute(message, 'seq', [(i, i ^ k) for i in range(count)])  8.6 us
    pallas_call x1, Pallas kernels, per_device(): pl.pallas_call(attend_kernel, out_shape=parted(senders), in_specs=[SMEM,...  6.79 us
    pallas_call x2, Pallas kernels, place(): pl.pallas_call(functools.partial(place_kernel, partners), out_shape=[hand...  4.88 us
    pallas_call x1, Pallas kernels, per_device(): pl.pallas_call(settle_kernel, out_shape=whole, in_specs=[ANY] * senders,...  0.92 us
    pallas_call x1, Pallas kernels, per_device(): pl.pallas_call(finish_kernel, out_shape=jax.ShapeDtypeStruct((width, HD),...  0.76 us
  transfers between devices with their start and end apart: 5, of which 2 were waited for; matrix products, arithmetic and copies ran while one was open for 0% of the time, Pallas kernels for 28%

profile of v4, /device:TPU:0, one launch (start us, length us, event | category | flops | bytes accessed | tf_op | source)
XLA Modules:
  0.0 36.2 jit_solution(13504598944391745133)
XLA Ops:
  0.6 0.0 copy-start
  0.6 2.3 %place.2 = bf16[1024,128]{1,0:T(8,128)(2,1)} custom-call(s32[128]{0:T(128)} %owner_any.3, bf16[4096,128]{1,0:T(8,128)(2,1)} %bitcast.14, f32[256,128]{1,0:T(8,128)} %bitcast.17, f32[2,128]{1,0:T(2,128)} %scales_ref.1), custom_call_target="tpu_custom_call" | custom-call | tf_op jit(solution)/shard_map/place/pallas_call | solution.py:319
  2.9 0.0 copy-start.1
  2.9 0.0 copy-start.3
  2.9 0.0 copy-start.4
  3.0 5.1 %collective-permute-start.2 = (bf16[1024,128]{1,0:T(8,128)(2,1)}, bf16[1024,128]{1,0:T(8,128)(2,1)S(1)}, u32[]{:S(2)}, u32[]{:S(2)}) collective-permute-start(bf16[1024,128]{1,0:T(8,128)(2,1)} %place.2), channel_id=1, source_target_pairs={{0,12},{4,8},{8,4},{12,0},{1,13},{5,9},{9,5},{13,1},{2,14},{6,10},... | collective-permute-start | bytes 786440 | tf_op jit(solution)/shard_map/ppermute | solution.py:25
  8.1 0.0 copy-start.6
  8.1 2.6 %place.3 = (bf16[1024,128]{1,0:T(8,128)(2,1)}, bf16[1024,128]{1,0:T(8,128)(2,1)}, bf16[4096,128]{1,0:T(8,128)(2,1)}) custom-call(s32[128]{0:T(128)} %owner_any.3, bf16[4096,128]{1,0:T(8,128)(2,1)} %bitcast.15, f32[256,128]{1,0:T(8,128)} %bitcast.18, f32[2,128]{1,0:T(2,128)} %scales_ref.1), custom_call_target="tpu_custom_call" | custom-call | tf_op jit(solution)/shard_map/place/pallas_call | solution.py:319
  10.7 0.1 collective-permute-start
  10.8 0.6 %collective-permute-start.1 = (bf16[1024,128]{1,0:T(8,128)(2,1)}, bf16[1024,128]{1,0:T(8,128)(2,1)S(1)}, u32[]{:S(2)}, u32[]{:S(2)}) collective-permute-start(bf16[1024,128]{1,0:T(8,128)(2,1)} %get-tuple-element.19), channel_id=1, source_target_pairs={{0,8},{4,12},{8,0},{12,4},{1,9},{5,13},{9,1},{13,5},{2,10},{6,14},... | collective-permute-start | bytes 786440 | tf_op jit(solution)/shard_map/ppermute | solution.py:25
  11.3 0.0 copy-start.2
  11.3 0.0 copy-start.5
  11.3 0.0 copy-done
  11.4 0.0 copy-done.1
  11.4 0.0 copy-done.3
  11.4 0.0 copy-done.4
  11.4 0.0 copy-done.6
  11.4 0.6 %copy-done.2 = f32[2,128]{1,0:T(2,128)S(1)} copy-done((f32[2,128]{1,0:T(2,128)S(1)}, f32[2,128]{1,0:T(2,128)}, u32[]{:S(2)}) %copy-start.2) | copy-done | bytes 1048
  12.0 0.0 copy-done.5
  12.0 6.8 %attend.1 = (bf16[2,144,256]{2,1,0:T(8,128)(2,1)S(1)}, f32[2,136,256]{2,1,0:T(8,128)S(1)}) custom-call(s32[4]{0:T(128)S(1)} %copy-done.5, s32[64]{0:T(128)S(1)} %copy-done.6, bf16[4096,128]{1,0:T(8,128)(2,1)S(1)} %bitcast.16, f32[256,128]{1,0:T(8,128)S(1)} %bitcast.19, f32[2,128]{1,0:T(2,128)S(1)} %copy-done.2, bf16[1024,128]{1,0:T(8,128)(2,1)S(1)} %bitcast.20, ...), custom_call_target="tpu_custom_call" | custom-call | flops 1610612736 | bytes 1572864 | tf_op jit(solution)/shard_map/attend/pallas_call | solution.py:353
  18.8 1.5 %collective-permute-start.3 = (bf16[2,144,256]{2,1,0:T(8,128)(2,1)S(1)}, bf16[2,144,256]{2,1,0:T(8,128)(2,1)S(1)}, u32[]{:S(2)}, u32[]{:S(2)}) collective-permute-start(bf16[2,144,256]{2,1,0:T(8,128)(2,1)S(1)} %get-tuple-element.23), channel_id=1, source_target_pairs={{0,4},{4,0},{8,12},{12,8},{1,5},{5,1},{9,13},{13,9},{2,6},{6,2},{1... | collective-permute-start | bytes 442376 | tf_op jit(solution)/shard_map/ppermute | solution.py:25
  20.3 8.0 %collective-permute-done.3.got_ref = bf16[2,144,256]{2,1,0:T(8,128)(2,1)S(1)} collective-permute-done((bf16[2,144,256]{2,1,0:T(8,128)(2,1)S(1)}, bf16[2,144,256]{2,1,0:T(8,128)(2,1)S(1)}, u32[]{:S(2)}, u32[]{:S(2)}) %collective-permute-start.3) | collective-permute-done | bytes 147488 | tf_op jit(solution)/shard_map/ppermute | solution.py:25
  28.4 0.1 join.1
  28.4 1.3 %collective-permute-start.4 = (bf16[1,144,256]{2,1,0:T(8,128)(2,1)S(1)}, bf16[1,144,256]{2,1,0:T(8,128)(2,1)S(1)}, u32[]{:S(2)}, u32[]{:S(2)}) collective-permute-start(bf16[1,144,256]{2,1,0:T(8,128)(2,1)S(1)} %get-tuple-element.25), channel_id=1, source_target_pairs={{0,8},{4,12},{8,0},{12,4},{1,9},{5,13},{9,1},{13,5},{2,10},{6,14},... | collective-permute-start | bytes 221192 | tf_op jit(solution)/shard_map/ppermute | solution.py:25
  29.8 4.7 %collective-permute-done.4.got_ref = bf16[1,144,256]{2,1,0:T(8,128)(2,1)S(1)} collective-permute-done((bf16[1,144,256]{2,1,0:T(8,128)(2,1)S(1)}, bf16[1,144,256]{2,1,0:T(8,128)(2,1)S(1)}, u32[]{:S(2)}, u32[]{:S(2)}) %collective-permute-start.4) | collective-permute-done | bytes 73760 | tf_op jit(solution)/shard_map/ppermute | solution.py:25
  34.5 0.8 %finish.1 = bf16[256,128]{1,0:T(8,128)(2,1)} custom-call(f32[1,136,256]{2,1,0:T(8,128)S(1)} %get-tuple-element.24.keep_ref, bf16[1,144,256]{2,1,0:T(8,128)(2,1)S(1)} %collective-permute-done.4.got_ref), custom_call_target="tpu_custom_call" | custom-call | tf_op jit(solution)/shard_map/finish/pallas_call | solution.py:384
  35.3 0.0 collective-permute-done.2.refs_3_
  35.3 0.0 collective-permute-done.refs_1_
  35.3 0.0 collective-permute-done.1.refs_2_
  35.3 0.9 %settle.1 = bf16[4096,128]{1,0:T(8,128)(2,1)} custom-call(bf16[4096,128]{1,0:T(8,128)(2,1)} %get-tuple-element.15.refs_0_, bf16[1024,128]{1,0:T(8,128)(2,1)S(1)} %collective-permute-done.refs_1_, bf16[1024,128]{1,0:T(8,128)(2,1)S(1)} %collective-permute-done.1.refs_2_, ...), custom_call_target="tpu_custom_call", output_to_operand_aliasing={{}: (0, {})} | custom-call | tf_op jit(solution)/shard_map/settle/pallas_call | solution.py:392
Async XLA Ops:
  0.6 10.7 %copy-start = (bf16[2048,2,128]{2,1,0:T(2,128)(2,1)S(1)}, bf16[2048,2,128]{2,1,0:T(2,128)(2,1)}, u32[]{:S(2)}) copy-start(bf16[2048,2,128]{2,1,0:T(2,128)(2,1)} %param.11) | copy-start | bytes 3145732
  2.9 8.4 %copy-start.1 = (f32[128,2,128]{2,1,0:T(2,128)S(1)}, f32[128,2,128]{2,1,0:T(2,128)}, u32[]{:S(2)}) copy-start(f32[128,2,128]{2,1,0:T(2,128)} %param.12) | copy-start | bytes 393220
  2.9 8.4 %copy-start.3 = (bf16[64,2,1024]{2,1,0:T(2,128)(2,1)S(1)}, bf16[64,2,1024]{2,1,0:T(2,128)(2,1)}, u32[]{:S(2)}) copy-start(bf16[64,2,1024]{2,1,0:T(2,128)(2,1)} %param.14) | copy-start | bytes 786436
  2.9 8.4 %copy-start.4 = (bf16[16,2,2,128]{3,2,1,0:T(2,128)(2,1)S(1)}, bf16[16,2,2,128]{3,2,1,0:T(2,128)(2,1)}, u32[]{:S(2)}) copy-start(bf16[16,2,2,128]{3,2,1,0:T(2,128)(2,1)} %param.15) | copy-start | bytes 49156
  3.0 32.3 %collective-permute-start.2 = (bf16[1024,128]{1,0:T(8,128)(2,1)}, bf16[1024,128]{1,0:T(8,128)(2,1)S(1)}, u32[]{:S(2)}, u32[]{:S(2)}) collective-permute-start(bf16[1024,128]{1,0:T(8,128)(2,1)} %place.2), channel_id=1, source_target_pairs={{0,12},{4,8},{8,4},{12,0},{1,13},{5,9},{9,5},{13,1},{2,14},{6,10},... | collective-permute-start | bytes 786440 | tf_op jit(solution)/shard_map/ppermute | solution.py:25
  8.1 3.3 %copy-start.6 = (s32[64]{0:T(128)S(1)}, s32[64]{0:T(128)}, u32[]{:S(2)}) copy-start(s32[64]{0:T(128)} %request_ref.1) | copy-start | bytes 772
  10.7 24.6 %collective-permute-start = (bf16[1024,128]{1,0:T(8,128)(2,1)}, bf16[1024,128]{1,0:T(8,128)(2,1)S(1)}, u32[]{:S(2)}, u32[]{:S(2)}) collective-permute-start(bf16[1024,128]{1,0:T(8,128)(2,1)} %get-tuple-element.18), channel_id=1, source_target_pairs={{0,4},{4,0},{8,12},{12,8},{1,5},{5,1},{9,13},{13,9},{2,6},{6,2},{1... | collective-permute-start | bytes 786440 | tf_op jit(solution)/shard_map/ppermute | solution.py:25
  10.8 24.5 %collective-permute-start.1 = (bf16[1024,128]{1,0:T(8,128)(2,1)}, bf16[1024,128]{1,0:T(8,128)(2,1)S(1)}, u32[]{:S(2)}, u32[]{:S(2)}) collective-permute-start(bf16[1024,128]{1,0:T(8,128)(2,1)} %get-tuple-element.19), channel_id=1, source_target_pairs={{0,8},{4,12},{8,0},{12,4},{1,9},{5,13},{9,1},{13,5},{2,10},{6,14},... | collective-permute-start | bytes 786440 | tf_op jit(solution)/shard_map/ppermute | solution.py:25
  11.3 0.7 %copy-start.2 = (f32[2,128]{1,0:T(2,128)S(1)}, f32[2,128]{1,0:T(2,128)}, u32[]{:S(2)}) copy-start(f32[2,128]{1,0:T(2,128)} %scales_ref.1) | copy-start | bytes 3076
  11.3 0.7 %copy-start.5 = (s32[4]{0:T(128)S(1)}, s32[4]{0:T(128)}, u32[]{:S(2)}) copy-start(s32[4]{0:T(128)} %lengths_ref.1) | copy-start | bytes 52
  18.8 9.6 %collective-permute-start.3 = (bf16[2,144,256]{2,1,0:T(8,128)(2,1)S(1)}, bf16[2,144,256]{2,1,0:T(8,128)(2,1)S(1)}, u32[]{:S(2)}, u32[]{:S(2)}) collective-permute-start(bf16[2,144,256]{2,1,0:T(8,128)(2,1)S(1)} %get-tuple-element.23), channel_id=1, source_target_pairs={{0,4},{4,0},{8,12},{12,8},{1,5},{5,1},{9,13},{13,9},{2,6},{6,2},{1... | collective-permute-start | bytes 442376 | tf_op jit(solution)/shard_map/ppermute | solution.py:25
  28.4 6.1 %collective-permute-start.4 = (bf16[1,144,256]{2,1,0:T(8,128)(2,1)S(1)}, bf16[1,144,256]{2,1,0:T(8,128)(2,1)S(1)}, u32[]{:S(2)}, u32[]{:S(2)}) collective-permute-start(bf16[1,144,256]{2,1,0:T(8,128)(2,1)S(1)} %get-tuple-element.25), channel_id=1, source_target_pairs={{0,8},{4,12},{8,0},{12,4},{1,9},{5,13},{9,1},{13,5},{2,10},{6,14},... | collective-permute-start | bytes 221192 | tf_op jit(solution)/shard_map/ppermute | solution.py:25

commit v5 on v4

--- a/solution.py
+++ b/solution.py
@@ -16,6 +16,7 @@
 RATE = HD ** (-0.5) * 1.4426950408889634
 
 VMEM = pl.BlockSpec(memory_space=pltpu.VMEM)
+HBM = pl.BlockSpec(memory_space=pltpu.HBM)
 ANY = pl.BlockSpec(memory_space=pl.ANY)
 SMEM = pl.BlockSpec(memory_space=pltpu.SMEM)
 
@@ -25,13 +26,11 @@
     return lax.ppermute(message, "seq", [(i, i ^ k) for i in range(count)])
 
 
-def place_kernel(partners, owner_any, deltas_any, anchors_any, scales_any, *refs):
+def place_kernel(owner_any, deltas_any, anchors_any, scales_any, *refs):
     receivers = lax.axis_size("seq")
     me = lax.axis_index("seq")
-    outs = refs[: len(partners)]
-    owner_ref, source_ref, count_ref, deltas_ref, anchors_ref, scales_ref, placed_ref, sems = refs[
-        len(partners) :
-    ]
+    outs = refs[:receivers]
+    owner_ref, source_ref, count_ref, deltas_ref, anchors_ref, scales_ref, sems = refs[receivers:]
     blocks = owner_ref.shape[0]
     rows = deltas_ref.shape[0] // blocks
     capacity = blocks // receivers
@@ -48,35 +47,34 @@
     ]
     for load in loads:
         load.start()
-    if len(partners) > 1:
+    bits = capacity.bit_length()
+    narrow = receivers * bits < 32
+    if not narrow:
         for owner in range(receivers):
             count_ref[owner] = owner * capacity
     loads[0].wait()
 
-    def find(block, carry):
+    def find(block, counts):
         owner = owner_ref[block]
-        slot = count_ref[owner]
-        count_ref[owner] = slot + 1
+        if narrow:
+            shift = owner * bits
+            slot = owner * capacity + ((counts >> shift) & ((1 << bits) - 1))
+            counts = counts + (jnp.int32(1) << shift)
+        else:
+            slot = count_ref[owner]
+            count_ref[owner] = slot + 1
         source_ref[slot] = block
-        return carry
-
-    def find_one(block, slot):
-        source_ref[slot] = block
-        return slot + (owner_ref[block] == (me ^ partners[0])).astype(jnp.int32)
-
-    if len(partners) > 1:
-        lax.fori_loop(0, blocks, find, 0, unroll=8)
-    else:
-        lax.fori_loop(0, blocks, find_one, 0, unroll=8)
+        return counts
+
+    lax.fori_loop(0, blocks, find, jnp.int32(0), unroll=8)
     for load in loads[1:]:
         load.wait()
     odd = lax.broadcasted_iota(jnp.int32, (8, HD), 0) % 2 == 1
     scale = jnp.where(odd, scales_ref[1:2, :], scales_ref[0:1, :])[None]
-    stores = []
-    for index, k in enumerate(partners):
-        first = (me ^ k) * capacity if len(partners) > 1 else 0
-
-        def one_slot(slot, carry, index=index, first=first):
+    for k, out_ref in zip(reversed(range(receivers)), outs):
+        first = (me ^ k) * capacity
+
+        def one_slot(slot, carry, first=first, out_ref=out_ref):
             block = source_ref[first + slot]
             anchor = jnp.where(
                 odd, anchors_ref[pl.ds(2 * block + 1, 1), :], anchors_ref[pl.ds(2 * block, 1), :]
@@ -84,19 +82,12 @@
             here = pl.ds(pl.multiple_of(block * rows, rows), rows)
             delta = deltas_ref[here, :].astype(jnp.float32)
             decoded = anchor + scale * delta.reshape(rows // 8, 8, HD)
-            placed_ref[index, pl.ds(pl.multiple_of(slot * rows, rows), rows), :] = decoded.reshape(
-                rows, HD
-            ).astype(jnp.bfloat16)
+            out_ref[pl.ds(pl.multiple_of(slot * rows, rows), rows), :] = decoded.reshape(rows, HD).astype(
+                jnp.bfloat16
+            )
             return carry
 
         lax.fori_loop(0, capacity, one_slot, 0, unroll=min(8, capacity))
-        size = capacity * rows
-        target = outs[index] if k else outs[index].at[pl.ds(pl.multiple_of(me * size, size), size), :]
-        store = pltpu.make_async_copy(placed_ref.at[index], target, sems.at[4 + index])
-        store.start()
-        stores.append(store)
-    for store in stores:
-        store.wait()
 
 
 def settle_kernel(*refs):
@@ -107,7 +98,7 @@
     copies = []
     for k in range(1, receivers):
         first = pl.multiple_of((me ^ k) * size, size)
-        copy = pltpu.make_async_copy(got[k - 1], pages.at[pl.ds(first, size), :], sems.at[k - 1])
+        copy = pltpu.make_async_copy(got[-k], pages.at[pl.ds(first, size), :], sems.at[k - 1])
         copy.start()
         copies.append(copy)
     for copy in copies:
@@ -165,10 +156,16 @@
     scales_ref,
     queries_ref,
     new_ref,
+    mine_any,
     *refs,
 ):
     me = lax.axis_index("seq")
-    send_ref, keep_ref, wide_ref, keys_ref, values_ref, asked_ref = refs
+    send_ref, keep_ref, pages_any, wide_ref, keys_ref, values_ref, asked_ref, sem = refs
+    size = mine_any.shape[0]
+    own_pages = pltpu.make_async_copy(
+        mine_any, pages_any.at[pl.ds(pl.multiple_of(me * size, size), size), :], sem
+    )
+    own_pages.start()
     blocks = anchors_ref.shape[0] // 2
     rows = deltas_ref.shape[0] // blocks
     tokens = rows // 2
@@ -280,6 +277,7 @@
             preferred_element_type=jnp.float32,
         )
     keep_ref[0] = held(joined(taken(keep_ref[0]), (own_summed, own_top, own_total)))
+    own_pages.wait()
 
 
 def join_kernel(keep_ref, got_ref, send_ref, next_ref):
@@ -304,7 +302,6 @@
     rows, steps, _ = queries.shape
     rows_dev = new_kv.shape[0]
     width = rows_dev * GQ * steps
-    limit = pltpu.CompilerParams(vmem_limit_bytes=60 * 1024 * 1024)
     small = pltpu.CompilerParams(vmem_limit_bytes=8 * 1024 * 1024)
 
     flat_deltas = deltas.reshape(tokens * 2, HD)
@@ -315,34 +312,29 @@
     hand = jax.ShapeDtypeStruct((tokens * 2 // senders, HD), jnp.bfloat16)
     whole = jax.ShapeDtypeStruct((tokens * 2, HD), jnp.bfloat16)
 
-    def place(partners, deltas):
-        return pl.pallas_call(
-            functools.partial(place_kernel, partners),
-            out_shape=[hand if k else whole for k in partners],
-            in_specs=[ANY] * 4,
-            out_specs=[ANY] * len(partners),
-            scratch_shapes=[
-                pltpu.SMEM((blocks,), jnp.int32),
-                pltpu.SMEM((blocks,), jnp.int32),
-                pltpu.SMEM((senders,), jnp.int32),
-                pltpu.VMEM((tokens * 2, HD), jnp.bfloat16),
-                pltpu.VMEM((blocks * 2, HD), jnp.float32),
-                pltpu.VMEM((2, HD), jnp.float32),
-                pltpu.VMEM((len(partners),) + hand.shape, jnp.bfloat16),
-                pltpu.SemaphoreType.DMA((4 + len(partners),)),
-            ],
-            compiler_params=limit,
-            name="place",
-        )(owner_map, deltas, flat_anchors, scales)
-
-    (farthest,) = place([senders - 1], flat_deltas)
-    farthest, late_deltas = lax.optimization_barrier((farthest, flat_deltas))
-    got = [exchange(farthest, senders - 1)]
-    *sent, pages = place(list(reversed(range(senders - 1))), late_deltas)
-    sent, late_deltas = lax.optimization_barrier((sent, late_deltas))
-    for k, message in zip(reversed(range(1, senders - 1)), sent):
-        got.append(exchange(message, k))
-    got.reverse()
+    *sent, mine = pl.pallas_call(
+        place_kernel,
+        out_shape=[hand] * senders,
+        in_specs=[HBM] * 4,
+        out_specs=[VMEM] * senders,
+        scratch_shapes=[
+            pltpu.SMEM((blocks,), jnp.int32),
+            pltpu.SMEM((blocks,), jnp.int32),
+            pltpu.SMEM((senders,), jnp.int32),
+            pltpu.VMEM((tokens * 2, HD), jnp.bfloat16),
+            pltpu.VMEM((blocks * 2, HD), jnp.float32),
+            pltpu.VMEM((2, HD), jnp.float32),
+            pltpu.SemaphoreType.DMA((4,)),
+        ],
+        compiler_params=small,
+        name="place",
+    )(*[pltpu.with_memory_space_constraint(x, pltpu.HBM) for x in (owner_map, flat_deltas, flat_anchors, scales)])
+    sent = [mine] + sent[::-1]
+
+    got = [None] * senders
+    sent, mine, late_deltas = lax.optimization_barrier((sent, mine, flat_deltas))
+    for k in reversed(range(1, senders)):
+        got[k] = exchange(sent[k], k)
 
     def parted(count):
         return [
@@ -350,16 +342,17 @@
             jax.ShapeDtypeStruct((count // 2, HD + KEEP_ROWS, width), jnp.float32),
         ]
 
-    send, keep = pl.pallas_call(
+    send, keep, pages = pl.pallas_call(
         attend_kernel,
-        out_shape=parted(senders),
-        in_specs=[SMEM, SMEM] + [VMEM] * 5,
-        out_specs=[VMEM] * 2,
+        out_shape=parted(senders) + [whole],
+        in_specs=[SMEM, SMEM] + [VMEM] * 5 + [ANY],
+        out_specs=[VMEM] * 2 + [HBM],
         scratch_shapes=[
             pltpu.VMEM((tokens * 2, HD), jnp.float32),
             pltpu.VMEM((tokens, 2 * HD), jnp.bfloat16),
             pltpu.VMEM((tokens, HD), jnp.bfloat16),
             pltpu.VMEM((rows * GQ * steps, 2 * HD), jnp.bfloat16),
+            pltpu.SemaphoreType.DMA,
         ],
         compiler_params=pltpu.CompilerParams(vmem_limit_bytes=32 * 1024 * 1024),
         cost_estimate=pl.CostEstimate(
@@ -368,9 +361,10 @@
             transcendentals=rows * GQ * steps * tokens,
         ),
         name="attend",
-    )(lengths, row_request, late_deltas, flat_anchors, scales, flat_queries, flat_new)
+    )(lengths, row_request, late_deltas, flat_anchors, scales, flat_queries, flat_new, mine)
 
     k, count = 1, senders // 2
+    passed = exchange(send, k)
     while count > 1:
         send, keep = pl.pallas_call(
             join_kernel,
@@ -379,8 +373,9 @@
             out_specs=[VMEM] * 2,
             compiler_params=small,
             name="join",
-        )(keep, exchange(send, k))
+        )(keep, passed)
         k, count = 2 * k, count // 2
+        passed = exchange(send, k)
     attended = pl.pallas_call(
         finish_kernel,
         out_shape=jax.ShapeDtypeStruct((width, HD), jnp.bfloat16),
@@ -388,17 +383,17 @@
         out_specs=VMEM,
         compiler_params=small,
         name="finish",
-    )(keep, exchange(send, k))
+    )(keep, passed)
     pages = pl.pallas_call(
         settle_kernel,
         out_shape=whole,
-        in_specs=[ANY] * senders,
-        out_specs=ANY,
+        in_specs=[HBM] + [ANY] * (senders - 1),
+        out_specs=HBM,
         scratch_shapes=[pltpu.SemaphoreType.DMA((senders - 1,))],
         input_output_aliases={0: 0},
         compiler_params=small,
         name="settle",
-    )(pages, *got)
+    )(pages, *reversed(got[1:]))
     pages = pages.reshape(blocks, tokens // blocks, 2, HD)
     attended = (
         attended.reshape(rows_dev, GQ, steps, HD).transpose(0, 2, 1, 3).reshape(rows_dev, steps, GQ * HD)

time: 36.4 us -> 35.9 us (0.986)
  Pallas kernels: 13.4 us -> 10.5 us
  local copies, waits for them, and re-layouts: 0.67 us -> 2.34 us
  waiting for transfers between devices: 12.8 us -> 13.5 us
    pallas_call x4 -> x3, Pallas kernels: 12.6 us -> 9.67 us  [the longest x1 6.8 us: per_device(): pl.pallas_call(attend_kernel, out_shape=parted(senders) + [whole], in_spe...]
    unnamed x14, local copies, waits for them, and re-layouts: 0.67 us -> 2.34 us
    ppermute x5, waiting for transfers between devices: 12.8 us -> 13.5 us  [exchange(): return lax.ppermute(message, 'seq', [(i, i ^ k) for i in range(count)])]
  transfers between devices with their start and end apart: 5 -> 5, of which waited for: 2 -> 2; matrix products, arithmetic and copies ran while one was open for 0% -> 0% of each run, Pallas kernels for 28% -> 21%
where the time goes in v5:
time: 35.9 us; the launch traced here: 35.6 us
  waiting for transfers between devices  13.5 us (38%)
  Pallas kernels  10.5 us (29%)
  starting transfers between devices  8.58 us (24%)
  local copies, waits for them, and re-layouts  2.34 us (7%)
  between operations  0.7 us (2%)
    ppermute x5, waiting for transfers between devices, exchange(): return lax.ppermute(message, 'seq', [(i, i ^ k) for i in range(count)])  13.5 us
    ppermute x5, starting transfers between devices, exchange(): return lax.ppermute(message, 'seq', [(i, i ^ k) for i in range(count)])  8.58 us
    pallas_call x1, Pallas kernels, per_device(): pl.pallas_call(attend_kernel, out_shape=parted(senders) + [whole], in_spe...  6.8 us
    unnamed x14, local copies, waits for them, and re-layouts  2.34 us
    pallas_call x1, Pallas kernels, per_device(): pl.pallas_call(place_kernel, out_shape=[hand] * senders, in_specs=[HBM] *...  1.95 us
    pallas_call x1, Pallas kernels, per_device(): pl.pallas_call(settle_kernel, out_shape=whole, in_specs=[HBM] + [ANY] * (...  0.92 us
    pallas_call x1, Pallas kernels, per_device(): pl.pallas_call(finish_kernel, out_shape=jax.ShapeDtypeStruct((width, HD),...  0.76 us
  transfers between devices with their start and end apart: 5, of which 2 were waited for; matrix products, arithmetic and copies ran while one was open for 0% of the time, Pallas kernels for 21%

profile of v5, /device:TPU:0, one launch (start us, length us, event | category | flops | bytes accessed | tf_op | source)
XLA Modules:
  0.0 35.6 jit_solution(5847183042249011724)
XLA Ops:
  0.6 0.0 copy-start
  0.6 0.0 copy-start.1
  0.7 0.0 copy-start.6
  0.7 1.9 %place.1 = (bf16[1024,128]{1,0:T(8,128)(2,1)S(1)}, bf16[1024,128]{1,0:T(8,128)(2,1)S(1)}, bf16[1024,128]{1,0:T(8,128)(2,1)S(1)}, bf16[1024,128]{1,0:T(8,128)(2,1)S(1)}) custom-call(s32[128]{0:T(128)} %owner_any.1, bf16[4096,128]{1,0:T(8,128)(2,1)} %bitcast.14, f32[256,128]{1,0:T(8,128)} %bitcast.16, f32[2,128]{1,0:T(2,128)} %scales_ref.1), custom_call_target="tpu_custom_call" | custom-call | tf_op jit(solution)/shard_map/place/pallas_call | solution.py:315
  2.6 5.1 %collective-permute-start = (bf16[1024,128]{1,0:T(8,128)(2,1)S(1)}, bf16[1024,128]{1,0:T(8,128)(2,1)S(1)}, u32[]{:S(2)}, u32[]{:S(2)}) collective-permute-start(bf16[1024,128]{1,0:T(8,128)(2,1)S(1)} %get-tuple-element.23), channel_id=1, source_target_pairs={{0,12},{4,8},{8,4},{12,0},{1,13},{5,9},{9,5},{13,1},{2,14},{6,10},... | collective-permute-start | bytes 786440 | tf_op jit(solution)/shard_map/ppermute | solution.py:26
  7.7 0.0 collective-permute-start.1
  7.7 0.6 %collective-permute-start.2 = (bf16[1024,128]{1,0:T(8,128)(2,1)S(1)}, bf16[1024,128]{1,0:T(8,128)(2,1)S(1)}, u32[]{:S(2)}, u32[]{:S(2)}) collective-permute-start(bf16[1024,128]{1,0:T(8,128)(2,1)S(1)} %get-tuple-element.25), channel_id=1, source_target_pairs={{0,4},{4,0},{8,12},{12,8},{1,5},{5,1},{9,13},{13,9},{2,6},{6,2},{1... | collective-permute-start | bytes 786440 | tf_op jit(solution)/shard_map/ppermute | solution.py:26
  8.4 0.0 copy-start.2
  8.4 0.0 copy-start.5
  8.4 0.0 copy-done
  8.4 0.0 copy-done.1
  8.4 0.0 copy-done.6
  8.4 0.7 %copy-done.2 = f32[2,128]{1,0:T(2,128)S(1)} copy-done((f32[2,128]{1,0:T(2,128)S(1)}, f32[2,128]{1,0:T(2,128)}, u32[]{:S(2)}) %copy-start.2) | copy-done | bytes 1048
  9.1 0.0 copy-done.5
  9.1 0.0 copy-start.3
  9.1 0.9 %copy-done.3 = bf16[64,2,1024]{2,1,0:T(2,128)(2,1)S(1)} copy-done((bf16[64,2,1024]{2,1,0:T(2,128)(2,1)S(1)}, bf16[64,2,1024]{2,1,0:T(2,128)(2,1)}, u32[]{:S(2)}) %copy-start.3) | copy-done | bytes 262168
  10.0 0.0 copy-start.4
  10.0 0.7 %copy-done.4 = bf16[16,2,2,128]{3,2,1,0:T(2,128)(2,1)S(1)} copy-done((bf16[16,2,2,128]{3,2,1,0:T(2,128)(2,1)S(1)}, bf16[16,2,2,128]{3,2,1,0:T(2,128)(2,1)}, u32[]{:S(2)}) %copy-start.4) | copy-done | bytes 16408
  10.7 6.8 %attend.1 = (bf16[2,144,256]{2,1,0:T(8,128)(2,1)S(1)}, f32[2,136,256]{2,1,0:T(8,128)S(1)}, bf16[4096,128]{1,0:T(8,128)(2,1)}) custom-call(s32[4]{0:T(128)S(1)} %copy-done.5, s32[64]{0:T(128)S(1)} %copy-done.6, bf16[4096,128]{1,0:T(8,128)(2,1)S(1)} %bitcast.15, f32[256,128]{1,0:T(8,128)S(1)} %bitcast.17, f32[2,128]{1,0:T(2,128)S(1)} %copy-done.2, ...), custom_call_target="tpu_custom_call" | custom-call | flops 1610612736 | bytes 1572864 | tf_op jit(solution)/shard_map/attend/pallas_call | solution.py:345
  17.5 1.5 %collective-permute-start.3 = (bf16[2,144,256]{2,1,0:T(8,128)(2,1)S(1)}, bf16[2,144,256]{2,1,0:T(8,128)(2,1)S(1)}, u32[]{:S(2)}, u32[]{:S(2)}) collective-permute-start(bf16[2,144,256]{2,1,0:T(8,128)(2,1)S(1)} %get-tuple-element.27), channel_id=1, source_target_pairs={{0,4},{4,0},{8,12},{12,8},{1,5},{5,1},{9,13},{13,9},{2,6},{6,2},{1... | collective-permute-start | bytes 442376 | tf_op jit(solution)/shard_map/ppermute | solution.py:26
  19.0 8.8 %collective-permute-done.3.got_ref = bf16[2,144,256]{2,1,0:T(8,128)(2,1)S(1)} collective-permute-done((bf16[2,144,256]{2,1,0:T(8,128)(2,1)S(1)}, bf16[2,144,256]{2,1,0:T(8,128)(2,1)S(1)}, u32[]{:S(2)}, u32[]{:S(2)}) %collective-permute-start.3) | collective-permute-done | bytes 147488 | tf_op jit(solution)/shard_map/ppermute | solution.py:26
  27.8 0.1 join.1
  27.9 1.4 %collective-permute-start.4 = (bf16[1,144,256]{2,1,0:T(8,128)(2,1)S(1)}, bf16[1,144,256]{2,1,0:T(8,128)(2,1)S(1)}, u32[]{:S(2)}, u32[]{:S(2)}) collective-permute-start(bf16[1,144,256]{2,1,0:T(8,128)(2,1)S(1)} %get-tuple-element.29), channel_id=1, source_target_pairs={{0,8},{4,12},{8,0},{12,4},{1,9},{5,13},{9,1},{13,5},{2,10},{6,14},... | collective-permute-start | bytes 221192 | tf_op jit(solution)/shard_map/ppermute | solution.py:26
  29.2 4.7 %collective-permute-done.4.got_ref = bf16[1,144,256]{2,1,0:T(8,128)(2,1)S(1)} collective-permute-done((bf16[1,144,256]{2,1,0:T(8,128)(2,1)S(1)}, bf16[1,144,256]{2,1,0:T(8,128)(2,1)S(1)}, u32[]{:S(2)}, u32[]{:S(2)}) %collective-permute-start.4) | collective-permute-done | bytes 73760 | tf_op jit(solution)/shard_map/ppermute | solution.py:26
  33.9 0.8 %finish.1 = bf16[256,128]{1,0:T(8,128)(2,1)} custom-call(f32[1,136,256]{2,1,0:T(8,128)S(1)} %get-tuple-element.28.keep_ref, bf16[1,144,256]{2,1,0:T(8,128)(2,1)S(1)} %collective-permute-done.4.got_ref), custom_call_target="tpu_custom_call" | custom-call | tf_op jit(solution)/shard_map/finish/pallas_call | solution.py:379
  34.7 0.0 collective-permute-done.refs_1_
  34.7 0.0 collective-permute-done.1.refs_2_
  34.7 0.0 collective-permute-done.2.refs_3_
  34.7 0.9 %settle.1 = bf16[4096,128]{1,0:T(8,128)(2,1)} custom-call(bf16[4096,128]{1,0:T(8,128)(2,1)} %get-tuple-element.22.refs_0_, bf16[1024,128]{1,0:T(8,128)(2,1)S(1)} %collective-permute-done.refs_1_, bf16[1024,128]{1,0:T(8,128)(2,1)S(1)} %collective-permute-done.1.refs_2_, ...), custom_call_target="tpu_custom_call", output_to_operand_aliasing={{}: (0, {})} | custom-call | tf_op jit(solution)/shard_map/settle/pallas_call | solution.py:387
Async XLA Ops:
  0.6 7.8 %copy-start = (bf16[2048,2,128]{2,1,0:T(2,128)(2,1)S(1)}, bf16[2048,2,128]{2,1,0:T(2,128)(2,1)}, u32[]{:S(2)}) copy-start(bf16[2048,2,128]{2,1,0:T(2,128)(2,1)} %param.11) | copy-start | bytes 3145732
  0.6 7.7 %copy-start.1 = (f32[128,2,128]{2,1,0:T(2,128)S(1)}, f32[128,2,128]{2,1,0:T(2,128)}, u32[]{:S(2)}) copy-start(f32[128,2,128]{2,1,0:T(2,128)} %param.12) | copy-start | bytes 393220
  0.7 7.7 %copy-start.6 = (s32[64]{0:T(128)S(1)}, s32[64]{0:T(128)}, u32[]{:S(2)}) copy-start(s32[64]{0:T(128)} %request_ref.1) | copy-start | bytes 772
  2.6 32.1 %collective-permute-start = (bf16[1024,128]{1,0:T(8,128)(2,1)S(1)}, bf16[1024,128]{1,0:T(8,128)(2,1)S(1)}, u32[]{:S(2)}, u32[]{:S(2)}) collective-permute-start(bf16[1024,128]{1,0:T(8,128)(2,1)S(1)} %get-tuple-element.23), channel_id=1, source_target_pairs={{0,12},{4,8},{8,4},{12,0},{1,13},{5,9},{9,5},{13,1},{2,14},{6,10},... | collective-permute-start | bytes 786440 | tf_op jit(solution)/shard_map/ppermute | solution.py:26
  7.7 27.0 %collective-permute-start.1 = (bf16[1024,128]{1,0:T(8,128)(2,1)S(1)}, bf16[1024,128]{1,0:T(8,128)(2,1)S(1)}, u32[]{:S(2)}, u32[]{:S(2)}) collective-permute-start(bf16[1024,128]{1,0:T(8,128)(2,1)S(1)} %get-tuple-element.24), channel_id=1, source_target_pairs={{0,8},{4,12},{8,0},{12,4},{1,9},{5,13},{9,1},{13,5},{2,10},{6,14},... | collective-permute-start | bytes 786440 | tf_op jit(solution)/shard_map/ppermute | solution.py:26
  7.7 27.0 %collective-permute-start.2 = (bf16[1024,128]{1,0:T(8,128)(2,1)S(1)}, bf16[1024,128]{1,0:T(8,128)(2,1)S(1)}, u32[]{:S(2)}, u32[]{:S(2)}) collective-permute-start(bf16[1024,128]{1,0:T(8,128)(2,1)S(1)} %get-tuple-element.25), channel_id=1, source_target_pairs={{0,4},{4,0},{8,12},{12,8},{1,5},{5,1},{9,13},{13,9},{2,6},{6,2},{1... | collective-permute-start | bytes 786440 | tf_op jit(solution)/shard_map/ppermute | solution.py:26
  8.4 0.7 %copy-start.2 = (f32[2,128]{1,0:T(2,128)S(1)}, f32[2,128]{1,0:T(2,128)}, u32[]{:S(2)}) copy-start(f32[2,128]{1,0:T(2,128)} %scales_ref.1) | copy-start | bytes 3076
  8.4 0.7 %copy-start.5 = (s32[4]{0:T(128)S(1)}, s32[4]{0:T(128)}, u32[]{:S(2)}) copy-start(s32[4]{0:T(128)} %lengths_ref.1) | copy-start | bytes 52
  9.1 1.0 %copy-start.3 = (bf16[64,2,1024]{2,1,0:T(2,128)(2,1)S(1)}, bf16[64,2,1024]{2,1,0:T(2,128)(2,1)}, u32[]{:S(2)}) copy-start(bf16[64,2,1024]{2,1,0:T(2,128)(2,1)} %param.14) | copy-start | bytes 786436
  10.0 0.7 %copy-start.4 = (bf16[16,2,2,128]{3,2,1,0:T(2,128)(2,1)S(1)}, bf16[16,2,2,128]{3,2,1,0:T(2,128)(2,1)}, u32[]{:S(2)}) copy-start(bf16[16,2,2,128]{3,2,1,0:T(2,128)(2,1)} %param.15) | copy-start | bytes 49156
  17.5 10.2 %collective-permute-start.3 = (bf16[2,144,256]{2,1,0:T(8,128)(2,1)S(1)}, bf16[2,144,256]{2,1,0:T(8,128)(2,1)S(1)}, u32[]{:S(2)}, u32[]{:S(2)}) collective-permute-start(bf16[2,144,256]{2,1,0:T(8,128)(2,1)S(1)} %get-tuple-element.27), channel_id=1, source_target_pairs={{0,4},{4,0},{8,12},{12,8},{1,5},{5,1},{9,13},{13,9},{2,6},{6,2},{1... | collective-permute-start | bytes 442376 | tf_op jit(solution)/shard_map/ppermute | solution.py:26
  27.9 6.1 %collective-permute-start.4 = (bf16[1,144,256]{2,1,0:T(8,128)(2,1)S(1)}, bf16[1,144,256]{2,1,0:T(8,128)(2,1)S(1)}, u32[]{:S(2)}, u32[]{:S(2)}) collective-permute-start(bf16[1,144,256]{2,1,0:T(8,128)(2,1)S(1)} %get-tuple-element.29), channel_id=1, source_target_pairs={{0,8},{4,12},{8,0},{12,4},{1,9},{5,13},{9,1},{13,5},{2,10},{6,14},... | collective-permute-start | bytes 221192 | tf_op jit(solution)/shard_map/ppermute | solution.py:26

commit v6 on v5

--- a/solution.py
+++ b/solution.py
@@ -12,6 +12,8 @@
 STEPS = 2
 STAT_ROWS = 16
 KEEP_ROWS = 8
+HEIGHTS = (80, 64)
+PIECES = len(HEIGHTS)
 FAR = -1e30
 RATE = HD ** (-0.5) * 1.4426950408889634
 
@@ -113,14 +115,19 @@
     return [high, middle, low]
 
 
-def packed(partial):
+def pack(refs, index, partial):
     summed, top, total = partial
     stats = pieces(top) + pieces(total)
     rest = jnp.zeros((STAT_ROWS - len(stats), top.shape[1]), jnp.bfloat16)
-    return jnp.concatenate([summed.astype(jnp.bfloat16)] + stats + [rest], axis=0)
-
-
-def unpacked(block):
+    block = jnp.concatenate([summed.astype(jnp.bfloat16)] + stats + [rest], axis=0)
+    first = 0
+    for height, ref in zip(HEIGHTS, refs):
+        ref[index] = block[first : first + height]
+        first += height
+
+
+def unpacked(refs, index):
+    block = jnp.concatenate([ref[index] for ref in refs], axis=0)
     stats = block[HD:, :].astype(jnp.float32)
     top = stats[0:1] + stats[1:2] + stats[2:3]
     total = stats[3:4] + stats[4:5] + stats[5:6]
@@ -148,24 +155,23 @@
     )
 
 
-def attend_kernel(
-    lengths_ref,
-    request_ref,
-    deltas_ref,
-    anchors_ref,
-    scales_ref,
-    queries_ref,
-    new_ref,
-    mine_any,
-    *refs,
-):
+def attend_kernel(*refs):
     me = lax.axis_index("seq")
-    send_ref, keep_ref, pages_any, wide_ref, keys_ref, values_ref, asked_ref, sem = refs
+    sources, mine_any, refs = refs[:7], refs[7], refs[8:]
+    send, refs = refs[:PIECES], refs[PIECES:]
+    keep_ref, pages_any, *targets, wide_ref, keys_ref, values_ref, asked_ref, sems = refs
+    loads = [
+        pltpu.make_async_copy(source, target, sems.at[index])
+        for index, (source, target) in enumerate(zip(sources, targets))
+    ]
+    for load in loads:
+        load.start()
     size = mine_any.shape[0]
     own_pages = pltpu.make_async_copy(
-        mine_any, pages_any.at[pl.ds(pl.multiple_of(me * size, size), size), :], sem
+        mine_any, pages_any.at[pl.ds(pl.multiple_of(me * size, size), size), :], sems.at[len(loads)]
     )
     own_pages.start()
+    deltas_ref, anchors_ref, scales_ref, lengths_ref, request_ref, queries_ref, new_ref = targets
     blocks = anchors_ref.shape[0] // 2
     rows = deltas_ref.shape[0] // blocks
     tokens = rows // 2
@@ -174,6 +180,8 @@
     per_row = asked // request_ref.shape[0]
     width = keep_ref.shape[2]
 
+    for load in loads:
+        load.wait()
     wide_ref[...] = deltas_ref[...].astype(jnp.float32)
     scale_key = scales_ref[0:1, :]
     scale_value = scales_ref[1:2, :]
@@ -237,7 +245,7 @@
 
             @pl.when(apart % 2 == 1)
             def _(partial=partial, apart=apart):
-                send_ref[apart // 2] = packed(partial)
+                pack(send, apart // 2, partial)
 
             @pl.when(apart % 2 == 0)
             def _(partial=partial, apart=apart):
@@ -280,18 +288,23 @@
     own_pages.wait()
 
 
-def join_kernel(keep_ref, got_ref, send_ref, next_ref):
+def join_kernel(keep_ref, *refs):
+    got, send, next_ref = refs[:PIECES], refs[PIECES : 2 * PIECES], refs[2 * PIECES]
     for index in range(keep_ref.shape[0]):
-        partial = joined(taken(keep_ref[index]), unpacked(got_ref[index]))
+        partial = joined(taken(keep_ref[index]), unpacked(got, index))
         if index % 2 == 1:
-            send_ref[index // 2] = packed(partial)
+            pack(send, index // 2, partial)
         else:
             next_ref[index // 2] = held(partial)
 
 
-def finish_kernel(keep_ref, got_ref, out_ref):
-    summed, _, total = joined(taken(keep_ref[0]), unpacked(got_ref[0]))
-    out_ref[...] = (summed / total).T.astype(jnp.bfloat16)
+def finish_kernel(keep_ref, *refs):
+    summed, _, total = joined(taken(keep_ref[0]), unpacked(refs[:PIECES], 0))
+    refs[PIECES][...] = (summed / total).T.astype(jnp.bfloat16)
+
+
+def in_hbm(arrays):
+    return [pltpu.with_memory_space_constraint(array, pltpu.HBM) for array in arrays]
 
 
 def per_device(lengths, owner_map, row_request, deltas, anchors, scales, queries, new_kv):
@@ -328,7 +341,7 @@
         ],
         compiler_params=small,
         name="place",
-    )(*[pltpu.with_memory_space_constraint(x, pltpu.HBM) for x in (owner_map, flat_deltas, flat_anchors, scales)])
+    )(*in_hbm([owner_map, flat_deltas, flat_anchors, scales]))
     sent = [mine] + sent[::-1]
 
     got = [None] * senders
@@ -337,22 +350,26 @@
         got[k] = exchange(sent[k], k)
 
     def parted(count):
-        return [
-            jax.ShapeDtypeStruct((count // 2, HD + STAT_ROWS, width), jnp.bfloat16),
-            jax.ShapeDtypeStruct((count // 2, HD + KEEP_ROWS, width), jnp.float32),
+        return [jax.ShapeDtypeStruct((count // 2, height, width), jnp.bfloat16) for height in HEIGHTS] + [
+            jax.ShapeDtypeStruct((count // 2, HD + KEEP_ROWS, width), jnp.float32)
         ]
 
-    send, keep, pages = pl.pallas_call(
+    needed = (late_deltas, flat_anchors, scales, lengths, row_request, flat_queries, flat_new)
+    *send, keep, pages = pl.pallas_call(
         attend_kernel,
         out_shape=parted(senders) + [whole],
-        in_specs=[SMEM, SMEM] + [VMEM] * 5 + [ANY],
-        out_specs=[VMEM] * 2 + [HBM],
+        in_specs=[HBM] * len(needed) + [ANY],
+        out_specs=[VMEM] * (PIECES + 1) + [HBM],
         scratch_shapes=[
+            (pltpu.SMEM if array.dtype == jnp.int32 else pltpu.VMEM)(array.shape, array.dtype)
+            for array in needed
+        ]
+        + [
             pltpu.VMEM((tokens * 2, HD), jnp.float32),
             pltpu.VMEM((tokens, 2 * HD), jnp.bfloat16),
             pltpu.VMEM((tokens, HD), jnp.bfloat16),
             pltpu.VMEM((rows * GQ * steps, 2 * HD), jnp.bfloat16),
-            pltpu.SemaphoreType.DMA,
+            pltpu.SemaphoreType.DMA((len(needed) + 1,)),
         ],
         compiler_params=pltpu.CompilerParams(vmem_limit_bytes=32 * 1024 * 1024),
         cost_estimate=pl.CostEstimate(
@@ -361,29 +378,27 @@
             transcendentals=rows * GQ * steps * tokens,
         ),
         name="attend",
-    )(lengths, row_request, late_deltas, flat_anchors, scales, flat_queries, flat_new, mine)
+    )(*in_hbm(needed), mine)
 
     k, count = 1, senders // 2
-    passed = exchange(send, k)
     while count > 1:
-        send, keep = pl.pallas_call(
+        *send, keep = pl.pallas_call(
             join_kernel,
             out_shape=parted(count),
-            in_specs=[VMEM] * 2,
-            out_specs=[VMEM] * 2,
+            in_specs=[VMEM] * (PIECES + 1),
+            out_specs=[VMEM] * (PIECES + 1),
             compiler_params=small,
             name="join",
-        )(keep, passed)
+        )(keep, *[exchange(piece, k) for piece in send])
         k, count = 2 * k, count // 2
-        passed = exchange(send, k)
     attended = pl.pallas_call(
         finish_kernel,
         out_shape=jax.ShapeDtypeStruct((width, HD), jnp.bfloat16),
-        in_specs=[VMEM] * 2,
+        in_specs=[VMEM] * (PIECES + 1),
         out_specs=VMEM,
         compiler_params=small,
         name="finish",
-    )(keep, passed)
+    )(keep, *[exchange(piece, k) for piece in send])
     pages = pl.pallas_call(
         settle_kernel,
         out_shape=whole,

time: 35.9 us -> 35.8 us (level)
  local copies, waits for them, and re-layouts: 2.34 us -> 0 us
  starting transfers between devices: 8.58 us -> 10.9 us
  Pallas kernels: 10.5 us -> 11.4 us
  waiting for transfers between devices: 13.5 us -> 12.7 us
    unnamed x14 -> x0, local copies, waits for them, and re-layouts: 2.34 us -> none
    ppermute x5 -> x7, starting transfers between devices: 8.58 us -> 10.9 us  [exchange(): return lax.ppermute(message, 'seq', [(i, i ^ k) for i in range(count)])]
    pallas_call x1, Pallas kernels: 6.8 us -> 7.74 us  [per_device(): pl.pallas_call(attend_kernel, out_shape=parted(senders) + [whole], in_spe...]
    ppermute x5 -> x7, waiting for transfers between devices: 13.5 us -> 12.7 us  [exchange(): return lax.ppermute(message, 'seq', [(i, i ^ k) for i in range(count)])]
  transfers between devices with their start and end apart: 5 -> 7, of which waited for: 2 -> 2; matrix products, arithmetic and copies ran while one was open for 0% -> 0% of each run, Pallas kernels for 21% -> 24%
where the time goes in v6:
time: 35.8 us; the launch traced here: 35.6 us
  waiting for transfers between devices  12.7 us (35%)
  Pallas kernels  11.4 us (32%)
  starting transfers between devices  10.9 us (30%)
  between operations  0.66 us (2%)
    ppermute x7, waiting for transfers between devices, exchange(): return lax.ppermute(message, 'seq', [(i, i ^ k) for i in range(count)])  12.7 us
    ppermute x7, starting transfers between devices, exchange(): return lax.ppermute(message, 'seq', [(i, i ^ k) for i in range(count)])  10.9 us
    pallas_call x1, Pallas kernels, per_device(): pl.pallas_call(attend_kernel, out_shape=parted(senders) + [whole], in_spe...  7.74 us
    pallas_call x1, Pallas kernels, per_device(): pl.pallas_call(place_kernel, out_shape=[hand] * senders, in_specs=[HBM] *...  1.87 us
    pallas_call x1, Pallas kernels, per_device(): pl.pallas_call(settle_kernel, out_shape=whole, in_specs=[HBM] + [ANY] * (...  0.92 us
    pallas_call x1, Pallas kernels, per_device(): pl.pallas_call(finish_kernel, out_shape=jax.ShapeDtypeStruct((width, HD),...  0.76 us
  transfers between devices with their start and end apart: 7, of which 2 were waited for; matrix products, arithmetic and copies ran while one was open for 0% of the time, Pallas kernels for 24%

profile of v6, /device:TPU:0, one launch (start us, length us, event | category | flops | bytes accessed | tf_op | source)
XLA Modules:
  0.0 35.6 jit_solution(17291731642771154098)
XLA Ops:
  0.6 1.9 %place.1 = (bf16[1024,128]{1,0:T(8,128)(2,1)S(1)}, bf16[1024,128]{1,0:T(8,128)(2,1)S(1)}, bf16[1024,128]{1,0:T(8,128)(2,1)S(1)}, bf16[1024,128]{1,0:T(8,128)(2,1)S(1)}) custom-call(s32[128]{0:T(128)} %owner_any.1, bf16[4096,128]{1,0:T(8,128)(2,1)} %bitcast.14, f32[256,128]{1,0:T(8,128)} %bitcast.17, f32[2,128]{1,0:T(2,128)} %refs_2_.1), custom_call_target="tpu_custom_call" | custom-call | tf_op jit(solution)/shard_map/place/pallas_call | solution.py:328
  2.5 5.1 %collective-permute-start = (bf16[1024,128]{1,0:T(8,128)(2,1)S(1)}, bf16[1024,128]{1,0:T(8,128)(2,1)S(1)}, u32[]{:S(2)}, u32[]{:S(2)}) collective-permute-start(bf16[1024,128]{1,0:T(8,128)(2,1)S(1)} %get-tuple-element.25), channel_id=1, source_target_pairs={{0,12},{4,8},{8,4},{12,0},{1,13},{5,9},{9,5},{13,1},{2,14},{6,10},... | collective-permute-start | bytes 786440 | tf_op jit(solution)/shard_map/ppermute | solution.py:28
  7.6 0.0 collective-permute-start.1
  7.6 0.6 %collective-permute-start.2 = (bf16[1024,128]{1,0:T(8,128)(2,1)S(1)}, bf16[1024,128]{1,0:T(8,128)(2,1)S(1)}, u32[]{:S(2)}, u32[]{:S(2)}) collective-permute-start(bf16[1024,128]{1,0:T(8,128)(2,1)S(1)} %get-tuple-element.27), channel_id=1, source_target_pairs={{0,4},{4,0},{8,12},{12,8},{1,5},{5,1},{9,13},{13,9},{2,6},{6,2},{1... | collective-permute-start | bytes 786440 | tf_op jit(solution)/shard_map/ppermute | solution.py:28
  8.3 7.7 %attend.1 = (bf16[2,80,256]{2,1,0:T(8,128)(2,1)S(1)}, bf16[2,64,256]{2,1,0:T(8,128)(2,1)S(1)}, f32[2,136,256]{2,1,0:T(8,128)S(1)}, bf16[4096,128]{1,0:T(8,128)(2,1)}) custom-call(bf16[4096,128]{1,0:T(8,128)(2,1)} %bitcast.15, f32[256,128]{1,0:T(8,128)} %bitcast.18, f32[2,128]{1,0:T(2,128)} %refs_2_.1, s32[4]{0:T(128)} %refs_3_.1, s32[64]{0:T(128)} %refs_4_.1, ...), custom_call_target="tpu_custom_call" | custom-call | flops 1610612736 | bytes 1572864 | tf_op jit(solution)/shard_map/attend/pallas_call | solution.py:358
  16.0 1.5 %collective-permute-start.3 = (bf16[2,80,256]{2,1,0:T(8,128)(2,1)S(1)}, bf16[2,80,256]{2,1,0:T(8,128)(2,1)S(1)}, u32[]{:S(2)}, u32[]{:S(2)}) collective-permute-start(bf16[2,80,256]{2,1,0:T(8,128)(2,1)S(1)} %get-tuple-element.29), channel_id=1, source_target_pairs={{0,4},{4,0},{8,12},{12,8},{1,5},{5,1},{9,13},{13,9},{2,6},{6,2},{1... | collective-permute-start | bytes 245768 | tf_op jit(solution)/shard_map/ppermute | solution.py:28
  17.5 0.7 %collective-permute-start.4 = (bf16[2,64,256]{2,1,0:T(8,128)(2,1)S(1)}, bf16[2,64,256]{2,1,0:T(8,128)(2,1)S(1)}, u32[]{:S(2)}, u32[]{:S(2)}) collective-permute-start(bf16[2,64,256]{2,1,0:T(8,128)(2,1)S(1)} %get-tuple-element.30), channel_id=1, source_target_pairs={{0,4},{4,0},{8,12},{12,8},{1,5},{5,1},{9,13},{13,9},{2,6},{6,2},{1... | collective-permute-start | bytes 196616 | tf_op jit(solution)/shard_map/ppermute | solution.py:28
  18.1 9.5 %collective-permute-done.4.refs_1_ = bf16[2,64,256]{2,1,0:T(8,128)(2,1)S(1)} collective-permute-done((bf16[2,64,256]{2,1,0:T(8,128)(2,1)S(1)}, bf16[2,64,256]{2,1,0:T(8,128)(2,1)S(1)}, u32[]{:S(2)}, u32[]{:S(2)}) %collective-permute-start.4) | collective-permute-done | bytes 65568 | tf_op jit(solution)/shard_map/ppermute | solution.py:28
  27.7 0.0 collective-permute-done.3.refs_0_
  27.7 0.1 join.1
  27.8 1.4 %collective-permute-start.5 = (bf16[1,80,256]{2,1,0:T(8,128)(2,1)S(1)}, bf16[1,80,256]{2,1,0:T(8,128)(2,1)S(1)}, u32[]{:S(2)}, u32[]{:S(2)}) collective-permute-start(bf16[1,80,256]{2,1,0:T(8,128)(2,1)S(1)} %get-tuple-element.32), channel_id=1, source_target_pairs={{0,8},{4,12},{8,0},{12,4},{1,9},{5,13},{9,1},{13,5},{2,10},{6,14},... | collective-permute-start | bytes 122888 | tf_op jit(solution)/shard_map/ppermute | solution.py:28
  29.1 1.6 %collective-permute-start.6 = (bf16[1,64,256]{2,1,0:T(8,128)(2,1)S(1)}, bf16[1,64,256]{2,1,0:T(8,128)(2,1)S(1)}, u32[]{:S(2)}, u32[]{:S(2)}) collective-permute-start(bf16[1,64,256]{2,1,0:T(8,128)(2,1)S(1)} %get-tuple-element.33), channel_id=1, source_target_pairs={{0,8},{4,12},{8,0},{12,4},{1,9},{5,13},{9,1},{13,5},{2,10},{6,14},... | collective-permute-start | bytes 98312 | tf_op jit(solution)/shard_map/ppermute | solution.py:28
  30.8 3.2 %collective-permute-done.6.refs_1_ = bf16[1,64,256]{2,1,0:T(8,128)(2,1)S(1)} collective-permute-done((bf16[1,64,256]{2,1,0:T(8,128)(2,1)S(1)}, bf16[1,64,256]{2,1,0:T(8,128)(2,1)S(1)}, u32[]{:S(2)}, u32[]{:S(2)}) %collective-permute-start.6) | collective-permute-done | bytes 32800 | tf_op jit(solution)/shard_map/ppermute | solution.py:28
  33.9 0.0 collective-permute-done.5.refs_0_
  33.9 0.8 %finish.1 = bf16[256,128]{1,0:T(8,128)(2,1)} custom-call(f32[1,136,256]{2,1,0:T(8,128)S(1)} %get-tuple-element.31.keep_ref, bf16[1,80,256]{2,1,0:T(8,128)(2,1)S(1)} %collective-permute-done.5.refs_0_, bf16[1,64,256]{2,1,0:T(8,128)(2,1)S(1)} %collective-permute-done.6.refs_1_), custom_call_target="tpu_custom_call" | custom-call | tf_op jit(solution)/shard_map/finish/pallas_call | solution.py:394
  34.7 0.0 collective-permute-done.refs_1_
  34.7 0.0 collective-permute-done.1.refs_2_
  34.7 0.0 collective-permute-done.2.refs_3_
  34.7 0.9 %settle.1 = bf16[4096,128]{1,0:T(8,128)(2,1)} custom-call(bf16[4096,128]{1,0:T(8,128)(2,1)} %get-tuple-element.24.refs_0_, bf16[1024,128]{1,0:T(8,128)(2,1)S(1)} %collective-permute-done.refs_1_, bf16[1024,128]{1,0:T(8,128)(2,1)S(1)} %collective-permute-done.1.refs_2_, ...), custom_call_target="tpu_custom_call", output_to_operand_aliasing={{}: (0, {})} | custom-call | tf_op jit(solution)/shard_map/settle/pallas_call | solution.py:402
Async XLA Ops:
  2.5 32.2 %collective-permute-start = (bf16[1024,128]{1,0:T(8,128)(2,1)S(1)}, bf16[1024,128]{1,0:T(8,128)(2,1)S(1)}, u32[]{:S(2)}, u32[]{:S(2)}) collective-permute-start(bf16[1024,128]{1,0:T(8,128)(2,1)S(1)} %get-tuple-element.25), channel_id=1, source_target_pairs={{0,12},{4,8},{8,4},{12,0},{1,13},{5,9},{9,5},{13,1},{2,14},{6,10},... | collective-permute-start | bytes 786440 | tf_op jit(solution)/shard_map/ppermute | solution.py:28
  7.6 27.1 %collective-permute-start.1 = (bf16[1024,128]{1,0:T(8,128)(2,1)S(1)}, bf16[1024,128]{1,0:T(8,128)(2,1)S(1)}, u32[]{:S(2)}, u32[]{:S(2)}) collective-permute-start(bf16[1024,128]{1,0:T(8,128)(2,1)S(1)} %get-tuple-element.26), channel_id=1, source_target_pairs={{0,8},{4,12},{8,0},{12,4},{1,9},{5,13},{9,1},{13,5},{2,10},{6,14},... | collective-permute-start | bytes 786440 | tf_op jit(solution)/shard_map/ppermute | solution.py:28
  7.6 27.1 %collective-permute-start.2 = (bf16[1024,128]{1,0:T(8,128)(2,1)S(1)}, bf16[1024,128]{1,0:T(8,128)(2,1)S(1)}, u32[]{:S(2)}, u32[]{:S(2)}) collective-permute-start(bf16[1024,128]{1,0:T(8,128)(2,1)S(1)} %get-tuple-element.27), channel_id=1, source_target_pairs={{0,4},{4,0},{8,12},{12,8},{1,5},{5,1},{9,13},{13,9},{2,6},{6,2},{1... | collective-permute-start | bytes 786440 | tf_op jit(solution)/shard_map/ppermute | solution.py:28
  16.0 11.7 %collective-permute-start.3 = (bf16[2,80,256]{2,1,0:T(8,128)(2,1)S(1)}, bf16[2,80,256]{2,1,0:T(8,128)(2,1)S(1)}, u32[]{:S(2)}, u32[]{:S(2)}) collective-permute-start(bf16[2,80,256]{2,1,0:T(8,128)(2,1)S(1)} %get-tuple-element.29), channel_id=1, source_target_pairs={{0,4},{4,0},{8,12},{12,8},{1,5},{5,1},{9,13},{13,9},{2,6},{6,2},{1... | collective-permute-start | bytes 245768 | tf_op jit(solution)/shard_map/ppermute | solution.py:28
  17.5 10.2 %collective-permute-start.4 = (bf16[2,64,256]{2,1,0:T(8,128)(2,1)S(1)}, bf16[2,64,256]{2,1,0:T(8,128)(2,1)S(1)}, u32[]{:S(2)}, u32[]{:S(2)}) collective-permute-start(bf16[2,64,256]{2,1,0:T(8,128)(2,1)S(1)} %get-tuple-element.30), channel_id=1, source_target_pairs={{0,4},{4,0},{8,12},{12,8},{1,5},{5,1},{9,13},{13,9},{2,6},{6,2},{1... | collective-permute-start | bytes 196616 | tf_op jit(solution)/shard_map/ppermute | solution.py:28
  27.8 6.2 %collective-permute-start.5 = (bf16[1,80,256]{2,1,0:T(8,128)(2,1)S(1)}, bf16[1,80,256]{2,1,0:T(8,128)(2,1)S(1)}, u32[]{:S(2)}, u32[]{:S(2)}) collective-permute-start(bf16[1,80,256]{2,1,0:T(8,128)(2,1)S(1)} %get-tuple-element.32), channel_id=1, source_target_pairs={{0,8},{4,12},{8,0},{12,4},{1,9},{5,13},{9,1},{13,5},{2,10},{6,14},... | collective-permute-start | bytes 122888 | tf_op jit(solution)/shard_map/ppermute | solution.py:28
  29.1 4.8 %collective-permute-start.6 = (bf16[1,64,256]{2,1,0:T(8,128)(2,1)S(1)}, bf16[1,64,256]{2,1,0:T(8,128)(2,1)S(1)}, u32[]{:S(2)}, u32[]{:S(2)}) collective-permute-start(bf16[1,64,256]{2,1,0:T(8,128)(2,1)S(1)} %get-tuple-element.33), channel_id=1, source_target_pairs={{0,8},{4,12},{8,0},{12,4},{1,9},{5,13},{9,1},{13,5},{2,10},{6,14},... | collective-permute-start | bytes 98312 | tf_op jit(solution)/shard_map/ppermute | solution.py:28

commit v7 on v6

--- a/solution.py
+++ b/solution.py
@@ -12,8 +12,6 @@
 STEPS = 2
 STAT_ROWS = 16
 KEEP_ROWS = 8
-HEIGHTS = (80, 64)
-PIECES = len(HEIGHTS)
 FAR = -1e30
 RATE = HD ** (-0.5) * 1.4426950408889634
 
@@ -28,11 +26,18 @@
     return lax.ppermute(message, "seq", [(i, i ^ k) for i in range(count)])
 
 
+def messages(count, capacity):
+    far = [(k, 0, capacity) for k in reversed(range(count // 2, count))]
+    half = capacity // 2
+    near = [(k, first, half) for k in reversed(range(1, count // 2)) for first in (0, half)]
+    return far + near + [(0, 0, capacity)]
+
+
 def place_kernel(owner_any, deltas_any, anchors_any, scales_any, *refs):
     receivers = lax.axis_size("seq")
     me = lax.axis_index("seq")
-    outs = refs[:receivers]
-    owner_ref, source_ref, count_ref, deltas_ref, anchors_ref, scales_ref, sems = refs[receivers:]
+    outs = refs[:-7]
+    owner_ref, source_ref, count_ref, deltas_ref, anchors_ref, scales_ref, sems = refs[-7:]
     blocks = owner_ref.shape[0]
     rows = deltas_ref.shape[0] // blocks
     capacity = blocks // receivers
@@ -73,8 +78,8 @@
         load.wait()
     odd = lax.broadcasted_iota(jnp.int32, (8, HD), 0) % 2 == 1
     scale = jnp.where(odd, scales_ref[1:2, :], scales_ref[0:1, :])[None]
-    for k, out_ref in zip(reversed(range(receivers)), outs):
-        first = (me ^ k) * capacity
+    for (k, start, count), out_ref in zip(messages(receivers, capacity), outs):
+        first = (me ^ k) * capacity + start
 
         def one_slot(slot, carry, first=first, out_ref=out_ref):
             block = source_ref[first + slot]
@@ -89,18 +94,18 @@
             )
             return carry
 
-        lax.fori_loop(0, capacity, one_slot, 0, unroll=min(8, capacity))
+        lax.fori_loop(0, count, one_slot, 0, unroll=min(8, count))
 
 
 def settle_kernel(*refs):
     receivers = lax.axis_size("seq")
     me = lax.axis_index("seq")
-    got, pages, sems = refs[1:receivers], refs[receivers], refs[receivers + 1]
-    size = got[0].shape[0]
+    got, pages, sems = refs[1:-2], refs[-2], refs[-1]
+    capacity = pages.shape[0] // receivers
     copies = []
-    for k in range(1, receivers):
-        first = pl.multiple_of((me ^ k) * size, size)
-        copy = pltpu.make_async_copy(got[-k], pages.at[pl.ds(first, size), :], sems.at[k - 1])
+    for index, (k, start, count) in enumerate(messages(receivers, capacity)[:-1]):
+        first = pl.multiple_of((me ^ k) * capacity + start, count)
+        copy = pltpu.make_async_copy(got[index], pages.at[pl.ds(first, count), :], sems.at[index])
         copy.start()
         copies.append(copy)
     for copy in copies:
@@ -121,9 +126,9 @@
     rest = jnp.zeros((STAT_ROWS - len(stats), top.shape[1]), jnp.bfloat16)
     block = jnp.concatenate([summed.astype(jnp.bfloat16)] + stats + [rest], axis=0)
     first = 0
-    for height, ref in zip(HEIGHTS, refs):
-        ref[index] = block[first : first + height]
-        first += height
+    for ref in refs:
+        ref[index] = block[first : first + ref.shape[1]]
+        first += ref.shape[1]
 
 
 def unpacked(refs, index):
@@ -157,9 +162,8 @@
 
 def attend_kernel(*refs):
     me = lax.axis_index("seq")
-    sources, mine_any, refs = refs[:7], refs[7], refs[8:]
-    send, refs = refs[:PIECES], refs[PIECES:]
-    keep_ref, pages_any, *targets, wide_ref, keys_ref, values_ref, asked_ref, sems = refs
+    sources, mine_any, *send, keep_ref, pages_any = refs[:7], refs[7], *refs[8:-12]
+    *targets, wide_ref, keys_ref, values_ref, asked_ref, sems = refs[-12:]
     loads = [
         pltpu.make_async_copy(source, target, sems.at[index])
         for index, (source, target) in enumerate(zip(sources, targets))
@@ -288,8 +292,8 @@
     own_pages.wait()
 
 
-def join_kernel(keep_ref, *refs):
-    got, send, next_ref = refs[:PIECES], refs[PIECES : 2 * PIECES], refs[2 * PIECES]
+def join_kernel(came, keep_ref, *refs):
+    got, send, next_ref = refs[:came], refs[came:-1], refs[-1]
     for index in range(keep_ref.shape[0]):
         partial = joined(taken(keep_ref[index]), unpacked(got, index))
         if index % 2 == 1:
@@ -299,8 +303,8 @@
 
 
 def finish_kernel(keep_ref, *refs):
-    summed, _, total = joined(taken(keep_ref[0]), unpacked(refs[:PIECES], 0))
-    refs[PIECES][...] = (summed / total).T.astype(jnp.bfloat16)
+    summed, _, total = joined(taken(keep_ref[0]), unpacked(refs[:-1], 0))
+    refs[-1][...] = (summed / total).T.astype(jnp.bfloat16)
 
 
 def in_hbm(arrays):
@@ -322,14 +326,14 @@
     flat_queries = queries.reshape(rows, steps, GQ, HD).transpose(0, 2, 1, 3).reshape(-1, HD)
     flat_new = new_kv.reshape(rows_dev * 4, HD)
 
-    hand = jax.ShapeDtypeStruct((tokens * 2 // senders, HD), jnp.bfloat16)
     whole = jax.ShapeDtypeStruct((tokens * 2, HD), jnp.bfloat16)
-
+    plan = messages(senders, blocks // senders)
+    block_rows = tokens * 2 // blocks
     *sent, mine = pl.pallas_call(
         place_kernel,
-        out_shape=[hand] * senders,
+        out_shape=[jax.ShapeDtypeStruct((slots * block_rows, HD), jnp.bfloat16) for _, _, slots in plan],
         in_specs=[HBM] * 4,
-        out_specs=[VMEM] * senders,
+        out_specs=[VMEM] * len(plan),
         scratch_shapes=[
             pltpu.SMEM((blocks,), jnp.int32),
             pltpu.SMEM((blocks,), jnp.int32),
@@ -342,15 +346,14 @@
         compiler_params=small,
         name="place",
     )(*in_hbm([owner_map, flat_deltas, flat_anchors, scales]))
-    sent = [mine] + sent[::-1]
-
-    got = [None] * senders
+
     sent, mine, late_deltas = lax.optimization_barrier((sent, mine, flat_deltas))
-    for k in reversed(range(1, senders)):
-        got[k] = exchange(sent[k], k)
+    distant = senders // 2
+    got = [exchange(message, k) for message, (k, _, _) in zip(sent[:distant], plan)]
 
     def parted(count):
-        return [jax.ShapeDtypeStruct((count // 2, height, width), jnp.bfloat16) for height in HEIGHTS] + [
+        heights = (HD // 2 + STAT_ROWS, HD // 2) if count > 2 else (HD + STAT_ROWS,)
+        return [jax.ShapeDtypeStruct((count // 2, height, width), jnp.bfloat16) for height in heights] + [
             jax.ShapeDtypeStruct((count // 2, HD + KEEP_ROWS, width), jnp.float32)
         ]
 
@@ -359,7 +362,7 @@
         attend_kernel,
         out_shape=parted(senders) + [whole],
         in_specs=[HBM] * len(needed) + [ANY],
-        out_specs=[VMEM] * (PIECES + 1) + [HBM],
+        out_specs=[VMEM] * len(parted(senders)) + [HBM],
         scratch_shapes=[
             (pltpu.SMEM if array.dtype == jnp.int32 else pltpu.VMEM)(array.shape, array.dtype)
             for array in needed
@@ -381,34 +384,38 @@
     )(*in_hbm(needed), mine)
 
     k, count = 1, senders // 2
+    passed = [exchange(piece, k) for piece in send]
+    rest, passed = lax.optimization_barrier((sent[distant:], passed))
+    got += [exchange(message, k) for message, (k, _, _) in zip(rest, plan[distant:])]
     while count > 1:
         *send, keep = pl.pallas_call(
-            join_kernel,
+            functools.partial(join_kernel, len(passed)),
             out_shape=parted(count),
-            in_specs=[VMEM] * (PIECES + 1),
-            out_specs=[VMEM] * (PIECES + 1),
+            in_specs=[VMEM] * (len(passed) + 1),
+            out_specs=[VMEM] * len(parted(count)),
             compiler_params=small,
             name="join",
-        )(keep, *[exchange(piece, k) for piece in send])
+        )(keep, *passed)
         k, count = 2 * k, count // 2
+        passed = [exchange(piece, k) for piece in send]
     attended = pl.pallas_call(
         finish_kernel,
         out_shape=jax.ShapeDtypeStruct((width, HD), jnp.bfloat16),
-        in_specs=[VMEM] * (PIECES + 1),
+        in_specs=[VMEM] * (len(passed) + 1),
         out_specs=VMEM,
         compiler_params=small,
         name="finish",
-    )(keep, *[exchange(piece, k) for piece in send])
+    )(keep, *passed)
     pages = pl.pallas_call(
         settle_kernel,
         out_shape=whole,
-        in_specs=[HBM] + [ANY] * (senders - 1),
+        in_specs=[HBM] + [ANY] * len(got),
         out_specs=HBM,
-        scratch_shapes=[pltpu.SemaphoreType.DMA((senders - 1,))],
+        scratch_shapes=[pltpu.SemaphoreType.DMA((len(got),))],
         input_output_aliases={0: 0},
         compiler_params=small,
         name="settle",
-    )(pages, *reversed(got[1:]))
+    )(pages, *got)
     pages = pages.reshape(blocks, tokens // blocks, 2, HD)
     attended = (
         attended.reshape(rows_dev, GQ, steps, HD).transpose(0, 2, 1, 3).reshape(rows_dev, steps, GQ * HD)

time: 35.8 us -> 37.8 us (1.056)
  waiting for transfers between devices: 12.7 us -> 14.8 us
    ppermute x7, waiting for transfers between devices: 12.7 us -> 14.8 us  [exchange(): return lax.ppermute(message, 'seq', [(i, i ^ k) for i in range(count)])]
  transfers between devices with their start and end apart: 7 -> 7, of which waited for: 2 -> 4; matrix products, arithmetic and copies ran while one was open for 0% -> 0% of each run, Pallas kernels for 24% -> 23%
where the time goes in v7:
time: 37.8 us; the launch traced here: 37.6 us
  waiting for transfers between devices  14.8 us (39%)
  Pallas kernels  11.4 us (30%)
  starting transfers between devices  10.8 us (29%)
  between operations  0.66 us (2%)
    ppermute x7, waiting for transfers between devices, exchange(): return lax.ppermute(message, 'seq', [(i, i ^ k) for i in range(count)])  14.8 us
    ppermute x7, starting transfers between devices, exchange(): return lax.ppermute(message, 'seq', [(i, i ^ k) for i in range(count)])  10.8 us
    pallas_call x1, Pallas kernels, per_device(): pl.pallas_call(attend_kernel, out_shape=parted(senders) + [whole], in_spe...  7.74 us
    pallas_call x1, Pallas kernels, per_device(): pl.pallas_call(place_kernel, out_shape=[jax.ShapeDtypeStruct((slots * blo...  1.87 us
    pallas_call x1, Pallas kernels, per_device(): pl.pallas_call(settle_kernel, out_shape=whole, in_specs=[HBM] + [ANY] * l...  0.91 us
    pallas_call x1, Pallas kernels, per_device(): pl.pallas_call(finish_kernel, out_shape=jax.ShapeDtypeStruct((width, HD),...  0.76 us
  transfers between devices with their start and end apart: 7, of which 4 were waited for; matrix products, arithmetic and copies ran while one was open for 0% of the time, Pallas kernels for 23%

profile of v7, /device:TPU:0, one launch (start us, length us, event | category | flops | bytes accessed | tf_op | source)
XLA Modules:
  0.0 37.6 jit_solution(4221282000341789387)
XLA Ops:
  0.6 1.9 %place.1 = (bf16[1024,128]{1,0:T(8,128)(2,1)S(1)}, bf16[1024,128]{1,0:T(8,128)(2,1)S(1)}, bf16[512,128]{1,0:T(8,128)(2,1)S(1)}, bf16[512,128]{1,0:T(8,128)(2,1)S(1)}, bf16[1024,128]{1,0:T(8,128)(2,1)S(1)}) custom-call(s32[128]{0:T(128)} %owner_any.1, bf16[4096,128]{1,0:T(8,128)(2,1)} %bitcast.14, f32[256,128]{1,0:T(8,128)} %bitcast.17, f32[2,128]{1,0:T(2,128)} %refs_2_.1), custom_call_target="tpu_custom_call" | custom-call | tf_op jit(solution)/shard_map/place/pallas_call | solution.py:332
  2.5 5.1 %collective-permute-start = (bf16[1024,128]{1,0:T(8,128)(2,1)S(1)}, bf16[1024,128]{1,0:T(8,128)(2,1)S(1)}, u32[]{:S(2)}, u32[]{:S(2)}) collective-permute-start(bf16[1024,128]{1,0:T(8,128)(2,1)S(1)} %get-tuple-element.31), channel_id=1, source_target_pairs={{0,12},{4,8},{8,4},{12,0},{1,13},{5,9},{9,5},{13,1},{2,14},{6,10},... | collective-permute-start | bytes 786440 | tf_op jit(solution)/shard_map/ppermute | solution.py:26
  7.6 0.0 collective-permute-start.1
  7.6 7.7 %attend.1 = (bf16[2,80,256]{2,1,0:T(8,128)(2,1)S(1)}, bf16[2,64,256]{2,1,0:T(8,128)(2,1)S(1)}, f32[2,136,256]{2,1,0:T(8,128)S(1)}, bf16[4096,128]{1,0:T(8,128)(2,1)}) custom-call(bf16[4096,128]{1,0:T(8,128)(2,1)} %bitcast.15, f32[256,128]{1,0:T(8,128)} %bitcast.18, f32[2,128]{1,0:T(2,128)} %refs_2_.1, s32[4]{0:T(128)} %refs_3_.1, s32[64]{0:T(128)} %refs_4_.1, ...), custom_call_target="tpu_custom_call" | custom-call | flops 1610612736 | bytes 1572864 | tf_op jit(solution)/shard_map/attend/pallas_call | solution.py:361
  15.4 0.7 %collective-permute-start.2 = (bf16[2,80,256]{2,1,0:T(8,128)(2,1)S(1)}, bf16[2,80,256]{2,1,0:T(8,128)(2,1)S(1)}, u32[]{:S(2)}, u32[]{:S(2)}) collective-permute-start(bf16[2,80,256]{2,1,0:T(8,128)(2,1)S(1)} %get-tuple-element.35), channel_id=1, source_target_pairs={{0,4},{4,0},{8,12},{12,8},{1,5},{5,1},{9,13},{13,9},{2,6},{6,2},{1... | collective-permute-start | bytes 245768 | tf_op jit(solution)/shard_map/ppermute | solution.py:26
  16.1 1.4 %collective-permute-start.3 = (bf16[2,64,256]{2,1,0:T(8,128)(2,1)S(1)}, bf16[2,64,256]{2,1,0:T(8,128)(2,1)S(1)}, u32[]{:S(2)}, u32[]{:S(2)}) collective-permute-start(bf16[2,64,256]{2,1,0:T(8,128)(2,1)S(1)} %get-tuple-element.36), channel_id=1, source_target_pairs={{0,4},{4,0},{8,12},{12,8},{1,5},{5,1},{9,13},{13,9},{2,6},{6,2},{1... | collective-permute-start | bytes 196616 | tf_op jit(solution)/shard_map/ppermute | solution.py:26
  17.5 4.5 %collective-permute-done.3.refs_1_ = bf16[2,64,256]{2,1,0:T(8,128)(2,1)S(1)} collective-permute-done((bf16[2,64,256]{2,1,0:T(8,128)(2,1)S(1)}, bf16[2,64,256]{2,1,0:T(8,128)(2,1)S(1)}, u32[]{:S(2)}, u32[]{:S(2)}) %collective-permute-start.3) | collective-permute-done | bytes 65568 | tf_op jit(solution)/shard_map/ppermute | solution.py:26
  22.0 0.0 collective-permute-done.2.refs_0_
  22.0 2.5 %collective-permute-start.4 = (bf16[512,128]{1,0:T(8,128)(2,1)S(1)}, bf16[512,128]{1,0:T(8,128)(2,1)S(1)}, u32[]{:S(2)}, u32[]{:S(2)}) collective-permute-start(bf16[512,128]{1,0:T(8,128)(2,1)S(1)} %get-tuple-element.37), channel_id=1, source_target_pairs={{0,4},{4,0},{8,12},{12,8},{1,5},{5,1},{9,13},{13,9},{2,6},{6,2},{1... | collective-permute-start | bytes 393224 | tf_op jit(solution)/shard_map/ppermute | solution.py:26
  24.5 0.0 collective-permute-start.5
  24.5 0.1 join.1
  24.6 1.1 %collective-permute-start.6 = (bf16[1,144,256]{2,1,0:T(8,128)(2,1)S(1)}, bf16[1,144,256]{2,1,0:T(8,128)(2,1)S(1)}, u32[]{:S(2)}, u32[]{:S(2)}) collective-permute-start(bf16[1,144,256]{2,1,0:T(8,128)(2,1)S(1)} %get-tuple-element.43), channel_id=1, source_target_pairs={{0,8},{4,12},{8,0},{12,4},{1,9},{5,13},{9,1},{13,5},{2,10},{6,14},... | collective-permute-start | bytes 221192 | tf_op jit(solution)/shard_map/ppermute | solution.py:26
  25.7 7.6 %collective-permute-done.6.refs_0_ = bf16[1,144,256]{2,1,0:T(8,128)(2,1)S(1)} collective-permute-done((bf16[1,144,256]{2,1,0:T(8,128)(2,1)S(1)}, bf16[1,144,256]{2,1,0:T(8,128)(2,1)S(1)}, u32[]{:S(2)}, u32[]{:S(2)}) %collective-permute-start.6) | collective-permute-done | bytes 73760 | tf_op jit(solution)/shard_map/ppermute | solution.py:26
  33.2 0.8 %finish.1 = bf16[256,128]{1,0:T(8,128)(2,1)} custom-call(f32[1,136,256]{2,1,0:T(8,128)S(1)} %get-tuple-element.42.keep_ref, bf16[1,144,256]{2,1,0:T(8,128)(2,1)S(1)} %collective-permute-done.6.refs_0_), custom_call_target="tpu_custom_call" | custom-call | tf_op jit(solution)/shard_map/finish/pallas_call | solution.py:401
  34.0 0.5 %collective-permute-done.4.refs_3_ = bf16[512,128]{1,0:T(8,128)(2,1)S(1)} collective-permute-done((bf16[512,128]{1,0:T(8,128)(2,1)S(1)}, bf16[512,128]{1,0:T(8,128)(2,1)S(1)}, u32[]{:S(2)}, u32[]{:S(2)}) %collective-permute-start.4) | collective-permute-done | bytes 131104 | tf_op jit(solution)/shard_map/ppermute | solution.py:26
  34.5 2.2 %collective-permute-done.5.refs_4_ = bf16[512,128]{1,0:T(8,128)(2,1)S(1)} collective-permute-done((bf16[512,128]{1,0:T(8,128)(2,1)S(1)}, bf16[512,128]{1,0:T(8,128)(2,1)S(1)}, u32[]{:S(2)}, u32[]{:S(2)}) %collective-permute-start.5) | collective-permute-done | bytes 131104 | tf_op jit(solution)/shard_map/ppermute | solution.py:26
  36.7 0.0 collective-permute-done.refs_1_
  36.7 0.0 collective-permute-done.1.refs_2_
  36.7 0.9 %settle.1 = bf16[4096,128]{1,0:T(8,128)(2,1)} custom-call(bf16[4096,128]{1,0:T(8,128)(2,1)} %get-tuple-element.30.refs_0_, bf16[1024,128]{1,0:T(8,128)(2,1)S(1)} %collective-permute-done.refs_1_, bf16[1024,128]{1,0:T(8,128)(2,1)S(1)} %collective-permute-done.1.refs_2_, ...), custom_call_target="tpu_custom_call", output_to_operand_aliasing={{}: (0, {})} | custom-call | tf_op jit(solution)/shard_map/settle/pallas_call | solution.py:409
Async XLA Ops:
  2.5 34.2 %collective-permute-start = (bf16[1024,128]{1,0:T(8,128)(2,1)S(1)}, bf16[1024,128]{1,0:T(8,128)(2,1)S(1)}, u32[]{:S(2)}, u32[]{:S(2)}) collective-permute-start(bf16[1024,128]{1,0:T(8,128)(2,1)S(1)} %get-tuple-element.31), channel_id=1, source_target_pairs={{0,12},{4,8},{8,4},{12,0},{1,13},{5,9},{9,5},{13,1},{2,14},{6,10},... | collective-permute-start | bytes 786440 | tf_op jit(solution)/shard_map/ppermute | solution.py:26
  7.6 29.1 %collective-permute-start.1 = (bf16[1024,128]{1,0:T(8,128)(2,1)S(1)}, bf16[1024,128]{1,0:T(8,128)(2,1)S(1)}, u32[]{:S(2)}, u32[]{:S(2)}) collective-permute-start(bf16[1024,128]{1,0:T(8,128)(2,1)S(1)} %get-tuple-element.32), channel_id=1, source_target_pairs={{0,8},{4,12},{8,0},{12,4},{1,9},{5,13},{9,1},{13,5},{2,10},{6,14},... | collective-permute-start | bytes 786440 | tf_op jit(solution)/shard_map/ppermute | solution.py:26
  15.4 6.6 %collective-permute-start.2 = (bf16[2,80,256]{2,1,0:T(8,128)(2,1)S(1)}, bf16[2,80,256]{2,1,0:T(8,128)(2,1)S(1)}, u32[]{:S(2)}, u32[]{:S(2)}) collective-permute-start(bf16[2,80,256]{2,1,0:T(8,128)(2,1)S(1)} %get-tuple-element.35), channel_id=1, source_target_pairs={{0,4},{4,0},{8,12},{12,8},{1,5},{5,1},{9,13},{13,9},{2,6},{6,2},{1... | collective-permute-start | bytes 245768 | tf_op jit(solution)/shard_map/ppermute | solution.py:26
  16.1 5.9 %collective-permute-start.3 = (bf16[2,64,256]{2,1,0:T(8,128)(2,1)S(1)}, bf16[2,64,256]{2,1,0:T(8,128)(2,1)S(1)}, u32[]{:S(2)}, u32[]{:S(2)}) collective-permute-start(bf16[2,64,256]{2,1,0:T(8,128)(2,1)S(1)} %get-tuple-element.36), channel_id=1, source_target_pairs={{0,4},{4,0},{8,12},{12,8},{1,5},{5,1},{9,13},{13,9},{2,6},{6,2},{1... | collective-permute-start | bytes 196616 | tf_op jit(solution)/shard_map/ppermute | solution.py:26
  22.0 12.5 %collective-permute-start.4 = (bf16[512,128]{1,0:T(8,128)(2,1)S(1)}, bf16[512,128]{1,0:T(8,128)(2,1)S(1)}, u32[]{:S(2)}, u32[]{:S(2)}) collective-permute-start(bf16[512,128]{1,0:T(8,128)(2,1)S(1)} %get-tuple-element.37), channel_id=1, source_target_pairs={{0,4},{4,0},{8,12},{12,8},{1,5},{5,1},{9,13},{13,9},{2,6},{6,2},{1... | collective-permute-start | bytes 393224 | tf_op jit(solution)/shard_map/ppermute | solution.py:26
  24.5 12.2 %collective-permute-start.5 = (bf16[512,128]{1,0:T(8,128)(2,1)S(1)}, bf16[512,128]{1,0:T(8,128)(2,1)S(1)}, u32[]{:S(2)}, u32[]{:S(2)}) collective-permute-start(bf16[512,128]{1,0:T(8,128)(2,1)S(1)} %get-tuple-element.38), channel_id=1, source_target_pairs={{0,4},{4,0},{8,12},{12,8},{1,5},{5,1},{9,13},{13,9},{2,6},{6,2},{1... | collective-permute-start | bytes 393224 | tf_op jit(solution)/shard_map/ppermute | solution.py:26
  24.6 8.6 %collective-permute-start.6 = (bf16[1,144,256]{2,1,0:T(8,128)(2,1)S(1)}, bf16[1,144,256]{2,1,0:T(8,128)(2,1)S(1)}, u32[]{:S(2)}, u32[]{:S(2)}) collective-permute-start(bf16[1,144,256]{2,1,0:T(8,128)(2,1)S(1)} %get-tuple-element.43), channel_id=1, source_target_pairs={{0,8},{4,12},{8,0},{12,4},{1,9},{5,13},{9,1},{13,5},{2,10},{6,14},... | collective-permute-start | bytes 221192 | tf_op jit(solution)/shard_map/ppermute | solution.py:26

commit v8 on v7

--- a/solution.py
+++ b/solution.py
@@ -384,8 +384,8 @@
     )(*in_hbm(needed), mine)
 
     k, count = 1, senders // 2
+    rest, send = lax.optimization_barrier((sent[distant:], send))
     passed = [exchange(piece, k) for piece in send]
-    rest, passed = lax.optimization_barrier((sent[distant:], passed))
     got += [exchange(message, k) for message, (k, _, _) in zip(rest, plan[distant:])]
     while count > 1:
         *send, keep = pl.pallas_call(

time: 37.8 us -> 35.1 us (0.929)
  waiting for transfers between devices: 14.8 us -> 11.2 us
  starting transfers between devices: 10.8 us -> 11.7 us
    ppermute x7, waiting for transfers between devices: 14.8 us -> 11.2 us  [exchange(): return lax.ppermute(message, 'seq', [(i, i ^ k) for i in range(count)])]
    ppermute x7, starting transfers between devices: 10.8 us -> 11.7 us  [exchange(): return lax.ppermute(message, 'seq', [(i, i ^ k) for i in range(count)])]
  transfers between devices with their start and end apart: 7 -> 7, of which waited for: 4 -> 2; matrix products, arithmetic and copies ran while one was open for 0% -> 0% of each run, Pallas kernels for 23% -> 25%
where the time goes in v8:
time: 35.1 us; the launch traced here: 34.9 us
  starting transfers between devices  11.7 us (33%)
  Pallas kernels  11.4 us (32%)
  waiting for transfers between devices  11.2 us (32%)
  between operations  0.67 us (2%)
    ppermute x7, starting transfers between devices, exchange(): return lax.ppermute(message, 'seq', [(i, i ^ k) for i in range(count)])  11.7 us
    ppermute x7, waiting for transfers between devices, exchange(): return lax.ppermute(message, 'seq', [(i, i ^ k) for i in range(count)])  11.2 us
    pallas_call x1, Pallas kernels, per_device(): pl.pallas_call(attend_kernel, out_shape=parted(senders) + [whole], in_spe...  7.74 us
    pallas_call x1, Pallas kernels, per_device(): pl.pallas_call(place_kernel, out_shape=[jax.ShapeDtypeStruct((slots * blo...  1.87 us
    pallas_call x1, Pallas kernels, per_device(): pl.pallas_call(settle_kernel, out_shape=whole, in_specs=[HBM] + [ANY] * l...  0.92 us
    pallas_call x1, Pallas kernels, per_device(): pl.pallas_call(finish_kernel, out_shape=jax.ShapeDtypeStruct((width, HD),...  0.76 us
  transfers between devices with their start and end apart: 7, of which 2 were waited for; matrix products, arithmetic and copies ran while one was open for 0% of the time, Pallas kernels for 25%

profile of v8, /device:TPU:0, one launch (start us, length us, event | category | flops | bytes accessed | tf_op | source)
XLA Modules:
  0.0 34.9 jit_solution(3526849285882454162)
XLA Ops:
  0.6 1.9 %place.1 = (bf16[1024,128]{1,0:T(8,128)(2,1)S(1)}, bf16[1024,128]{1,0:T(8,128)(2,1)S(1)}, bf16[512,128]{1,0:T(8,128)(2,1)S(1)}, bf16[512,128]{1,0:T(8,128)(2,1)S(1)}, bf16[1024,128]{1,0:T(8,128)(2,1)S(1)}) custom-call(s32[128]{0:T(128)} %owner_any.1, bf16[4096,128]{1,0:T(8,128)(2,1)} %bitcast.14, f32[256,128]{1,0:T(8,128)} %bitcast.17, f32[2,128]{1,0:T(2,128)} %refs_2_.1), custom_call_target="tpu_custom_call" | custom-call | tf_op jit(solution)/shard_map/place/pallas_call | solution.py:332
  2.5 5.1 %collective-permute-start = (bf16[1024,128]{1,0:T(8,128)(2,1)S(1)}, bf16[1024,128]{1,0:T(8,128)(2,1)S(1)}, u32[]{:S(2)}, u32[]{:S(2)}) collective-permute-start(bf16[1024,128]{1,0:T(8,128)(2,1)S(1)} %get-tuple-element.31), channel_id=1, source_target_pairs={{0,12},{4,8},{8,4},{12,0},{1,13},{5,9},{9,5},{13,1},{2,14},{6,10},... | collective-permute-start | bytes 786440 | tf_op jit(solution)/shard_map/ppermute | solution.py:26
  7.6 0.0 collective-permute-start.1
  7.6 7.7 %attend.1 = (bf16[2,80,256]{2,1,0:T(8,128)(2,1)S(1)}, bf16[2,64,256]{2,1,0:T(8,128)(2,1)S(1)}, f32[2,136,256]{2,1,0:T(8,128)S(1)}, bf16[4096,128]{1,0:T(8,128)(2,1)}) custom-call(bf16[4096,128]{1,0:T(8,128)(2,1)} %bitcast.15, f32[256,128]{1,0:T(8,128)} %bitcast.18, f32[2,128]{1,0:T(2,128)} %refs_2_.1, s32[4]{0:T(128)} %refs_3_.1, s32[64]{0:T(128)} %refs_4_.1, ...), custom_call_target="tpu_custom_call" | custom-call | flops 1610612736 | bytes 1572864 | tf_op jit(solution)/shard_map/attend/pallas_call | solution.py:361
  15.4 0.7 %collective-permute-start.5 = (bf16[2,64,256]{2,1,0:T(8,128)(2,1)S(1)}, bf16[2,64,256]{2,1,0:T(8,128)(2,1)S(1)}, u32[]{:S(2)}, u32[]{:S(2)}) collective-permute-start(bf16[2,64,256]{2,1,0:T(8,128)(2,1)S(1)} %get-tuple-element.41), channel_id=1, source_target_pairs={{0,4},{4,0},{8,12},{12,8},{1,5},{5,1},{9,13},{13,9},{2,6},{6,2},{1... | collective-permute-start | bytes 196616 | tf_op jit(solution)/shard_map/ppermute | solution.py:26
  16.1 1.4 %collective-permute-start.4 = (bf16[2,80,256]{2,1,0:T(8,128)(2,1)S(1)}, bf16[2,80,256]{2,1,0:T(8,128)(2,1)S(1)}, u32[]{:S(2)}, u32[]{:S(2)}) collective-permute-start(bf16[2,80,256]{2,1,0:T(8,128)(2,1)S(1)} %get-tuple-element.40), channel_id=1, source_target_pairs={{0,4},{4,0},{8,12},{12,8},{1,5},{5,1},{9,13},{13,9},{2,6},{6,2},{1... | collective-permute-start | bytes 245768 | tf_op jit(solution)/shard_map/ppermute | solution.py:26
  17.5 0.7 %collective-permute-start.2 = (bf16[512,128]{1,0:T(8,128)(2,1)S(1)}, bf16[512,128]{1,0:T(8,128)(2,1)S(1)}, u32[]{:S(2)}, u32[]{:S(2)}) collective-permute-start(bf16[512,128]{1,0:T(8,128)(2,1)S(1)} %get-tuple-element.37), channel_id=1, source_target_pairs={{0,4},{4,0},{8,12},{12,8},{1,5},{5,1},{9,13},{13,9},{2,6},{6,2},{1... | collective-permute-start | bytes 393224 | tf_op jit(solution)/shard_map/ppermute | solution.py:26
  18.1 3.2 %collective-permute-done.5.refs_1_ = bf16[2,64,256]{2,1,0:T(8,128)(2,1)S(1)} collective-permute-done((bf16[2,64,256]{2,1,0:T(8,128)(2,1)S(1)}, bf16[2,64,256]{2,1,0:T(8,128)(2,1)S(1)}, u32[]{:S(2)}, u32[]{:S(2)}) %collective-permute-start.5) | collective-permute-done | bytes 65568 | tf_op jit(solution)/shard_map/ppermute | solution.py:26
  21.4 2.5 %collective-permute-start.3 = (bf16[512,128]{1,0:T(8,128)(2,1)S(1)}, bf16[512,128]{1,0:T(8,128)(2,1)S(1)}, u32[]{:S(2)}, u32[]{:S(2)}) collective-permute-start(bf16[512,128]{1,0:T(8,128)(2,1)S(1)} %get-tuple-element.38), channel_id=1, source_target_pairs={{0,4},{4,0},{8,12},{12,8},{1,5},{5,1},{9,13},{13,9},{2,6},{6,2},{1... | collective-permute-start | bytes 393224 | tf_op jit(solution)/shard_map/ppermute | solution.py:26
  23.8 0.0 collective-permute-done.4.refs_0_
  23.8 0.1 join.1
  23.9 1.4 %collective-permute-start.6 = (bf16[1,144,256]{2,1,0:T(8,128)(2,1)S(1)}, bf16[1,144,256]{2,1,0:T(8,128)(2,1)S(1)}, u32[]{:S(2)}, u32[]{:S(2)}) collective-permute-start(bf16[1,144,256]{2,1,0:T(8,128)(2,1)S(1)} %get-tuple-element.43), channel_id=1, source_target_pairs={{0,8},{4,12},{8,0},{12,4},{1,9},{5,13},{9,1},{13,5},{2,10},{6,14},... | collective-permute-start | bytes 221192 | tf_op jit(solution)/shard_map/ppermute | solution.py:26
  25.3 7.9 %collective-permute-done.6.refs_0_ = bf16[1,144,256]{2,1,0:T(8,128)(2,1)S(1)} collective-permute-done((bf16[1,144,256]{2,1,0:T(8,128)(2,1)S(1)}, bf16[1,144,256]{2,1,0:T(8,128)(2,1)S(1)}, u32[]{:S(2)}, u32[]{:S(2)}) %collective-permute-start.6) | collective-permute-done | bytes 73760 | tf_op jit(solution)/shard_map/ppermute | solution.py:26
  33.2 0.8 %finish.1 = bf16[256,128]{1,0:T(8,128)(2,1)} custom-call(f32[1,136,256]{2,1,0:T(8,128)S(1)} %get-tuple-element.42.keep_ref, bf16[1,144,256]{2,1,0:T(8,128)(2,1)S(1)} %collective-permute-done.6.refs_0_), custom_call_target="tpu_custom_call" | custom-call | tf_op jit(solution)/shard_map/finish/pallas_call | solution.py:401
  34.0 0.0 collective-permute-done.2.refs_3_
  34.0 0.0 collective-permute-done.3.refs_4_
  34.0 0.0 collective-permute-done.refs_1_
  34.0 0.0 collective-permute-done.1.refs_2_
  34.0 0.9 %settle.1 = bf16[4096,128]{1,0:T(8,128)(2,1)} custom-call(bf16[4096,128]{1,0:T(8,128)(2,1)} %get-tuple-element.30.refs_0_, bf16[1024,128]{1,0:T(8,128)(2,1)S(1)} %collective-permute-done.refs_1_, bf16[1024,128]{1,0:T(8,128)(2,1)S(1)} %collective-permute-done.1.refs_2_, ...), custom_call_target="tpu_custom_call", output_to_operand_aliasing={{}: (0, {})} | custom-call | tf_op jit(solution)/shard_map/settle/pallas_call | solution.py:409
Async XLA Ops:
  2.5 31.5 %collective-permute-start = (bf16[1024,128]{1,0:T(8,128)(2,1)S(1)}, bf16[1024,128]{1,0:T(8,128)(2,1)S(1)}, u32[]{:S(2)}, u32[]{:S(2)}) collective-permute-start(bf16[1024,128]{1,0:T(8,128)(2,1)S(1)} %get-tuple-element.31), channel_id=1, source_target_pairs={{0,12},{4,8},{8,4},{12,0},{1,13},{5,9},{9,5},{13,1},{2,14},{6,10},... | collective-permute-start | bytes 786440 | tf_op jit(solution)/shard_map/ppermute | solution.py:26
  7.6 26.4 %collective-permute-start.1 = (bf16[1024,128]{1,0:T(8,128)(2,1)S(1)}, bf16[1024,128]{1,0:T(8,128)(2,1)S(1)}, u32[]{:S(2)}, u32[]{:S(2)}) collective-permute-start(bf16[1024,128]{1,0:T(8,128)(2,1)S(1)} %get-tuple-element.32), channel_id=1, source_target_pairs={{0,8},{4,12},{8,0},{12,4},{1,9},{5,13},{9,1},{13,5},{2,10},{6,14},... | collective-permute-start | bytes 786440 | tf_op jit(solution)/shard_map/ppermute | solution.py:26
  15.4 6.0 %collective-permute-start.5 = (bf16[2,64,256]{2,1,0:T(8,128)(2,1)S(1)}, bf16[2,64,256]{2,1,0:T(8,128)(2,1)S(1)}, u32[]{:S(2)}, u32[]{:S(2)}) collective-permute-start(bf16[2,64,256]{2,1,0:T(8,128)(2,1)S(1)} %get-tuple-element.41), channel_id=1, source_target_pairs={{0,4},{4,0},{8,12},{12,8},{1,5},{5,1},{9,13},{13,9},{2,6},{6,2},{1... | collective-permute-start | bytes 196616 | tf_op jit(solution)/shard_map/ppermute | solution.py:26
  16.1 7.8 %collective-permute-start.4 = (bf16[2,80,256]{2,1,0:T(8,128)(2,1)S(1)}, bf16[2,80,256]{2,1,0:T(8,128)(2,1)S(1)}, u32[]{:S(2)}, u32[]{:S(2)}) collective-permute-start(bf16[2,80,256]{2,1,0:T(8,128)(2,1)S(1)} %get-tuple-element.40), channel_id=1, source_target_pairs={{0,4},{4,0},{8,12},{12,8},{1,5},{5,1},{9,13},{13,9},{2,6},{6,2},{1... | collective-permute-start | bytes 245768 | tf_op jit(solution)/shard_map/ppermute | solution.py:26
  17.5 16.5 %collective-permute-start.2 = (bf16[512,128]{1,0:T(8,128)(2,1)S(1)}, bf16[512,128]{1,0:T(8,128)(2,1)S(1)}, u32[]{:S(2)}, u32[]{:S(2)}) collective-permute-start(bf16[512,128]{1,0:T(8,128)(2,1)S(1)} %get-tuple-element.37), channel_id=1, source_target_pairs={{0,4},{4,0},{8,12},{12,8},{1,5},{5,1},{9,13},{13,9},{2,6},{6,2},{1... | collective-permute-start | bytes 393224 | tf_op jit(solution)/shard_map/ppermute | solution.py:26
  21.4 12.7 %collective-permute-start.3 = (bf16[512,128]{1,0:T(8,128)(2,1)S(1)}, bf16[512,128]{1,0:T(8,128)(2,1)S(1)}, u32[]{:S(2)}, u32[]{:S(2)}) collective-permute-start(bf16[512,128]{1,0:T(8,128)(2,1)S(1)} %get-tuple-element.38), channel_id=1, source_target_pairs={{0,4},{4,0},{8,12},{12,8},{1,5},{5,1},{9,13},{13,9},{2,6},{6,2},{1... | collective-permute-start | bytes 393224 | tf_op jit(solution)/shard_map/ppermute | solution.py:26
  23.9 9.3 %collective-permute-start.6 = (bf16[1,144,256]{2,1,0:T(8,128)(2,1)S(1)}, bf16[1,144,256]{2,1,0:T(8,128)(2,1)S(1)}, u32[]{:S(2)}, u32[]{:S(2)}) collective-permute-start(bf16[1,144,256]{2,1,0:T(8,128)(2,1)S(1)} %get-tuple-element.43), channel_id=1, source_target_pairs={{0,8},{4,12},{8,0},{12,4},{1,9},{5,13},{9,1},{13,5},{2,10},{6,14},... | collective-permute-start | bytes 221192 | tf_op jit(solution)/shard_map/ppermute | solution.py:26

commit v9 on v8

--- a/solution.py
+++ b/solution.py
@@ -33,7 +33,7 @@
     return far + near + [(0, 0, capacity)]
 
 
-def place_kernel(owner_any, deltas_any, anchors_any, scales_any, *refs):
+def place_kernel(plan, owner_any, deltas_any, anchors_any, scales_any, *refs):
     receivers = lax.axis_size("seq")
     me = lax.axis_index("seq")
     outs = refs[:-7]
@@ -55,8 +55,9 @@
     for load in loads:
         load.start()
     bits = capacity.bit_length()
+    single = len(plan) == 1
     narrow = receivers * bits < 32
-    if not narrow:
+    if not narrow and not single:
         for owner in range(receivers):
             count_ref[owner] = owner * capacity
     loads[0].wait()
@@ -73,13 +74,17 @@
         source_ref[slot] = block
         return counts
 
-    lax.fori_loop(0, blocks, find, jnp.int32(0), unroll=8)
+    def find_one(block, slot):
+        source_ref[slot] = block
+        return slot + (owner_ref[block] == (me ^ plan[0][0])).astype(jnp.int32)
+
+    lax.fori_loop(0, blocks, find_one if single else find, jnp.int32(0), unroll=8)
     for load in loads[1:]:
         load.wait()
     odd = lax.broadcasted_iota(jnp.int32, (8, HD), 0) % 2 == 1
     scale = jnp.where(odd, scales_ref[1:2, :], scales_ref[0:1, :])[None]
-    for (k, start, count), out_ref in zip(messages(receivers, capacity), outs):
-        first = (me ^ k) * capacity + start
+    for (k, start, count), out_ref in zip(plan, outs):
+        first = start if single else (me ^ k) * capacity + start
 
         def one_slot(slot, carry, first=first, out_ref=out_ref):
             block = source_ref[first + slot]
@@ -97,21 +102,6 @@
         lax.fori_loop(0, count, one_slot, 0, unroll=min(8, count))
 
 
-def settle_kernel(*refs):
-    receivers = lax.axis_size("seq")
-    me = lax.axis_index("seq")
-    got, pages, sems = refs[1:-2], refs[-2], refs[-1]
-    capacity = pages.shape[0] // receivers
-    copies = []
-    for index, (k, start, count) in enumerate(messages(receivers, capacity)[:-1]):
-        first = pl.multiple_of((me ^ k) * capacity + start, count)
-        copy = pltpu.make_async_copy(got[index], pages.at[pl.ds(first, count), :], sems.at[index])
-        copy.start()
-        copies.append(copy)
-    for copy in copies:
-        copy.wait()
-
-
 def pieces(values):
     high = values.astype(jnp.bfloat16)
     rest = values - high.astype(jnp.float32)
@@ -120,19 +110,14 @@
     return [high, middle, low]
 
 
-def pack(refs, index, partial):
+def packed(partial):
     summed, top, total = partial
     stats = pieces(top) + pieces(total)
     rest = jnp.zeros((STAT_ROWS - len(stats), top.shape[1]), jnp.bfloat16)
-    block = jnp.concatenate([summed.astype(jnp.bfloat16)] + stats + [rest], axis=0)
-    first = 0
-    for ref in refs:
-        ref[index] = block[first : first + ref.shape[1]]
-        first += ref.shape[1]
-
-
-def unpacked(refs, index):
-    block = jnp.concatenate([ref[index] for ref in refs], axis=0)
+    return jnp.concatenate([summed.astype(jnp.bfloat16)] + stats + [rest], axis=0)
+
+
+def unpacked(block):
     stats = block[HD:, :].astype(jnp.float32)
     top = stats[0:1] + stats[1:2] + stats[2:3]
     total = stats[3:4] + stats[4:5] + stats[5:6]
@@ -162,7 +147,7 @@
 
 def attend_kernel(*refs):
     me = lax.axis_index("seq")
-    sources, mine_any, *send, keep_ref, pages_any = refs[:7], refs[7], *refs[8:-12]
+    sources, mine_any, send_ref, keep_ref, pages_any = refs[:7], *refs[7:-12]
     *targets, wide_ref, keys_ref, values_ref, asked_ref, sems = refs[-12:]
     loads = [
         pltpu.make_async_copy(source, target, sems.at[index])
@@ -249,7 +234,7 @@
 
             @pl.when(apart % 2 == 1)
             def _(partial=partial, apart=apart):
-                pack(send, apart // 2, partial)
+                send_ref[apart // 2] = packed(partial)
 
             @pl.when(apart % 2 == 0)
             def _(partial=partial, apart=apart):
@@ -292,19 +277,30 @@
     own_pages.wait()
 
 
-def join_kernel(came, keep_ref, *refs):
-    got, send, next_ref = refs[:came], refs[came:-1], refs[-1]
+def join_kernel(keep_ref, got_ref, send_ref, next_ref):
     for index in range(keep_ref.shape[0]):
-        partial = joined(taken(keep_ref[index]), unpacked(got, index))
+        partial = joined(taken(keep_ref[index]), unpacked(got_ref[index]))
         if index % 2 == 1:
-            pack(send, index // 2, partial)
+            send_ref[index // 2] = packed(partial)
         else:
             next_ref[index // 2] = held(partial)
 
 
-def finish_kernel(keep_ref, *refs):
-    summed, _, total = joined(taken(keep_ref[0]), unpacked(refs[:-1], 0))
-    refs[-1][...] = (summed / total).T.astype(jnp.bfloat16)
+def finish_kernel(keep_ref, got_ref, _, *refs):
+    *handed, out_ref, pages, sems = refs
+    receivers = lax.axis_size("seq")
+    me = lax.axis_index("seq")
+    size = pages.shape[0] // receivers
+    copies = []
+    for index, (k, start, count) in enumerate(messages(receivers, size)[:-1]):
+        first = pl.multiple_of((me ^ k) * size + start, count)
+        copy = pltpu.make_async_copy(handed[index], pages.at[pl.ds(first, count), :], sems.at[index])
+        copy.start()
+        copies.append(copy)
+    summed, _, total = joined(taken(keep_ref[0]), unpacked(got_ref[0]))
+    out_ref[...] = (summed / total).T.astype(jnp.bfloat16)
+    for copy in copies:
+        copy.wait()
 
 
 def in_hbm(arrays):
@@ -329,40 +325,46 @@
     whole = jax.ShapeDtypeStruct((tokens * 2, HD), jnp.bfloat16)
     plan = messages(senders, blocks // senders)
     block_rows = tokens * 2 // blocks
-    *sent, mine = pl.pallas_call(
-        place_kernel,
-        out_shape=[jax.ShapeDtypeStruct((slots * block_rows, HD), jnp.bfloat16) for _, _, slots in plan],
-        in_specs=[HBM] * 4,
-        out_specs=[VMEM] * len(plan),
-        scratch_shapes=[
-            pltpu.SMEM((blocks,), jnp.int32),
-            pltpu.SMEM((blocks,), jnp.int32),
-            pltpu.SMEM((senders,), jnp.int32),
-            pltpu.VMEM((tokens * 2, HD), jnp.bfloat16),
-            pltpu.VMEM((blocks * 2, HD), jnp.float32),
-            pltpu.VMEM((2, HD), jnp.float32),
-            pltpu.SemaphoreType.DMA((4,)),
-        ],
-        compiler_params=small,
-        name="place",
-    )(*in_hbm([owner_map, flat_deltas, flat_anchors, scales]))
-
-    sent, mine, late_deltas = lax.optimization_barrier((sent, mine, flat_deltas))
+
+    def place(plan, deltas):
+        return pl.pallas_call(
+            functools.partial(place_kernel, plan),
+            out_shape=[jax.ShapeDtypeStruct((slots * block_rows, HD), jnp.bfloat16) for _, _, slots in plan],
+            in_specs=[HBM] * 4,
+            out_specs=[VMEM] * len(plan),
+            scratch_shapes=[
+                pltpu.SMEM((blocks,), jnp.int32),
+                pltpu.SMEM((blocks,), jnp.int32),
+                pltpu.SMEM((senders,), jnp.int32),
+                pltpu.VMEM((tokens * 2, HD), jnp.bfloat16),
+                pltpu.VMEM((blocks * 2, HD), jnp.float32),
+                pltpu.VMEM((2, HD), jnp.float32),
+                pltpu.SemaphoreType.DMA((4,)),
+            ],
+            compiler_params=small,
+            name="place",
+        )(*in_hbm([owner_map, deltas, flat_anchors, scales]))
+
+    (farthest,) = place(plan[:1], flat_deltas)
+    farthest, late_deltas = lax.optimization_barrier((farthest, flat_deltas))
+    *sent, mine = place(plan[1:], late_deltas)
+    sent, mine, late_deltas = lax.optimization_barrier((sent, mine, late_deltas))
+    sent = [farthest] + sent
     distant = senders // 2
     got = [exchange(message, k) for message, (k, _, _) in zip(sent[:distant], plan)]
 
     def parted(count):
-        heights = (HD // 2 + STAT_ROWS, HD // 2) if count > 2 else (HD + STAT_ROWS,)
-        return [jax.ShapeDtypeStruct((count // 2, height, width), jnp.bfloat16) for height in heights] + [
-            jax.ShapeDtypeStruct((count // 2, HD + KEEP_ROWS, width), jnp.float32)
+        return [
+            jax.ShapeDtypeStruct((count // 2, HD + STAT_ROWS, width), jnp.bfloat16),
+            jax.ShapeDtypeStruct((count // 2, HD + KEEP_ROWS, width), jnp.float32),
         ]
 
     needed = (late_deltas, flat_anchors, scales, lengths, row_request, flat_queries, flat_new)
-    *send, keep, pages = pl.pallas_call(
+    send, keep, pages = pl.pallas_call(
         attend_kernel,
         out_shape=parted(senders) + [whole],
         in_specs=[HBM] * len(needed) + [ANY],
-        out_specs=[VMEM] * len(parted(senders)) + [HBM],
+        out_specs=[VMEM] * 2 + [HBM],
         scratch_shapes=[
             (pltpu.SMEM if array.dtype == jnp.int32 else pltpu.VMEM)(array.shape, array.dtype)
             for array in needed
@@ -385,37 +387,29 @@
 
     k, count = 1, senders // 2
     rest, send = lax.optimization_barrier((sent[distant:], send))
-    passed = [exchange(piece, k) for piece in send]
+    passed = exchange(send, k)
     got += [exchange(message, k) for message, (k, _, _) in zip(rest, plan[distant:])]
     while count > 1:
-        *send, keep = pl.pallas_call(
-            functools.partial(join_kernel, len(passed)),
+        send, keep = pl.pallas_call(
+            join_kernel,
             out_shape=parted(count),
-            in_specs=[VMEM] * (len(passed) + 1),
-            out_specs=[VMEM] * len(parted(count)),
+            in_specs=[VMEM] * 2,
+            out_specs=[VMEM] * 2,
             compiler_params=small,
             name="join",
-        )(keep, *passed)
+        )(keep, passed)
         k, count = 2 * k, count // 2
-        passed = [exchange(piece, k) for piece in send]
-    attended = pl.pallas_call(
+        passed = exchange(send, k)
+    attended, pages = pl.pallas_call(
         finish_kernel,
-        out_shape=jax.ShapeDtypeStruct((width, HD), jnp.bfloat16),
-        in_specs=[VMEM] * (len(passed) + 1),
-        out_specs=VMEM,
+        out_shape=[jax.ShapeDtypeStruct((width, HD), jnp.bfloat16), whole],
+        in_specs=[VMEM] * 2 + [HBM] + [ANY] * len(got),
+        out_specs=[VMEM, HBM],
+        scratch_shapes=[pltpu.SemaphoreType.DMA((len(got),))],
+        input_output_aliases={2: 1},
         compiler_params=small,
         name="finish",
-    )(keep, *passed)
-    pages = pl.pallas_call(
-        settle_kernel,
-        out_shape=whole,
-        in_specs=[HBM] + [ANY] * len(got),
-        out_specs=HBM,
-        scratch_shapes=[pltpu.SemaphoreType.DMA((len(got),))],
-        input_output_aliases={0: 0},
-        compiler_params=small,
-        name="settle",
-    )(pages, *got)
+    )(keep, passed, pages, *got)
     pages = pages.reshape(blocks, tokens // blocks, 2, HD)
     attended = (
         attended.reshape(rows_dev, GQ, steps, HD).transpose(0, 2, 1, 3).reshape(rows_dev, steps, GQ * HD)

time: 35.1 us -> 36.8 us (1.048)
  waiting for transfers between devices: 11.2 us -> 13.2 us
  starting transfers between devices: 11.7 us -> 10.1 us
  Pallas kernels: 11.4 us -> 12.6 us
    ppermute x7 -> x6, waiting for transfers between devices: 11.2 us -> 13.2 us  [exchange(): return lax.ppermute(message, 'seq', [(i, i ^ k) for i in range(count)])]
    ppermute x7 -> x6, starting transfers between devices: 11.7 us -> 10.1 us  [exchange(): return lax.ppermute(message, 'seq', [(i, i ^ k) for i in range(count)])]
    pallas_call x4, Pallas kernels: 3.63 us -> 4.86 us  [the longest x2 3.21 us: place(): pl.pallas_call(functools.partial(place_kernel, plan), out_shape=[jax.Shap...]
  transfers between devices with their start and end apart: 7 -> 6, of which waited for: 2 -> 3; matrix products, arithmetic and copies ran while one was open for 0% -> 0% of each run, Pallas kernels for 25% -> 26%
where the time goes in v9:
time: 36.8 us; the launch traced here: 36.6 us
  waiting for transfers between devices  13.2 us (36%)
  Pallas kernels  12.6 us (34%)
  starting transfers between devices  10.1 us (27%)
  between operations  0.67 us (2%)
    ppermute x6, waiting for transfers between devices, exchange(): return lax.ppermute(message, 'seq', [(i, i ^ k) for i in range(count)])  13.2 us
    ppermute x6, starting transfers between devices, exchange(): return lax.ppermute(message, 'seq', [(i, i ^ k) for i in range(count)])  10.1 us
    pallas_call x1, Pallas kernels, per_device(): pl.pallas_call(attend_kernel, out_shape=parted(senders) + [whole], in_spe...  7.74 us
    pallas_call x2, Pallas kernels, place(): pl.pallas_call(functools.partial(place_kernel, plan), out_shape=[jax.Shap...  3.21 us
    pallas_call x1, Pallas kernels, per_device(): pl.pallas_call(finish_kernel, out_shape=[jax.ShapeDtypeStruct((width, HD)...  1.58 us
  transfers between devices with their start and end apart: 6, of which 3 were waited for; matrix products, arithmetic and copies ran while one was open for 0% of the time, Pallas kernels for 26%

profile of v9, /device:TPU:0, one launch (start us, length us, event | category | flops | bytes accessed | tf_op | source)
XLA Modules:
  0.0 36.6 jit_solution(4574016751692522113)
XLA Ops:
  0.6 1.5 %place.2 = bf16[1024,128]{1,0:T(8,128)(2,1)S(1)} custom-call(s32[128]{0:T(128)} %owner_any.3, bf16[4096,128]{1,0:T(8,128)(2,1)} %bitcast.14, f32[256,128]{1,0:T(8,128)} %bitcast.18, f32[2,128]{1,0:T(2,128)} %refs_2_.1), custom_call_target="tpu_custom_call" | custom-call | tf_op jit(solution)/shard_map/place/pallas_call | solution.py:330
  2.1 5.1 %collective-permute-start.2 = (bf16[1024,128]{1,0:T(8,128)(2,1)S(1)}, bf16[1024,128]{1,0:T(8,128)(2,1)S(1)}, u32[]{:S(2)}, u32[]{:S(2)}) collective-permute-start(bf16[1024,128]{1,0:T(8,128)(2,1)S(1)} %place.2), channel_id=1, source_target_pairs={{0,12},{4,8},{8,4},{12,0},{1,13},{5,9},{9,5},{13,1},{2,14},{6,10},... | collective-permute-start | bytes 786440 | tf_op jit(solution)/shard_map/ppermute | solution.py:26
  7.2 1.7 %place.3 = (bf16[1024,128]{1,0:T(8,128)(2,1)S(1)}, bf16[512,128]{1,0:T(8,128)(2,1)S(1)}, bf16[512,128]{1,0:T(8,128)(2,1)S(1)}, bf16[1024,128]{1,0:T(8,128)(2,1)S(1)}) custom-call(s32[128]{0:T(128)} %owner_any.3, bf16[4096,128]{1,0:T(8,128)(2,1)} %bitcast.15, f32[256,128]{1,0:T(8,128)} %bitcast.19, f32[2,128]{1,0:T(2,128)} %refs_2_.1), custom_call_target="tpu_custom_call" | custom-call | tf_op jit(solution)/shard_map/place/pallas_call | solution.py:330
  9.0 0.1 collective-permute-start.3
  9.0 7.7 %attend.1 = (bf16[2,144,256]{2,1,0:T(8,128)(2,1)S(1)}, f32[2,136,256]{2,1,0:T(8,128)S(1)}, bf16[4096,128]{1,0:T(8,128)(2,1)}) custom-call(bf16[4096,128]{1,0:T(8,128)(2,1)} %bitcast.16, f32[256,128]{1,0:T(8,128)} %bitcast.20, f32[2,128]{1,0:T(2,128)} %refs_2_.1, s32[4]{0:T(128)} %refs_3_.1, s32[64]{0:T(128)} %refs_4_.1, bf16[1024,128]{1,0:T(8,128)(2,1)} %bitcast.21, ...), custom_call_target="tpu_custom_call" | custom-call | flops 1610612736 | bytes 1572864 | tf_op jit(solution)/shard_map/attend/pallas_call | solution.py:363
  16.8 0.6 %collective-permute-start = (bf16[2,144,256]{2,1,0:T(8,128)(2,1)S(1)}, bf16[2,144,256]{2,1,0:T(8,128)(2,1)S(1)}, u32[]{:S(2)}, u32[]{:S(2)}) collective-permute-start(bf16[2,144,256]{2,1,0:T(8,128)(2,1)S(1)} %get-tuple-element.34), channel_id=1, source_target_pairs={{0,4},{4,0},{8,12},{12,8},{1,5},{5,1},{9,13},{13,9},{2,6},{6,2},{1... | collective-permute-start | bytes 442376 | tf_op jit(solution)/shard_map/ppermute | solution.py:26
  17.4 1.5 %collective-permute-start.4 = (bf16[512,128]{1,0:T(8,128)(2,1)S(1)}, bf16[512,128]{1,0:T(8,128)(2,1)S(1)}, u32[]{:S(2)}, u32[]{:S(2)}) collective-permute-start(bf16[512,128]{1,0:T(8,128)(2,1)S(1)} %get-tuple-element.40), channel_id=1, source_target_pairs={{0,4},{4,0},{8,12},{12,8},{1,5},{5,1},{9,13},{13,9},{2,6},{6,2},{1... | collective-permute-start | bytes 393224 | tf_op jit(solution)/shard_map/ppermute | solution.py:26
  18.9 0.6 %collective-permute-start.5 = (bf16[512,128]{1,0:T(8,128)(2,1)S(1)}, bf16[512,128]{1,0:T(8,128)(2,1)S(1)}, u32[]{:S(2)}, u32[]{:S(2)}) collective-permute-start(bf16[512,128]{1,0:T(8,128)(2,1)S(1)} %get-tuple-element.41), channel_id=1, source_target_pairs={{0,4},{4,0},{8,12},{12,8},{1,5},{5,1},{9,13},{13,9},{2,6},{6,2},{1... | collective-permute-start | bytes 393224 | tf_op jit(solution)/shard_map/ppermute | solution.py:26
  19.5 4.9 %collective-permute-done.got_ref = bf16[2,144,256]{2,1,0:T(8,128)(2,1)S(1)} collective-permute-done((bf16[2,144,256]{2,1,0:T(8,128)(2,1)S(1)}, bf16[2,144,256]{2,1,0:T(8,128)(2,1)S(1)}, u32[]{:S(2)}, u32[]{:S(2)}) %collective-permute-start) | collective-permute-done | bytes 147488 | tf_op jit(solution)/shard_map/ppermute | solution.py:26
  24.3 0.1 join.1
  24.4 2.3 %collective-permute-start.1 = (bf16[1,144,256]{2,1,0:T(8,128)(2,1)S(1)}, bf16[1,144,256]{2,1,0:T(8,128)(2,1)S(1)}, u32[]{:S(2)}, u32[]{:S(2)}) collective-permute-start(bf16[1,144,256]{2,1,0:T(8,128)(2,1)S(1)} %get-tuple-element.36), channel_id=1, source_target_pairs={{0,8},{4,12},{8,0},{12,4},{1,9},{5,13},{9,1},{13,5},{2,10},{6,14},... | collective-permute-start | bytes 221192 | tf_op jit(solution)/shard_map/ppermute | solution.py:26
  26.7 6.9 %collective-permute-done.4.refs_2_ = bf16[512,128]{1,0:T(8,128)(2,1)S(1)} collective-permute-done((bf16[512,128]{1,0:T(8,128)(2,1)S(1)}, bf16[512,128]{1,0:T(8,128)(2,1)S(1)}, u32[]{:S(2)}, u32[]{:S(2)}) %collective-permute-start.4) | collective-permute-done | bytes 131104 | tf_op jit(solution)/shard_map/ppermute | solution.py:26
  33.6 1.4 %collective-permute-done.5.refs_3_ = bf16[512,128]{1,0:T(8,128)(2,1)S(1)} collective-permute-done((bf16[512,128]{1,0:T(8,128)(2,1)S(1)}, bf16[512,128]{1,0:T(8,128)(2,1)S(1)}, u32[]{:S(2)}, u32[]{:S(2)}) %collective-permute-start.5) | collective-permute-done | bytes 131104 | tf_op jit(solution)/shard_map/ppermute | solution.py:26
  35.0 0.0 collective-permute-done.1.got_ref
  35.0 0.0 collective-permute-done.2.refs_0_
  35.0 0.0 collective-permute-done.3.refs_1_
  35.0 1.6 %finish.1 = (bf16[256,128]{1,0:T(8,128)(2,1)}, bf16[4096,128]{1,0:T(8,128)(2,1)}) custom-call(f32[1,136,256]{2,1,0:T(8,128)S(1)} %get-tuple-element.35.keep_ref, bf16[1,144,256]{2,1,0:T(8,128)(2,1)S(1)} %collective-permute-done.1.got_ref, bf16[4096,128]{1,0:T(8,128)(2,1)} %get-tuple-element.37._, ...), custom_call_target="tpu_custom_call", output_to_operand_aliasing={{1}: (2, {})} | custom-call | tf_op jit(solution)/shard_map/finish/pallas_call | solution.py:403
Async XLA Ops:
  2.1 32.9 %collective-permute-start.2 = (bf16[1024,128]{1,0:T(8,128)(2,1)S(1)}, bf16[1024,128]{1,0:T(8,128)(2,1)S(1)}, u32[]{:S(2)}, u32[]{:S(2)}) collective-permute-start(bf16[1024,128]{1,0:T(8,128)(2,1)S(1)} %place.2), channel_id=1, source_target_pairs={{0,12},{4,8},{8,4},{12,0},{1,13},{5,9},{9,5},{13,1},{2,14},{6,10},... | collective-permute-start | bytes 786440 | tf_op jit(solution)/shard_map/ppermute | solution.py:26
  9.0 26.0 %collective-permute-start.3 = (bf16[1024,128]{1,0:T(8,128)(2,1)S(1)}, bf16[1024,128]{1,0:T(8,128)(2,1)S(1)}, u32[]{:S(2)}, u32[]{:S(2)}) collective-permute-start(bf16[1024,128]{1,0:T(8,128)(2,1)S(1)} %get-tuple-element.39), channel_id=1, source_target_pairs={{0,8},{4,12},{8,0},{12,4},{1,9},{5,13},{9,1},{13,5},{2,10},{6,14},... | collective-permute-start | bytes 786440 | tf_op jit(solution)/shard_map/ppermute | solution.py:26
  16.8 7.5 %collective-permute-start = (bf16[2,144,256]{2,1,0:T(8,128)(2,1)S(1)}, bf16[2,144,256]{2,1,0:T(8,128)(2,1)S(1)}, u32[]{:S(2)}, u32[]{:S(2)}) collective-permute-start(bf16[2,144,256]{2,1,0:T(8,128)(2,1)S(1)} %get-tuple-element.34), channel_id=1, source_target_pairs={{0,4},{4,0},{8,12},{12,8},{1,5},{5,1},{9,13},{13,9},{2,6},{6,2},{1... | collective-permute-start | bytes 442376 | tf_op jit(solution)/shard_map/ppermute | solution.py:26
  17.4 16.2 %collective-permute-start.4 = (bf16[512,128]{1,0:T(8,128)(2,1)S(1)}, bf16[512,128]{1,0:T(8,128)(2,1)S(1)}, u32[]{:S(2)}, u32[]{:S(2)}) collective-permute-start(bf16[512,128]{1,0:T(8,128)(2,1)S(1)} %get-tuple-element.40), channel_id=1, source_target_pairs={{0,4},{4,0},{8,12},{12,8},{1,5},{5,1},{9,13},{13,9},{2,6},{6,2},{1... | collective-permute-start | bytes 393224 | tf_op jit(solution)/shard_map/ppermute | solution.py:26
  18.9 16.1 %collective-permute-start.5 = (bf16[512,128]{1,0:T(8,128)(2,1)S(1)}, bf16[512,128]{1,0:T(8,128)(2,1)S(1)}, u32[]{:S(2)}, u32[]{:S(2)}) collective-permute-start(bf16[512,128]{1,0:T(8,128)(2,1)S(1)} %get-tuple-element.41), channel_id=1, source_target_pairs={{0,4},{4,0},{8,12},{12,8},{1,5},{5,1},{9,13},{13,9},{2,6},{6,2},{1... | collective-permute-start | bytes 393224 | tf_op jit(solution)/shard_map/ppermute | solution.py:26
  24.4 10.6 %collective-permute-start.1 = (bf16[1,144,256]{2,1,0:T(8,128)(2,1)S(1)}, bf16[1,144,256]{2,1,0:T(8,128)(2,1)S(1)}, u32[]{:S(2)}, u32[]{:S(2)}) collective-permute-start(bf16[1,144,256]{2,1,0:T(8,128)(2,1)S(1)} %get-tuple-element.36), channel_id=1, source_target_pairs={{0,8},{4,12},{8,0},{12,4},{1,9},{5,13},{9,1},{13,5},{2,10},{6,14},... | collective-permute-start | bytes 221192 | tf_op jit(solution)/shard_map/ppermute | solution.py:26

commit v10 on v9

--- a/solution.py
+++ b/solution.py
@@ -27,10 +27,10 @@
 
 
 def messages(count, capacity):
-    far = [(k, 0, capacity) for k in reversed(range(count // 2, count))]
+    early = [(k, 0, capacity) for k in [count - 1] + list(range(1, count // 2))]
     half = capacity // 2
-    near = [(k, first, half) for k in reversed(range(1, count // 2)) for first in (0, half)]
-    return far + near + [(0, 0, capacity)]
+    late = [(k, first, half) for k in range(count // 2, count - 1) for first in (0, half)]
+    return early + late + [(0, 0, capacity)]
 
 
 def place_kernel(plan, owner_any, deltas_any, anchors_any, scales_any, *refs):
@@ -287,7 +287,7 @@
 
 
 def finish_kernel(keep_ref, got_ref, _, *refs):
-    *handed, out_ref, pages, sems = refs
+    *handed, out_any, pages, out_ref, sems = refs
     receivers = lax.axis_size("seq")
     me = lax.axis_index("seq")
     size = pages.shape[0] // receivers
@@ -299,6 +299,8 @@
         copies.append(copy)
     summed, _, total = joined(taken(keep_ref[0]), unpacked(got_ref[0]))
     out_ref[...] = (summed / total).T.astype(jnp.bfloat16)
+    copies.append(pltpu.make_async_copy(out_ref, out_any, sems.at[len(copies)]))
+    copies[-1].start()
     for copy in copies:
         copy.wait()
 
@@ -404,8 +406,11 @@
         finish_kernel,
         out_shape=[jax.ShapeDtypeStruct((width, HD), jnp.bfloat16), whole],
         in_specs=[VMEM] * 2 + [HBM] + [ANY] * len(got),
-        out_specs=[VMEM, HBM],
-        scratch_shapes=[pltpu.SemaphoreType.DMA((len(got),))],
+        out_specs=[HBM, HBM],
+        scratch_shapes=[
+            pltpu.VMEM((width, HD), jnp.bfloat16),
+            pltpu.SemaphoreType.DMA((len(got) + 1,)),
+        ],
         input_output_aliases={2: 1},
         compiler_params=small,
         name="finish",

time: 36.8 us -> 36.8 us (level)
  starting transfers between devices: 10.1 us -> 14.8 us
  waiting for transfers between devices: 13.2 us -> 9.11 us
  Pallas kernels: 12.6 us -> 12 us
    ppermute x6, starting transfers between devices: 10.1 us -> 14.8 us  [exchange(): return lax.ppermute(message, 'seq', [(i, i ^ k) for i in range(count)])]
    ppermute x6, waiting for transfers between devices: 13.2 us -> 9.11 us  [exchange(): return lax.ppermute(message, 'seq', [(i, i ^ k) for i in range(count)])]
    pallas_call x1, Pallas kernels: 1.58 us -> 0.97 us  [per_device(): pl.pallas_call(finish_kernel, out_shape=[jax.ShapeDtypeStruct((width, HD)...]
  transfers between devices with their start and end apart: 6 -> 6, of which waited for: 3 -> 4; matrix products, arithmetic and copies ran while one was open for 0% -> 0% of each run, Pallas kernels for 26% -> 26%
where the time goes in v10:
time: 36.8 us; the launch traced here: 36.6 us
  starting transfers between devices  14.8 us (40%)
  Pallas kernels  12 us (33%)
  waiting for transfers between devices  9.11 us (25%)
  between operations  0.67 us (2%)
    ppermute x6, starting transfers between devices, exchange(): return lax.ppermute(message, 'seq', [(i, i ^ k) for i in range(count)])  14.8 us
    ppermute x6, waiting for transfers between devices, exchange(): return lax.ppermute(message, 'seq', [(i, i ^ k) for i in range(count)])  9.11 us
    pallas_call x1, Pallas kernels, per_device(): pl.pallas_call(attend_kernel, out_shape=parted(senders) + [whole], in_spe...  7.74 us
    pallas_call x2, Pallas kernels, place(): pl.pallas_call(functools.partial(place_kernel, plan), out_shape=[jax.Shap...  3.21 us
    pallas_call x1, Pallas kernels, per_device(): pl.pallas_call(finish_kernel, out_shape=[jax.ShapeDtypeStruct((width, HD)...  0.97 us
  transfers between devices with their start and end apart: 6, of which 4 were waited for; matrix products, arithmetic and copies ran while one was open for 0% of the time, Pallas kernels for 26%

profile of v10, /device:TPU:0, one launch (start us, length us, event | category | flops | bytes accessed | tf_op | source)
XLA Modules:
  0.0 36.6 jit_solution(611824866854747327)
XLA Ops:
  0.6 1.5 %place.2 = bf16[1024,128]{1,0:T(8,128)(2,1)S(1)} custom-call(s32[128]{0:T(128)} %owner_any.3, bf16[4096,128]{1,0:T(8,128)(2,1)} %bitcast.14, f32[256,128]{1,0:T(8,128)} %bitcast.18, f32[2,128]{1,0:T(2,128)} %refs_2_.1), custom_call_target="tpu_custom_call" | custom-call | tf_op jit(solution)/shard_map/place/pallas_call | solution.py:332
  2.1 5.1 %collective-permute-start.2 = (bf16[1024,128]{1,0:T(8,128)(2,1)S(1)}, bf16[1024,128]{1,0:T(8,128)(2,1)S(1)}, u32[]{:S(2)}, u32[]{:S(2)}) collective-permute-start(bf16[1024,128]{1,0:T(8,128)(2,1)S(1)} %place.2), channel_id=1, source_target_pairs={{0,12},{4,8},{8,4},{12,0},{1,13},{5,9},{9,5},{13,1},{2,14},{6,10},... | collective-permute-start | bytes 786440 | tf_op jit(solution)/shard_map/ppermute | solution.py:26
  7.2 1.7 %place.3 = (bf16[1024,128]{1,0:T(8,128)(2,1)S(1)}, bf16[512,128]{1,0:T(8,128)(2,1)S(1)}, bf16[512,128]{1,0:T(8,128)(2,1)S(1)}, bf16[1024,128]{1,0:T(8,128)(2,1)S(1)}) custom-call(s32[128]{0:T(128)} %owner_any.3, bf16[4096,128]{1,0:T(8,128)(2,1)} %bitcast.15, f32[256,128]{1,0:T(8,128)} %bitcast.19, f32[2,128]{1,0:T(2,128)} %refs_2_.1), custom_call_target="tpu_custom_call" | custom-call | tf_op jit(solution)/shard_map/place/pallas_call | solution.py:332
  9.0 0.1 collective-permute-start.3
  9.0 7.7 %attend.1 = (bf16[2,144,256]{2,1,0:T(8,128)(2,1)S(1)}, f32[2,136,256]{2,1,0:T(8,128)S(1)}, bf16[4096,128]{1,0:T(8,128)(2,1)}) custom-call(bf16[4096,128]{1,0:T(8,128)(2,1)} %bitcast.16, f32[256,128]{1,0:T(8,128)} %bitcast.20, f32[2,128]{1,0:T(2,128)} %refs_2_.1, s32[4]{0:T(128)} %refs_3_.1, s32[64]{0:T(128)} %refs_4_.1, bf16[1024,128]{1,0:T(8,128)(2,1)} %bitcast.21, ...), custom_call_target="tpu_custom_call" | custom-call | flops 1610612736 | bytes 1572864 | tf_op jit(solution)/shard_map/attend/pallas_call | solution.py:365
  16.8 2.1 %collective-permute-start = (bf16[2,144,256]{2,1,0:T(8,128)(2,1)S(1)}, bf16[2,144,256]{2,1,0:T(8,128)(2,1)S(1)}, u32[]{:S(2)}, u32[]{:S(2)}) collective-permute-start(bf16[2,144,256]{2,1,0:T(8,128)(2,1)S(1)} %get-tuple-element.34), channel_id=1, source_target_pairs={{0,4},{4,0},{8,12},{12,8},{1,5},{5,1},{9,13},{13,9},{2,6},{6,2},{1... | collective-permute-start | bytes 442376 | tf_op jit(solution)/shard_map/ppermute | solution.py:26
  18.9 0.0 collective-permute-start.4
  18.9 2.9 %collective-permute-start.5 = (bf16[512,128]{1,0:T(8,128)(2,1)S(1)}, bf16[512,128]{1,0:T(8,128)(2,1)S(1)}, u32[]{:S(2)}, u32[]{:S(2)}) collective-permute-start(bf16[512,128]{1,0:T(8,128)(2,1)S(1)} %get-tuple-element.41), channel_id=1, source_target_pairs={{0,8},{4,12},{8,0},{12,4},{1,9},{5,13},{9,1},{13,5},{2,10},{6,14},... | collective-permute-start | bytes 393224 | tf_op jit(solution)/shard_map/ppermute | solution.py:26
  21.8 1.7 %collective-permute-done.got_ref = bf16[2,144,256]{2,1,0:T(8,128)(2,1)S(1)} collective-permute-done((bf16[2,144,256]{2,1,0:T(8,128)(2,1)S(1)}, bf16[2,144,256]{2,1,0:T(8,128)(2,1)S(1)}, u32[]{:S(2)}, u32[]{:S(2)}) %collective-permute-start) | collective-permute-done | bytes 147488 | tf_op jit(solution)/shard_map/ppermute | solution.py:26
  23.5 0.1 join.1
  23.5 4.7 %collective-permute-start.1 = (bf16[1,144,256]{2,1,0:T(8,128)(2,1)S(1)}, bf16[1,144,256]{2,1,0:T(8,128)(2,1)S(1)}, u32[]{:S(2)}, u32[]{:S(2)}) collective-permute-start(bf16[1,144,256]{2,1,0:T(8,128)(2,1)S(1)} %get-tuple-element.36), channel_id=1, source_target_pairs={{0,8},{4,12},{8,0},{12,4},{1,9},{5,13},{9,1},{13,5},{2,10},{6,14},... | collective-permute-start | bytes 221192 | tf_op jit(solution)/shard_map/ppermute | solution.py:26
  28.2 2.5 %collective-permute-done.4.refs_2_ = bf16[512,128]{1,0:T(8,128)(2,1)S(1)} collective-permute-done((bf16[512,128]{1,0:T(8,128)(2,1)S(1)}, bf16[512,128]{1,0:T(8,128)(2,1)S(1)}, u32[]{:S(2)}, u32[]{:S(2)}) %collective-permute-start.4) | collective-permute-done | bytes 131104 | tf_op jit(solution)/shard_map/ppermute | solution.py:26
  30.7 4.1 %collective-permute-done.5.refs_3_ = bf16[512,128]{1,0:T(8,128)(2,1)S(1)} collective-permute-done((bf16[512,128]{1,0:T(8,128)(2,1)S(1)}, bf16[512,128]{1,0:T(8,128)(2,1)S(1)}, u32[]{:S(2)}, u32[]{:S(2)}) %collective-permute-start.5) | collective-permute-done | bytes 131104 | tf_op jit(solution)/shard_map/ppermute | solution.py:26
  34.8 0.8 %collective-permute-done.1.got_ref = bf16[1,144,256]{2,1,0:T(8,128)(2,1)S(1)} collective-permute-done((bf16[1,144,256]{2,1,0:T(8,128)(2,1)S(1)}, bf16[1,144,256]{2,1,0:T(8,128)(2,1)S(1)}, u32[]{:S(2)}, u32[]{:S(2)}) %collective-permute-start.1) | collective-permute-done | bytes 73760 | tf_op jit(solution)/shard_map/ppermute | solution.py:26
  35.6 0.0 collective-permute-done.2.refs_0_
  35.6 0.0 collective-permute-done.3.refs_1_
  35.6 1.0 %finish.1 = (bf16[256,128]{1,0:T(8,128)(2,1)}, bf16[4096,128]{1,0:T(8,128)(2,1)}) custom-call(f32[1,136,256]{2,1,0:T(8,128)S(1)} %get-tuple-element.35.keep_ref, bf16[1,144,256]{2,1,0:T(8,128)(2,1)S(1)} %collective-permute-done.1.got_ref, bf16[4096,128]{1,0:T(8,128)(2,1)} %get-tuple-element.37._, ...), custom_call_target="tpu_custom_call", output_to_operand_aliasing={{1}: (2, {})} | custom-call | tf_op jit(solution)/shard_map/finish/pallas_call | solution.py:405
Async XLA Ops:
  2.1 33.5 %collective-permute-start.2 = (bf16[1024,128]{1,0:T(8,128)(2,1)S(1)}, bf16[1024,128]{1,0:T(8,128)(2,1)S(1)}, u32[]{:S(2)}, u32[]{:S(2)}) collective-permute-start(bf16[1024,128]{1,0:T(8,128)(2,1)S(1)} %place.2), channel_id=1, source_target_pairs={{0,12},{4,8},{8,4},{12,0},{1,13},{5,9},{9,5},{13,1},{2,14},{6,10},... | collective-permute-start | bytes 786440 | tf_op jit(solution)/shard_map/ppermute | solution.py:26
  9.0 26.7 %collective-permute-start.3 = (bf16[1024,128]{1,0:T(8,128)(2,1)S(1)}, bf16[1024,128]{1,0:T(8,128)(2,1)S(1)}, u32[]{:S(2)}, u32[]{:S(2)}) collective-permute-start(bf16[1024,128]{1,0:T(8,128)(2,1)S(1)} %get-tuple-element.39), channel_id=1, source_target_pairs={{0,4},{4,0},{8,12},{12,8},{1,5},{5,1},{9,13},{13,9},{2,6},{6,2},{1... | collective-permute-start | bytes 786440 | tf_op jit(solution)/shard_map/ppermute | solution.py:26
  16.8 6.7 %collective-permute-start = (bf16[2,144,256]{2,1,0:T(8,128)(2,1)S(1)}, bf16[2,144,256]{2,1,0:T(8,128)(2,1)S(1)}, u32[]{:S(2)}, u32[]{:S(2)}) collective-permute-start(bf16[2,144,256]{2,1,0:T(8,128)(2,1)S(1)} %get-tuple-element.34), channel_id=1, source_target_pairs={{0,4},{4,0},{8,12},{12,8},{1,5},{5,1},{9,13},{13,9},{2,6},{6,2},{1... | collective-permute-start | bytes 442376 | tf_op jit(solution)/shard_map/ppermute | solution.py:26
  18.9 11.8 %collective-permute-start.4 = (bf16[512,128]{1,0:T(8,128)(2,1)S(1)}, bf16[512,128]{1,0:T(8,128)(2,1)S(1)}, u32[]{:S(2)}, u32[]{:S(2)}) collective-permute-start(bf16[512,128]{1,0:T(8,128)(2,1)S(1)} %get-tuple-element.40), channel_id=1, source_target_pairs={{0,8},{4,12},{8,0},{12,4},{1,9},{5,13},{9,1},{13,5},{2,10},{6,14},... | collective-permute-start | bytes 393224 | tf_op jit(solution)/shard_map/ppermute | solution.py:26
  18.9 16.0 %collective-permute-start.5 = (bf16[512,128]{1,0:T(8,128)(2,1)S(1)}, bf16[512,128]{1,0:T(8,128)(2,1)S(1)}, u32[]{:S(2)}, u32[]{:S(2)}) collective-permute-start(bf16[512,128]{1,0:T(8,128)(2,1)S(1)} %get-tuple-element.41), channel_id=1, source_target_pairs={{0,8},{4,12},{8,0},{12,4},{1,9},{5,13},{9,1},{13,5},{2,10},{6,14},... | collective-permute-start | bytes 393224 | tf_op jit(solution)/shard_map/ppermute | solution.py:26
  23.5 12.1 %collective-permute-start.1 = (bf16[1,144,256]{2,1,0:T(8,128)(2,1)S(1)}, bf16[1,144,256]{2,1,0:T(8,128)(2,1)S(1)}, u32[]{:S(2)}, u32[]{:S(2)}) collective-permute-start(bf16[1,144,256]{2,1,0:T(8,128)(2,1)S(1)} %get-tuple-element.36), channel_id=1, source_target_pairs={{0,8},{4,12},{8,0},{12,4},{1,9},{5,13},{9,1},{13,5},{2,10},{6,14},... | collective-permute-start | bytes 221192 | tf_op jit(solution)/shard_map/ppermute | solution.py:26

commit v11 on v10

--- a/solution.py
+++ b/solution.py
@@ -30,7 +30,7 @@
     early = [(k, 0, capacity) for k in [count - 1] + list(range(1, count // 2))]
     half = capacity // 2
     late = [(k, first, half) for k in range(count // 2, count - 1) for first in (0, half)]
-    return early + late + [(0, 0, capacity)]
+    return early, late + [(0, 0, capacity)]
 
 
 def place_kernel(plan, owner_any, deltas_any, anchors_any, scales_any, *refs):
@@ -55,9 +55,8 @@
     for load in loads:
         load.start()
     bits = capacity.bit_length()
-    single = len(plan) == 1
     narrow = receivers * bits < 32
-    if not narrow and not single:
+    if not narrow:
         for owner in range(receivers):
             count_ref[owner] = owner * capacity
     loads[0].wait()
@@ -74,17 +73,13 @@
         source_ref[slot] = block
         return counts
 
-    def find_one(block, slot):
-        source_ref[slot] = block
-        return slot + (owner_ref[block] == (me ^ plan[0][0])).astype(jnp.int32)
-
-    lax.fori_loop(0, blocks, find_one if single else find, jnp.int32(0), unroll=8)
+    lax.fori_loop(0, blocks, find, jnp.int32(0), unroll=16)
     for load in loads[1:]:
         load.wait()
     odd = lax.broadcasted_iota(jnp.int32, (8, HD), 0) % 2 == 1
     scale = jnp.where(odd, scales_ref[1:2, :], scales_ref[0:1, :])[None]
     for (k, start, count), out_ref in zip(plan, outs):
-        first = start if single else (me ^ k) * capacity + start
+        first = (me ^ k) * capacity + start
 
         def one_slot(slot, carry, first=first, out_ref=out_ref):
             block = source_ref[first + slot]
@@ -146,20 +141,16 @@
 
 
 def attend_kernel(*refs):
+    receivers = lax.axis_size("seq")
     me = lax.axis_index("seq")
-    sources, mine_any, send_ref, keep_ref, pages_any = refs[:7], *refs[7:-12]
-    *targets, wide_ref, keys_ref, values_ref, asked_ref, sems = refs[-12:]
+    sources, send_ref, keep_ref, *targets = refs[:7], *refs[7:-7]
+    wide_ref, keys_ref, values_ref, turned_ref, asked_ref, own_ref, sems = refs[-7:]
     loads = [
         pltpu.make_async_copy(source, target, sems.at[index])
         for index, (source, target) in enumerate(zip(sources, targets))
     ]
     for load in loads:
         load.start()
-    size = mine_any.shape[0]
-    own_pages = pltpu.make_async_copy(
-        mine_any, pages_any.at[pl.ds(pl.multiple_of(me * size, size), size), :], sems.at[len(loads)]
-    )
-    own_pages.start()
     deltas_ref, anchors_ref, scales_ref, lengths_ref, request_ref, queries_ref, new_ref = targets
     blocks = anchors_ref.shape[0] // 2
     rows = deltas_ref.shape[0] // blocks
@@ -168,24 +159,8 @@
     asked = queries_ref.shape[0]
     per_row = asked // request_ref.shape[0]
     width = keep_ref.shape[2]
-
-    for load in loads:
+    for load in loads[2:]:
         load.wait()
-    wide_ref[...] = deltas_ref[...].astype(jnp.float32)
-    scale_key = scales_ref[0:1, :]
-    scale_value = scales_ref[1:2, :]
-
-    def one_block(block, carry):
-        here = pl.ds(pl.multiple_of(block * tokens, tokens), tokens)
-        key = wide_ref[pl.ds(block * rows, tokens, stride=2), :]
-        value = wide_ref[pl.ds(block * rows + 1, tokens, stride=2), :]
-        keys_ref[here, 0:HD] = (anchors_ref[pl.ds(2 * block, 1), :] + scale_key * key).astype(jnp.bfloat16)
-        values_ref[here, :] = (anchors_ref[pl.ds(2 * block + 1, 1), :] + scale_value * value).astype(
-            jnp.bfloat16
-        )
-        return carry
-
-    lax.fori_loop(0, blocks, one_block, 0, unroll=4)
 
     lane = lax.broadcasted_iota(jnp.int32, (1, HD), 1)
     first = jnp.zeros((1, HD), jnp.int32)
@@ -208,41 +183,7 @@
         ).astype(jnp.bfloat16)
         return carry
 
-    lax.fori_loop(0, request_ref.shape[0], one_row, 0, unroll=4)
-
-    tile = min(256, asked)
-    parts = max(1, tile // width)
-
-    def one_tile(index, carry):
-        here = asked_ref[pl.ds(pl.multiple_of(index * tile, tile), tile), :]
-        scores = lax.dot_general(
-            keys_ref[...], here, (((1,), (1,)), ((), ())), preferred_element_type=jnp.float32
-        )
-        top = jnp.max(scores, axis=0, keepdims=True)
-        weights = jnp.exp2((scores - top) * RATE)
-        total = jnp.sum(weights, axis=0, keepdims=True)
-        summed = lax.dot_general(
-            values_ref[...],
-            weights.astype(jnp.bfloat16),
-            (((0,), (0,)), ((), ())),
-            preferred_element_type=jnp.float32,
-        )
-        for part in range(parts):
-            lanes = slice(part * width, (part + 1) * width)
-            partial = summed[:, lanes], top[:, lanes], total[:, lanes]
-            apart = (index * parts + part) ^ me
-
-            @pl.when(apart % 2 == 1)
-            def _(partial=partial, apart=apart):
-                send_ref[apart // 2] = packed(partial)
-
-            @pl.when(apart % 2 == 0)
-            def _(partial=partial, apart=apart):
-                keep_ref[apart // 2] = held(partial)
-
-        return carry
-
-    lax.fori_loop(0, asked // tile, one_tile, 0)
+    lax.fori_loop(0, request_ref.shape[0], one_row, 0, unroll=16)
 
     fresh = new_ref.shape[0] // 4
     new = new_ref[...].astype(jnp.float32).reshape(fresh, 4, HD)
@@ -273,8 +214,71 @@
             (((0,), (0,)), ((), ())),
             preferred_element_type=jnp.float32,
         )
-    keep_ref[0] = held(joined(taken(keep_ref[0]), (own_summed, own_top, own_total)))
-    own_pages.wait()
+    own_ref[...] = held((own_summed, own_top, own_total))
+
+    for load in loads[:2]:
+        load.wait()
+    wide_ref[...] = deltas_ref[...].astype(jnp.float32)
+    scale_key = scales_ref[0:1, :]
+    scale_value = scales_ref[1:2, :]
+
+    def one_block(block, carry):
+        here = pl.ds(pl.multiple_of(block * tokens, tokens), tokens)
+        key = wide_ref[pl.ds(block * rows, tokens, stride=2), :]
+        value = wide_ref[pl.ds(block * rows + 1, tokens, stride=2), :]
+        keys_ref[here, 0:HD] = (anchors_ref[pl.ds(2 * block, 1), :] + scale_key * key).astype(jnp.bfloat16)
+        values_ref[here, :] = (anchors_ref[pl.ds(2 * block + 1, 1), :] + scale_value * value).astype(
+            jnp.bfloat16
+        )
+        return carry
+
+    lax.fori_loop(0, blocks, one_block, 0, unroll=16)
+    turned_ref[...] = values_ref[...].T
+
+    def partial_of(here):
+        scores = lax.dot_general(
+            keys_ref[...], here, (((1,), (1,)), ((), ())), preferred_element_type=jnp.float32
+        )
+        top = jnp.max(scores, axis=0, keepdims=True)
+        weights = jnp.exp2((scores - top) * RATE)
+        total = jnp.sum(weights, axis=0, keepdims=True)
+        summed = jnp.dot(turned_ref[...], weights.astype(jnp.bfloat16), preferred_element_type=jnp.float32)
+        return summed, top, total
+
+    if width % HD == 0:
+        for apart in range(receivers):
+            there = pl.ds(pl.multiple_of((me ^ apart) * width, width), width)
+            partial = partial_of(asked_ref[there, :])
+            if apart % 2 == 1:
+                send_ref[apart // 2] = packed(partial)
+            elif apart:
+                keep_ref[apart // 2] = held(partial)
+            else:
+                keep_ref[0] = held(joined(partial, taken(own_ref[...])))
+    else:
+        tile = min(2 * HD, asked)
+        parts = tile // width
+
+        def one_tile(index, carry):
+            here = asked_ref[pl.ds(pl.multiple_of(index * tile, tile), tile), :]
+            summed, top, total = partial_of(here)
+            for part in range(parts):
+                lanes = slice(part * width, (part + 1) * width)
+                partial = summed[:, lanes], top[:, lanes], total[:, lanes]
+                apart = (index * parts + part) ^ me
+
+                @pl.when(apart % 2 == 1)
+                def _(partial=partial, apart=apart):
+                    send_ref[apart // 2] = packed(partial)
+
+                @pl.when(apart % 2 == 0)
+                def _(partial=partial, apart=apart):
+                    keep_ref[apart // 2] = held(partial)
+
+            return carry
+
+        lax.fori_loop(0, asked // tile, one_tile, 0)
+        keep_ref[0] = held(joined(taken(keep_ref[0]), taken(own_ref[...])))
 
 
 def join_kernel(keep_ref, got_ref, send_ref, next_ref):
@@ -286,13 +290,13 @@
             next_ref[index // 2] = held(partial)
 
 
-def finish_kernel(keep_ref, got_ref, _, *refs):
+def finish_kernel(keep_ref, got_ref, *refs):
     *handed, out_any, pages, out_ref, sems = refs
     receivers = lax.axis_size("seq")
     me = lax.axis_index("seq")
     size = pages.shape[0] // receivers
     copies = []
-    for index, (k, start, count) in enumerate(messages(receivers, size)[:-1]):
+    for index, (k, start, count) in enumerate(sum(messages(receivers, size), [])):
         first = pl.multiple_of((me ^ k) * size + start, count)
         copy = pltpu.make_async_copy(handed[index], pages.at[pl.ds(first, count), :], sems.at[index])
         copy.start()
@@ -325,7 +329,7 @@
     flat_new = new_kv.reshape(rows_dev * 4, HD)
 
     whole = jax.ShapeDtypeStruct((tokens * 2, HD), jnp.bfloat16)
-    plan = messages(senders, blocks // senders)
+    early, late = messages(senders, blocks // senders)
     block_rows = tokens * 2 // blocks
 
     def place(plan, deltas):
@@ -347,13 +351,9 @@
             name="place",
         )(*in_hbm([owner_map, deltas, flat_anchors, scales]))
 
-    (farthest,) = place(plan[:1], flat_deltas)
-    farthest, late_deltas = lax.optimization_barrier((farthest, flat_deltas))
-    *sent, mine = place(plan[1:], late_deltas)
-    sent, mine, late_deltas = lax.optimization_barrier((sent, mine, late_deltas))
-    sent = [farthest] + sent
-    distant = senders // 2
-    got = [exchange(message, k) for message, (k, _, _) in zip(sent[:distant], plan)]
+    sent = place(early, flat_deltas)
+    sent, late_deltas = lax.optimization_barrier((sent, flat_deltas))
+    got = [exchange(message, k) for message, (k, _, _) in zip(sent, early)]
 
     def parted(count):
         return [
@@ -362,11 +362,11 @@
         ]
 
     needed = (late_deltas, flat_anchors, scales, lengths, row_request, flat_queries, flat_new)
-    send, keep, pages = pl.pallas_call(
+    send, keep = pl.pallas_call(
         attend_kernel,
-        out_shape=parted(senders) + [whole],
-        in_specs=[HBM] * len(needed) + [ANY],
-        out_specs=[VMEM] * 2 + [HBM],
+        out_shape=parted(senders),
+        in_specs=[HBM] * len(needed),
+        out_specs=[VMEM] * 2,
         scratch_shapes=[
             (pltpu.SMEM if array.dtype == jnp.int32 else pltpu.VMEM)(array.shape, array.dtype)
             for array in needed
@@ -375,8 +375,10 @@
             pltpu.VMEM((tokens * 2, HD), jnp.float32),
             pltpu.VMEM((tokens, 2 * HD), jnp.bfloat16),
             pltpu.VMEM((tokens, HD), jnp.bfloat16),
+            pltpu.VMEM((HD, tokens), jnp.bfloat16),
             pltpu.VMEM((rows * GQ * steps, 2 * HD), jnp.bfloat16),
-            pltpu.SemaphoreType.DMA((len(needed) + 1,)),
+            pltpu.VMEM((HD + KEEP_ROWS, width), jnp.float32),
+            pltpu.SemaphoreType.DMA((len(needed),)),
         ],
         compiler_params=pltpu.CompilerParams(vmem_limit_bytes=32 * 1024 * 1024),
         cost_estimate=pl.CostEstimate(
@@ -385,12 +387,13 @@
             transcendentals=rows * GQ * steps * tokens,
         ),
         name="attend",
-    )(*in_hbm(needed), mine)
+    )(*in_hbm(needed))
 
     k, count = 1, senders // 2
-    rest, send = lax.optimization_barrier((sent[distant:], send))
+    send, late_deltas = lax.optimization_barrier((send, late_deltas))
     passed = exchange(send, k)
-    got += [exchange(message, k) for message, (k, _, _) in zip(rest, plan[distant:])]
+    *sent, mine = place(late, late_deltas)
+    got += [exchange(message, k) for message, (k, _, _) in zip(sent, late)] + [mine]
     while count > 1:
         send, keep = pl.pallas_call(
             join_kernel,
@@ -405,16 +408,15 @@
     attended, pages = pl.pallas_call(
         finish_kernel,
         out_shape=[jax.ShapeDtypeStruct((width, HD), jnp.bfloat16), whole],
-        in_specs=[VMEM] * 2 + [HBM] + [ANY] * len(got),
+        in_specs=[VMEM] * 2 + [ANY] * len(got),
         out_specs=[HBM, HBM],
         scratch_shapes=[
             pltpu.VMEM((width, HD), jnp.bfloat16),
             pltpu.SemaphoreType.DMA((len(got) + 1,)),
         ],
-        input_output_aliases={2: 1},
         compiler_params=small,
         name="finish",
-    )(keep, passed, pages, *got)
+    )(keep, passed, *got)
     pages = pages.reshape(blocks, tokens // blocks, 2, HD)
     attended = (
         attended.reshape(rows_dev, GQ, steps, HD).transpose(0, 2, 1, 3).reshape(rows_dev, steps, GQ * HD)

time: 36.8 us -> 36.9 us (level)
  waiting for transfers between devices: 9.11 us -> 11.2 us
  starting transfers between devices: 14.8 us -> 12.9 us
    ppermute x6, waiting for transfers between devices: 9.11 us -> 11.2 us  [exchange(): return lax.ppermute(message, 'seq', [(i, i ^ k) for i in range(count)])]
    ppermute x6, starting transfers between devices: 14.8 us -> 12.9 us  [exchange(): return lax.ppermute(message, 'seq', [(i, i ^ k) for i in range(count)])]
  transfers between devices with their start and end apart: 6 -> 6, of which waited for: 4 -> 4; matrix products, arithmetic and copies ran while one was open for 0% -> 0% of each run, Pallas kernels for 26% -> 25%
where the time goes in v11:
time: 36.9 us; the launch traced here: 36.7 us
  starting transfers between devices  12.9 us (35%)
  Pallas kernels  12 us (33%)
  waiting for transfers between devices  11.2 us (30%)
  between operations  0.67 us (2%)
    ppermute x6, starting transfers between devices, exchange(): return lax.ppermute(message, 'seq', [(i, i ^ k) for i in range(count)])  12.9 us
    ppermute x6, waiting for transfers between devices, exchange(): return lax.ppermute(message, 'seq', [(i, i ^ k) for i in range(count)])  11.2 us
    pallas_call x1, Pallas kernels, per_device(): pl.pallas_call(attend_kernel, out_shape=parted(senders), in_specs=[HBM] *...  7.63 us
    pallas_call x2, Pallas kernels, place(): pl.pallas_call(functools.partial(place_kernel, plan), out_shape=[jax.Shap...  3.22 us
    pallas_call x1, Pallas kernels, per_device(): pl.pallas_call(finish_kernel, out_shape=[jax.ShapeDtypeStruct((width, HD)...  1.07 us
  transfers between devices with their start and end apart: 6, of which 4 were waited for; matrix products, arithmetic and copies ran while one was open for 0% of the time, Pallas kernels for 25%

profile of v11, /device:TPU:0, one launch (start us, length us, event | category | flops | bytes accessed | tf_op | source)
XLA Modules:
  0.0 36.7 jit_solution(3568381727112667359)
XLA Ops:
  0.6 1.6 %place.2 = (bf16[1024,128]{1,0:T(8,128)(2,1)S(1)}, bf16[1024,128]{1,0:T(8,128)(2,1)S(1)}) custom-call(s32[128]{0:T(128)} %owner_any.3, bf16[4096,128]{1,0:T(8,128)(2,1)} %bitcast.14, f32[256,128]{1,0:T(8,128)} %bitcast.17, f32[2,128]{1,0:T(2,128)} %scales_any.3), custom_call_target="tpu_custom_call" | custom-call | tf_op jit(solution)/shard_map/place/pallas_call | solution.py:336
  2.2 5.1 %collective-permute-start.2 = (bf16[1024,128]{1,0:T(8,128)(2,1)S(1)}, bf16[1024,128]{1,0:T(8,128)(2,1)S(1)}, u32[]{:S(2)}, u32[]{:S(2)}) collective-permute-start(bf16[1024,128]{1,0:T(8,128)(2,1)S(1)} %get-tuple-element.26), channel_id=1, source_target_pairs={{0,12},{4,8},{8,4},{12,0},{1,13},{5,9},{9,5},{13,1},{2,14},{6,10},... | collective-permute-start | bytes 786440 | tf_op jit(solution)/shard_map/ppermute | solution.py:26
  7.4 0.0 collective-permute-start.3
  7.4 7.6 %attend.1 = (bf16[2,144,256]{2,1,0:T(8,128)(2,1)S(1)}, f32[2,136,256]{2,1,0:T(8,128)S(1)}) custom-call(bf16[4096,128]{1,0:T(8,128)(2,1)} %bitcast.15, f32[256,128]{1,0:T(8,128)} %bitcast.18, f32[2,128]{1,0:T(2,128)} %scales_any.3, s32[4]{0:T(128)} %refs_3_.1, s32[64]{0:T(128)} %refs_4_.1, bf16[1024,128]{1,0:T(8,128)(2,1)} %bitcast.21, bf16[64,128]{1,0:T(8,128)(2,1)} %bitcast.23), custom_call_target="tpu_custom_call" | custom-call | flops 1610612736 | bytes 1572864 | tf_op jit(solution)/shard_map/attend/pallas_call | solution.py:365
  15.0 2.1 %collective-permute-start = (bf16[2,144,256]{2,1,0:T(8,128)(2,1)S(1)}, bf16[2,144,256]{2,1,0:T(8,128)(2,1)S(1)}, u32[]{:S(2)}, u32[]{:S(2)}) collective-permute-start(bf16[2,144,256]{2,1,0:T(8,128)(2,1)S(1)} %get-tuple-element.23), channel_id=1, source_target_pairs={{0,4},{4,0},{8,12},{12,8},{1,5},{5,1},{9,13},{13,9},{2,6},{6,2},{1... | collective-permute-start | bytes 442376 | tf_op jit(solution)/shard_map/ppermute | solution.py:26
  17.1 1.6 %place.3 = (bf16[512,128]{1,0:T(8,128)(2,1)S(1)}, bf16[512,128]{1,0:T(8,128)(2,1)S(1)}, bf16[1024,128]{1,0:T(8,128)(2,1)S(1)}) custom-call(s32[128]{0:T(128)} %owner_any.3, bf16[4096,128]{1,0:T(8,128)(2,1)} %bitcast.16, f32[256,128]{1,0:T(8,128)} %bitcast.19, f32[2,128]{1,0:T(2,128)} %scales_any.3), custom_call_target="tpu_custom_call" | custom-call | tf_op jit(solution)/shard_map/place/pallas_call | solution.py:336
  18.7 0.1 collective-permute-start.4
  18.8 2.9 %collective-permute-start.5 = (bf16[512,128]{1,0:T(8,128)(2,1)S(1)}, bf16[512,128]{1,0:T(8,128)(2,1)S(1)}, u32[]{:S(2)}, u32[]{:S(2)}) collective-permute-start(bf16[512,128]{1,0:T(8,128)(2,1)S(1)} %get-tuple-element.30), channel_id=1, source_target_pairs={{0,8},{4,12},{8,0},{12,4},{1,9},{5,13},{9,1},{13,5},{2,10},{6,14},... | collective-permute-start | bytes 393224 | tf_op jit(solution)/shard_map/ppermute | solution.py:26
  21.7 2.2 %collective-permute-done.got_ref = bf16[2,144,256]{2,1,0:T(8,128)(2,1)S(1)} collective-permute-done((bf16[2,144,256]{2,1,0:T(8,128)(2,1)S(1)}, bf16[2,144,256]{2,1,0:T(8,128)(2,1)S(1)}, u32[]{:S(2)}, u32[]{:S(2)}) %collective-permute-start) | collective-permute-done | bytes 147488 | tf_op jit(solution)/shard_map/ppermute | solution.py:26
  23.9 0.1 join.1
  24.0 2.7 %collective-permute-start.1 = (bf16[1,144,256]{2,1,0:T(8,128)(2,1)S(1)}, bf16[1,144,256]{2,1,0:T(8,128)(2,1)S(1)}, u32[]{:S(2)}, u32[]{:S(2)}) collective-permute-start(bf16[1,144,256]{2,1,0:T(8,128)(2,1)S(1)} %get-tuple-element.25), channel_id=1, source_target_pairs={{0,8},{4,12},{8,0},{12,4},{1,9},{5,13},{9,1},{13,5},{2,10},{6,14},... | collective-permute-start | bytes 221192 | tf_op jit(solution)/shard_map/ppermute | solution.py:26
  26.7 5.8 %collective-permute-done.4.refs_2_ = bf16[512,128]{1,0:T(8,128)(2,1)S(1)} collective-permute-done((bf16[512,128]{1,0:T(8,128)(2,1)S(1)}, bf16[512,128]{1,0:T(8,128)(2,1)S(1)}, u32[]{:S(2)}, u32[]{:S(2)}) %collective-permute-start.4) | collective-permute-done | bytes 131104 | tf_op jit(solution)/shard_map/ppermute | solution.py:26
  32.5 2.3 %collective-permute-done.5.refs_3_ = bf16[512,128]{1,0:T(8,128)(2,1)S(1)} collective-permute-done((bf16[512,128]{1,0:T(8,128)(2,1)S(1)}, bf16[512,128]{1,0:T(8,128)(2,1)S(1)}, u32[]{:S(2)}, u32[]{:S(2)}) %collective-permute-start.5) | collective-permute-done | bytes 131104 | tf_op jit(solution)/shard_map/ppermute | solution.py:26
  34.9 0.8 %collective-permute-done.1.got_ref = bf16[1,144,256]{2,1,0:T(8,128)(2,1)S(1)} collective-permute-done((bf16[1,144,256]{2,1,0:T(8,128)(2,1)S(1)}, bf16[1,144,256]{2,1,0:T(8,128)(2,1)S(1)}, u32[]{:S(2)}, u32[]{:S(2)}) %collective-permute-start.1) | collective-permute-done | bytes 73760 | tf_op jit(solution)/shard_map/ppermute | solution.py:26
  35.7 0.0 collective-permute-done.2.refs_0_
  35.7 0.0 collective-permute-done.3.refs_1_
  35.7 1.1 %finish.1 = (bf16[256,128]{1,0:T(8,128)(2,1)}, bf16[4096,128]{1,0:T(8,128)(2,1)}) custom-call(f32[1,136,256]{2,1,0:T(8,128)S(1)} %get-tuple-element.24.keep_ref, bf16[1,144,256]{2,1,0:T(8,128)(2,1)S(1)} %collective-permute-done.1.got_ref, bf16[1024,128]{1,0:T(8,128)(2,1)S(1)} %collective-permute-done.2.refs_0_, ...), custom_call_target="tpu_custom_call" | custom-call | tf_op jit(solution)/shard_map/finish/pallas_call | solution.py:408
Async XLA Ops:
  2.2 33.4 %collective-permute-start.2 = (bf16[1024,128]{1,0:T(8,128)(2,1)S(1)}, bf16[1024,128]{1,0:T(8,128)(2,1)S(1)}, u32[]{:S(2)}, u32[]{:S(2)}) collective-permute-start(bf16[1024,128]{1,0:T(8,128)(2,1)S(1)} %get-tuple-element.26), channel_id=1, source_target_pairs={{0,12},{4,8},{8,4},{12,0},{1,13},{5,9},{9,5},{13,1},{2,14},{6,10},... | collective-permute-start | bytes 786440 | tf_op jit(solution)/shard_map/ppermute | solution.py:26
  7.4 28.3 %collective-permute-start.3 = (bf16[1024,128]{1,0:T(8,128)(2,1)S(1)}, bf16[1024,128]{1,0:T(8,128)(2,1)S(1)}, u32[]{:S(2)}, u32[]{:S(2)}) collective-permute-start(bf16[1024,128]{1,0:T(8,128)(2,1)S(1)} %get-tuple-element.27), channel_id=1, source_target_pairs={{0,4},{4,0},{8,12},{12,8},{1,5},{5,1},{9,13},{13,9},{2,6},{6,2},{1... | collective-permute-start | bytes 786440 | tf_op jit(solution)/shard_map/ppermute | solution.py:26
  15.0 8.9 %collective-permute-start = (bf16[2,144,256]{2,1,0:T(8,128)(2,1)S(1)}, bf16[2,144,256]{2,1,0:T(8,128)(2,1)S(1)}, u32[]{:S(2)}, u32[]{:S(2)}) collective-permute-start(bf16[2,144,256]{2,1,0:T(8,128)(2,1)S(1)} %get-tuple-element.23), channel_id=1, source_target_pairs={{0,4},{4,0},{8,12},{12,8},{1,5},{5,1},{9,13},{13,9},{2,6},{6,2},{1... | collective-permute-start | bytes 442376 | tf_op jit(solution)/shard_map/ppermute | solution.py:26
  18.7 13.8 %collective-permute-start.4 = (bf16[512,128]{1,0:T(8,128)(2,1)S(1)}, bf16[512,128]{1,0:T(8,128)(2,1)S(1)}, u32[]{:S(2)}, u32[]{:S(2)}) collective-permute-start(bf16[512,128]{1,0:T(8,128)(2,1)S(1)} %get-tuple-element.29), channel_id=1, source_target_pairs={{0,8},{4,12},{8,0},{12,4},{1,9},{5,13},{9,1},{13,5},{2,10},{6,14},... | collective-permute-start | bytes 393224 | tf_op jit(solution)/shard_map/ppermute | solution.py:26
  18.8 16.1 %collective-permute-start.5 = (bf16[512,128]{1,0:T(8,128)(2,1)S(1)}, bf16[512,128]{1,0:T(8,128)(2,1)S(1)}, u32[]{:S(2)}, u32[]{:S(2)}) collective-permute-start(bf16[512,128]{1,0:T(8,128)(2,1)S(1)} %get-tuple-element.30), channel_id=1, source_target_pairs={{0,8},{4,12},{8,0},{12,4},{1,9},{5,13},{9,1},{13,5},{2,10},{6,14},... | collective-permute-start | bytes 393224 | tf_op jit(solution)/shard_map/ppermute | solution.py:26
  24.0 11.7 %collective-permute-start.1 = (bf16[1,144,256]{2,1,0:T(8,128)(2,1)S(1)}, bf16[1,144,256]{2,1,0:T(8,128)(2,1)S(1)}, u32[]{:S(2)}, u32[]{:S(2)}) collective-permute-start(bf16[1,144,256]{2,1,0:T(8,128)(2,1)S(1)} %get-tuple-element.25), channel_id=1, source_target_pairs={{0,8},{4,12},{8,0},{12,4},{1,9},{5,13},{9,1},{13,5},{2,10},{6,14},... | collective-permute-start | bytes 221192 | tf_op jit(solution)/shard_map/ppermute | solution.py:26

commit v12 on v11

--- a/solution.py
+++ b/solution.py
@@ -27,10 +27,11 @@
 
 
 def messages(count, capacity):
-    early = [(k, 0, capacity) for k in [count - 1] + list(range(1, count // 2))]
     half = capacity // 2
-    late = [(k, first, half) for k in range(count // 2, count - 1) for first in (0, half)]
-    return early, late + [(0, 0, capacity)]
+    ahead = [(count - 1, 0, capacity)]
+    beyond = [(k, first, half) for k in range(count // 2, count - 1) for first in (0, half)]
+    near = [(k, first, half) for k in range(1, count // 2) for first in (0, half)]
+    return ahead, beyond, near, [(0, 0, capacity)]
 
 
 def place_kernel(plan, owner_any, deltas_any, anchors_any, scales_any, *refs):
@@ -140,11 +141,48 @@
     )
 
 
-def attend_kernel(*refs):
-    receivers = lax.axis_size("seq")
+def attend(parity, width, keys_ref, turned_ref, asked_ref, store):
     me = lax.axis_index("seq")
-    sources, send_ref, keep_ref, *targets = refs[:7], *refs[7:-7]
-    wide_ref, keys_ref, values_ref, turned_ref, asked_ref, own_ref, sems = refs[-7:]
+    asked = asked_ref.shape[0]
+
+    def partial_of(here):
+        scores = lax.dot_general(
+            keys_ref[...], here, (((1,), (1,)), ((), ())), preferred_element_type=jnp.float32
+        )
+        top = jnp.max(scores, axis=0, keepdims=True)
+        weights = jnp.exp2((scores - top) * RATE)
+        total = jnp.sum(weights, axis=0, keepdims=True)
+        summed = jnp.dot(turned_ref[...], weights.astype(jnp.bfloat16), preferred_element_type=jnp.float32)
+        return summed, top, total
+
+    if width % HD == 0:
+        for index in range(asked // width // 2):
+            there = (me ^ (2 * index + parity)) * width
+            store(index, partial_of(asked_ref[pl.ds(pl.multiple_of(there, width), width), :]))
+        return
+    tile = min(2 * HD, asked)
+    parts = tile // width
+
+    def one_tile(tile_index, carry):
+        here = asked_ref[pl.ds(pl.multiple_of(tile_index * tile, tile), tile), :]
+        summed, top, total = partial_of(here)
+        for part in range(parts):
+            lanes = slice(part * width, (part + 1) * width)
+            apart = (tile_index * parts + part) ^ me
+
+            @pl.when(apart % 2 == parity)
+            def _(lanes=lanes, apart=apart):
+                store(apart // 2, (summed[:, lanes], top[:, lanes], total[:, lanes]))
+
+        return carry
+
+    lax.fori_loop(0, asked // tile, one_tile, 0)
+
+
+def first_kernel(*refs):
+    me = lax.axis_index("seq")
+    sources, send_ref, keys_ref, turned_ref, asked_ref, own_ref, *targets = refs[:7], *refs[7:-3]
+    wide_ref, values_ref, sems = refs[-3:]
     loads = [
         pltpu.make_async_copy(source, target, sems.at[index])
         for index, (source, target) in enumerate(zip(sources, targets))
@@ -158,7 +196,7 @@
     requests = lengths_ref.shape[0]
     asked = queries_ref.shape[0]
     per_row = asked // request_ref.shape[0]
-    width = keep_ref.shape[2]
+    width = send_ref.shape[2]
     for load in loads[2:]:
         load.wait()
 
@@ -235,50 +273,18 @@
     lax.fori_loop(0, blocks, one_block, 0, unroll=16)
     turned_ref[...] = values_ref[...].T
 
-    def partial_of(here):
-        scores = lax.dot_general(
-            keys_ref[...], here, (((1,), (1,)), ((), ())), preferred_element_type=jnp.float32
-        )
-        top = jnp.max(scores, axis=0, keepdims=True)
-        weights = jnp.exp2((scores - top) * RATE)
-        total = jnp.sum(weights, axis=0, keepdims=True)
-        summed = jnp.dot(turned_ref[...], weights.astype(jnp.bfloat16), preferred_element_type=jnp.float32)
-        return summed, top, total
-
-    if width % HD == 0:
-        for apart in range(receivers):
-            there = pl.ds(pl.multiple_of((me ^ apart) * width, width), width)
-            partial = partial_of(asked_ref[there, :])
-            if apart % 2 == 1:
-                send_ref[apart // 2] = packed(partial)
-            elif apart:
-                keep_ref[apart // 2] = held(partial)
-            else:
-                keep_ref[0] = held(joined(partial, taken(own_ref[...])))
-    else:
-        tile = min(2 * HD, asked)
-        parts = tile // width
-
-        def one_tile(index, carry):
-            here = asked_ref[pl.ds(pl.multiple_of(index * tile, tile), tile), :]
-            summed, top, total = partial_of(here)
-            for part in range(parts):
-                lanes = slice(part * width, (part + 1) * width)
-                partial = summed[:, lanes], top[:, lanes], total[:, lanes]
-                apart = (index * parts + part) ^ me
-
-                @pl.when(apart % 2 == 1)
-                def _(partial=partial, apart=apart):
-                    send_ref[apart // 2] = packed(partial)
-
-                @pl.when(apart % 2 == 0)
-                def _(partial=partial, apart=apart):
-                    keep_ref[apart // 2] = held(partial)
-
-            return carry
-
-        lax.fori_loop(0, asked // tile, one_tile, 0)
-        keep_ref[0] = held(joined(taken(keep_ref[0]), taken(own_ref[...])))
+    def store(index, partial):
+        send_ref[index] = packed(partial)
+
+    attend(1, width, keys_ref, turned_ref, asked_ref, store)
+
+
+def second_kernel(keys_ref, turned_ref, asked_ref, own_ref, keep_ref):
+    def store(index, partial):
+        keep_ref[index] = held(partial)
+
+    attend(0, keep_ref.shape[2], keys_ref, turned_ref, asked_ref, store)
+    keep_ref[0] = held(joined(taken(keep_ref[0]), taken(own_ref[...])))
 
 
 def join_kernel(keep_ref, got_ref, send_ref, next_ref):
@@ -290,17 +296,28 @@
             next_ref[index // 2] = held(partial)
 
 
-def finish_kernel(keep_ref, got_ref, *refs):
-    *handed, out_any, pages, out_ref, sems = refs
+def settle(plan, handed, pages, sems):
     receivers = lax.axis_size("seq")
     me = lax.axis_index("seq")
-    size = pages.shape[0] // receivers
+    rows = pages.shape[0] // receivers
     copies = []
-    for index, (k, start, count) in enumerate(sum(messages(receivers, size), [])):
-        first = pl.multiple_of((me ^ k) * size + start, count)
-        copy = pltpu.make_async_copy(handed[index], pages.at[pl.ds(first, count), :], sems.at[index])
-        copy.start()
-        copies.append(copy)
+    for index, (k, start, slots) in enumerate(plan):
+        size = handed[index].shape[0]
+        first = pl.multiple_of((me ^ k) * rows + start * (size // slots), size)
+        copies.append(pltpu.make_async_copy(handed[index], pages.at[pl.ds(first, size), :], sems.at[index]))
+        copies[-1].start()
+    return copies
+
+
+def settle_kernel(plan, *refs):
+    *handed, pages, sems = refs
+    for copy in settle(plan, handed, pages, sems):
+        copy.wait()
+
+
+def finish_kernel(plan, keep_ref, got_ref, _, *refs):
+    *handed, out_any, pages, out_ref, sems = refs
+    copies = settle(plan, handed, pages, sems)
     summed, _, total = joined(taken(keep_ref[0]), unpacked(got_ref[0]))
     out_ref[...] = (summed / total).T.astype(jnp.bfloat16)
     copies.append(pltpu.make_async_copy(out_ref, out_any, sems.at[len(copies)]))
@@ -329,7 +346,7 @@
     flat_new = new_kv.reshape(rows_dev * 4, HD)
 
     whole = jax.ShapeDtypeStruct((tokens * 2, HD), jnp.bfloat16)
-    early, late = messages(senders, blocks // senders)
+    ahead, beyond, near, own = messages(senders, blocks // senders)
     block_rows = tokens * 2 // blocks
 
     def place(plan, deltas):
@@ -351,72 +368,98 @@
             name="place",
         )(*in_hbm([owner_map, deltas, flat_anchors, scales]))
 
-    sent = place(early, flat_deltas)
+    def hand(sent, plan):
+        return [exchange(message, k) for message, (k, _, _) in zip(sent, plan)]
+
+    sent = place(ahead, flat_deltas)
     sent, late_deltas = lax.optimization_barrier((sent, flat_deltas))
-    got = [exchange(message, k) for message, (k, _, _) in zip(sent, early)]
-
-    def parted(count):
-        return [
-            jax.ShapeDtypeStruct((count // 2, HD + STAT_ROWS, width), jnp.bfloat16),
-            jax.ShapeDtypeStruct((count // 2, HD + KEEP_ROWS, width), jnp.float32),
-        ]
+    got_ahead = hand(sent, ahead)
+
+    def leaving(count):
+        return jax.ShapeDtypeStruct((count // 2, HD + STAT_ROWS, width), jnp.bfloat16)
+
+    def staying(count):
+        return jax.ShapeDtypeStruct((count // 2, HD + KEEP_ROWS, width), jnp.float32)
 
     needed = (late_deltas, flat_anchors, scales, lengths, row_request, flat_queries, flat_new)
-    send, keep = pl.pallas_call(
-        attend_kernel,
-        out_shape=parted(senders),
+    roomy = pltpu.CompilerParams(vmem_limit_bytes=32 * 1024 * 1024)
+    send, *common = pl.pallas_call(
+        first_kernel,
+        out_shape=[
+            leaving(senders),
+            jax.ShapeDtypeStruct((tokens, 2 * HD), jnp.bfloat16),
+            jax.ShapeDtypeStruct((HD, tokens), jnp.bfloat16),
+            jax.ShapeDtypeStruct((rows * GQ * steps, 2 * HD), jnp.bfloat16),
+            jax.ShapeDtypeStruct((HD + KEEP_ROWS, width), jnp.float32),
+        ],
         in_specs=[HBM] * len(needed),
-        out_specs=[VMEM] * 2,
+        out_specs=[VMEM] * 5,
         scratch_shapes=[
             (pltpu.SMEM if array.dtype == jnp.int32 else pltpu.VMEM)(array.shape, array.dtype)
             for array in needed
         ]
         + [
             pltpu.VMEM((tokens * 2, HD), jnp.float32),
-            pltpu.VMEM((tokens, 2 * HD), jnp.bfloat16),
             pltpu.VMEM((tokens, HD), jnp.bfloat16),
-            pltpu.VMEM((HD, tokens), jnp.bfloat16),
-            pltpu.VMEM((rows * GQ * steps, 2 * HD), jnp.bfloat16),
-            pltpu.VMEM((HD + KEEP_ROWS, width), jnp.float32),
             pltpu.SemaphoreType.DMA((len(needed),)),
         ],
-        compiler_params=pltpu.CompilerParams(vmem_limit_bytes=32 * 1024 * 1024),
-        cost_estimate=pl.CostEstimate(
-            flops=6 * rows * GQ * steps * tokens * HD,
-            bytes_accessed=tokens * 4 * HD + rows * GQ * steps * 4 * HD,
-            transcendentals=rows * GQ * steps * tokens,
-        ),
-        name="attend",
+        compiler_params=roomy,
+        name="attend_leaving",
     )(*in_hbm(needed))
 
     k, count = 1, senders // 2
     send, late_deltas = lax.optimization_barrier((send, late_deltas))
     passed = exchange(send, k)
-    *sent, mine = place(late, late_deltas)
-    got += [exchange(message, k) for message, (k, _, _) in zip(sent, late)] + [mine]
+    *sent, mine = place(beyond + near + own, late_deltas)
+    got = hand(sent[: len(beyond)], beyond)
+    sent = sent[len(beyond) :]
+    keep = pl.pallas_call(
+        second_kernel,
+        out_shape=staying(senders),
+        in_specs=[VMEM] * 4,
+        out_specs=VMEM,
+        compiler_params=roomy,
+        name="attend_staying",
+    )(*common)
     while count > 1:
         send, keep = pl.pallas_call(
             join_kernel,
-            out_shape=parted(count),
+            out_shape=[leaving(count), staying(count)],
             in_specs=[VMEM] * 2,
             out_specs=[VMEM] * 2,
             compiler_params=small,
             name="join",
         )(keep, passed)
+        if k == 1:
+            sent, send = lax.optimization_barrier((sent, send))
+            got += hand(sent, near)
         k, count = 2 * k, count // 2
+        if count == 1:
+            settled = ahead + own
+            pages = pl.pallas_call(
+                functools.partial(settle_kernel, settled),
+                out_shape=whole,
+                in_specs=[ANY] * len(settled),
+                out_specs=HBM,
+                scratch_shapes=[pltpu.SemaphoreType.DMA((len(settled),))],
+                compiler_params=small,
+                name="settle",
+            )(*got_ahead, mine)
+            send, pages = lax.optimization_barrier((send, pages))
         passed = exchange(send, k)
     attended, pages = pl.pallas_call(
-        finish_kernel,
+        functools.partial(finish_kernel, beyond + near),
         out_shape=[jax.ShapeDtypeStruct((width, HD), jnp.bfloat16), whole],
-        in_specs=[VMEM] * 2 + [ANY] * len(got),
+        in_specs=[VMEM] * 2 + [HBM] + [ANY] * len(got),
         out_specs=[HBM, HBM],
         scratch_shapes=[
             pltpu.VMEM((width, HD), jnp.bfloat16),
             pltpu.SemaphoreType.DMA((len(got) + 1,)),
         ],
+        input_output_aliases={2: 1},
         compiler_params=small,
         name="finish",
-    )(keep, passed, *got)
+    )(keep, passed, pages, *got)
     pages = pages.reshape(blocks, tokens // blocks, 2, HD)
     attended = (
         attended.reshape(rows_dev, GQ, steps, HD).transpose(0, 2, 1, 3).reshape(rows_dev, steps, GQ * HD)

time: 36.9 us -> 35 us (0.949)
  waiting for transfers between devices: 11.2 us -> 6.4 us
  starting transfers between devices: 12.9 us -> 14.8 us
  Pallas kernels: 12 us -> 12.9 us
    ppermute x6 -> x7, waiting for transfers between devices: 11.2 us -> 6.4 us  [exchange(): return lax.ppermute(message, 'seq', [(i, i ^ k) for i in range(count)])]
    ppermute x6 -> x7, starting transfers between devices: 12.9 us -> 14.8 us  [exchange(): return lax.ppermute(message, 'seq', [(i, i ^ k) for i in range(count)])]
    pallas_call x3 -> x5, Pallas kernels: 8.77 us -> 9.66 us  [the longest x1 5.23 us: per_device(): pl.pallas_call(first_kernel, out_shape=[leaving(senders), jax.ShapeDtypeS...]
  transfers between devices with their start and end apart: 6 -> 7, of which waited for: 4 -> 3; matrix products, arithmetic and copies ran while one was open for 0% -> 0% of each run, Pallas kernels for 25% -> 30%
where the time goes in v12:
time: 35 us; the launch traced here: 34.8 us
  starting transfers between devices  14.8 us (42%)
  Pallas kernels  12.9 us (37%)
  waiting for transfers between devices  6.4 us (18%)
  between operations  0.69 us (2%)
    ppermute x7, starting transfers between devices, exchange(): return lax.ppermute(message, 'seq', [(i, i ^ k) for i in range(count)])  14.8 us
    ppermute x7, waiting for transfers between devices, exchange(): return lax.ppermute(message, 'seq', [(i, i ^ k) for i in range(count)])  6.4 us
    pallas_call x1, Pallas kernels, per_device(): pl.pallas_call(first_kernel, out_shape=[leaving(senders), jax.ShapeDtypeS...  5.23 us
    pallas_call x2, Pallas kernels, place(): pl.pallas_call(functools.partial(place_kernel, plan), out_shape=[jax.Shap...  3.22 us
    pallas_call x1, Pallas kernels, per_device(): pl.pallas_call(second_kernel, out_shape=staying(senders), in_specs=[VMEM]...  2.67 us
    pallas_call x1, Pallas kernels, per_device(): pl.pallas_call(functools.partial(finish_kernel, beyond + near), out_shape...  0.89 us
    pallas_call x1, Pallas kernels, per_device(): pl.pallas_call(functools.partial(settle_kernel, settled), out_shape=whole...  0.81 us
  transfers between devices with their start and end apart: 7, of which 3 were waited for; matrix products, arithmetic and copies ran while one was open for 0% of the time, Pallas kernels for 30%

profile of v12, /device:TPU:0, one launch (start us, length us, event | category | flops | bytes accessed | tf_op | source)
XLA Modules:
  0.0 34.8 jit_solution(11169777479936064438)
XLA Ops:
  0.6 1.5 %place.2 = bf16[1024,128]{1,0:T(8,128)(2,1)S(1)} custom-call(s32[128]{0:T(128)} %owner_any.3, bf16[4096,128]{1,0:T(8,128)(2,1)} %bitcast.14, f32[256,128]{1,0:T(8,128)} %bitcast.18, f32[2,128]{1,0:T(2,128)} %scales_any.3), custom_call_target="tpu_custom_call" | custom-call | tf_op jit(solution)/shard_map/place/pallas_call | solution.py:353
  2.1 5.1 %collective-permute-start.1 = (bf16[1024,128]{1,0:T(8,128)(2,1)S(1)}, bf16[1024,128]{1,0:T(8,128)(2,1)S(1)}, u32[]{:S(2)}, u32[]{:S(2)}) collective-permute-start(bf16[1024,128]{1,0:T(8,128)(2,1)S(1)} %place.2), channel_id=1, source_target_pairs={{0,12},{4,8},{8,4},{12,0},{1,13},{5,9},{9,5},{13,1},{2,14},{6,10},... | collective-permute-start | bytes 786440 | tf_op jit(solution)/shard_map/ppermute | solution.py:26
  7.2 5.2 %attend_leaving.1 = (bf16[2,144,256]{2,1,0:T(8,128)(2,1)S(1)}, bf16[2048,256]{1,0:T(8,128)(2,1)S(1)}, bf16[128,2048]{1,0:T(8,128)(2,1)S(1)}, bf16[1024,256]{1,0:T(8,128)(2,1)S(1)}, f32[136,256]{1,0:T(8,128)S(1)}) custom-call(bf16[4096,128]{1,0:T(8,128)(2,1)} %bitcast.15, f32[256,128]{1,0:T(8,128)} %bitcast.19, f32[2,128]{1,0:T(2,128)} %scales_any.3, ...), custom_call_target="tpu_custom_call" | custom-call | tf_op jit(solution)/shard_map/attend_leaving/pallas_call | solution.py:386
  12.5 0.1 collective-permute-start
  12.5 1.7 %place.3 = (bf16[512,128]{1,0:T(8,128)(2,1)S(1)}, bf16[512,128]{1,0:T(8,128)(2,1)S(1)}, bf16[512,128]{1,0:T(8,128)(2,1)S(1)}, bf16[512,128]{1,0:T(8,128)(2,1)S(1)}, bf16[1024,128]{1,0:T(8,128)(2,1)S(1)}) custom-call(s32[128]{0:T(128)} %owner_any.3, bf16[4096,128]{1,0:T(8,128)(2,1)} %bitcast.16, f32[256,128]{1,0:T(8,128)} %bitcast.20, f32[2,128]{1,0:T(2,128)} %scales_any.3), custom_call_target="tpu_custom_call" | custom-call | tf_op jit(solution)/shard_map/place/pallas_call | solution.py:353
  14.3 0.6 %collective-permute-start.3 = (bf16[512,128]{1,0:T(8,128)(2,1)S(1)}, bf16[512,128]{1,0:T(8,128)(2,1)S(1)}, u32[]{:S(2)}, u32[]{:S(2)}) collective-permute-start(bf16[512,128]{1,0:T(8,128)(2,1)S(1)} %get-tuple-element.42), channel_id=1, source_target_pairs={{0,8},{4,12},{8,0},{12,4},{1,9},{5,13},{9,1},{13,5},{2,10},{6,14},... | collective-permute-start | bytes 393224 | tf_op jit(solution)/shard_map/ppermute | solution.py:26
  14.9 2.4 %collective-permute-start.4 = (bf16[512,128]{1,0:T(8,128)(2,1)S(1)}, bf16[512,128]{1,0:T(8,128)(2,1)S(1)}, u32[]{:S(2)}, u32[]{:S(2)}) collective-permute-start(bf16[512,128]{1,0:T(8,128)(2,1)S(1)} %get-tuple-element.43), channel_id=1, source_target_pairs={{0,8},{4,12},{8,0},{12,4},{1,9},{5,13},{9,1},{13,5},{2,10},{6,14},... | collective-permute-start | bytes 393224 | tf_op jit(solution)/shard_map/ppermute | solution.py:26
  17.3 2.7 %attend_staying.1.keep_ref = f32[2,136,256]{2,1,0:T(8,128)S(1)} custom-call(bf16[2048,256]{1,0:T(8,128)(2,1)S(1)} %get-tuple-element.26.keys_ref, bf16[128,2048]{1,0:T(8,128)(2,1)S(1)} %get-tuple-element.27.turned_ref, bf16[1024,256]{1,0:T(8,128)(2,1)S(1)} %get-tuple-element.28.asked_ref, f32[136,256]{1,0:T(8,128)S(1)} %get-tuple-element.29.own_ref), custom_call_target="tpu_custom_call" | custom-call | tf_op jit(solution)/shard_map/attend_staying/pallas_call | solution.py:416
  20.0 0.0 collective-permute-done.got_ref
  20.0 0.1 join.1
  20.1 2.1 %collective-permute-start.5 = (bf16[512,128]{1,0:T(8,128)(2,1)S(1)}, bf16[512,128]{1,0:T(8,128)(2,1)S(1)}, u32[]{:S(2)}, u32[]{:S(2)}) collective-permute-start(bf16[512,128]{1,0:T(8,128)(2,1)S(1)} %get-tuple-element.44), channel_id=1, source_target_pairs={{0,4},{4,0},{8,12},{12,8},{1,5},{5,1},{9,13},{13,9},{2,6},{6,2},{1... | collective-permute-start | bytes 393224 | tf_op jit(solution)/shard_map/ppermute | solution.py:26
  22.1 0.1 collective-permute-start.6
  22.2 0.0 collective-permute-done.1.refs_0_
  22.2 0.8 %settle.1._ = bf16[4096,128]{1,0:T(8,128)(2,1)} custom-call(bf16[1024,128]{1,0:T(8,128)(2,1)S(1)} %collective-permute-done.1.refs_0_, bf16[1024,128]{1,0:T(8,128)(2,1)S(1)} %get-tuple-element.39.refs_1_), custom_call_target="tpu_custom_call" | custom-call | tf_op jit(solution)/shard_map/settle/pallas_call | solution.py:439
  23.0 4.5 %collective-permute-start.2 = (bf16[1,144,256]{2,1,0:T(8,128)(2,1)S(1)}, bf16[1,144,256]{2,1,0:T(8,128)(2,1)S(1)}, u32[]{:S(2)}, u32[]{:S(2)}) collective-permute-start(bf16[1,144,256]{2,1,0:T(8,128)(2,1)S(1)} %get-tuple-element.40), channel_id=1, source_target_pairs={{0,8},{4,12},{8,0},{12,4},{1,9},{5,13},{9,1},{13,5},{2,10},{6,14},... | collective-permute-start | bytes 221192 | tf_op jit(solution)/shard_map/ppermute | solution.py:26
  27.5 0.1 collective-permute-done.3.refs_0_
  27.7 4.4 %collective-permute-done.4.refs_1_ = bf16[512,128]{1,0:T(8,128)(2,1)S(1)} collective-permute-done((bf16[512,128]{1,0:T(8,128)(2,1)S(1)}, bf16[512,128]{1,0:T(8,128)(2,1)S(1)}, u32[]{:S(2)}, u32[]{:S(2)}) %collective-permute-start.4) | collective-permute-done | bytes 131104 | tf_op jit(solution)/shard_map/ppermute | solution.py:26
  32.1 0.0 collective-permute-done.5.refs_2_
  32.1 1.9 %collective-permute-done.6.refs_3_ = bf16[512,128]{1,0:T(8,128)(2,1)S(1)} collective-permute-done((bf16[512,128]{1,0:T(8,128)(2,1)S(1)}, bf16[512,128]{1,0:T(8,128)(2,1)S(1)}, u32[]{:S(2)}, u32[]{:S(2)}) %collective-permute-start.6) | collective-permute-done | bytes 131104 | tf_op jit(solution)/shard_map/ppermute | solution.py:26
  33.9 0.0 collective-permute-done.2.got_ref
  33.9 0.9 %finish.1 = (bf16[256,128]{1,0:T(8,128)(2,1)}, bf16[4096,128]{1,0:T(8,128)(2,1)}) custom-call(f32[1,136,256]{2,1,0:T(8,128)S(1)} %get-tuple-element.32.keep_ref, bf16[1,144,256]{2,1,0:T(8,128)(2,1)S(1)} %collective-permute-done.2.got_ref, bf16[4096,128]{1,0:T(8,128)(2,1)} %settle.1._, ...), custom_call_target="tpu_custom_call", output_to_operand_aliasing={{1}: (2, {})} | custom-call | tf_op jit(solution)/shard_map/finish/pallas_call | solution.py:450
Async XLA Ops:
  2.1 20.1 %collective-permute-start.1 = (bf16[1024,128]{1,0:T(8,128)(2,1)S(1)}, bf16[1024,128]{1,0:T(8,128)(2,1)S(1)}, u32[]{:S(2)}, u32[]{:S(2)}) collective-permute-start(bf16[1024,128]{1,0:T(8,128)(2,1)S(1)} %place.2), channel_id=1, source_target_pairs={{0,12},{4,8},{8,4},{12,0},{1,13},{5,9},{9,5},{13,1},{2,14},{6,10},... | collective-permute-start | bytes 786440 | tf_op jit(solution)/shard_map/ppermute | solution.py:26
  12.5 7.5 %collective-permute-start = (bf16[2,144,256]{2,1,0:T(8,128)(2,1)S(1)}, bf16[2,144,256]{2,1,0:T(8,128)(2,1)S(1)}, u32[]{:S(2)}, u32[]{:S(2)}) collective-permute-start(bf16[2,144,256]{2,1,0:T(8,128)(2,1)S(1)} %get-tuple-element.31), channel_id=1, source_target_pairs={{0,4},{4,0},{8,12},{12,8},{1,5},{5,1},{9,13},{13,9},{2,6},{6,2},{1... | collective-permute-start | bytes 442376 | tf_op jit(solution)/shard_map/ppermute | solution.py:26
  14.3 13.4 %collective-permute-start.3 = (bf16[512,128]{1,0:T(8,128)(2,1)S(1)}, bf16[512,128]{1,0:T(8,128)(2,1)S(1)}, u32[]{:S(2)}, u32[]{:S(2)}) collective-permute-start(bf16[512,128]{1,0:T(8,128)(2,1)S(1)} %get-tuple-element.42), channel_id=1, source_target_pairs={{0,8},{4,12},{8,0},{12,4},{1,9},{5,13},{9,1},{13,5},{2,10},{6,14},... | collective-permute-start | bytes 393224 | tf_op jit(solution)/shard_map/ppermute | solution.py:26
  14.9 17.1 %collective-permute-start.4 = (bf16[512,128]{1,0:T(8,128)(2,1)S(1)}, bf16[512,128]{1,0:T(8,128)(2,1)S(1)}, u32[]{:S(2)}, u32[]{:S(2)}) collective-permute-start(bf16[512,128]{1,0:T(8,128)(2,1)S(1)} %get-tuple-element.43), channel_id=1, source_target_pairs={{0,8},{4,12},{8,0},{12,4},{1,9},{5,13},{9,1},{13,5},{2,10},{6,14},... | collective-permute-start | bytes 393224 | tf_op jit(solution)/shard_map/ppermute | solution.py:26
  20.1 12.0 %collective-permute-start.5 = (bf16[512,128]{1,0:T(8,128)(2,1)S(1)}, bf16[512,128]{1,0:T(8,128)(2,1)S(1)}, u32[]{:S(2)}, u32[]{:S(2)}) collective-permute-start(bf16[512,128]{1,0:T(8,128)(2,1)S(1)} %get-tuple-element.44), channel_id=1, source_target_pairs={{0,4},{4,0},{8,12},{12,8},{1,5},{5,1},{9,13},{13,9},{2,6},{6,2},{1... | collective-permute-start | bytes 393224 | tf_op jit(solution)/shard_map/ppermute | solution.py:26
  22.1 11.8 %collective-permute-start.6 = (bf16[512,128]{1,0:T(8,128)(2,1)S(1)}, bf16[512,128]{1,0:T(8,128)(2,1)S(1)}, u32[]{:S(2)}, u32[]{:S(2)}) collective-permute-start(bf16[512,128]{1,0:T(8,128)(2,1)S(1)} %get-tuple-element.45), channel_id=1, source_target_pairs={{0,4},{4,0},{8,12},{12,8},{1,5},{5,1},{9,13},{13,9},{2,6},{6,2},{1... | collective-permute-start | bytes 393224 | tf_op jit(solution)/shard_map/ppermute | solution.py:26
  23.0 10.9 %collective-permute-start.2 = (bf16[1,144,256]{2,1,0:T(8,128)(2,1)S(1)}, bf16[1,144,256]{2,1,0:T(8,128)(2,1)S(1)}, u32[]{:S(2)}, u32[]{:S(2)}) collective-permute-start(bf16[1,144,256]{2,1,0:T(8,128)(2,1)S(1)} %get-tuple-element.40), channel_id=1, source_target_pairs={{0,8},{4,12},{8,0},{12,4},{1,9},{5,13},{9,1},{13,5},{2,10},{6,14},... | collective-permute-start | bytes 221192 | tf_op jit(solution)/shard_map/ppermute | solution.py:26

commit v13 on v12

--- a/solution.py
+++ b/solution.py
@@ -21,17 +21,43 @@
 SMEM = pl.BlockSpec(memory_space=pltpu.SMEM)
 
 
+def inner(device, count):
+    return (device ^ (device // (count // 2))) & 1
+
+
+def partner(device, k, count):
+    far = count // 2
+    if k == far:
+        return device ^ (1 + inner(device, count) * (far - 1))
+    if k == 1:
+        return device ^ (far - inner(device, count) * (far - 1))
+    return device ^ k
+
+
+def source(device, k, count):
+    far = count // 2
+    if k == far:
+        return device ^ (far - inner(device, count) * (far - 1))
+    if k == 1:
+        return device ^ (1 + inner(device, count) * (far - 1))
+    return device ^ k
+
+
 def exchange(message, k):
     count = lax.axis_size("seq")
     return lax.ppermute(message, "seq", [(i, i ^ k) for i in range(count)])
 
 
+def hand(message, k):
+    count = lax.axis_size("seq")
+    return lax.ppermute(message, "seq", [(i, partner(i, k, count)) for i in range(count)])
+
+
 def messages(count, capacity):
     half = capacity // 2
-    ahead = [(count - 1, 0, capacity)]
-    beyond = [(k, first, half) for k in range(count // 2, count - 1) for first in (0, half)]
-    near = [(k, first, half) for k in range(1, count // 2) for first in (0, half)]
-    return ahead, beyond, near, [(0, 0, capacity)]
+    ahead = [(k, 0, capacity) for k in reversed(range(count // 2, count))]
+    behind = [(k, first, half) for k in reversed(range(1, count // 2)) for first in (0, half)]
+    return ahead, behind, [(0, 0, capacity)]
 
 
 def place_kernel(plan, owner_any, deltas_any, anchors_any, scales_any, *refs):
@@ -80,7 +106,7 @@
     odd = lax.broadcasted_iota(jnp.int32, (8, HD), 0) % 2 == 1
     scale = jnp.where(odd, scales_ref[1:2, :], scales_ref[0:1, :])[None]
     for (k, start, count), out_ref in zip(plan, outs):
-        first = (me ^ k) * capacity + start
+        first = partner(me, k, receivers) * capacity + start
 
         def one_slot(slot, carry, first=first, out_ref=out_ref):
             block = source_ref[first + slot]
@@ -296,28 +322,18 @@
             next_ref[index // 2] = held(partial)
 
 
-def settle(plan, handed, pages, sems):
+def finish_kernel(plan, keep_ref, got_ref, *refs):
+    *handed, out_any, pages, out_ref, sems = refs
     receivers = lax.axis_size("seq")
     me = lax.axis_index("seq")
     rows = pages.shape[0] // receivers
     copies = []
     for index, (k, start, slots) in enumerate(plan):
         size = handed[index].shape[0]
-        first = pl.multiple_of((me ^ k) * rows + start * (size // slots), size)
+        sender = source(me, k, receivers) if k else me
+        first = pl.multiple_of(sender * rows + start * (size // slots), size)
         copies.append(pltpu.make_async_copy(handed[index], pages.at[pl.ds(first, size), :], sems.at[index]))
         copies[-1].start()
-    return copies
-
-
-def settle_kernel(plan, *refs):
-    *handed, pages, sems = refs
-    for copy in settle(plan, handed, pages, sems):
-        copy.wait()
-
-
-def finish_kernel(plan, keep_ref, got_ref, _, *refs):
-    *handed, out_any, pages, out_ref, sems = refs
-    copies = settle(plan, handed, pages, sems)
     summed, _, total = joined(taken(keep_ref[0]), unpacked(got_ref[0]))
     out_ref[...] = (summed / total).T.astype(jnp.bfloat16)
     copies.append(pltpu.make_async_copy(out_ref, out_any, sems.at[len(copies)]))
@@ -346,7 +362,7 @@
     flat_new = new_kv.reshape(rows_dev * 4, HD)
 
     whole = jax.ShapeDtypeStruct((tokens * 2, HD), jnp.bfloat16)
-    ahead, beyond, near, own = messages(senders, blocks // senders)
+    ahead, behind, own = messages(senders, blocks // senders)
     block_rows = tokens * 2 // blocks
 
     def place(plan, deltas):
@@ -368,12 +384,12 @@
             name="place",
         )(*in_hbm([owner_map, deltas, flat_anchors, scales]))
 
-    def hand(sent, plan):
-        return [exchange(message, k) for message, (k, _, _) in zip(sent, plan)]
-
-    sent = place(ahead, flat_deltas)
-    sent, late_deltas = lax.optimization_barrier((sent, flat_deltas))
-    got_ahead = hand(sent, ahead)
+    (farthest,) = place(ahead[:1], flat_deltas)
+    farthest, late_deltas = lax.optimization_barrier((farthest, flat_deltas))
+    sent = place(ahead[1:] + behind + own, late_deltas)
+    sent, late_deltas = lax.optimization_barrier((sent, late_deltas))
+    sent = [farthest, *sent]
+    got = [hand(message, k) for message, (k, _, _) in zip(sent, ahead)]
 
     def leaving(count):
         return jax.ShapeDtypeStruct((count // 2, HD + STAT_ROWS, width), jnp.bfloat16)
@@ -408,11 +424,9 @@
     )(*in_hbm(needed))
 
     k, count = 1, senders // 2
-    send, late_deltas = lax.optimization_barrier((send, late_deltas))
+    rest, send = lax.optimization_barrier((sent[len(ahead) : -1], send))
     passed = exchange(send, k)
-    *sent, mine = place(beyond + near + own, late_deltas)
-    got = hand(sent[: len(beyond)], beyond)
-    sent = sent[len(beyond) :]
+    got += [hand(message, k) for message, (k, _, _) in zip(rest, behind)] + sent[-1:]
     keep = pl.pallas_call(
         second_kernel,
         out_shape=staying(senders),
@@ -430,36 +444,20 @@
             compiler_params=small,
             name="join",
         )(keep, passed)
-        if k == 1:
-            sent, send = lax.optimization_barrier((sent, send))
-            got += hand(sent, near)
         k, count = 2 * k, count // 2
-        if count == 1:
-            settled = ahead + own
-            pages = pl.pallas_call(
-                functools.partial(settle_kernel, settled),
-                out_shape=whole,
-                in_specs=[ANY] * len(settled),
-                out_specs=HBM,
-                scratch_shapes=[pltpu.SemaphoreType.DMA((len(settled),))],
-                compiler_params=small,
-                name="settle",
-            )(*got_ahead, mine)
-            send, pages = lax.optimization_barrier((send, pages))
         passed = exchange(send, k)
     attended, pages = pl.pallas_call(
-        functools.partial(finish_kernel, beyond + near),
+        functools.partial(finish_kernel, ahead + behind + own),
         out_shape=[jax.ShapeDtypeStruct((width, HD), jnp.bfloat16), whole],
-        in_specs=[VMEM] * 2 + [HBM] + [ANY] * len(got),
+        in_specs=[VMEM] * 2 + [ANY] * len(got),
         out_specs=[HBM, HBM],
         scratch_shapes=[
             pltpu.VMEM((width, HD), jnp.bfloat16),
             pltpu.SemaphoreType.DMA((len(got) + 1,)),
         ],
-        input_output_aliases={2: 1},
         compiler_params=small,
         name="finish",
-    )(keep, passed, pages, *got)
+    )(keep, passed, *got)
     pages = pages.reshape(blocks, tokens // blocks, 2, HD)
     attended = (
         attended.reshape(rows_dev, GQ, steps, HD).transpose(0, 2, 1, 3).reshape(rows_dev, steps, GQ * HD)

time: 35 us -> 34.1 us (0.974)
  starting transfers between devices: 14.8 us -> 11.7 us
  waiting for transfers between devices: 6.4 us -> 9.23 us
  Pallas kernels: 12.9 us -> 12.3 us
    ppermute x7 -> x2, starting transfers between devices: 14.8 us -> 2.16 us  [exchange(): return lax.ppermute(message, 'seq', [(i, i ^ k) for i in range(count)])]
    ppermute x0 -> x4, starting transfers between devices: none -> 9.54 us  [hand(): lax.ppermute(message, 'seq', [(i, partner(i, k, count)) for i in range(co...]
    ppermute x0 -> x4, waiting for transfers between devices: none -> 4.04 us  [hand(): lax.ppermute(message, 'seq', [(i, partner(i, k, count)) for i in range(co...]
    ppermute x7 -> x2, waiting for transfers between devices: 6.4 us -> 5.2 us  [exchange(): return lax.ppermute(message, 'seq', [(i, i ^ k) for i in range(count)])]
    pallas_call x2 -> x1, Pallas kernels: 1.69 us -> 1.07 us  [per_device(): pl.pallas_call(functools.partial(finish_kernel, ahead + behind + own), ou...]
  transfers between devices with their start and end apart: 7 -> 6, of which waited for: 3 -> 4; matrix products, arithmetic and copies ran while one was open for 0% -> 0% of each run, Pallas kernels for 30% -> 29%
where the time goes in v13:
time: 34.1 us; the launch traced here: 33.9 us
  Pallas kernels  12.3 us (36%)
  starting transfers between devices  11.7 us (34%)
  waiting for transfers between devices  9.23 us (27%)
  between operations  0.68 us (2%)
    ppermute x4, starting transfers between devices, hand(): lax.ppermute(message, 'seq', [(i, partner(i, k, count)) for i in range(co...  9.54 us
    pallas_call x1, Pallas kernels, per_device(): pl.pallas_call(first_kernel, out_shape=[leaving(senders), jax.ShapeDtypeS...  5.23 us
    ppermute x2, waiting for transfers between devices, exchange(): return lax.ppermute(message, 'seq', [(i, i ^ k) for i in range(count)])  5.2 us
    ppermute x4, waiting for transfers between devices, hand(): lax.ppermute(message, 'seq', [(i, partner(i, k, count)) for i in range(co...  4.04 us
    pallas_call x2, Pallas kernels, place(): pl.pallas_call(functools.partial(place_kernel, plan), out_shape=[jax.Shap...  3.22 us
    pallas_call x1, Pallas kernels, per_device(): pl.pallas_call(second_kernel, out_shape=staying(senders), in_specs=[VMEM]...  2.67 us
    ppermute x2, starting transfers between devices, exchange(): return lax.ppermute(message, 'seq', [(i, i ^ k) for i in range(count)])  2.16 us
    pallas_call x1, Pallas kernels, per_device(): pl.pallas_call(functools.partial(finish_kernel, ahead + behind + own), ou...  1.07 us
  transfers between devices with their start and end apart: 6, of which 4 were waited for; matrix products, arithmetic and copies ran while one was open for 0% of the time, Pallas kernels for 29%

profile of v13, /device:TPU:0, one launch (start us, length us, event | category | flops | bytes accessed | tf_op | source)
XLA Modules:
  0.0 33.9 jit_solution(1396688993057121393)
XLA Ops:
  0.6 1.5 %place.2 = bf16[1024,128]{1,0:T(8,128)(2,1)S(1)} custom-call(s32[128]{0:T(128)} %owner_any.3, bf16[4096,128]{1,0:T(8,128)(2,1)} %bitcast.14, f32[256,128]{1,0:T(8,128)} %bitcast.17, f32[2,128]{1,0:T(2,128)} %refs_2_.1), custom_call_target="tpu_custom_call" | custom-call | tf_op jit(solution)/shard_map/place/pallas_call | solution.py:369
  2.1 5.1 %collective-permute-start.2 = (bf16[1024,128]{1,0:T(8,128)(2,1)S(1)}, bf16[1024,128]{1,0:T(8,128)(2,1)S(1)}, u32[]{:S(2)}, u32[]{:S(2)}) collective-permute-start(bf16[1024,128]{1,0:T(8,128)(2,1)S(1)} %place.2), channel_id=1, source_target_pairs={{0,12},{4,8},{8,4},{12,0},{1,13},{5,9},{9,5},{13,1},{2,14},{6,10},... | collective-permute-start | bytes 786440 | tf_op jit(solution)/shard_map/ppermute | solution.py:53
  7.2 1.7 %place.3 = (bf16[1024,128]{1,0:T(8,128)(2,1)S(1)}, bf16[512,128]{1,0:T(8,128)(2,1)S(1)}, bf16[512,128]{1,0:T(8,128)(2,1)S(1)}, bf16[1024,128]{1,0:T(8,128)(2,1)S(1)}) custom-call(s32[128]{0:T(128)} %owner_any.3, bf16[4096,128]{1,0:T(8,128)(2,1)} %bitcast.15, f32[256,128]{1,0:T(8,128)} %bitcast.18, f32[2,128]{1,0:T(2,128)} %refs_2_.1), custom_call_target="tpu_custom_call" | custom-call | tf_op jit(solution)/shard_map/place/pallas_call | solution.py:369
  9.0 0.1 collective-permute-start.3
  9.0 5.2 %attend_leaving.1 = (bf16[2,144,256]{2,1,0:T(8,128)(2,1)S(1)}, bf16[2048,256]{1,0:T(8,128)(2,1)S(1)}, bf16[128,2048]{1,0:T(8,128)(2,1)S(1)}, bf16[1024,256]{1,0:T(8,128)(2,1)S(1)}, f32[136,256]{1,0:T(8,128)S(1)}) custom-call(bf16[4096,128]{1,0:T(8,128)(2,1)} %bitcast.16, f32[256,128]{1,0:T(8,128)} %bitcast.19, f32[2,128]{1,0:T(2,128)} %refs_2_.1, s32[4]{0:T(128)} %refs_3_.1, ...), custom_call_target="tpu_custom_call" | custom-call | tf_op jit(solution)/shard_map/attend_leaving/pallas_call | solution.py:402
  14.3 0.6 %collective-permute-start = (bf16[2,144,256]{2,1,0:T(8,128)(2,1)S(1)}, bf16[2,144,256]{2,1,0:T(8,128)(2,1)S(1)}, u32[]{:S(2)}, u32[]{:S(2)}) collective-permute-start(bf16[2,144,256]{2,1,0:T(8,128)(2,1)S(1)} %get-tuple-element.38), channel_id=1, source_target_pairs={{0,4},{4,0},{8,12},{12,8},{1,5},{5,1},{9,13},{13,9},{2,6},{6,2},{1... | collective-permute-start | bytes 442376 | tf_op jit(solution)/shard_map/ppermute | solution.py:48
  14.9 2.4 %collective-permute-start.4 = (bf16[512,128]{1,0:T(8,128)(2,1)S(1)}, bf16[512,128]{1,0:T(8,128)(2,1)S(1)}, u32[]{:S(2)}, u32[]{:S(2)}) collective-permute-start(bf16[512,128]{1,0:T(8,128)(2,1)S(1)} %get-tuple-element.43), channel_id=1, source_target_pairs={{0,8},{4,0},{8,12},{12,4},{1,9},{5,1},{9,13},{13,5},{2,10},{6,2},{... | collective-permute-start | bytes 393224 | tf_op jit(solution)/shard_map/ppermute | solution.py:53
  17.3 2.0 %collective-permute-start.5 = (bf16[512,128]{1,0:T(8,128)(2,1)S(1)}, bf16[512,128]{1,0:T(8,128)(2,1)S(1)}, u32[]{:S(2)}, u32[]{:S(2)}) collective-permute-start(bf16[512,128]{1,0:T(8,128)(2,1)S(1)} %get-tuple-element.44), channel_id=1, source_target_pairs={{0,8},{4,0},{8,12},{12,4},{1,9},{5,1},{9,13},{13,5},{2,10},{6,2},{... | collective-permute-start | bytes 393224 | tf_op jit(solution)/shard_map/ppermute | solution.py:53
  19.3 2.7 %attend_staying.1.keep_ref = f32[2,136,256]{2,1,0:T(8,128)S(1)} custom-call(bf16[2048,256]{1,0:T(8,128)(2,1)S(1)} %get-tuple-element.31.keys_ref, bf16[128,2048]{1,0:T(8,128)(2,1)S(1)} %get-tuple-element.32.turned_ref, bf16[1024,256]{1,0:T(8,128)(2,1)S(1)} %get-tuple-element.33.asked_ref, f32[136,256]{1,0:T(8,128)S(1)} %get-tuple-element.34.own_ref), custom_call_target="tpu_custom_call" | custom-call | tf_op jit(solution)/shard_map/attend_staying/pallas_call | solution.py:430
  22.0 3.0 %collective-permute-done.got_ref = bf16[2,144,256]{2,1,0:T(8,128)(2,1)S(1)} collective-permute-done((bf16[2,144,256]{2,1,0:T(8,128)(2,1)S(1)}, bf16[2,144,256]{2,1,0:T(8,128)(2,1)S(1)}, u32[]{:S(2)}, u32[]{:S(2)}) %collective-permute-start) | collective-permute-done | bytes 147488 | tf_op jit(solution)/shard_map/ppermute | solution.py:48
  24.9 0.1 join.1
  25.0 1.5 %collective-permute-start.1 = (bf16[1,144,256]{2,1,0:T(8,128)(2,1)S(1)}, bf16[1,144,256]{2,1,0:T(8,128)(2,1)S(1)}, u32[]{:S(2)}, u32[]{:S(2)}) collective-permute-start(bf16[1,144,256]{2,1,0:T(8,128)(2,1)S(1)} %get-tuple-element.40), channel_id=1, source_target_pairs={{0,8},{4,12},{8,0},{12,4},{1,9},{5,13},{9,1},{13,5},{2,10},{6,14},... | collective-permute-start | bytes 221192 | tf_op jit(solution)/shard_map/ppermute | solution.py:48
  26.6 1.2 %collective-permute-done.4.refs_2_ = bf16[512,128]{1,0:T(8,128)(2,1)S(1)} collective-permute-done((bf16[512,128]{1,0:T(8,128)(2,1)S(1)}, bf16[512,128]{1,0:T(8,128)(2,1)S(1)}, u32[]{:S(2)}, u32[]{:S(2)}) %collective-permute-start.4) | collective-permute-done | bytes 131104 | tf_op jit(solution)/shard_map/ppermute | solution.py:53
  27.8 2.8 %collective-permute-done.5.refs_3_ = bf16[512,128]{1,0:T(8,128)(2,1)S(1)} collective-permute-done((bf16[512,128]{1,0:T(8,128)(2,1)S(1)}, bf16[512,128]{1,0:T(8,128)(2,1)S(1)}, u32[]{:S(2)}, u32[]{:S(2)}) %collective-permute-start.5) | collective-permute-done | bytes 131104 | tf_op jit(solution)/shard_map/ppermute | solution.py:53
  30.6 2.2 %collective-permute-done.1.got_ref = bf16[1,144,256]{2,1,0:T(8,128)(2,1)S(1)} collective-permute-done((bf16[1,144,256]{2,1,0:T(8,128)(2,1)S(1)}, bf16[1,144,256]{2,1,0:T(8,128)(2,1)S(1)}, u32[]{:S(2)}, u32[]{:S(2)}) %collective-permute-start.1) | collective-permute-done | bytes 73760 | tf_op jit(solution)/shard_map/ppermute | solution.py:48
  32.8 0.0 collective-permute-done.2.refs_0_
  32.8 0.0 collective-permute-done.3.refs_1_
  32.8 1.1 %finish.1 = (bf16[256,128]{1,0:T(8,128)(2,1)}, bf16[4096,128]{1,0:T(8,128)(2,1)}) custom-call(f32[1,136,256]{2,1,0:T(8,128)S(1)} %get-tuple-element.39.keep_ref, bf16[1,144,256]{2,1,0:T(8,128)(2,1)S(1)} %collective-permute-done.1.got_ref, bf16[1024,128]{1,0:T(8,128)(2,1)S(1)} %collective-permute-done.2.refs_0_, ...), custom_call_target="tpu_custom_call" | custom-call | tf_op jit(solution)/shard_map/finish/pallas_call | solution.py:449
Async XLA Ops:
  2.1 30.7 %collective-permute-start.2 = (bf16[1024,128]{1,0:T(8,128)(2,1)S(1)}, bf16[1024,128]{1,0:T(8,128)(2,1)S(1)}, u32[]{:S(2)}, u32[]{:S(2)}) collective-permute-start(bf16[1024,128]{1,0:T(8,128)(2,1)S(1)} %place.2), channel_id=1, source_target_pairs={{0,12},{4,8},{8,4},{12,0},{1,13},{5,9},{9,5},{13,1},{2,14},{6,10},... | collective-permute-start | bytes 786440 | tf_op jit(solution)/shard_map/ppermute | solution.py:53
  9.0 23.8 %collective-permute-start.3 = (bf16[1024,128]{1,0:T(8,128)(2,1)S(1)}, bf16[1024,128]{1,0:T(8,128)(2,1)S(1)}, u32[]{:S(2)}, u32[]{:S(2)}) collective-permute-start(bf16[1024,128]{1,0:T(8,128)(2,1)S(1)} %get-tuple-element.42), channel_id=1, source_target_pairs={{0,4},{4,12},{8,0},{12,8},{1,5},{5,13},{9,1},{13,9},{2,6},{6,14},{... | collective-permute-start | bytes 786440 | tf_op jit(solution)/shard_map/ppermute | solution.py:53
  14.3 10.7 %collective-permute-start = (bf16[2,144,256]{2,1,0:T(8,128)(2,1)S(1)}, bf16[2,144,256]{2,1,0:T(8,128)(2,1)S(1)}, u32[]{:S(2)}, u32[]{:S(2)}) collective-permute-start(bf16[2,144,256]{2,1,0:T(8,128)(2,1)S(1)} %get-tuple-element.38), channel_id=1, source_target_pairs={{0,4},{4,0},{8,12},{12,8},{1,5},{5,1},{9,13},{13,9},{2,6},{6,2},{1... | collective-permute-start | bytes 442376 | tf_op jit(solution)/shard_map/ppermute | solution.py:48
  14.9 12.8 %collective-permute-start.4 = (bf16[512,128]{1,0:T(8,128)(2,1)S(1)}, bf16[512,128]{1,0:T(8,128)(2,1)S(1)}, u32[]{:S(2)}, u32[]{:S(2)}) collective-permute-start(bf16[512,128]{1,0:T(8,128)(2,1)S(1)} %get-tuple-element.43), channel_id=1, source_target_pairs={{0,8},{4,0},{8,12},{12,4},{1,9},{5,1},{9,13},{13,5},{2,10},{6,2},{... | collective-permute-start | bytes 393224 | tf_op jit(solution)/shard_map/ppermute | solution.py:53
  17.3 13.3 %collective-permute-start.5 = (bf16[512,128]{1,0:T(8,128)(2,1)S(1)}, bf16[512,128]{1,0:T(8,128)(2,1)S(1)}, u32[]{:S(2)}, u32[]{:S(2)}) collective-permute-start(bf16[512,128]{1,0:T(8,128)(2,1)S(1)} %get-tuple-element.44), channel_id=1, source_target_pairs={{0,8},{4,0},{8,12},{12,4},{1,9},{5,1},{9,13},{13,5},{2,10},{6,2},{... | collective-permute-start | bytes 393224 | tf_op jit(solution)/shard_map/ppermute | solution.py:53
  25.0 7.8 %collective-permute-start.1 = (bf16[1,144,256]{2,1,0:T(8,128)(2,1)S(1)}, bf16[1,144,256]{2,1,0:T(8,128)(2,1)S(1)}, u32[]{:S(2)}, u32[]{:S(2)}) collective-permute-start(bf16[1,144,256]{2,1,0:T(8,128)(2,1)S(1)} %get-tuple-element.40), channel_id=1, source_target_pairs={{0,8},{4,12},{8,0},{12,4},{1,9},{5,13},{9,1},{13,5},{2,10},{6,14},... | collective-permute-start | bytes 221192 | tf_op jit(solution)/shard_map/ppermute | solution.py:48

commit v14 on v13

--- a/solution.py
+++ b/solution.py
@@ -322,8 +322,7 @@
             next_ref[index // 2] = held(partial)
 
 
-def finish_kernel(plan, keep_ref, got_ref, *refs):
-    *handed, out_any, pages, out_ref, sems = refs
+def settle(plan, handed, pages, sems):
     receivers = lax.axis_size("seq")
     me = lax.axis_index("seq")
     rows = pages.shape[0] // receivers
@@ -334,6 +333,18 @@
         first = pl.multiple_of(sender * rows + start * (size // slots), size)
         copies.append(pltpu.make_async_copy(handed[index], pages.at[pl.ds(first, size), :], sems.at[index]))
         copies[-1].start()
+    return copies
+
+
+def settle_kernel(plan, *refs):
+    *handed, pages, sems = refs
+    for copy in settle(plan, handed, pages, sems):
+        copy.wait()
+
+
+def finish_kernel(plan, keep_ref, got_ref, _, *refs):
+    *handed, out_any, pages, out_ref, sems = refs
+    copies = settle(plan, handed, pages, sems)
     summed, _, total = joined(taken(keep_ref[0]), unpacked(got_ref[0]))
     out_ref[...] = (summed / total).T.astype(jnp.bfloat16)
     copies.append(pltpu.make_async_copy(out_ref, out_any, sems.at[len(copies)]))
@@ -384,12 +395,9 @@
             name="place",
         )(*in_hbm([owner_map, deltas, flat_anchors, scales]))
 
-    (farthest,) = place(ahead[:1], flat_deltas)
-    farthest, late_deltas = lax.optimization_barrier((farthest, flat_deltas))
-    sent = place(ahead[1:] + behind + own, late_deltas)
-    sent, late_deltas = lax.optimization_barrier((sent, late_deltas))
-    sent = [farthest, *sent]
-    got = [hand(message, k) for message, (k, _, _) in zip(sent, ahead)]
+    sent = place(ahead, flat_deltas)
+    sent, late_deltas = lax.optimization_barrier((sent, flat_deltas))
+    got_ahead = [hand(message, k) for message, (k, _, _) in zip(sent, ahead)]
 
     def leaving(count):
         return jax.ShapeDtypeStruct((count // 2, HD + STAT_ROWS, width), jnp.bfloat16)
@@ -424,9 +432,10 @@
     )(*in_hbm(needed))
 
     k, count = 1, senders // 2
-    rest, send = lax.optimization_barrier((sent[len(ahead) : -1], send))
+    send, late_deltas = lax.optimization_barrier((send, late_deltas))
     passed = exchange(send, k)
-    got += [hand(message, k) for message, (k, _, _) in zip(rest, behind)] + sent[-1:]
+    *sent, mine = place(behind + own, late_deltas)
+    got = got_ahead[1:] + [hand(message, k) for message, (k, _, _) in zip(sent, behind)]
     keep = pl.pallas_call(
         second_kernel,
         out_shape=staying(senders),
@@ -446,18 +455,29 @@
         )(keep, passed)
         k, count = 2 * k, count // 2
         passed = exchange(send, k)
+    settled = ahead[:1] + own
+    pages = pl.pallas_call(
+        functools.partial(settle_kernel, settled),
+        out_shape=whole,
+        in_specs=[ANY] * len(settled),
+        out_specs=HBM,
+        scratch_shapes=[pltpu.SemaphoreType.DMA((len(settled),))],
+        compiler_params=small,
+        name="settle",
+    )(got_ahead[0], mine)
     attended, pages = pl.pallas_call(
-        functools.partial(finish_kernel, ahead + behind + own),
+        functools.partial(finish_kernel, ahead[1:] + behind),
         out_shape=[jax.ShapeDtypeStruct((width, HD), jnp.bfloat16), whole],
-        in_specs=[VMEM] * 2 + [ANY] * len(got),
+        in_specs=[VMEM] * 2 + [HBM] + [ANY] * len(got),
         out_specs=[HBM, HBM],
         scratch_shapes=[
             pltpu.VMEM((width, HD), jnp.bfloat16),
             pltpu.SemaphoreType.DMA((len(got) + 1,)),
         ],
+        input_output_aliases={2: 1},
         compiler_params=small,
         name="finish",
-    )(keep, passed, *got)
+    )(keep, passed, pages, *got)
     pages = pages.reshape(blocks, tokens // blocks, 2, HD)
     attended = (
         attended.reshape(rows_dev, GQ, steps, HD).transpose(0, 2, 1, 3).reshape(rows_dev, steps, GQ * HD)

time: 34.1 us -> 34 us (level)
  Pallas kernels: 12.3 us -> 12.9 us
  waiting for transfers between devices: 9.23 us -> 8.81 us
    ppermute x4, waiting for transfers between devices: 4.04 us -> 3.04 us  [hand(): lax.ppermute(message, 'seq', [(i, partner(i, k, count)) for i in range(co...]
    pallas_call x1 -> x2, Pallas kernels: 1.07 us -> 1.69 us  [the longest x1 0.89 us: per_device(): pl.pallas_call(functools.partial(finish_kernel, ahead[1:] + behind), out_...]
    ppermute x2, waiting for transfers between devices: 5.2 us -> 5.77 us  [exchange(): return lax.ppermute(message, 'seq', [(i, i ^ k) for i in range(count)])]
  transfers between devices with their start and end apart: 6 -> 6, of which waited for: 4 -> 4; matrix products, arithmetic and copies ran while one was open for 0% -> 0% of each run, Pallas kernels for 29% -> 31%
where the time goes in v14:
time: 34 us; the launch traced here: 33.8 us
  Pallas kernels  12.9 us (38%)
  starting transfers between devices  11.4 us (34%)
  waiting for transfers between devices  8.81 us (26%)
  between operations  0.68 us (2%)
    ppermute x4, starting transfers between devices, hand(): lax.ppermute(message, 'seq', [(i, partner(i, k, count)) for i in range(co...  9.49 us
    ppermute x2, waiting for transfers between devices, exchange(): return lax.ppermute(message, 'seq', [(i, i ^ k) for i in range(count)])  5.77 us
    pallas_call x1, Pallas kernels, per_device(): pl.pallas_call(first_kernel, out_shape=[leaving(senders), jax.ShapeDtypeS...  5.22 us
    pallas_call x2, Pallas kernels, place(): pl.pallas_call(functools.partial(place_kernel, plan), out_shape=[jax.Shap...  3.22 us
    ppermute x4, waiting for transfers between devices, hand(): lax.ppermute(message, 'seq', [(i, partner(i, k, count)) for i in range(co...  3.04 us
    pallas_call x1, Pallas kernels, per_device(): pl.pallas_call(second_kernel, out_shape=staying(senders), in_specs=[VMEM]...  2.67 us
    ppermute x2, starting transfers between devices, exchange(): return lax.ppermute(message, 'seq', [(i, i ^ k) for i in range(count)])  1.92 us
    pallas_call x1, Pallas kernels, per_device(): pl.pallas_call(functools.partial(finish_kernel, ahead[1:] + behind), out_...  0.89 us
  transfers between devices with their start and end apart: 6, of which 4 were waited for; matrix products, arithmetic and copies ran while one was open for 0% of the time, Pallas kernels for 31%

profile of v14, /device:TPU:0, one launch (start us, length us, event | category | flops | bytes accessed | tf_op | source)
XLA Modules:
  0.0 33.8 jit_solution(11377099791046406300)
XLA Ops:
  0.6 1.6 %place.2 = (bf16[1024,128]{1,0:T(8,128)(2,1)S(1)}, bf16[1024,128]{1,0:T(8,128)(2,1)S(1)}) custom-call(s32[128]{0:T(128)} %owner_any.3, bf16[4096,128]{1,0:T(8,128)(2,1)} %bitcast.14, f32[256,128]{1,0:T(8,128)} %bitcast.18, f32[2,128]{1,0:T(2,128)} %scales_any.3), custom_call_target="tpu_custom_call" | custom-call | tf_op jit(solution)/shard_map/place/pallas_call | solution.py:380
  2.3 5.1 %collective-permute-start.2 = (bf16[1024,128]{1,0:T(8,128)(2,1)S(1)}, bf16[1024,128]{1,0:T(8,128)(2,1)S(1)}, u32[]{:S(2)}, u32[]{:S(2)}) collective-permute-start(bf16[1024,128]{1,0:T(8,128)(2,1)S(1)} %get-tuple-element.32), channel_id=1, source_target_pairs={{0,12},{4,8},{8,4},{12,0},{1,13},{5,9},{9,5},{13,1},{2,14},{6,10},... | collective-permute-start | bytes 786440 | tf_op jit(solution)/shard_map/ppermute | solution.py:53
  7.4 0.0 collective-permute-start.3
  7.4 5.2 %attend_leaving.1 = (bf16[2,144,256]{2,1,0:T(8,128)(2,1)S(1)}, bf16[2048,256]{1,0:T(8,128)(2,1)S(1)}, bf16[128,2048]{1,0:T(8,128)(2,1)S(1)}, bf16[1024,256]{1,0:T(8,128)(2,1)S(1)}, f32[136,256]{1,0:T(8,128)S(1)}) custom-call(bf16[4096,128]{1,0:T(8,128)(2,1)} %bitcast.15, f32[256,128]{1,0:T(8,128)} %bitcast.19, f32[2,128]{1,0:T(2,128)} %scales_any.3, ...), custom_call_target="tpu_custom_call" | custom-call | tf_op jit(solution)/shard_map/attend_leaving/pallas_call | solution.py:410
  12.6 0.7 %collective-permute-start = (bf16[2,144,256]{2,1,0:T(8,128)(2,1)S(1)}, bf16[2,144,256]{2,1,0:T(8,128)(2,1)S(1)}, u32[]{:S(2)}, u32[]{:S(2)}) collective-permute-start(bf16[2,144,256]{2,1,0:T(8,128)(2,1)S(1)} %get-tuple-element.29), channel_id=1, source_target_pairs={{0,4},{4,0},{8,12},{12,8},{1,5},{5,1},{9,13},{13,9},{2,6},{6,2},{1... | collective-permute-start | bytes 442376 | tf_op jit(solution)/shard_map/ppermute | solution.py:48
  13.3 1.6 %place.3 = (bf16[512,128]{1,0:T(8,128)(2,1)S(1)}, bf16[512,128]{1,0:T(8,128)(2,1)S(1)}, bf16[1024,128]{1,0:T(8,128)(2,1)S(1)}) custom-call(s32[128]{0:T(128)} %owner_any.3, bf16[4096,128]{1,0:T(8,128)(2,1)} %bitcast.16, f32[256,128]{1,0:T(8,128)} %bitcast.20, f32[2,128]{1,0:T(2,128)} %scales_any.3), custom_call_target="tpu_custom_call" | custom-call | tf_op jit(solution)/shard_map/place/pallas_call | solution.py:380
  14.9 2.4 %collective-permute-start.4 = (bf16[512,128]{1,0:T(8,128)(2,1)S(1)}, bf16[512,128]{1,0:T(8,128)(2,1)S(1)}, u32[]{:S(2)}, u32[]{:S(2)}) collective-permute-start(bf16[512,128]{1,0:T(8,128)(2,1)S(1)} %get-tuple-element.36), channel_id=1, source_target_pairs={{0,8},{4,0},{8,12},{12,4},{1,9},{5,1},{9,13},{13,5},{2,10},{6,2},{... | collective-permute-start | bytes 393224 | tf_op jit(solution)/shard_map/ppermute | solution.py:53
  17.3 2.0 %collective-permute-start.5 = (bf16[512,128]{1,0:T(8,128)(2,1)S(1)}, bf16[512,128]{1,0:T(8,128)(2,1)S(1)}, u32[]{:S(2)}, u32[]{:S(2)}) collective-permute-start(bf16[512,128]{1,0:T(8,128)(2,1)S(1)} %get-tuple-element.37), channel_id=1, source_target_pairs={{0,8},{4,0},{8,12},{12,4},{1,9},{5,1},{9,13},{13,5},{2,10},{6,2},{... | collective-permute-start | bytes 393224 | tf_op jit(solution)/shard_map/ppermute | solution.py:53
  19.3 2.7 %attend_staying.1.keep_ref = f32[2,136,256]{2,1,0:T(8,128)S(1)} custom-call(bf16[2048,256]{1,0:T(8,128)(2,1)S(1)} %get-tuple-element.24.keys_ref, bf16[128,2048]{1,0:T(8,128)(2,1)S(1)} %get-tuple-element.25.turned_ref, bf16[1024,256]{1,0:T(8,128)(2,1)S(1)} %get-tuple-element.26.asked_ref, f32[136,256]{1,0:T(8,128)S(1)} %get-tuple-element.27.own_ref), custom_call_target="tpu_custom_call" | custom-call | tf_op jit(solution)/shard_map/attend_staying/pallas_call | solution.py:439
  22.0 1.1 %collective-permute-done.got_ref = bf16[2,144,256]{2,1,0:T(8,128)(2,1)S(1)} collective-permute-done((bf16[2,144,256]{2,1,0:T(8,128)(2,1)S(1)}, bf16[2,144,256]{2,1,0:T(8,128)(2,1)S(1)}, u32[]{:S(2)}, u32[]{:S(2)}) %collective-permute-start) | collective-permute-done | bytes 147488 | tf_op jit(solution)/shard_map/ppermute | solution.py:48
  23.1 0.1 join.1
  23.1 1.2 %collective-permute-start.1 = (bf16[1,144,256]{2,1,0:T(8,128)(2,1)S(1)}, bf16[1,144,256]{2,1,0:T(8,128)(2,1)S(1)}, u32[]{:S(2)}, u32[]{:S(2)}) collective-permute-start(bf16[1,144,256]{2,1,0:T(8,128)(2,1)S(1)} %get-tuple-element.31), channel_id=1, source_target_pairs={{0,8},{4,12},{8,0},{12,4},{1,9},{5,13},{9,1},{13,5},{2,10},{6,14},... | collective-permute-start | bytes 221192 | tf_op jit(solution)/shard_map/ppermute | solution.py:48
  24.4 0.0 collective-permute-done.2.refs_0_
  24.4 0.8 %settle.1._ = bf16[4096,128]{1,0:T(8,128)(2,1)} custom-call(bf16[1024,128]{1,0:T(8,128)(2,1)S(1)} %collective-permute-done.2.refs_0_, bf16[1024,128]{1,0:T(8,128)(2,1)S(1)} %get-tuple-element.34.refs_1_), custom_call_target="tpu_custom_call" | custom-call | tf_op jit(solution)/shard_map/settle/pallas_call | solution.py:459
  25.2 0.9 %collective-permute-done.4.refs_1_ = bf16[512,128]{1,0:T(8,128)(2,1)S(1)} collective-permute-done((bf16[512,128]{1,0:T(8,128)(2,1)S(1)}, bf16[512,128]{1,0:T(8,128)(2,1)S(1)}, u32[]{:S(2)}, u32[]{:S(2)}) %collective-permute-start.4) | collective-permute-done | bytes 131104 | tf_op jit(solution)/shard_map/ppermute | solution.py:53
  26.1 2.1 %collective-permute-done.5.refs_2_ = bf16[512,128]{1,0:T(8,128)(2,1)S(1)} collective-permute-done((bf16[512,128]{1,0:T(8,128)(2,1)S(1)}, bf16[512,128]{1,0:T(8,128)(2,1)S(1)}, u32[]{:S(2)}, u32[]{:S(2)}) %collective-permute-start.5) | collective-permute-done | bytes 131104 | tf_op jit(solution)/shard_map/ppermute | solution.py:53
  28.2 4.7 %collective-permute-done.1.got_ref = bf16[1,144,256]{2,1,0:T(8,128)(2,1)S(1)} collective-permute-done((bf16[1,144,256]{2,1,0:T(8,128)(2,1)S(1)}, bf16[1,144,256]{2,1,0:T(8,128)(2,1)S(1)}, u32[]{:S(2)}, u32[]{:S(2)}) %collective-permute-start.1) | collective-permute-done | bytes 73760 | tf_op jit(solution)/shard_map/ppermute | solution.py:48
  32.9 0.0 collective-permute-done.3.refs_0_
  32.9 0.9 %finish.1 = (bf16[256,128]{1,0:T(8,128)(2,1)}, bf16[4096,128]{1,0:T(8,128)(2,1)}) custom-call(f32[1,136,256]{2,1,0:T(8,128)S(1)} %get-tuple-element.30.keep_ref, bf16[1,144,256]{2,1,0:T(8,128)(2,1)S(1)} %collective-permute-done.1.got_ref, bf16[4096,128]{1,0:T(8,128)(2,1)} %settle.1._, ...), custom_call_target="tpu_custom_call", output_to_operand_aliasing={{1}: (2, {})} | custom-call | tf_op jit(solution)/shard_map/finish/pallas_call | solution.py:468
Async XLA Ops:
  2.3 22.1 %collective-permute-start.2 = (bf16[1024,128]{1,0:T(8,128)(2,1)S(1)}, bf16[1024,128]{1,0:T(8,128)(2,1)S(1)}, u32[]{:S(2)}, u32[]{:S(2)}) collective-permute-start(bf16[1024,128]{1,0:T(8,128)(2,1)S(1)} %get-tuple-element.32), channel_id=1, source_target_pairs={{0,12},{4,8},{8,4},{12,0},{1,13},{5,9},{9,5},{13,1},{2,14},{6,10},... | collective-permute-start | bytes 786440 | tf_op jit(solution)/shard_map/ppermute | solution.py:53
  7.4 25.5 %collective-permute-start.3 = (bf16[1024,128]{1,0:T(8,128)(2,1)S(1)}, bf16[1024,128]{1,0:T(8,128)(2,1)S(1)}, u32[]{:S(2)}, u32[]{:S(2)}) collective-permute-start(bf16[1024,128]{1,0:T(8,128)(2,1)S(1)} %get-tuple-element.35), channel_id=1, source_target_pairs={{0,4},{4,12},{8,0},{12,8},{1,5},{5,13},{9,1},{13,9},{2,6},{6,14},{... | collective-permute-start | bytes 786440 | tf_op jit(solution)/shard_map/ppermute | solution.py:53
  12.6 10.5 %collective-permute-start = (bf16[2,144,256]{2,1,0:T(8,128)(2,1)S(1)}, bf16[2,144,256]{2,1,0:T(8,128)(2,1)S(1)}, u32[]{:S(2)}, u32[]{:S(2)}) collective-permute-start(bf16[2,144,256]{2,1,0:T(8,128)(2,1)S(1)} %get-tuple-element.29), channel_id=1, source_target_pairs={{0,4},{4,0},{8,12},{12,8},{1,5},{5,1},{9,13},{13,9},{2,6},{6,2},{1... | collective-permute-start | bytes 442376 | tf_op jit(solution)/shard_map/ppermute | solution.py:48
  14.9 11.2 %collective-permute-start.4 = (bf16[512,128]{1,0:T(8,128)(2,1)S(1)}, bf16[512,128]{1,0:T(8,128)(2,1)S(1)}, u32[]{:S(2)}, u32[]{:S(2)}) collective-permute-start(bf16[512,128]{1,0:T(8,128)(2,1)S(1)} %get-tuple-element.36), channel_id=1, source_target_pairs={{0,8},{4,0},{8,12},{12,4},{1,9},{5,1},{9,13},{13,5},{2,10},{6,2},{... | collective-permute-start | bytes 393224 | tf_op jit(solution)/shard_map/ppermute | solution.py:53
  17.3 10.9 %collective-permute-start.5 = (bf16[512,128]{1,0:T(8,128)(2,1)S(1)}, bf16[512,128]{1,0:T(8,128)(2,1)S(1)}, u32[]{:S(2)}, u32[]{:S(2)}) collective-permute-start(bf16[512,128]{1,0:T(8,128)(2,1)S(1)} %get-tuple-element.37), channel_id=1, source_target_pairs={{0,8},{4,0},{8,12},{12,4},{1,9},{5,1},{9,13},{13,5},{2,10},{6,2},{... | collective-permute-start | bytes 393224 | tf_op jit(solution)/shard_map/ppermute | solution.py:53
  23.1 9.8 %collective-permute-start.1 = (bf16[1,144,256]{2,1,0:T(8,128)(2,1)S(1)}, bf16[1,144,256]{2,1,0:T(8,128)(2,1)S(1)}, u32[]{:S(2)}, u32[]{:S(2)}) collective-permute-start(bf16[1,144,256]{2,1,0:T(8,128)(2,1)S(1)} %get-tuple-element.31), channel_id=1, source_target_pairs={{0,8},{4,12},{8,0},{12,4},{1,9},{5,13},{9,1},{13,5},{2,10},{6,14},... | collective-permute-start | bytes 221192 | tf_op jit(solution)/shard_map/ppermute | solution.py:48

commit v15 on v14

--- a/solution.py
+++ b/solution.py
@@ -55,8 +55,9 @@
 
 def messages(count, capacity):
     half = capacity // 2
-    ahead = [(k, 0, capacity) for k in reversed(range(count // 2, count))]
-    behind = [(k, first, half) for k in reversed(range(1, count // 2)) for first in (0, half)]
+    ahead = [(count - 1, 0, capacity)]
+    behind = [(k, 0, capacity) for k in reversed(range(count // 2, count - 1))]
+    behind += [(k, first, half) for k in reversed(range(1, count // 2)) for first in (0, half)]
     return ahead, behind, [(0, 0, capacity)]
 
 

time: 34 us -> 33.9 us (level)
  starting transfers between devices: 11.4 us -> 10.8 us
  waiting for transfers between devices: 8.81 us -> 9.35 us
    ppermute x2, starting transfers between devices: 1.92 us -> 1.28 us  [exchange(): return lax.ppermute(message, 'seq', [(i, i ^ k) for i in range(count)])]
    ppermute x2, waiting for transfers between devices: 5.77 us -> 6.14 us  [exchange(): return lax.ppermute(message, 'seq', [(i, i ^ k) for i in range(count)])]
where the time goes in v15:
time: 33.9 us; the launch traced here: 33.7 us
  Pallas kernels  12.9 us (38%)
  starting transfers between devices  10.8 us (32%)
  waiting for transfers between devices  9.35 us (28%)
  between operations  0.68 us (2%)
    ppermute x4, starting transfers between devices, hand(): lax.ppermute(message, 'seq', [(i, partner(i, k, count)) for i in range(co...  9.54 us
    ppermute x2, waiting for transfers between devices, exchange(): return lax.ppermute(message, 'seq', [(i, i ^ k) for i in range(count)])  6.14 us
    pallas_call x1, Pallas kernels, per_device(): pl.pallas_call(first_kernel, out_shape=[leaving(senders), jax.ShapeDtypeS...  5.23 us
    pallas_call x2, Pallas kernels, place(): pl.pallas_call(functools.partial(place_kernel, plan), out_shape=[jax.Shap...  3.22 us
    ppermute x4, waiting for transfers between devices, hand(): lax.ppermute(message, 'seq', [(i, partner(i, k, count)) for i in range(co...  3.21 us
    pallas_call x1, Pallas kernels, per_device(): pl.pallas_call(second_kernel, out_shape=staying(senders), in_specs=[VMEM]...  2.67 us
    ppermute x2, starting transfers between devices, exchange(): return lax.ppermute(message, 'seq', [(i, i ^ k) for i in range(count)])  1.28 us
    pallas_call x1, Pallas kernels, per_device(): pl.pallas_call(functools.partial(finish_kernel, ahead[1:] + behind), out_...  0.89 us
  transfers between devices with their start and end apart: 6, of which 4 were waited for; matrix products, arithmetic and copies ran while one was open for 0% of the time, Pallas kernels for 31%

profile of v15, /device:TPU:0, one launch (start us, length us, event | category | flops | bytes accessed | tf_op | source)
XLA Modules:
  0.0 33.7 jit_solution(5547183186010903323)
XLA Ops:
  0.6 1.5 %place.2 = bf16[1024,128]{1,0:T(8,128)(2,1)S(1)} custom-call(s32[128]{0:T(128)} %owner_any.3, bf16[4096,128]{1,0:T(8,128)(2,1)} %bitcast.14, f32[256,128]{1,0:T(8,128)} %bitcast.18, f32[2,128]{1,0:T(2,128)} %scales_any.3), custom_call_target="tpu_custom_call" | custom-call | tf_op jit(solution)/shard_map/place/pallas_call | solution.py:381
  2.1 5.1 %collective-permute-start.2 = (bf16[1024,128]{1,0:T(8,128)(2,1)S(1)}, bf16[1024,128]{1,0:T(8,128)(2,1)S(1)}, u32[]{:S(2)}, u32[]{:S(2)}) collective-permute-start(bf16[1024,128]{1,0:T(8,128)(2,1)S(1)} %place.2), channel_id=1, source_target_pairs={{0,12},{4,8},{8,4},{12,0},{1,13},{5,9},{9,5},{13,1},{2,14},{6,10},... | collective-permute-start | bytes 786440 | tf_op jit(solution)/shard_map/ppermute | solution.py:53
  7.2 5.2 %attend_leaving.1 = (bf16[2,144,256]{2,1,0:T(8,128)(2,1)S(1)}, bf16[2048,256]{1,0:T(8,128)(2,1)S(1)}, bf16[128,2048]{1,0:T(8,128)(2,1)S(1)}, bf16[1024,256]{1,0:T(8,128)(2,1)S(1)}, f32[136,256]{1,0:T(8,128)S(1)}) custom-call(bf16[4096,128]{1,0:T(8,128)(2,1)} %bitcast.15, f32[256,128]{1,0:T(8,128)} %bitcast.19, f32[2,128]{1,0:T(2,128)} %scales_any.3, ...), custom_call_target="tpu_custom_call" | custom-call | tf_op jit(solution)/shard_map/attend_leaving/pallas_call | solution.py:411
  12.5 1.7 %place.3 = (bf16[1024,128]{1,0:T(8,128)(2,1)S(1)}, bf16[512,128]{1,0:T(8,128)(2,1)S(1)}, bf16[512,128]{1,0:T(8,128)(2,1)S(1)}, bf16[1024,128]{1,0:T(8,128)(2,1)S(1)}) custom-call(s32[128]{0:T(128)} %owner_any.3, bf16[4096,128]{1,0:T(8,128)(2,1)} %bitcast.16, f32[256,128]{1,0:T(8,128)} %bitcast.20, f32[2,128]{1,0:T(2,128)} %scales_any.3), custom_call_target="tpu_custom_call" | custom-call | tf_op jit(solution)/shard_map/place/pallas_call | solution.py:381
  14.2 0.1 collective-permute-start.3
  14.3 0.6 %collective-permute-start = (bf16[2,144,256]{2,1,0:T(8,128)(2,1)S(1)}, bf16[2,144,256]{2,1,0:T(8,128)(2,1)S(1)}, u32[]{:S(2)}, u32[]{:S(2)}) collective-permute-start(bf16[2,144,256]{2,1,0:T(8,128)(2,1)S(1)} %get-tuple-element.25), channel_id=1, source_target_pairs={{0,4},{4,0},{8,12},{12,8},{1,5},{5,1},{9,13},{13,9},{2,6},{6,2},{1... | collective-permute-start | bytes 442376 | tf_op jit(solution)/shard_map/ppermute | solution.py:48
  14.9 2.3 %collective-permute-start.4 = (bf16[512,128]{1,0:T(8,128)(2,1)S(1)}, bf16[512,128]{1,0:T(8,128)(2,1)S(1)}, u32[]{:S(2)}, u32[]{:S(2)}) collective-permute-start(bf16[512,128]{1,0:T(8,128)(2,1)S(1)} %get-tuple-element.32), channel_id=1, source_target_pairs={{0,8},{4,0},{8,12},{12,4},{1,9},{5,1},{9,13},{13,5},{2,10},{6,2},{... | collective-permute-start | bytes 393224 | tf_op jit(solution)/shard_map/ppermute | solution.py:53
  17.2 2.0 %collective-permute-start.5 = (bf16[512,128]{1,0:T(8,128)(2,1)S(1)}, bf16[512,128]{1,0:T(8,128)(2,1)S(1)}, u32[]{:S(2)}, u32[]{:S(2)}) collective-permute-start(bf16[512,128]{1,0:T(8,128)(2,1)S(1)} %get-tuple-element.33), channel_id=1, source_target_pairs={{0,8},{4,0},{8,12},{12,4},{1,9},{5,1},{9,13},{13,5},{2,10},{6,2},{... | collective-permute-start | bytes 393224 | tf_op jit(solution)/shard_map/ppermute | solution.py:53
  19.2 2.7 %attend_staying.1.keep_ref = f32[2,136,256]{2,1,0:T(8,128)S(1)} custom-call(bf16[2048,256]{1,0:T(8,128)(2,1)S(1)} %get-tuple-element.20.keys_ref, bf16[128,2048]{1,0:T(8,128)(2,1)S(1)} %get-tuple-element.21.turned_ref, bf16[1024,256]{1,0:T(8,128)(2,1)S(1)} %get-tuple-element.22.asked_ref, f32[136,256]{1,0:T(8,128)S(1)} %get-tuple-element.23.own_ref), custom_call_target="tpu_custom_call" | custom-call | tf_op jit(solution)/shard_map/attend_staying/pallas_call | solution.py:440
  21.9 4.6 %collective-permute-done.got_ref = bf16[2,144,256]{2,1,0:T(8,128)(2,1)S(1)} collective-permute-done((bf16[2,144,256]{2,1,0:T(8,128)(2,1)S(1)}, bf16[2,144,256]{2,1,0:T(8,128)(2,1)S(1)}, u32[]{:S(2)}, u32[]{:S(2)}) %collective-permute-start) | collective-permute-done | bytes 147488 | tf_op jit(solution)/shard_map/ppermute | solution.py:48
  26.5 0.1 join.1
  26.5 0.7 %collective-permute-start.1 = (bf16[1,144,256]{2,1,0:T(8,128)(2,1)S(1)}, bf16[1,144,256]{2,1,0:T(8,128)(2,1)S(1)}, u32[]{:S(2)}, u32[]{:S(2)}) collective-permute-start(bf16[1,144,256]{2,1,0:T(8,128)(2,1)S(1)} %get-tuple-element.27), channel_id=1, source_target_pairs={{0,8},{4,12},{8,0},{12,4},{1,9},{5,13},{9,1},{13,5},{2,10},{6,14},... | collective-permute-start | bytes 221192 | tf_op jit(solution)/shard_map/ppermute | solution.py:48
  27.2 0.0 collective-permute-done.2.refs_0_
  27.2 0.8 %settle.1._ = bf16[4096,128]{1,0:T(8,128)(2,1)} custom-call(bf16[1024,128]{1,0:T(8,128)(2,1)S(1)} %collective-permute-done.2.refs_0_, bf16[1024,128]{1,0:T(8,128)(2,1)S(1)} %get-tuple-element.30.refs_1_), custom_call_target="tpu_custom_call" | custom-call | tf_op jit(solution)/shard_map/settle/pallas_call | solution.py:460
  28.1 1.3 %collective-permute-done.4.refs_1_ = bf16[512,128]{1,0:T(8,128)(2,1)S(1)} collective-permute-done((bf16[512,128]{1,0:T(8,128)(2,1)S(1)}, bf16[512,128]{1,0:T(8,128)(2,1)S(1)}, u32[]{:S(2)}, u32[]{:S(2)}) %collective-permute-start.4) | collective-permute-done | bytes 131104 | tf_op jit(solution)/shard_map/ppermute | solution.py:53
  29.4 1.9 %collective-permute-done.5.refs_2_ = bf16[512,128]{1,0:T(8,128)(2,1)S(1)} collective-permute-done((bf16[512,128]{1,0:T(8,128)(2,1)S(1)}, bf16[512,128]{1,0:T(8,128)(2,1)S(1)}, u32[]{:S(2)}, u32[]{:S(2)}) %collective-permute-start.5) | collective-permute-done | bytes 131104 | tf_op jit(solution)/shard_map/ppermute | solution.py:53
  31.3 1.6 %collective-permute-done.1.got_ref = bf16[1,144,256]{2,1,0:T(8,128)(2,1)S(1)} collective-permute-done((bf16[1,144,256]{2,1,0:T(8,128)(2,1)S(1)}, bf16[1,144,256]{2,1,0:T(8,128)(2,1)S(1)}, u32[]{:S(2)}, u32[]{:S(2)}) %collective-permute-start.1) | collective-permute-done | bytes 73760 | tf_op jit(solution)/shard_map/ppermute | solution.py:48
  32.8 0.0 collective-permute-done.3.refs_0_
  32.9 0.9 %finish.1 = (bf16[256,128]{1,0:T(8,128)(2,1)}, bf16[4096,128]{1,0:T(8,128)(2,1)}) custom-call(f32[1,136,256]{2,1,0:T(8,128)S(1)} %get-tuple-element.26.keep_ref, bf16[1,144,256]{2,1,0:T(8,128)(2,1)S(1)} %collective-permute-done.1.got_ref, bf16[4096,128]{1,0:T(8,128)(2,1)} %settle.1._, ...), custom_call_target="tpu_custom_call", output_to_operand_aliasing={{1}: (2, {})} | custom-call | tf_op jit(solution)/shard_map/finish/pallas_call | solution.py:469
Async XLA Ops:
  2.1 25.1 %collective-permute-start.2 = (bf16[1024,128]{1,0:T(8,128)(2,1)S(1)}, bf16[1024,128]{1,0:T(8,128)(2,1)S(1)}, u32[]{:S(2)}, u32[]{:S(2)}) collective-permute-start(bf16[1024,128]{1,0:T(8,128)(2,1)S(1)} %place.2), channel_id=1, source_target_pairs={{0,12},{4,8},{8,4},{12,0},{1,13},{5,9},{9,5},{13,1},{2,14},{6,10},... | collective-permute-start | bytes 786440 | tf_op jit(solution)/shard_map/ppermute | solution.py:53
  14.2 18.6 %collective-permute-start.3 = (bf16[1024,128]{1,0:T(8,128)(2,1)S(1)}, bf16[1024,128]{1,0:T(8,128)(2,1)S(1)}, u32[]{:S(2)}, u32[]{:S(2)}) collective-permute-start(bf16[1024,128]{1,0:T(8,128)(2,1)S(1)} %get-tuple-element.31), channel_id=1, source_target_pairs={{0,4},{4,12},{8,0},{12,8},{1,5},{5,13},{9,1},{13,9},{2,6},{6,14},{... | collective-permute-start | bytes 786440 | tf_op jit(solution)/shard_map/ppermute | solution.py:53
  14.3 12.2 %collective-permute-start = (bf16[2,144,256]{2,1,0:T(8,128)(2,1)S(1)}, bf16[2,144,256]{2,1,0:T(8,128)(2,1)S(1)}, u32[]{:S(2)}, u32[]{:S(2)}) collective-permute-start(bf16[2,144,256]{2,1,0:T(8,128)(2,1)S(1)} %get-tuple-element.25), channel_id=1, source_target_pairs={{0,4},{4,0},{8,12},{12,8},{1,5},{5,1},{9,13},{13,9},{2,6},{6,2},{1... | collective-permute-start | bytes 442376 | tf_op jit(solution)/shard_map/ppermute | solution.py:48
  14.9 14.5 %collective-permute-start.4 = (bf16[512,128]{1,0:T(8,128)(2,1)S(1)}, bf16[512,128]{1,0:T(8,128)(2,1)S(1)}, u32[]{:S(2)}, u32[]{:S(2)}) collective-permute-start(bf16[512,128]{1,0:T(8,128)(2,1)S(1)} %get-tuple-element.32), channel_id=1, source_target_pairs={{0,8},{4,0},{8,12},{12,4},{1,9},{5,1},{9,13},{13,5},{2,10},{6,2},{... | collective-permute-start | bytes 393224 | tf_op jit(solution)/shard_map/ppermute | solution.py:53
  17.2 14.1 %collective-permute-start.5 = (bf16[512,128]{1,0:T(8,128)(2,1)S(1)}, bf16[512,128]{1,0:T(8,128)(2,1)S(1)}, u32[]{:S(2)}, u32[]{:S(2)}) collective-permute-start(bf16[512,128]{1,0:T(8,128)(2,1)S(1)} %get-tuple-element.33), channel_id=1, source_target_pairs={{0,8},{4,0},{8,12},{12,4},{1,9},{5,1},{9,13},{13,5},{2,10},{6,2},{... | collective-permute-start | bytes 393224 | tf_op jit(solution)/shard_map/ppermute | solution.py:53
  26.5 6.3 %collective-permute-start.1 = (bf16[1,144,256]{2,1,0:T(8,128)(2,1)S(1)}, bf16[1,144,256]{2,1,0:T(8,128)(2,1)S(1)}, u32[]{:S(2)}, u32[]{:S(2)}) collective-permute-start(bf16[1,144,256]{2,1,0:T(8,128)(2,1)S(1)} %get-tuple-element.27), channel_id=1, source_target_pairs={{0,8},{4,12},{8,0},{12,4},{1,9},{5,13},{9,1},{13,5},{2,10},{6,14},... | collective-permute-start | bytes 221192 | tf_op jit(solution)/shard_map/ppermute | solution.py:48

commit v16 on v14

--- a/solution.py
+++ b/solution.py
@@ -10,7 +10,7 @@
 HD = 128
 GQ = 8
 STEPS = 2
-STAT_ROWS = 16
+STAT_ROWS = 8
 KEEP_ROWS = 8
 FAR = -1e30
 RATE = HD ** (-0.5) * 1.4426950408889634
@@ -55,7 +55,7 @@
 
 def messages(count, capacity):
     half = capacity // 2
-    ahead = [(k, 0, capacity) for k in reversed(range(count // 2, count))]
+    ahead = [(k, 0, capacity) for k in range(count // 2, count)]
     behind = [(k, first, half) for k in reversed(range(1, count // 2)) for first in (0, half)]
     return ahead, behind, [(0, 0, capacity)]
 

time: 34 us -> 33.6 us (0.988)
  starting transfers between devices: 11.4 us -> 10.9 us
    ppermute x4, starting transfers between devices: 9.49 us -> 9.09 us  [hand(): lax.ppermute(message, 'seq', [(i, partner(i, k, count)) for i in range(co...]
where the time goes in v16:
time: 33.6 us; the launch traced here: 33.4 us
  Pallas kernels  12.9 us (38%)
  starting transfers between devices  10.9 us (32%)
  waiting for transfers between devices  8.83 us (26%)
  between operations  0.68 us (2%)
    ppermute x4, starting transfers between devices, hand(): lax.ppermute(message, 'seq', [(i, partner(i, k, count)) for i in range(co...  9.09 us
    ppermute x2, waiting for transfers between devices, exchange(): return lax.ppermute(message, 'seq', [(i, i ^ k) for i in range(count)])  5.96 us
    pallas_call x1, Pallas kernels, per_device(): pl.pallas_call(first_kernel, out_shape=[leaving(senders), jax.ShapeDtypeS...  5.24 us
    pallas_call x2, Pallas kernels, place(): pl.pallas_call(functools.partial(place_kernel, plan), out_shape=[jax.Shap...  3.22 us
    ppermute x4, waiting for transfers between devices, hand(): lax.ppermute(message, 'seq', [(i, partner(i, k, count)) for i in range(co...  2.87 us
    pallas_call x1, Pallas kernels, per_device(): pl.pallas_call(second_kernel, out_shape=staying(senders), in_specs=[VMEM]...  2.7 us
    ppermute x2, starting transfers between devices, exchange(): return lax.ppermute(message, 'seq', [(i, i ^ k) for i in range(count)])  1.86 us
    pallas_call x1, Pallas kernels, per_device(): pl.pallas_call(functools.partial(finish_kernel, ahead[1:] + behind), out_...  0.88 us
  transfers between devices with their start and end apart: 6, of which 4 were waited for; matrix products, arithmetic and copies ran while one was open for 0% of the time, Pallas kernels for 31%

profile of v16, /device:TPU:0, one launch (start us, length us, event | category | flops | bytes accessed | tf_op | source)
XLA Modules:
  0.0 33.4 jit_solution(163276148810045141)
XLA Ops:
  0.6 1.6 %place.2 = (bf16[1024,128]{1,0:T(8,128)(2,1)S(1)}, bf16[1024,128]{1,0:T(8,128)(2,1)S(1)}) custom-call(s32[128]{0:T(128)} %owner_any.3, bf16[4096,128]{1,0:T(8,128)(2,1)} %bitcast.14, f32[256,128]{1,0:T(8,128)} %bitcast.18, f32[2,128]{1,0:T(2,128)} %scales_any.3), custom_call_target="tpu_custom_call" | custom-call | tf_op jit(solution)/shard_map/place/pallas_call | solution.py:380
  2.2 3.1 %collective-permute-start.2 = (bf16[1024,128]{1,0:T(8,128)(2,1)S(1)}, bf16[1024,128]{1,0:T(8,128)(2,1)S(1)}, u32[]{:S(2)}, u32[]{:S(2)}) collective-permute-start(bf16[1024,128]{1,0:T(8,128)(2,1)S(1)} %get-tuple-element.32), channel_id=1, source_target_pairs={{0,4},{4,12},{8,0},{12,8},{1,5},{5,13},{9,1},{13,9},{2,6},{6,14},{... | collective-permute-start | bytes 786440 | tf_op jit(solution)/shard_map/ppermute | solution.py:53
  5.3 2.5 %collective-permute-start.3 = (bf16[1024,128]{1,0:T(8,128)(2,1)S(1)}, bf16[1024,128]{1,0:T(8,128)(2,1)S(1)}, u32[]{:S(2)}, u32[]{:S(2)}) collective-permute-start(bf16[1024,128]{1,0:T(8,128)(2,1)S(1)} %get-tuple-element.35), channel_id=1, source_target_pairs={{0,12},{4,8},{8,4},{12,0},{1,13},{5,9},{9,5},{13,1},{2,14},{6,10},... | collective-permute-start | bytes 786440 | tf_op jit(solution)/shard_map/ppermute | solution.py:53
  7.8 5.2 %attend_leaving.1 = (bf16[2,136,256]{2,1,0:T(8,128)(2,1)S(1)}, bf16[2048,256]{1,0:T(8,128)(2,1)S(1)}, bf16[128,2048]{1,0:T(8,128)(2,1)S(1)}, bf16[1024,256]{1,0:T(8,128)(2,1)S(1)}, f32[136,256]{1,0:T(8,128)S(1)}) custom-call(bf16[4096,128]{1,0:T(8,128)(2,1)} %bitcast.15, f32[256,128]{1,0:T(8,128)} %bitcast.19, f32[2,128]{1,0:T(2,128)} %scales_any.3, ...), custom_call_target="tpu_custom_call" | custom-call | tf_op jit(solution)/shard_map/attend_leaving/pallas_call | solution.py:410
  13.1 0.2 collective-permute-start
  13.2 1.6 %place.3 = (bf16[512,128]{1,0:T(8,128)(2,1)S(1)}, bf16[512,128]{1,0:T(8,128)(2,1)S(1)}, bf16[1024,128]{1,0:T(8,128)(2,1)S(1)}) custom-call(s32[128]{0:T(128)} %owner_any.3, bf16[4096,128]{1,0:T(8,128)(2,1)} %bitcast.16, f32[256,128]{1,0:T(8,128)} %bitcast.20, f32[2,128]{1,0:T(2,128)} %scales_any.3), custom_call_target="tpu_custom_call" | custom-call | tf_op jit(solution)/shard_map/place/pallas_call | solution.py:380
  14.8 1.8 %collective-permute-start.4 = (bf16[512,128]{1,0:T(8,128)(2,1)S(1)}, bf16[512,128]{1,0:T(8,128)(2,1)S(1)}, u32[]{:S(2)}, u32[]{:S(2)}) collective-permute-start(bf16[512,128]{1,0:T(8,128)(2,1)S(1)} %get-tuple-element.36), channel_id=1, source_target_pairs={{0,8},{4,0},{8,12},{12,4},{1,9},{5,1},{9,13},{13,5},{2,10},{6,2},{... | collective-permute-start | bytes 393224 | tf_op jit(solution)/shard_map/ppermute | solution.py:53
  16.7 1.7 %collective-permute-start.5 = (bf16[512,128]{1,0:T(8,128)(2,1)S(1)}, bf16[512,128]{1,0:T(8,128)(2,1)S(1)}, u32[]{:S(2)}, u32[]{:S(2)}) collective-permute-start(bf16[512,128]{1,0:T(8,128)(2,1)S(1)} %get-tuple-element.37), channel_id=1, source_target_pairs={{0,8},{4,0},{8,12},{12,4},{1,9},{5,1},{9,13},{13,5},{2,10},{6,2},{... | collective-permute-start | bytes 393224 | tf_op jit(solution)/shard_map/ppermute | solution.py:53
  18.4 2.7 %attend_staying.1.keep_ref = f32[2,136,256]{2,1,0:T(8,128)S(1)} custom-call(bf16[2048,256]{1,0:T(8,128)(2,1)S(1)} %get-tuple-element.24.keys_ref, bf16[128,2048]{1,0:T(8,128)(2,1)S(1)} %get-tuple-element.25.turned_ref, bf16[1024,256]{1,0:T(8,128)(2,1)S(1)} %get-tuple-element.26.asked_ref, f32[136,256]{1,0:T(8,128)S(1)} %get-tuple-element.27.own_ref), custom_call_target="tpu_custom_call" | custom-call | tf_op jit(solution)/shard_map/attend_staying/pallas_call | solution.py:439
  21.1 1.5 %collective-permute-done.got_ref = bf16[2,136,256]{2,1,0:T(8,128)(2,1)S(1)} collective-permute-done((bf16[2,136,256]{2,1,0:T(8,128)(2,1)S(1)}, bf16[2,136,256]{2,1,0:T(8,128)(2,1)S(1)}, u32[]{:S(2)}, u32[]{:S(2)}) %collective-permute-start) | collective-permute-done | bytes 139296 | tf_op jit(solution)/shard_map/ppermute | solution.py:48
  22.6 0.1 join.1
  22.7 1.7 %collective-permute-start.1 = (bf16[1,136,256]{2,1,0:T(8,128)(2,1)S(1)}, bf16[1,136,256]{2,1,0:T(8,128)(2,1)S(1)}, u32[]{:S(2)}, u32[]{:S(2)}) collective-permute-start(bf16[1,136,256]{2,1,0:T(8,128)(2,1)S(1)} %get-tuple-element.31), channel_id=1, source_target_pairs={{0,8},{4,12},{8,0},{12,4},{1,9},{5,13},{9,1},{13,5},{2,10},{6,14},... | collective-permute-start | bytes 208904 | tf_op jit(solution)/shard_map/ppermute | solution.py:48
  24.4 0.0 collective-permute-done.2.refs_0_
  24.4 0.8 %settle.1._ = bf16[4096,128]{1,0:T(8,128)(2,1)} custom-call(bf16[1024,128]{1,0:T(8,128)(2,1)S(1)} %collective-permute-done.2.refs_0_, bf16[1024,128]{1,0:T(8,128)(2,1)S(1)} %get-tuple-element.34.refs_1_), custom_call_target="tpu_custom_call" | custom-call | tf_op jit(solution)/shard_map/settle/pallas_call | solution.py:459
  25.2 0.2 collective-permute-done.4.refs_1_
  25.4 2.6 %collective-permute-done.5.refs_2_ = bf16[512,128]{1,0:T(8,128)(2,1)S(1)} collective-permute-done((bf16[512,128]{1,0:T(8,128)(2,1)S(1)}, bf16[512,128]{1,0:T(8,128)(2,1)S(1)}, u32[]{:S(2)}, u32[]{:S(2)}) %collective-permute-start.5) | collective-permute-done | bytes 131104 | tf_op jit(solution)/shard_map/ppermute | solution.py:53
  28.0 4.4 %collective-permute-done.1.got_ref = bf16[1,136,256]{2,1,0:T(8,128)(2,1)S(1)} collective-permute-done((bf16[1,136,256]{2,1,0:T(8,128)(2,1)S(1)}, bf16[1,136,256]{2,1,0:T(8,128)(2,1)S(1)}, u32[]{:S(2)}, u32[]{:S(2)}) %collective-permute-start.1) | collective-permute-done | bytes 69664 | tf_op jit(solution)/shard_map/ppermute | solution.py:48
  32.5 0.0 collective-permute-done.3.refs_0_
  32.5 0.9 %finish.1 = (bf16[256,128]{1,0:T(8,128)(2,1)}, bf16[4096,128]{1,0:T(8,128)(2,1)}) custom-call(f32[1,136,256]{2,1,0:T(8,128)S(1)} %get-tuple-element.30.keep_ref, bf16[1,136,256]{2,1,0:T(8,128)(2,1)S(1)} %collective-permute-done.1.got_ref, bf16[4096,128]{1,0:T(8,128)(2,1)} %settle.1._, ...), custom_call_target="tpu_custom_call", output_to_operand_aliasing={{1}: (2, {})} | custom-call | tf_op jit(solution)/shard_map/finish/pallas_call | solution.py:468
Async XLA Ops:
  2.2 22.1 %collective-permute-start.2 = (bf16[1024,128]{1,0:T(8,128)(2,1)S(1)}, bf16[1024,128]{1,0:T(8,128)(2,1)S(1)}, u32[]{:S(2)}, u32[]{:S(2)}) collective-permute-start(bf16[1024,128]{1,0:T(8,128)(2,1)S(1)} %get-tuple-element.32), channel_id=1, source_target_pairs={{0,4},{4,12},{8,0},{12,8},{1,5},{5,13},{9,1},{13,9},{2,6},{6,14},{... | collective-permute-start | bytes 786440 | tf_op jit(solution)/shard_map/ppermute | solution.py:53
  5.3 27.2 %collective-permute-start.3 = (bf16[1024,128]{1,0:T(8,128)(2,1)S(1)}, bf16[1024,128]{1,0:T(8,128)(2,1)S(1)}, u32[]{:S(2)}, u32[]{:S(2)}) collective-permute-start(bf16[1024,128]{1,0:T(8,128)(2,1)S(1)} %get-tuple-element.35), channel_id=1, source_target_pairs={{0,12},{4,8},{8,4},{12,0},{1,13},{5,9},{9,5},{13,1},{2,14},{6,10},... | collective-permute-start | bytes 786440 | tf_op jit(solution)/shard_map/ppermute | solution.py:53
  13.1 9.6 %collective-permute-start = (bf16[2,136,256]{2,1,0:T(8,128)(2,1)S(1)}, bf16[2,136,256]{2,1,0:T(8,128)(2,1)S(1)}, u32[]{:S(2)}, u32[]{:S(2)}) collective-permute-start(bf16[2,136,256]{2,1,0:T(8,128)(2,1)S(1)} %get-tuple-element.29), channel_id=1, source_target_pairs={{0,4},{4,0},{8,12},{12,8},{1,5},{5,1},{9,13},{13,9},{2,6},{6,2},{1... | collective-permute-start | bytes 417800 | tf_op jit(solution)/shard_map/ppermute | solution.py:48
  14.8 10.6 %collective-permute-start.4 = (bf16[512,128]{1,0:T(8,128)(2,1)S(1)}, bf16[512,128]{1,0:T(8,128)(2,1)S(1)}, u32[]{:S(2)}, u32[]{:S(2)}) collective-permute-start(bf16[512,128]{1,0:T(8,128)(2,1)S(1)} %get-tuple-element.36), channel_id=1, source_target_pairs={{0,8},{4,0},{8,12},{12,4},{1,9},{5,1},{9,13},{13,5},{2,10},{6,2},{... | collective-permute-start | bytes 393224 | tf_op jit(solution)/shard_map/ppermute | solution.py:53
  16.7 11.4 %collective-permute-start.5 = (bf16[512,128]{1,0:T(8,128)(2,1)S(1)}, bf16[512,128]{1,0:T(8,128)(2,1)S(1)}, u32[]{:S(2)}, u32[]{:S(2)}) collective-permute-start(bf16[512,128]{1,0:T(8,128)(2,1)S(1)} %get-tuple-element.37), channel_id=1, source_target_pairs={{0,8},{4,0},{8,12},{12,4},{1,9},{5,1},{9,13},{13,5},{2,10},{6,2},{... | collective-permute-start | bytes 393224 | tf_op jit(solution)/shard_map/ppermute | solution.py:53
  22.7 9.8 %collective-permute-start.1 = (bf16[1,136,256]{2,1,0:T(8,128)(2,1)S(1)}, bf16[1,136,256]{2,1,0:T(8,128)(2,1)S(1)}, u32[]{:S(2)}, u32[]{:S(2)}) collective-permute-start(bf16[1,136,256]{2,1,0:T(8,128)(2,1)S(1)} %get-tuple-element.31), channel_id=1, source_target_pairs={{0,8},{4,12},{8,0},{12,4},{1,9},{5,13},{9,1},{13,5},{2,10},{6,14},... | collective-permute-start | bytes 208904 | tf_op jit(solution)/shard_map/ppermute | solution.py:48

commit v17 on v16

--- a/solution.py
+++ b/solution.py
@@ -48,15 +48,16 @@
     return lax.ppermute(message, "seq", [(i, i ^ k) for i in range(count)])
 
 
-def hand(message, k):
+def hand(message, k, kinds=(0, 1)):
     count = lax.axis_size("seq")
-    return lax.ppermute(message, "seq", [(i, partner(i, k, count)) for i in range(count)])
+    senders = [i for i in range(count) if inner(i, count) in kinds]
+    return lax.ppermute(message, "seq", [(i, partner(i, k, count)) for i in senders])
 
 
 def messages(count, capacity):
-    half = capacity // 2
-    ahead = [(k, 0, capacity) for k in range(count // 2, count)]
-    behind = [(k, first, half) for k in reversed(range(1, count // 2)) for first in (0, half)]
+    far = count // 2
+    ahead = [(k, 0, capacity) for k in [far, 1] + [k for k in reversed(range(2, count)) if k != far]]
+    behind = [(1, first, capacity // 2) for first in (0, capacity // 2)]
     return ahead, behind, [(0, 0, capacity)]
 
 
@@ -332,25 +333,39 @@
         sender = source(me, k, receivers) if k else me
         first = pl.multiple_of(sender * rows + start * (size // slots), size)
         copies.append(pltpu.make_async_copy(handed[index], pages.at[pl.ds(first, size), :], sems.at[index]))
-        copies[-1].start()
     return copies
+
+
+def started(copies, some, kind):
+    here = inner(lax.axis_index("seq"), lax.axis_size("seq")) == kind
+
+    def every(act):
+        for index, copy in enumerate(copies):
+            if index in some:
+                pl.when(here)(functools.partial(act, copy))
+            else:
+                act(copy)
+
+    every(lambda copy: copy.start())
+    return functools.partial(every, lambda copy: copy.wait())
 
 
 def settle_kernel(plan, *refs):
     *handed, pages, sems = refs
-    for copy in settle(plan, handed, pages, sems):
-        copy.wait()
+    started(settle(plan, handed, pages, sems), [index for index, (k, _, _) in enumerate(plan) if k == 1], 0)()
 
 
 def finish_kernel(plan, keep_ref, got_ref, _, *refs):
     *handed, out_any, pages, out_ref, sems = refs
-    copies = settle(plan, handed, pages, sems)
+    wait = started(
+        settle(plan, handed, pages, sems), [index for index, (k, _, _) in enumerate(plan) if k == 1], 1
+    )
     summed, _, total = joined(taken(keep_ref[0]), unpacked(got_ref[0]))
     out_ref[...] = (summed / total).T.astype(jnp.bfloat16)
-    copies.append(pltpu.make_async_copy(out_ref, out_any, sems.at[len(copies)]))
-    copies[-1].start()
-    for copy in copies:
-        copy.wait()
+    store = pltpu.make_async_copy(out_ref, out_any, sems.at[len(handed)])
+    store.start()
+    wait()
+    store.wait()
 
 
 def in_hbm(arrays):
@@ -397,7 +412,9 @@
 
     sent = place(ahead, flat_deltas)
     sent, late_deltas = lax.optimization_barrier((sent, flat_deltas))
-    got_ahead = [hand(message, k) for message, (k, _, _) in zip(sent, ahead)]
+    got_ahead = [
+        hand(message, k, (1,) if k == 1 else (0, 1)) for message, (k, _, _) in zip(sent, ahead)
+    ]
 
     def leaving(count):
         return jax.ShapeDtypeStruct((count // 2, HD + STAT_ROWS, width), jnp.bfloat16)
@@ -435,7 +452,18 @@
     send, late_deltas = lax.optimization_barrier((send, late_deltas))
     passed = exchange(send, k)
     *sent, mine = place(behind + own, late_deltas)
-    got = got_ahead[1:] + [hand(message, k) for message, (k, _, _) in zip(sent, behind)]
+    settled = ahead[:2] + own
+    pages = pl.pallas_call(
+        functools.partial(settle_kernel, settled),
+        out_shape=whole,
+        in_specs=[ANY] * len(settled),
+        out_specs=HBM,
+        scratch_shapes=[pltpu.SemaphoreType.DMA((len(settled),))],
+        compiler_params=small,
+        name="settle",
+    )(*got_ahead[:2], mine)
+    sent, pages = lax.optimization_barrier((sent, pages))
+    got = got_ahead[2:] + [hand(message, k, (0,)) for message, (k, _, _) in zip(sent, behind)]
     keep = pl.pallas_call(
         second_kernel,
         out_shape=staying(senders),
@@ -455,18 +483,8 @@
         )(keep, passed)
         k, count = 2 * k, count // 2
         passed = exchange(send, k)
-    settled = ahead[:1] + own
-    pages = pl.pallas_call(
-        functools.partial(settle_kernel, settled),
-        out_shape=whole,
-        in_specs=[ANY] * len(settled),
-        out_specs=HBM,
-        scratch_shapes=[pltpu.SemaphoreType.DMA((len(settled),))],
-        compiler_params=small,
-        name="settle",
-    )(got_ahead[0], mine)
     attended, pages = pl.pallas_call(
-        functools.partial(finish_kernel, ahead[1:] + behind),
+        functools.partial(finish_kernel, ahead[2:] + behind),
         out_shape=[jax.ShapeDtypeStruct((width, HD), jnp.bfloat16), whole],
         in_specs=[VMEM] * 2 + [HBM] + [ANY] * len(got),
         out_specs=[HBM, HBM],

time: 33.6 us -> 40.4 us (1.20)
  waiting for transfers between devices: 8.83 us -> 12.7 us
  starting transfers between devices: 10.9 us -> 13.6 us
    ppermute x4 -> x5, waiting for transfers between devices: 2.87 us -> 6.14 us  [hand(): lax.ppermute(message, 'seq', [(i, partner(i, k, count)) for i in senders])]
    ppermute x4 -> x5, starting transfers between devices: 9.09 us -> 11.8 us  [hand(): lax.ppermute(message, 'seq', [(i, partner(i, k, count)) for i in senders])]
    ppermute x2, waiting for transfers between devices: 5.96 us -> 6.56 us  [exchange(): return lax.ppermute(message, 'seq', [(i, i ^ k) for i in range(count)])]
  transfers between devices with their start and end apart: 6 -> 7, of which waited for: 4 -> 2; matrix products, arithmetic and copies ran while one was open for 0% -> 0% of each run, Pallas kernels for 31% -> 26%
where the time goes in v17:
time: 40.4 us; the launch traced here: 40.1 us
  starting transfers between devices  13.6 us (34%)
  Pallas kernels  13.1 us (32%)
  waiting for transfers between devices  12.7 us (31%)
  between operations  0.73 us (2%)
    ppermute x5, starting transfers between devices, hand(): lax.ppermute(message, 'seq', [(i, partner(i, k, count)) for i in senders])  11.8 us
    ppermute x2, waiting for transfers between devices, exchange(): return lax.ppermute(message, 'seq', [(i, i ^ k) for i in range(count)])  6.56 us
    ppermute x5, waiting for transfers between devices, hand(): lax.ppermute(message, 'seq', [(i, partner(i, k, count)) for i in senders])  6.14 us
    pallas_call x1, Pallas kernels, per_device(): pl.pallas_call(first_kernel, out_shape=[leaving(senders), jax.ShapeDtypeS...  5.24 us
    pallas_call x2, Pallas kernels, place(): pl.pallas_call(functools.partial(place_kernel, plan), out_shape=[jax.Shap...  3.35 us
    pallas_call x1, Pallas kernels, per_device(): pl.pallas_call(second_kernel, out_shape=staying(senders), in_specs=[VMEM]...  2.71 us
    ppermute x2, starting transfers between devices, exchange(): return lax.ppermute(message, 'seq', [(i, i ^ k) for i in range(count)])  1.89 us
    pallas_call x1, Pallas kernels, per_device(): pl.pallas_call(functools.partial(settle_kernel, settled), out_shape=whole...  0.9 us
  transfers between devices with their start and end apart: 7, of which 2 were waited for; matrix products, arithmetic and copies ran while one was open for 0% of the time, Pallas kernels for 26%

profile of v17, /device:TPU:0, one launch (start us, length us, event | category | flops | bytes accessed | tf_op | source)
XLA Modules:
  0.0 40.1 jit_solution(138273389701295419)
XLA Ops:
  0.6 1.7 %place.2 = (bf16[1024,128]{1,0:T(8,128)(2,1)S(1)}, bf16[1024,128]{1,0:T(8,128)(2,1)S(1)}, bf16[1024,128]{1,0:T(8,128)(2,1)S(1)}) custom-call(s32[128]{0:T(128)} %owner_any.3, bf16[4096,128]{1,0:T(8,128)(2,1)} %bitcast.14, f32[256,128]{1,0:T(8,128)} %bitcast.18, f32[2,128]{1,0:T(2,128)} %scales_any.3), custom_call_target="tpu_custom_call" | custom-call | tf_op jit(solution)/shard_map/place/pallas_call | solution.py:395
  2.4 3.1 %collective-permute-start.2 = (bf16[1024,128]{1,0:T(8,128)(2,1)S(1)}, bf16[1024,128]{1,0:T(8,128)(2,1)S(1)}, u32[]{:S(2)}, u32[]{:S(2)}) collective-permute-start(bf16[1024,128]{1,0:T(8,128)(2,1)S(1)} %get-tuple-element.41), channel_id=1, source_target_pairs={{0,4},{4,12},{8,0},{12,8},{1,5},{5,13},{9,1},{13,9},{2,6},{6,14},{... | collective-permute-start | bytes 786440 | tf_op jit(solution)/shard_map/ppermute | solution.py:54
  5.5 1.3 %collective-permute-start.3 = (bf16[1024,128]{1,0:T(8,128)(2,1)S(1)}, bf16[1024,128]{1,0:T(8,128)(2,1)S(1)}, u32[]{:S(2)}, u32[]{:S(2)}) collective-permute-start(bf16[1024,128]{1,0:T(8,128)(2,1)S(1)} %get-tuple-element.42), channel_id=1, source_target_pairs={{4,0},{8,12},{5,1},{9,13},{6,2},{10,14},{7,3},{11,15},{20,16},{24,... | collective-permute-start | bytes 786440 | tf_op jit(solution)/shard_map/ppermute | solution.py:54
  6.7 2.5 %collective-permute-start.4 = (bf16[1024,128]{1,0:T(8,128)(2,1)S(1)}, bf16[1024,128]{1,0:T(8,128)(2,1)S(1)}, u32[]{:S(2)}, u32[]{:S(2)}) collective-permute-start(bf16[1024,128]{1,0:T(8,128)(2,1)S(1)} %get-tuple-element.45), channel_id=1, source_target_pairs={{0,12},{4,8},{8,4},{12,0},{1,13},{5,9},{9,5},{13,1},{2,14},{6,10},... | collective-permute-start | bytes 786440 | tf_op jit(solution)/shard_map/ppermute | solution.py:54
  9.3 5.2 %attend_leaving.1 = (bf16[2,136,256]{2,1,0:T(8,128)(2,1)S(1)}, bf16[2048,256]{1,0:T(8,128)(2,1)S(1)}, bf16[128,2048]{1,0:T(8,128)(2,1)S(1)}, bf16[1024,256]{1,0:T(8,128)(2,1)S(1)}, f32[136,256]{1,0:T(8,128)S(1)}) custom-call(bf16[4096,128]{1,0:T(8,128)(2,1)} %bitcast.15, f32[256,128]{1,0:T(8,128)} %bitcast.19, f32[2,128]{1,0:T(2,128)} %scales_any.3, ...), custom_call_target="tpu_custom_call" | custom-call | tf_op jit(solution)/shard_map/attend_leaving/pallas_call | solution.py:427
  14.5 1.8 %collective-permute-start = (bf16[2,136,256]{2,1,0:T(8,128)(2,1)S(1)}, bf16[2,136,256]{2,1,0:T(8,128)(2,1)S(1)}, u32[]{:S(2)}, u32[]{:S(2)}) collective-permute-start(bf16[2,136,256]{2,1,0:T(8,128)(2,1)S(1)} %get-tuple-element.35), channel_id=1, source_target_pairs={{0,4},{4,0},{8,12},{12,8},{1,5},{5,1},{9,13},{13,9},{2,6},{6,2},{1... | collective-permute-start | bytes 417800 | tf_op jit(solution)/shard_map/ppermute | solution.py:48
  16.4 1.6 %place.3 = (bf16[512,128]{1,0:T(8,128)(2,1)S(1)}, bf16[512,128]{1,0:T(8,128)(2,1)S(1)}, bf16[1024,128]{1,0:T(8,128)(2,1)S(1)}) custom-call(s32[128]{0:T(128)} %owner_any.3, bf16[4096,128]{1,0:T(8,128)(2,1)} %bitcast.16, f32[256,128]{1,0:T(8,128)} %bitcast.20, f32[2,128]{1,0:T(2,128)} %scales_any.3), custom_call_target="tpu_custom_call" | custom-call | tf_op jit(solution)/shard_map/place/pallas_call | solution.py:395
  18.0 0.0 collective-permute-done.2.refs_0_
  18.0 6.1 %collective-permute-done.3.refs_1_ = bf16[1024,128]{1,0:T(8,128)(2,1)S(1)} collective-permute-done((bf16[1024,128]{1,0:T(8,128)(2,1)S(1)}, bf16[1024,128]{1,0:T(8,128)(2,1)S(1)}, u32[]{:S(2)}, u32[]{:S(2)}) %collective-permute-start.3) | collective-permute-done | bytes 262176 | tf_op jit(solution)/shard_map/ppermute | solution.py:54
  24.1 0.9 %settle.1._ = bf16[4096,128]{1,0:T(8,128)(2,1)} custom-call(bf16[1024,128]{1,0:T(8,128)(2,1)S(1)} %collective-permute-done.2.refs_0_, bf16[1024,128]{1,0:T(8,128)(2,1)S(1)} %collective-permute-done.3.refs_1_, bf16[1024,128]{1,0:T(8,128)(2,1)S(1)} %get-tuple-element.43.refs_2_), custom_call_target="tpu_custom_call" | custom-call | tf_op jit(solution)/shard_map/settle/pallas_call | solution.py:456
  25.0 3.6 %collective-permute-start.5 = (bf16[512,128]{1,0:T(8,128)(2,1)S(1)}, bf16[512,128]{1,0:T(8,128)(2,1)S(1)}, u32[]{:S(2)}, u32[]{:S(2)}) collective-permute-start(bf16[512,128]{1,0:T(8,128)(2,1)S(1)} %get-tuple-element.46), channel_id=1, source_target_pairs={{0,8},{12,4},{1,9},{13,5},{2,10},{14,6},{3,11},{15,7},{16,24},{28,... | collective-permute-start | bytes 393224 | tf_op jit(solution)/shard_map/ppermute | solution.py:54
  28.6 1.3 %collective-permute-start.6 = (bf16[512,128]{1,0:T(8,128)(2,1)S(1)}, bf16[512,128]{1,0:T(8,128)(2,1)S(1)}, u32[]{:S(2)}, u32[]{:S(2)}) collective-permute-start(bf16[512,128]{1,0:T(8,128)(2,1)S(1)} %get-tuple-element.47), channel_id=1, source_target_pairs={{0,8},{12,4},{1,9},{13,5},{2,10},{14,6},{3,11},{15,7},{16,24},{28,... | collective-permute-start | bytes 393224 | tf_op jit(solution)/shard_map/ppermute | solution.py:54
  29.9 2.7 %attend_staying.1.keep_ref = f32[2,136,256]{2,1,0:T(8,128)S(1)} custom-call(bf16[2048,256]{1,0:T(8,128)(2,1)S(1)} %get-tuple-element.30.keys_ref, bf16[128,2048]{1,0:T(8,128)(2,1)S(1)} %get-tuple-element.31.turned_ref, bf16[1024,256]{1,0:T(8,128)(2,1)S(1)} %get-tuple-element.32.asked_ref, f32[136,256]{1,0:T(8,128)S(1)} %get-tuple-element.33.own_ref), custom_call_target="tpu_custom_call" | custom-call | tf_op jit(solution)/shard_map/attend_staying/pallas_call | solution.py:467
  32.6 0.0 collective-permute-done.got_ref
  32.6 0.1 join.1
  32.7 0.1 collective-permute-start.1
  32.8 6.6 %collective-permute-done.1.got_ref = bf16[1,136,256]{2,1,0:T(8,128)(2,1)S(1)} collective-permute-done((bf16[1,136,256]{2,1,0:T(8,128)(2,1)S(1)}, bf16[1,136,256]{2,1,0:T(8,128)(2,1)S(1)}, u32[]{:S(2)}, u32[]{:S(2)}) %collective-permute-start.1) | collective-permute-done | bytes 69664 | tf_op jit(solution)/shard_map/ppermute | solution.py:48
  39.3 0.0 collective-permute-done.4.refs_0_
  39.3 0.0 collective-permute-done.5.refs_1_
  39.3 0.0 collective-permute-done.6.refs_2_
  39.3 0.8 %finish.1 = (bf16[256,128]{1,0:T(8,128)(2,1)}, bf16[4096,128]{1,0:T(8,128)(2,1)}) custom-call(f32[1,136,256]{2,1,0:T(8,128)S(1)} %get-tuple-element.36.keep_ref, bf16[1,136,256]{2,1,0:T(8,128)(2,1)S(1)} %collective-permute-done.1.got_ref, bf16[4096,128]{1,0:T(8,128)(2,1)} %settle.1._, ...), custom_call_target="tpu_custom_call", output_to_operand_aliasing={{1}: (2, {})} | custom-call | tf_op jit(solution)/shard_map/finish/pallas_call | solution.py:486
Async XLA Ops:
  2.4 15.6 %collective-permute-start.2 = (bf16[1024,128]{1,0:T(8,128)(2,1)S(1)}, bf16[1024,128]{1,0:T(8,128)(2,1)S(1)}, u32[]{:S(2)}, u32[]{:S(2)}) collective-permute-start(bf16[1024,128]{1,0:T(8,128)(2,1)S(1)} %get-tuple-element.41), channel_id=1, source_target_pairs={{0,4},{4,12},{8,0},{12,8},{1,5},{5,13},{9,1},{13,9},{2,6},{6,14},{... | collective-permute-start | bytes 786440 | tf_op jit(solution)/shard_map/ppermute | solution.py:54
  5.5 18.6 %collective-permute-start.3 = (bf16[1024,128]{1,0:T(8,128)(2,1)S(1)}, bf16[1024,128]{1,0:T(8,128)(2,1)S(1)}, u32[]{:S(2)}, u32[]{:S(2)}) collective-permute-start(bf16[1024,128]{1,0:T(8,128)(2,1)S(1)} %get-tuple-element.42), channel_id=1, source_target_pairs={{4,0},{8,12},{5,1},{9,13},{6,2},{10,14},{7,3},{11,15},{20,16},{24,... | collective-permute-start | bytes 786440 | tf_op jit(solution)/shard_map/ppermute | solution.py:54
  6.7 32.6 %collective-permute-start.4 = (bf16[1024,128]{1,0:T(8,128)(2,1)S(1)}, bf16[1024,128]{1,0:T(8,128)(2,1)S(1)}, u32[]{:S(2)}, u32[]{:S(2)}) collective-permute-start(bf16[1024,128]{1,0:T(8,128)(2,1)S(1)} %get-tuple-element.45), channel_id=1, source_target_pairs={{0,12},{4,8},{8,4},{12,0},{1,13},{5,9},{9,5},{13,1},{2,14},{6,10},... | collective-permute-start | bytes 786440 | tf_op jit(solution)/shard_map/ppermute | solution.py:54
  14.5 18.1 %collective-permute-start = (bf16[2,136,256]{2,1,0:T(8,128)(2,1)S(1)}, bf16[2,136,256]{2,1,0:T(8,128)(2,1)S(1)}, u32[]{:S(2)}, u32[]{:S(2)}) collective-permute-start(bf16[2,136,256]{2,1,0:T(8,128)(2,1)S(1)} %get-tuple-element.35), channel_id=1, source_target_pairs={{0,4},{4,0},{8,12},{12,8},{1,5},{5,1},{9,13},{13,9},{2,6},{6,2},{1... | collective-permute-start | bytes 417800 | tf_op jit(solution)/shard_map/ppermute | solution.py:48
  25.0 14.3 %collective-permute-start.5 = (bf16[512,128]{1,0:T(8,128)(2,1)S(1)}, bf16[512,128]{1,0:T(8,128)(2,1)S(1)}, u32[]{:S(2)}, u32[]{:S(2)}) collective-permute-start(bf16[512,128]{1,0:T(8,128)(2,1)S(1)} %get-tuple-element.46), channel_id=1, source_target_pairs={{0,8},{12,4},{1,9},{13,5},{2,10},{14,6},{3,11},{15,7},{16,24},{28,... | collective-permute-start | bytes 393224 | tf_op jit(solution)/shard_map/ppermute | solution.py:54
  28.6 10.7 %collective-permute-start.6 = (bf16[512,128]{1,0:T(8,128)(2,1)S(1)}, bf16[512,128]{1,0:T(8,128)(2,1)S(1)}, u32[]{:S(2)}, u32[]{:S(2)}) collective-permute-start(bf16[512,128]{1,0:T(8,128)(2,1)S(1)} %get-tuple-element.47), channel_id=1, source_target_pairs={{0,8},{12,4},{1,9},{13,5},{2,10},{14,6},{3,11},{15,7},{16,24},{28,... | collective-permute-start | bytes 393224 | tf_op jit(solution)/shard_map/ppermute | solution.py:54
  32.7 6.6 %collective-permute-start.1 = (bf16[1,136,256]{2,1,0:T(8,128)(2,1)S(1)}, bf16[1,136,256]{2,1,0:T(8,128)(2,1)S(1)}, u32[]{:S(2)}, u32[]{:S(2)}) collective-permute-start(bf16[1,136,256]{2,1,0:T(8,128)(2,1)S(1)} %get-tuple-element.37), channel_id=1, source_target_pairs={{0,8},{4,12},{8,0},{12,4},{1,9},{5,13},{9,1},{13,5},{2,10},{6,14},... | collective-permute-start | bytes 208904 | tf_op jit(solution)/shard_map/ppermute | solution.py:48

commit v18 on v16

--- a/solution.py
+++ b/solution.py
@@ -54,9 +54,10 @@
 
 
 def messages(count, capacity):
-    half = capacity // 2
-    ahead = [(k, 0, capacity) for k in range(count // 2, count)]
-    behind = [(k, first, half) for k in reversed(range(1, count // 2)) for first in (0, half)]
+    far = count // 2
+    ahead = [(k, 0, capacity) for k in (far, 1)]
+    rest = [k for k in reversed(range(2, count)) if k != far]
+    behind = [(k, first, capacity // 2) for k in rest for first in (0, capacity // 2)]
     return ahead, behind, [(0, 0, capacity)]
 
 
@@ -435,7 +436,7 @@
     send, late_deltas = lax.optimization_barrier((send, late_deltas))
     passed = exchange(send, k)
     *sent, mine = place(behind + own, late_deltas)
-    got = got_ahead[1:] + [hand(message, k) for message, (k, _, _) in zip(sent, behind)]
+    got = [hand(message, k) for message, (k, _, _) in zip(sent, behind)]
     keep = pl.pallas_call(
         second_kernel,
         out_shape=staying(senders),
@@ -455,7 +456,7 @@
         )(keep, passed)
         k, count = 2 * k, count // 2
         passed = exchange(send, k)
-    settled = ahead[:1] + own
+    settled = ahead + own
     pages = pl.pallas_call(
         functools.partial(settle_kernel, settled),
         out_shape=whole,
@@ -464,9 +465,9 @@
         scratch_shapes=[pltpu.SemaphoreType.DMA((len(settled),))],
         compiler_params=small,
         name="settle",
-    )(got_ahead[0], mine)
+    )(*got_ahead, mine)
     attended, pages = pl.pallas_call(
-        functools.partial(finish_kernel, ahead[1:] + behind),
+        functools.partial(finish_kernel, behind),
         out_shape=[jax.ShapeDtypeStruct((width, HD), jnp.bfloat16), whole],
         in_specs=[VMEM] * 2 + [HBM] + [ANY] * len(got),
         out_specs=[HBM, HBM],

time: 33.6 us -> 34.6 us (1.030)
  starting transfers between devices: 10.9 us -> 15.1 us
  waiting for transfers between devices: 8.83 us -> 5.78 us
    ppermute x2, starting transfers between devices: 1.86 us -> 7.01 us  [exchange(): return lax.ppermute(message, 'seq', [(i, i ^ k) for i in range(count)])]
    ppermute x4, waiting for transfers between devices: 2.87 us -> 1.01 us  [hand(): lax.ppermute(message, 'seq', [(i, partner(i, k, count)) for i in range(co...]
    ppermute x2, waiting for transfers between devices: 5.96 us -> 4.77 us  [exchange(): return lax.ppermute(message, 'seq', [(i, i ^ k) for i in range(count)])]
    ppermute x4, starting transfers between devices: 9.09 us -> 8.04 us  [hand(): lax.ppermute(message, 'seq', [(i, partner(i, k, count)) for i in range(co...]
  transfers between devices with their start and end apart: 6 -> 6, of which waited for: 4 -> 2; matrix products, arithmetic and copies ran while one was open for 0% -> 0% of each run, Pallas kernels for 31% -> 31%
where the time goes in v18:
time: 34.6 us; the launch traced here: 34.4 us
  starting transfers between devices  15.1 us (44%)
  Pallas kernels  12.9 us (37%)
  waiting for transfers between devices  5.78 us (17%)
  between operations  0.69 us (2%)
    ppermute x4, starting transfers between devices, hand(): lax.ppermute(message, 'seq', [(i, partner(i, k, count)) for i in range(co...  8.04 us
    ppermute x2, starting transfers between devices, exchange(): return lax.ppermute(message, 'seq', [(i, i ^ k) for i in range(count)])  7.01 us
    pallas_call x1, Pallas kernels, per_device(): pl.pallas_call(first_kernel, out_shape=[leaving(senders), jax.ShapeDtypeS...  5.24 us
    ppermute x2, waiting for transfers between devices, exchange(): return lax.ppermute(message, 'seq', [(i, i ^ k) for i in range(count)])  4.77 us
    pallas_call x2, Pallas kernels, place(): pl.pallas_call(functools.partial(place_kernel, plan), out_shape=[jax.Shap...  3.22 us
    pallas_call x1, Pallas kernels, per_device(): pl.pallas_call(second_kernel, out_shape=staying(senders), in_specs=[VMEM]...  2.7 us
    ppermute x4, waiting for transfers between devices, hand(): lax.ppermute(message, 'seq', [(i, partner(i, k, count)) for i in range(co...  1.01 us
    pallas_call x1, Pallas kernels, per_device(): pl.pallas_call(functools.partial(settle_kernel, settled), out_shape=whole...  0.9 us
  transfers between devices with their start and end apart: 6, of which 2 were waited for; matrix products, arithmetic and copies ran while one was open for 0% of the time, Pallas kernels for 31%

profile of v18, /device:TPU:0, one launch (start us, length us, event | category | flops | bytes accessed | tf_op | source)
XLA Modules:
  0.0 34.4 jit_solution(9189784129587278755)
XLA Ops:
  0.6 1.6 %place.2 = (bf16[1024,128]{1,0:T(8,128)(2,1)S(1)}, bf16[1024,128]{1,0:T(8,128)(2,1)S(1)}) custom-call(s32[128]{0:T(128)} %owner_any.3, bf16[4096,128]{1,0:T(8,128)(2,1)} %bitcast.14, f32[256,128]{1,0:T(8,128)} %bitcast.18, f32[2,128]{1,0:T(2,128)} %scales_any.3), custom_call_target="tpu_custom_call" | custom-call | tf_op jit(solution)/shard_map/place/pallas_call | solution.py:381
  2.2 3.1 %collective-permute-start.2 = (bf16[1024,128]{1,0:T(8,128)(2,1)S(1)}, bf16[1024,128]{1,0:T(8,128)(2,1)S(1)}, u32[]{:S(2)}, u32[]{:S(2)}) collective-permute-start(bf16[1024,128]{1,0:T(8,128)(2,1)S(1)} %get-tuple-element.32), channel_id=1, source_target_pairs={{0,4},{4,12},{8,0},{12,8},{1,5},{5,13},{9,1},{13,9},{2,6},{6,14},{... | collective-permute-start | bytes 786440 | tf_op jit(solution)/shard_map/ppermute | solution.py:53
  5.3 1.1 %collective-permute-start.3 = (bf16[1024,128]{1,0:T(8,128)(2,1)S(1)}, bf16[1024,128]{1,0:T(8,128)(2,1)S(1)}, u32[]{:S(2)}, u32[]{:S(2)}) collective-permute-start(bf16[1024,128]{1,0:T(8,128)(2,1)S(1)} %get-tuple-element.33), channel_id=1, source_target_pairs={{0,8},{4,0},{8,12},{12,4},{1,9},{5,1},{9,13},{13,5},{2,10},{6,2},{... | collective-permute-start | bytes 786440 | tf_op jit(solution)/shard_map/ppermute | solution.py:53
  6.4 5.2 %attend_leaving.1 = (bf16[2,136,256]{2,1,0:T(8,128)(2,1)S(1)}, bf16[2048,256]{1,0:T(8,128)(2,1)S(1)}, bf16[128,2048]{1,0:T(8,128)(2,1)S(1)}, bf16[1024,256]{1,0:T(8,128)(2,1)S(1)}, f32[136,256]{1,0:T(8,128)S(1)}) custom-call(bf16[4096,128]{1,0:T(8,128)(2,1)} %bitcast.15, f32[256,128]{1,0:T(8,128)} %bitcast.19, f32[2,128]{1,0:T(2,128)} %scales_any.3, ...), custom_call_target="tpu_custom_call" | custom-call | tf_op jit(solution)/shard_map/attend_leaving/pallas_call | solution.py:411
  11.7 1.6 %collective-permute-start = (bf16[2,136,256]{2,1,0:T(8,128)(2,1)S(1)}, bf16[2,136,256]{2,1,0:T(8,128)(2,1)S(1)}, u32[]{:S(2)}, u32[]{:S(2)}) collective-permute-start(bf16[2,136,256]{2,1,0:T(8,128)(2,1)S(1)} %get-tuple-element.29), channel_id=1, source_target_pairs={{0,4},{4,0},{8,12},{12,8},{1,5},{5,1},{9,13},{13,9},{2,6},{6,2},{1... | collective-permute-start | bytes 417800 | tf_op jit(solution)/shard_map/ppermute | solution.py:48
  13.2 1.6 %place.3 = (bf16[512,128]{1,0:T(8,128)(2,1)S(1)}, bf16[512,128]{1,0:T(8,128)(2,1)S(1)}, bf16[1024,128]{1,0:T(8,128)(2,1)S(1)}) custom-call(s32[128]{0:T(128)} %owner_any.3, bf16[4096,128]{1,0:T(8,128)(2,1)} %bitcast.16, f32[256,128]{1,0:T(8,128)} %bitcast.20, f32[2,128]{1,0:T(2,128)} %scales_any.3), custom_call_target="tpu_custom_call" | custom-call | tf_op jit(solution)/shard_map/place/pallas_call | solution.py:381
  14.8 2.4 %collective-permute-start.4 = (bf16[512,128]{1,0:T(8,128)(2,1)S(1)}, bf16[512,128]{1,0:T(8,128)(2,1)S(1)}, u32[]{:S(2)}, u32[]{:S(2)}) collective-permute-start(bf16[512,128]{1,0:T(8,128)(2,1)S(1)} %get-tuple-element.36), channel_id=1, source_target_pairs={{0,12},{4,8},{8,4},{12,0},{1,13},{5,9},{9,5},{13,1},{2,14},{6,10},... | collective-permute-start | bytes 393224 | tf_op jit(solution)/shard_map/ppermute | solution.py:53
  17.3 1.4 %collective-permute-start.5 = (bf16[512,128]{1,0:T(8,128)(2,1)S(1)}, bf16[512,128]{1,0:T(8,128)(2,1)S(1)}, u32[]{:S(2)}, u32[]{:S(2)}) collective-permute-start(bf16[512,128]{1,0:T(8,128)(2,1)S(1)} %get-tuple-element.37), channel_id=1, source_target_pairs={{0,12},{4,8},{8,4},{12,0},{1,13},{5,9},{9,5},{13,1},{2,14},{6,10},... | collective-permute-start | bytes 393224 | tf_op jit(solution)/shard_map/ppermute | solution.py:53
  18.7 2.7 %attend_staying.1.keep_ref = f32[2,136,256]{2,1,0:T(8,128)S(1)} custom-call(bf16[2048,256]{1,0:T(8,128)(2,1)S(1)} %get-tuple-element.24.keys_ref, bf16[128,2048]{1,0:T(8,128)(2,1)S(1)} %get-tuple-element.25.turned_ref, bf16[1024,256]{1,0:T(8,128)(2,1)S(1)} %get-tuple-element.26.asked_ref, f32[136,256]{1,0:T(8,128)S(1)} %get-tuple-element.27.own_ref), custom_call_target="tpu_custom_call" | custom-call | tf_op jit(solution)/shard_map/attend_staying/pallas_call | solution.py:440
  21.4 0.0 collective-permute-done.got_ref
  21.5 0.1 join.1
  21.5 5.4 %collective-permute-start.1 = (bf16[1,136,256]{2,1,0:T(8,128)(2,1)S(1)}, bf16[1,136,256]{2,1,0:T(8,128)(2,1)S(1)}, u32[]{:S(2)}, u32[]{:S(2)}) collective-permute-start(bf16[1,136,256]{2,1,0:T(8,128)(2,1)S(1)} %get-tuple-element.31), channel_id=1, source_target_pairs={{0,8},{4,12},{8,0},{12,4},{1,9},{5,13},{9,1},{13,5},{2,10},{6,14},... | collective-permute-start | bytes 208904 | tf_op jit(solution)/shard_map/ppermute | solution.py:48
  27.0 0.0 collective-permute-done.2.refs_0_
  27.0 0.0 collective-permute-done.3.refs_1_
  27.0 0.9 %settle.1._ = bf16[4096,128]{1,0:T(8,128)(2,1)} custom-call(bf16[1024,128]{1,0:T(8,128)(2,1)S(1)} %collective-permute-done.2.refs_0_, bf16[1024,128]{1,0:T(8,128)(2,1)S(1)} %collective-permute-done.3.refs_1_, bf16[1024,128]{1,0:T(8,128)(2,1)S(1)} %get-tuple-element.35.refs_2_), custom_call_target="tpu_custom_call" | custom-call | tf_op jit(solution)/shard_map/settle/pallas_call | solution.py:460
  27.9 0.0 collective-permute-done.4.refs_0_
  27.9 1.0 %collective-permute-done.5.refs_1_ = bf16[512,128]{1,0:T(8,128)(2,1)S(1)} collective-permute-done((bf16[512,128]{1,0:T(8,128)(2,1)S(1)}, bf16[512,128]{1,0:T(8,128)(2,1)S(1)}, u32[]{:S(2)}, u32[]{:S(2)}) %collective-permute-start.5) | collective-permute-done | bytes 131104 | tf_op jit(solution)/shard_map/ppermute | solution.py:53
  28.9 4.8 %collective-permute-done.1.got_ref = bf16[1,136,256]{2,1,0:T(8,128)(2,1)S(1)} collective-permute-done((bf16[1,136,256]{2,1,0:T(8,128)(2,1)S(1)}, bf16[1,136,256]{2,1,0:T(8,128)(2,1)S(1)}, u32[]{:S(2)}, u32[]{:S(2)}) %collective-permute-start.1) | collective-permute-done | bytes 69664 | tf_op jit(solution)/shard_map/ppermute | solution.py:48
  33.7 0.8 %finish.1 = (bf16[256,128]{1,0:T(8,128)(2,1)}, bf16[4096,128]{1,0:T(8,128)(2,1)}) custom-call(f32[1,136,256]{2,1,0:T(8,128)S(1)} %get-tuple-element.30.keep_ref, bf16[1,136,256]{2,1,0:T(8,128)(2,1)S(1)} %collective-permute-done.1.got_ref, bf16[4096,128]{1,0:T(8,128)(2,1)} %settle.1._, ...), custom_call_target="tpu_custom_call", output_to_operand_aliasing={{1}: (2, {})} | custom-call | tf_op jit(solution)/shard_map/finish/pallas_call | solution.py:469
Async XLA Ops:
  2.2 24.7 %collective-permute-start.2 = (bf16[1024,128]{1,0:T(8,128)(2,1)S(1)}, bf16[1024,128]{1,0:T(8,128)(2,1)S(1)}, u32[]{:S(2)}, u32[]{:S(2)}) collective-permute-start(bf16[1024,128]{1,0:T(8,128)(2,1)S(1)} %get-tuple-element.32), channel_id=1, source_target_pairs={{0,4},{4,12},{8,0},{12,8},{1,5},{5,13},{9,1},{13,9},{2,6},{6,14},{... | collective-permute-start | bytes 786440 | tf_op jit(solution)/shard_map/ppermute | solution.py:53
  5.3 21.6 %collective-permute-start.3 = (bf16[1024,128]{1,0:T(8,128)(2,1)S(1)}, bf16[1024,128]{1,0:T(8,128)(2,1)S(1)}, u32[]{:S(2)}, u32[]{:S(2)}) collective-permute-start(bf16[1024,128]{1,0:T(8,128)(2,1)S(1)} %get-tuple-element.33), channel_id=1, source_target_pairs={{0,8},{4,0},{8,12},{12,4},{1,9},{5,1},{9,13},{13,5},{2,10},{6,2},{... | collective-permute-start | bytes 786440 | tf_op jit(solution)/shard_map/ppermute | solution.py:53
  11.7 9.8 %collective-permute-start = (bf16[2,136,256]{2,1,0:T(8,128)(2,1)S(1)}, bf16[2,136,256]{2,1,0:T(8,128)(2,1)S(1)}, u32[]{:S(2)}, u32[]{:S(2)}) collective-permute-start(bf16[2,136,256]{2,1,0:T(8,128)(2,1)S(1)} %get-tuple-element.29), channel_id=1, source_target_pairs={{0,4},{4,0},{8,12},{12,8},{1,5},{5,1},{9,13},{13,9},{2,6},{6,2},{1... | collective-permute-start | bytes 417800 | tf_op jit(solution)/shard_map/ppermute | solution.py:48
  14.8 13.0 %collective-permute-start.4 = (bf16[512,128]{1,0:T(8,128)(2,1)S(1)}, bf16[512,128]{1,0:T(8,128)(2,1)S(1)}, u32[]{:S(2)}, u32[]{:S(2)}) collective-permute-start(bf16[512,128]{1,0:T(8,128)(2,1)S(1)} %get-tuple-element.36), channel_id=1, source_target_pairs={{0,12},{4,8},{8,4},{12,0},{1,13},{5,9},{9,5},{13,1},{2,14},{6,10},... | collective-permute-start | bytes 393224 | tf_op jit(solution)/shard_map/ppermute | solution.py:53
  17.3 11.6 %collective-permute-start.5 = (bf16[512,128]{1,0:T(8,128)(2,1)S(1)}, bf16[512,128]{1,0:T(8,128)(2,1)S(1)}, u32[]{:S(2)}, u32[]{:S(2)}) collective-permute-start(bf16[512,128]{1,0:T(8,128)(2,1)S(1)} %get-tuple-element.37), channel_id=1, source_target_pairs={{0,12},{4,8},{8,4},{12,0},{1,13},{5,9},{9,5},{13,1},{2,14},{6,10},... | collective-permute-start | bytes 393224 | tf_op jit(solution)/shard_map/ppermute | solution.py:53
  21.5 12.1 %collective-permute-start.1 = (bf16[1,136,256]{2,1,0:T(8,128)(2,1)S(1)}, bf16[1,136,256]{2,1,0:T(8,128)(2,1)S(1)}, u32[]{:S(2)}, u32[]{:S(2)}) collective-permute-start(bf16[1,136,256]{2,1,0:T(8,128)(2,1)S(1)} %get-tuple-element.31), channel_id=1, source_target_pairs={{0,8},{4,12},{8,0},{12,4},{1,9},{5,13},{9,1},{13,5},{2,10},{6,14},... | collective-permute-start | bytes 208904 | tf_op jit(solution)/shard_map/ppermute | solution.py:48

commit v19 on v16

--- a/solution.py
+++ b/solution.py
@@ -207,8 +207,8 @@
 
 def first_kernel(*refs):
     me = lax.axis_index("seq")
-    sources, send_ref, keys_ref, turned_ref, asked_ref, own_ref, *targets = refs[:7], *refs[7:-3]
-    wide_ref, values_ref, sems = refs[-3:]
+    *targets, wide_ref, values_ref, sems = refs[-10:]
+    sources, *send, keys_ref, turned_ref, asked_ref, own_ref = refs[:7], *refs[7:-10]
     loads = [
         pltpu.make_async_copy(source, target, sems.at[index])
         for index, (source, target) in enumerate(zip(sources, targets))
@@ -222,7 +222,7 @@
     requests = lengths_ref.shape[0]
     asked = queries_ref.shape[0]
     per_row = asked // request_ref.shape[0]
-    width = send_ref.shape[2]
+    width = own_ref.shape[1]
     for load in loads[2:]:
         load.wait()
 
@@ -300,7 +300,15 @@
     turned_ref[...] = values_ref[...].T
 
     def store(index, partial):
-        send_ref[index] = packed(partial)
+        many = send[0].shape[0]
+        if isinstance(index, int):
+            send[index // many][index % many] = packed(partial)
+            return
+        for piece, send_ref in enumerate(send):
+
+            @pl.when(index // many == piece)
+            def _(piece=piece, send_ref=send_ref):
+                send_ref[index - piece * many] = packed(partial)
 
     attend(1, width, keys_ref, turned_ref, asked_ref, store)
 
@@ -313,11 +321,14 @@
     keep_ref[0] = held(joined(taken(keep_ref[0]), taken(own_ref[...])))
 
 
-def join_kernel(keep_ref, got_ref, send_ref, next_ref):
+def join_kernel(came, keep_ref, *refs):
+    got, send, next_ref = refs[:came], refs[came:-1], refs[-1]
     for index in range(keep_ref.shape[0]):
-        partial = joined(taken(keep_ref[index]), unpacked(got_ref[index]))
+        many = got[0].shape[0]
+        partial = joined(taken(keep_ref[index]), unpacked(got[index // many][index % many]))
         if index % 2 == 1:
-            send_ref[index // 2] = packed(partial)
+            many = send[0].shape[0]
+            send[index // 2 // many][index // 2 % many] = packed(partial)
         else:
             next_ref[index // 2] = held(partial)
 
@@ -400,24 +411,25 @@
     got_ahead = [hand(message, k) for message, (k, _, _) in zip(sent, ahead)]
 
     def leaving(count):
-        return jax.ShapeDtypeStruct((count // 2, HD + STAT_ROWS, width), jnp.bfloat16)
+        many = max(1, count // 4)
+        return [jax.ShapeDtypeStruct((many, HD + STAT_ROWS, width), jnp.bfloat16)] * (count // 2 // many)
 
     def staying(count):
         return jax.ShapeDtypeStruct((count // 2, HD + KEEP_ROWS, width), jnp.float32)
 
     needed = (late_deltas, flat_anchors, scales, lengths, row_request, flat_queries, flat_new)
     roomy = pltpu.CompilerParams(vmem_limit_bytes=32 * 1024 * 1024)
-    send, *common = pl.pallas_call(
+    outs = pl.pallas_call(
         first_kernel,
         out_shape=[
-            leaving(senders),
+            *leaving(senders),
             jax.ShapeDtypeStruct((tokens, 2 * HD), jnp.bfloat16),
             jax.ShapeDtypeStruct((HD, tokens), jnp.bfloat16),
             jax.ShapeDtypeStruct((rows * GQ * steps, 2 * HD), jnp.bfloat16),
             jax.ShapeDtypeStruct((HD + KEEP_ROWS, width), jnp.float32),
         ],
         in_specs=[HBM] * len(needed),
-        out_specs=[VMEM] * 5,
+        out_specs=[VMEM] * (len(leaving(senders)) + 4),
         scratch_shapes=[
             (pltpu.SMEM if array.dtype == jnp.int32 else pltpu.VMEM)(array.shape, array.dtype)
             for array in needed
@@ -430,12 +442,12 @@
         compiler_params=roomy,
         name="attend_leaving",
     )(*in_hbm(needed))
+    send, common = outs[:-4], outs[-4:]
 
     k, count = 1, senders // 2
     send, late_deltas = lax.optimization_barrier((send, late_deltas))
-    passed = exchange(send, k)
+    passed = [exchange(message, k) for message in send]
     *sent, mine = place(behind + own, late_deltas)
-    got = got_ahead[1:] + [hand(message, k) for message, (k, _, _) in zip(sent, behind)]
     keep = pl.pallas_call(
         second_kernel,
         out_shape=staying(senders),
@@ -445,17 +457,20 @@
         name="attend_staying",
     )(*common)
     while count > 1:
-        send, keep = pl.pallas_call(
-            join_kernel,
-            out_shape=[leaving(count), staying(count)],
-            in_specs=[VMEM] * 2,
-            out_specs=[VMEM] * 2,
+        *send, keep = pl.pallas_call(
+            functools.partial(join_kernel, len(passed)),
+            out_shape=leaving(count) + [staying(count)],
+            in_specs=[VMEM] * (len(passed) + 1),
+            out_specs=[VMEM] * (len(leaving(count)) + 1),
             compiler_params=small,
             name="join",
-        )(keep, passed)
+        )(keep, *passed)
+        if k == 1:
+            sent, send = lax.optimization_barrier((sent, send))
+            got = [hand(message, k) for message, (k, _, _) in zip(sent, behind)]
         k, count = 2 * k, count // 2
-        passed = exchange(send, k)
-    settled = ahead[:1] + own
+        passed = [exchange(message, k) for message in send]
+    settled = ahead + own
     pages = pl.pallas_call(
         functools.partial(settle_kernel, settled),
         out_shape=whole,
@@ -464,9 +479,9 @@
         scratch_shapes=[pltpu.SemaphoreType.DMA((len(settled),))],
         compiler_params=small,
         name="settle",
-    )(got_ahead[0], mine)
+    )(*got_ahead, mine)
     attended, pages = pl.pallas_call(
-        functools.partial(finish_kernel, ahead[1:] + behind),
+        functools.partial(finish_kernel, behind),
         out_shape=[jax.ShapeDtypeStruct((width, HD), jnp.bfloat16), whole],
         in_specs=[VMEM] * 2 + [HBM] + [ANY] * len(got),
         out_specs=[HBM, HBM],
@@ -477,7 +492,7 @@
         input_output_aliases={2: 1},
         compiler_params=small,
         name="finish",
-    )(keep, passed, pages, *got)
+    )(keep, *passed, pages, *got)
     pages = pages.reshape(blocks, tokens // blocks, 2, HD)
     attended = (
         attended.reshape(rows_dev, GQ, steps, HD).transpose(0, 2, 1, 3).reshape(rows_dev, steps, GQ * HD)

time: 33.6 us -> 35.5 us (1.057)
  waiting for transfers between devices: 8.83 us -> 10.9 us
    ppermute x2 -> x3, waiting for transfers between devices: 5.96 us -> 10.8 us  [exchange(): return lax.ppermute(message, 'seq', [(i, i ^ k) for i in range(count)])]
    ppermute x4, waiting for transfers between devices: 2.87 us -> 0.01 us  [hand(): lax.ppermute(message, 'seq', [(i, partner(i, k, count)) for i in range(co...]
    ppermute x4, starting transfers between devices: 9.09 us -> 8.65 us  [hand(): lax.ppermute(message, 'seq', [(i, partner(i, k, count)) for i in range(co...]
    ppermute x2 -> x3, starting transfers between devices: 1.86 us -> 2.16 us  [exchange(): return lax.ppermute(message, 'seq', [(i, i ^ k) for i in range(count)])]
  transfers between devices with their start and end apart: 6 -> 7, of which waited for: 4 -> 3; matrix products, arithmetic and copies ran while one was open for 0% -> 0% of each run, Pallas kernels for 31% -> 30%
where the time goes in v19:
time: 35.5 us; the launch traced here: 35.3 us
  Pallas kernels  12.9 us (36%)
  waiting for transfers between devices  10.9 us (31%)
  starting transfers between devices  10.8 us (30%)
  between operations  0.68 us (2%)
    ppermute x3, waiting for transfers between devices, exchange(): return lax.ppermute(message, 'seq', [(i, i ^ k) for i in range(count)])  10.8 us
    ppermute x4, starting transfers between devices, hand(): lax.ppermute(message, 'seq', [(i, partner(i, k, count)) for i in range(co...  8.65 us
    pallas_call x1, Pallas kernels, per_device(): pl.pallas_call(first_kernel, out_shape=[*leaving(senders), jax.ShapeDtype...  5.24 us
    pallas_call x2, Pallas kernels, place(): pl.pallas_call(functools.partial(place_kernel, plan), out_shape=[jax.Shap...  3.22 us
    pallas_call x1, Pallas kernels, per_device(): pl.pallas_call(second_kernel, out_shape=staying(senders), in_specs=[VMEM]...  2.71 us
    ppermute x3, starting transfers between devices, exchange(): return lax.ppermute(message, 'seq', [(i, i ^ k) for i in range(count)])  2.16 us
    pallas_call x1, Pallas kernels, per_device(): pl.pallas_call(functools.partial(settle_kernel, settled), out_shape=whole...  0.9 us
    pallas_call x1, Pallas kernels, per_device(): pl.pallas_call(functools.partial(finish_kernel, behind), out_shape=[jax.S...  0.79 us
  transfers between devices with their start and end apart: 7, of which 3 were waited for; matrix products, arithmetic and copies ran while one was open for 0% of the time, Pallas kernels for 30%

profile of v19, /device:TPU:0, one launch (start us, length us, event | category | flops | bytes accessed | tf_op | source)
XLA Modules:
  0.0 35.3 jit_solution(13696442432597394794)
XLA Ops:
  0.6 1.6 %place.2 = (bf16[1024,128]{1,0:T(8,128)(2,1)S(1)}, bf16[1024,128]{1,0:T(8,128)(2,1)S(1)}) custom-call(s32[128]{0:T(128)} %owner_any.3, bf16[4096,128]{1,0:T(8,128)(2,1)} %bitcast.14, f32[256,128]{1,0:T(8,128)} %bitcast.18, f32[2,128]{1,0:T(2,128)} %scales_any.3), custom_call_target="tpu_custom_call" | custom-call | tf_op jit(solution)/shard_map/place/pallas_call | solution.py:391
  2.2 3.1 %collective-permute-start.3 = (bf16[1024,128]{1,0:T(8,128)(2,1)S(1)}, bf16[1024,128]{1,0:T(8,128)(2,1)S(1)}, u32[]{:S(2)}, u32[]{:S(2)}) collective-permute-start(bf16[1024,128]{1,0:T(8,128)(2,1)S(1)} %get-tuple-element.43), channel_id=1, source_target_pairs={{0,4},{4,12},{8,0},{12,8},{1,5},{5,13},{9,1},{13,9},{2,6},{6,14},{... | collective-permute-start | bytes 786440 | tf_op jit(solution)/shard_map/ppermute | solution.py:53
  5.3 2.5 %collective-permute-start.4 = (bf16[1024,128]{1,0:T(8,128)(2,1)S(1)}, bf16[1024,128]{1,0:T(8,128)(2,1)S(1)}, u32[]{:S(2)}, u32[]{:S(2)}) collective-permute-start(bf16[1024,128]{1,0:T(8,128)(2,1)S(1)} %get-tuple-element.44), channel_id=1, source_target_pairs={{0,12},{4,8},{8,4},{12,0},{1,13},{5,9},{9,5},{13,1},{2,14},{6,10},... | collective-permute-start | bytes 786440 | tf_op jit(solution)/shard_map/ppermute | solution.py:53
  7.8 5.2 %attend_leaving.1 = (bf16[1,136,256]{2,1,0:T(8,128)(2,1)S(1)}, bf16[1,136,256]{2,1,0:T(8,128)(2,1)S(1)}, bf16[2048,256]{1,0:T(8,128)(2,1)S(1)}, bf16[128,2048]{1...) custom-call(bf16[4096,128]{1,0:T(8,128)(2,1)} %bitcast.15, f32[256,128]{1,0:T(8,128)} %bitcast.19, ...), custom_call_target="tpu_custom_call" | custom-call | tf_op jit(solution)/shard_map/attend_leaving/pallas_call | solution.py:422
  13.1 0.2 collective-permute-start
  13.2 1.9 %collective-permute-start.1 = (bf16[1,136,256]{2,1,0:T(8,128)(2,1)S(1)}, bf16[1,136,256]{2,1,0:T(8,128)(2,1)S(1)}, u32[]{:S(2)}, u32[]{:S(2)}) collective-permute-start(bf16[1,136,256]{2,1,0:T(8,128)(2,1)S(1)} %get-tuple-element.36), channel_id=1, source_target_pairs={{0,4},{4,0},{8,12},{12,8},{1,5},{5,1},{9,13},{13,9},{2,6},{6,2},{1... | collective-permute-start | bytes 208904 | tf_op jit(solution)/shard_map/ppermute | solution.py:48
  15.1 1.6 %place.3 = (bf16[512,128]{1,0:T(8,128)(2,1)S(1)}, bf16[512,128]{1,0:T(8,128)(2,1)S(1)}, bf16[1024,128]{1,0:T(8,128)(2,1)S(1)}) custom-call(s32[128]{0:T(128)} %owner_any.3, bf16[4096,128]{1,0:T(8,128)(2,1)} %bitcast.16, f32[256,128]{1,0:T(8,128)} %bitcast.20, f32[2,128]{1,0:T(2,128)} %scales_any.3), custom_call_target="tpu_custom_call" | custom-call | tf_op jit(solution)/shard_map/place/pallas_call | solution.py:391
  16.8 2.7 %attend_staying.1.keep_ref = f32[2,136,256]{2,1,0:T(8,128)S(1)} custom-call(bf16[2048,256]{1,0:T(8,128)(2,1)S(1)} %get-tuple-element.29.keys_ref, bf16[128,2048]{1,0:T(8,128)(2,1)S(1)} %get-tuple-element.30.turned_ref, bf16[1024,256]{1,0:T(8,128)(2,1)S(1)} %get-tuple-element.31.asked_ref, f32[136,256]{1,0:T(8,128)S(1)} %get-tuple-element.32.own_ref), custom_call_target="tpu_custom_call" | custom-call | tf_op jit(solution)/shard_map/attend_staying/pallas_call | solution.py:451
  19.5 1.7 %collective-permute-done.refs_0_ = bf16[1,136,256]{2,1,0:T(8,128)(2,1)S(1)} collective-permute-done((bf16[1,136,256]{2,1,0:T(8,128)(2,1)S(1)}, bf16[1,136,256]{2,1,0:T(8,128)(2,1)S(1)}, u32[]{:S(2)}, u32[]{:S(2)}) %collective-permute-start) | collective-permute-done | bytes 69664 | tf_op jit(solution)/shard_map/ppermute | solution.py:48
  21.1 1.3 %collective-permute-done.1.refs_1_ = bf16[1,136,256]{2,1,0:T(8,128)(2,1)S(1)} collective-permute-done((bf16[1,136,256]{2,1,0:T(8,128)(2,1)S(1)}, bf16[1,136,256]{2,1,0:T(8,128)(2,1)S(1)}, u32[]{:S(2)}, u32[]{:S(2)}) %collective-permute-start.1) | collective-permute-done | bytes 69664 | tf_op jit(solution)/shard_map/ppermute | solution.py:48
  22.4 0.1 join.1
  22.5 0.7 %collective-permute-start.5 = (bf16[512,128]{1,0:T(8,128)(2,1)S(1)}, bf16[512,128]{1,0:T(8,128)(2,1)S(1)}, u32[]{:S(2)}, u32[]{:S(2)}) collective-permute-start(bf16[512,128]{1,0:T(8,128)(2,1)S(1)} %get-tuple-element.46), channel_id=1, source_target_pairs={{0,8},{4,0},{8,12},{12,4},{1,9},{5,1},{9,13},{13,5},{2,10},{6,2},{... | collective-permute-start | bytes 393224 | tf_op jit(solution)/shard_map/ppermute | solution.py:53
  23.2 2.4 %collective-permute-start.6 = (bf16[512,128]{1,0:T(8,128)(2,1)S(1)}, bf16[512,128]{1,0:T(8,128)(2,1)S(1)}, u32[]{:S(2)}, u32[]{:S(2)}) collective-permute-start(bf16[512,128]{1,0:T(8,128)(2,1)S(1)} %get-tuple-element.47), channel_id=1, source_target_pairs={{0,8},{4,0},{8,12},{12,4},{1,9},{5,1},{9,13},{13,5},{2,10},{6,2},{... | collective-permute-start | bytes 393224 | tf_op jit(solution)/shard_map/ppermute | solution.py:53
  25.6 0.1 collective-permute-start.2
  25.7 0.0 collective-permute-done.3.refs_0_
  25.7 0.0 collective-permute-done.4.refs_1_
  25.7 0.9 %settle.1._ = bf16[4096,128]{1,0:T(8,128)(2,1)} custom-call(bf16[1024,128]{1,0:T(8,128)(2,1)S(1)} %collective-permute-done.3.refs_0_, bf16[1024,128]{1,0:T(8,128)(2,1)S(1)} %collective-permute-done.4.refs_1_, bf16[1024,128]{1,0:T(8,128)(2,1)S(1)} %get-tuple-element.45.refs_2_), custom_call_target="tpu_custom_call" | custom-call | tf_op jit(solution)/shard_map/settle/pallas_call | solution.py:474
  26.6 7.9 %collective-permute-done.2.got_ref = bf16[1,136,256]{2,1,0:T(8,128)(2,1)S(1)} collective-permute-done((bf16[1,136,256]{2,1,0:T(8,128)(2,1)S(1)}, bf16[1,136,256]{2,1,0:T(8,128)(2,1)S(1)}, u32[]{:S(2)}, u32[]{:S(2)}) %collective-permute-start.2) | collective-permute-done | bytes 69664 | tf_op jit(solution)/shard_map/ppermute | solution.py:48
  34.5 0.0 collective-permute-done.5.refs_0_
  34.5 0.0 collective-permute-done.6.refs_1_
  34.5 0.8 %finish.1 = (bf16[256,128]{1,0:T(8,128)(2,1)}, bf16[4096,128]{1,0:T(8,128)(2,1)}) custom-call(f32[1,136,256]{2,1,0:T(8,128)S(1)} %get-tuple-element.37.keep_ref, bf16[1,136,256]{2,1,0:T(8,128)(2,1)S(1)} %collective-permute-done.2.got_ref, bf16[4096,128]{1,0:T(8,128)(2,1)} %settle.1._, ...), custom_call_target="tpu_custom_call", output_to_operand_aliasing={{1}: (2, {})} | custom-call | tf_op jit(solution)/shard_map/finish/pallas_call | solution.py:483
Async XLA Ops:
  2.2 23.4 %collective-permute-start.3 = (bf16[1024,128]{1,0:T(8,128)(2,1)S(1)}, bf16[1024,128]{1,0:T(8,128)(2,1)S(1)}, u32[]{:S(2)}, u32[]{:S(2)}) collective-permute-start(bf16[1024,128]{1,0:T(8,128)(2,1)S(1)} %get-tuple-element.43), channel_id=1, source_target_pairs={{0,4},{4,12},{8,0},{12,8},{1,5},{5,13},{9,1},{13,9},{2,6},{6,14},{... | collective-permute-start | bytes 786440 | tf_op jit(solution)/shard_map/ppermute | solution.py:53
  5.3 20.4 %collective-permute-start.4 = (bf16[1024,128]{1,0:T(8,128)(2,1)S(1)}, bf16[1024,128]{1,0:T(8,128)(2,1)S(1)}, u32[]{:S(2)}, u32[]{:S(2)}) collective-permute-start(bf16[1024,128]{1,0:T(8,128)(2,1)S(1)} %get-tuple-element.44), channel_id=1, source_target_pairs={{0,12},{4,8},{8,4},{12,0},{1,13},{5,9},{9,5},{13,1},{2,14},{6,10},... | collective-permute-start | bytes 786440 | tf_op jit(solution)/shard_map/ppermute | solution.py:53
  13.1 8.1 %collective-permute-start = (bf16[1,136,256]{2,1,0:T(8,128)(2,1)S(1)}, bf16[1,136,256]{2,1,0:T(8,128)(2,1)S(1)}, u32[]{:S(2)}, u32[]{:S(2)}) collective-permute-start(bf16[1,136,256]{2,1,0:T(8,128)(2,1)S(1)} %get-tuple-element.35), channel_id=1, source_target_pairs={{0,4},{4,0},{8,12},{12,8},{1,5},{5,1},{9,13},{13,9},{2,6},{6,2},{1... | collective-permute-start | bytes 208904 | tf_op jit(solution)/shard_map/ppermute | solution.py:48
  13.2 9.2 %collective-permute-start.1 = (bf16[1,136,256]{2,1,0:T(8,128)(2,1)S(1)}, bf16[1,136,256]{2,1,0:T(8,128)(2,1)S(1)}, u32[]{:S(2)}, u32[]{:S(2)}) collective-permute-start(bf16[1,136,256]{2,1,0:T(8,128)(2,1)S(1)} %get-tuple-element.36), channel_id=1, source_target_pairs={{0,4},{4,0},{8,12},{12,8},{1,5},{5,1},{9,13},{13,9},{2,6},{6,2},{1... | collective-permute-start | bytes 208904 | tf_op jit(solution)/shard_map/ppermute | solution.py:48
  22.5 12.0 %collective-permute-start.5 = (bf16[512,128]{1,0:T(8,128)(2,1)S(1)}, bf16[512,128]{1,0:T(8,128)(2,1)S(1)}, u32[]{:S(2)}, u32[]{:S(2)}) collective-permute-start(bf16[512,128]{1,0:T(8,128)(2,1)S(1)} %get-tuple-element.46), channel_id=1, source_target_pairs={{0,8},{4,0},{8,12},{12,4},{1,9},{5,1},{9,13},{13,5},{2,10},{6,2},{... | collective-permute-start | bytes 393224 | tf_op jit(solution)/shard_map/ppermute | solution.py:53
  23.2 11.3 %collective-permute-start.6 = (bf16[512,128]{1,0:T(8,128)(2,1)S(1)}, bf16[512,128]{1,0:T(8,128)(2,1)S(1)}, u32[]{:S(2)}, u32[]{:S(2)}) collective-permute-start(bf16[512,128]{1,0:T(8,128)(2,1)S(1)} %get-tuple-element.47), channel_id=1, source_target_pairs={{0,8},{4,0},{8,12},{12,4},{1,9},{5,1},{9,13},{13,5},{2,10},{6,2},{... | collective-permute-start | bytes 393224 | tf_op jit(solution)/shard_map/ppermute | solution.py:53
  25.6 8.9 %collective-permute-start.2 = (bf16[1,136,256]{2,1,0:T(8,128)(2,1)S(1)}, bf16[1,136,256]{2,1,0:T(8,128)(2,1)S(1)}, u32[]{:S(2)}, u32[]{:S(2)}) collective-permute-start(bf16[1,136,256]{2,1,0:T(8,128)(2,1)S(1)} %get-tuple-element.42), channel_id=1, source_target_pairs={{0,8},{4,12},{8,0},{12,4},{1,9},{5,13},{9,1},{13,5},{2,10},{6,14},... | collective-permute-start | bytes 208904 | tf_op jit(solution)/shard_map/ppermute | solution.py:48

commit v20 on v16

--- a/solution.py
+++ b/solution.py
@@ -68,15 +68,13 @@
     blocks = owner_ref.shape[0]
     rows = deltas_ref.shape[0] // blocks
     capacity = blocks // receivers
+    quarter = deltas_ref.shape[0] // 4
+    parts = [pl.ds(index * quarter, quarter) for index in range(4)]
     loads = [
         pltpu.make_async_copy(source, target, sems.at[index])
         for index, (source, target) in enumerate(
-            [
-                (owner_any, owner_ref),
-                (scales_any, scales_ref),
-                (anchors_any, anchors_ref),
-                (deltas_any, deltas_ref),
-            ]
+            [(owner_any, owner_ref), (scales_any, scales_ref), (anchors_any, anchors_ref)]
+            + [(deltas_any.at[part], deltas_ref.at[part]) for part in parts]
         )
     ]
     for load in loads:
@@ -121,7 +119,7 @@
             )
             return carry
 
-        lax.fori_loop(0, count, one_slot, 0, unroll=min(8, count))
+        lax.fori_loop(0, count, one_slot, 0, unroll=min(16, count))
 
 
 def pieces(values):
@@ -389,7 +387,7 @@
                 pltpu.VMEM((tokens * 2, HD), jnp.bfloat16),
                 pltpu.VMEM((blocks * 2, HD), jnp.float32),
                 pltpu.VMEM((2, HD), jnp.float32),
-                pltpu.SemaphoreType.DMA((4,)),
+                pltpu.SemaphoreType.DMA((7,)),
             ],
             compiler_params=small,
             name="place",

time: 33.6 us -> 33.5 us (level)
  no operation moved by 1% of the time
where the time goes in v20:
time: 33.5 us; the launch traced here: 33.3 us
  Pallas kernels  12.8 us (38%)
  starting transfers between devices  10.9 us (33%)
  waiting for transfers between devices  8.92 us (27%)
  between operations  0.68 us (2%)
    ppermute x4, starting transfers between devices, hand(): lax.ppermute(message, 'seq', [(i, partner(i, k, count)) for i in range(co...  9.09 us
    ppermute x2, waiting for transfers between devices, exchange(): return lax.ppermute(message, 'seq', [(i, i ^ k) for i in range(count)])  6.04 us
    pallas_call x1, Pallas kernels, per_device(): pl.pallas_call(first_kernel, out_shape=[leaving(senders), jax.ShapeDtypeS...  5.24 us
    pallas_call x2, Pallas kernels, place(): pl.pallas_call(functools.partial(place_kernel, plan), out_shape=[jax.Shap...  3.09 us
    ppermute x4, waiting for transfers between devices, hand(): lax.ppermute(message, 'seq', [(i, partner(i, k, count)) for i in range(co...  2.87 us
    pallas_call x1, Pallas kernels, per_device(): pl.pallas_call(second_kernel, out_shape=staying(senders), in_specs=[VMEM]...  2.7 us
    ppermute x2, starting transfers between devices, exchange(): return lax.ppermute(message, 'seq', [(i, i ^ k) for i in range(count)])  1.85 us
    pallas_call x1, Pallas kernels, per_device(): pl.pallas_call(functools.partial(finish_kernel, ahead[1:] + behind), out_...  0.88 us
  transfers between devices with their start and end apart: 6, of which 4 were waited for; matrix products, arithmetic and copies ran while one was open for 0% of the time, Pallas kernels for 31%

profile of v20, /device:TPU:0, one launch (start us, length us, event | category | flops | bytes accessed | tf_op | source)
XLA Modules:
  0.0 33.3 jit_solution(11351499163842006830)
XLA Ops:
  0.6 1.6 %place.2 = (bf16[1024,128]{1,0:T(8,128)(2,1)S(1)}, bf16[1024,128]{1,0:T(8,128)(2,1)S(1)}) custom-call(s32[128]{0:T(128)} %owner_any.3, bf16[4096,128]{1,0:T(8,128)(2,1)} %bitcast.14, f32[256,128]{1,0:T(8,128)} %bitcast.18, f32[2,128]{1,0:T(2,128)} %scales_any.3), custom_call_target="tpu_custom_call" | custom-call | tf_op jit(solution)/shard_map/place/pallas_call | solution.py:378
  2.2 3.1 %collective-permute-start.2 = (bf16[1024,128]{1,0:T(8,128)(2,1)S(1)}, bf16[1024,128]{1,0:T(8,128)(2,1)S(1)}, u32[]{:S(2)}, u32[]{:S(2)}) collective-permute-start(bf16[1024,128]{1,0:T(8,128)(2,1)S(1)} %get-tuple-element.32), channel_id=1, source_target_pairs={{0,4},{4,12},{8,0},{12,8},{1,5},{5,13},{9,1},{13,9},{2,6},{6,14},{... | collective-permute-start | bytes 786440 | tf_op jit(solution)/shard_map/ppermute | solution.py:53
  5.3 2.5 %collective-permute-start.3 = (bf16[1024,128]{1,0:T(8,128)(2,1)S(1)}, bf16[1024,128]{1,0:T(8,128)(2,1)S(1)}, u32[]{:S(2)}, u32[]{:S(2)}) collective-permute-start(bf16[1024,128]{1,0:T(8,128)(2,1)S(1)} %get-tuple-element.35), channel_id=1, source_target_pairs={{0,12},{4,8},{8,4},{12,0},{1,13},{5,9},{9,5},{13,1},{2,14},{6,10},... | collective-permute-start | bytes 786440 | tf_op jit(solution)/shard_map/ppermute | solution.py:53
  7.8 5.2 %attend_leaving.1 = (bf16[2,136,256]{2,1,0:T(8,128)(2,1)S(1)}, bf16[2048,256]{1,0:T(8,128)(2,1)S(1)}, bf16[128,2048]{1,0:T(8,128)(2,1)S(1)}, bf16[1024,256]{1,0:T(8,128)(2,1)S(1)}, f32[136,256]{1,0:T(8,128)S(1)}) custom-call(bf16[4096,128]{1,0:T(8,128)(2,1)} %bitcast.15, f32[256,128]{1,0:T(8,128)} %bitcast.19, f32[2,128]{1,0:T(2,128)} %scales_any.3, ...), custom_call_target="tpu_custom_call" | custom-call | tf_op jit(solution)/shard_map/attend_leaving/pallas_call | solution.py:408
  13.0 0.2 collective-permute-start
  13.2 1.5 %place.3 = (bf16[512,128]{1,0:T(8,128)(2,1)S(1)}, bf16[512,128]{1,0:T(8,128)(2,1)S(1)}, bf16[1024,128]{1,0:T(8,128)(2,1)S(1)}) custom-call(s32[128]{0:T(128)} %owner_any.3, bf16[4096,128]{1,0:T(8,128)(2,1)} %bitcast.16, f32[256,128]{1,0:T(8,128)} %bitcast.20, f32[2,128]{1,0:T(2,128)} %scales_any.3), custom_call_target="tpu_custom_call" | custom-call | tf_op jit(solution)/shard_map/place/pallas_call | solution.py:378
  14.7 1.9 %collective-permute-start.4 = (bf16[512,128]{1,0:T(8,128)(2,1)S(1)}, bf16[512,128]{1,0:T(8,128)(2,1)S(1)}, u32[]{:S(2)}, u32[]{:S(2)}) collective-permute-start(bf16[512,128]{1,0:T(8,128)(2,1)S(1)} %get-tuple-element.36), channel_id=1, source_target_pairs={{0,8},{4,0},{8,12},{12,4},{1,9},{5,1},{9,13},{13,5},{2,10},{6,2},{... | collective-permute-start | bytes 393224 | tf_op jit(solution)/shard_map/ppermute | solution.py:53
  16.6 1.7 %collective-permute-start.5 = (bf16[512,128]{1,0:T(8,128)(2,1)S(1)}, bf16[512,128]{1,0:T(8,128)(2,1)S(1)}, u32[]{:S(2)}, u32[]{:S(2)}) collective-permute-start(bf16[512,128]{1,0:T(8,128)(2,1)S(1)} %get-tuple-element.37), channel_id=1, source_target_pairs={{0,8},{4,0},{8,12},{12,4},{1,9},{5,1},{9,13},{13,5},{2,10},{6,2},{... | collective-permute-start | bytes 393224 | tf_op jit(solution)/shard_map/ppermute | solution.py:53
  18.3 2.7 %attend_staying.1.keep_ref = f32[2,136,256]{2,1,0:T(8,128)S(1)} custom-call(bf16[2048,256]{1,0:T(8,128)(2,1)S(1)} %get-tuple-element.24.keys_ref, bf16[128,2048]{1,0:T(8,128)(2,1)S(1)} %get-tuple-element.25.turned_ref, bf16[1024,256]{1,0:T(8,128)(2,1)S(1)} %get-tuple-element.26.asked_ref, f32[136,256]{1,0:T(8,128)S(1)} %get-tuple-element.27.own_ref), custom_call_target="tpu_custom_call" | custom-call | tf_op jit(solution)/shard_map/attend_staying/pallas_call | solution.py:437
  21.0 1.6 %collective-permute-done.got_ref = bf16[2,136,256]{2,1,0:T(8,128)(2,1)S(1)} collective-permute-done((bf16[2,136,256]{2,1,0:T(8,128)(2,1)S(1)}, bf16[2,136,256]{2,1,0:T(8,128)(2,1)S(1)}, u32[]{:S(2)}, u32[]{:S(2)}) %collective-permute-start) | collective-permute-done | bytes 139296 | tf_op jit(solution)/shard_map/ppermute | solution.py:48
  22.6 0.1 join.1
  22.6 1.7 %collective-permute-start.1 = (bf16[1,136,256]{2,1,0:T(8,128)(2,1)S(1)}, bf16[1,136,256]{2,1,0:T(8,128)(2,1)S(1)}, u32[]{:S(2)}, u32[]{:S(2)}) collective-permute-start(bf16[1,136,256]{2,1,0:T(8,128)(2,1)S(1)} %get-tuple-element.31), channel_id=1, source_target_pairs={{0,8},{4,12},{8,0},{12,4},{1,9},{5,13},{9,1},{13,5},{2,10},{6,14},... | collective-permute-start | bytes 208904 | tf_op jit(solution)/shard_map/ppermute | solution.py:48
  24.3 0.0 collective-permute-done.2.refs_0_
  24.3 0.8 %settle.1._ = bf16[4096,128]{1,0:T(8,128)(2,1)} custom-call(bf16[1024,128]{1,0:T(8,128)(2,1)S(1)} %collective-permute-done.2.refs_0_, bf16[1024,128]{1,0:T(8,128)(2,1)S(1)} %get-tuple-element.34.refs_1_), custom_call_target="tpu_custom_call" | custom-call | tf_op jit(solution)/shard_map/settle/pallas_call | solution.py:457
  25.1 0.2 collective-permute-done.4.refs_1_
  25.4 2.6 %collective-permute-done.5.refs_2_ = bf16[512,128]{1,0:T(8,128)(2,1)S(1)} collective-permute-done((bf16[512,128]{1,0:T(8,128)(2,1)S(1)}, bf16[512,128]{1,0:T(8,128)(2,1)S(1)}, u32[]{:S(2)}, u32[]{:S(2)}) %collective-permute-start.5) | collective-permute-done | bytes 131104 | tf_op jit(solution)/shard_map/ppermute | solution.py:53
  28.0 4.4 %collective-permute-done.1.got_ref = bf16[1,136,256]{2,1,0:T(8,128)(2,1)S(1)} collective-permute-done((bf16[1,136,256]{2,1,0:T(8,128)(2,1)S(1)}, bf16[1,136,256]{2,1,0:T(8,128)(2,1)S(1)}, u32[]{:S(2)}, u32[]{:S(2)}) %collective-permute-start.1) | collective-permute-done | bytes 69664 | tf_op jit(solution)/shard_map/ppermute | solution.py:48
  32.4 0.0 collective-permute-done.3.refs_0_
  32.4 0.9 %finish.1 = (bf16[256,128]{1,0:T(8,128)(2,1)}, bf16[4096,128]{1,0:T(8,128)(2,1)}) custom-call(f32[1,136,256]{2,1,0:T(8,128)S(1)} %get-tuple-element.30.keep_ref, bf16[1,136,256]{2,1,0:T(8,128)(2,1)S(1)} %collective-permute-done.1.got_ref, bf16[4096,128]{1,0:T(8,128)(2,1)} %settle.1._, ...), custom_call_target="tpu_custom_call", output_to_operand_aliasing={{1}: (2, {})} | custom-call | tf_op jit(solution)/shard_map/finish/pallas_call | solution.py:466
Async XLA Ops:
  2.2 22.1 %collective-permute-start.2 = (bf16[1024,128]{1,0:T(8,128)(2,1)S(1)}, bf16[1024,128]{1,0:T(8,128)(2,1)S(1)}, u32[]{:S(2)}, u32[]{:S(2)}) collective-permute-start(bf16[1024,128]{1,0:T(8,128)(2,1)S(1)} %get-tuple-element.32), channel_id=1, source_target_pairs={{0,4},{4,12},{8,0},{12,8},{1,5},{5,13},{9,1},{13,9},{2,6},{6,14},{... | collective-permute-start | bytes 786440 | tf_op jit(solution)/shard_map/ppermute | solution.py:53
  5.3 27.2 %collective-permute-start.3 = (bf16[1024,128]{1,0:T(8,128)(2,1)S(1)}, bf16[1024,128]{1,0:T(8,128)(2,1)S(1)}, u32[]{:S(2)}, u32[]{:S(2)}) collective-permute-start(bf16[1024,128]{1,0:T(8,128)(2,1)S(1)} %get-tuple-element.35), channel_id=1, source_target_pairs={{0,12},{4,8},{8,4},{12,0},{1,13},{5,9},{9,5},{13,1},{2,14},{6,10},... | collective-permute-start | bytes 786440 | tf_op jit(solution)/shard_map/ppermute | solution.py:53
  13.0 9.6 %collective-permute-start = (bf16[2,136,256]{2,1,0:T(8,128)(2,1)S(1)}, bf16[2,136,256]{2,1,0:T(8,128)(2,1)S(1)}, u32[]{:S(2)}, u32[]{:S(2)}) collective-permute-start(bf16[2,136,256]{2,1,0:T(8,128)(2,1)S(1)} %get-tuple-element.29), channel_id=1, source_target_pairs={{0,4},{4,0},{8,12},{12,8},{1,5},{5,1},{9,13},{13,9},{2,6},{6,2},{1... | collective-permute-start | bytes 417800 | tf_op jit(solution)/shard_map/ppermute | solution.py:48
  14.7 10.7 %collective-permute-start.4 = (bf16[512,128]{1,0:T(8,128)(2,1)S(1)}, bf16[512,128]{1,0:T(8,128)(2,1)S(1)}, u32[]{:S(2)}, u32[]{:S(2)}) collective-permute-start(bf16[512,128]{1,0:T(8,128)(2,1)S(1)} %get-tuple-element.36), channel_id=1, source_target_pairs={{0,8},{4,0},{8,12},{12,4},{1,9},{5,1},{9,13},{13,5},{2,10},{6,2},{... | collective-permute-start | bytes 393224 | tf_op jit(solution)/shard_map/ppermute | solution.py:53
  16.6 11.4 %collective-permute-start.5 = (bf16[512,128]{1,0:T(8,128)(2,1)S(1)}, bf16[512,128]{1,0:T(8,128)(2,1)S(1)}, u32[]{:S(2)}, u32[]{:S(2)}) collective-permute-start(bf16[512,128]{1,0:T(8,128)(2,1)S(1)} %get-tuple-element.37), channel_id=1, source_target_pairs={{0,8},{4,0},{8,12},{12,4},{1,9},{5,1},{9,13},{13,5},{2,10},{6,2},{... | collective-permute-start | bytes 393224 | tf_op jit(solution)/shard_map/ppermute | solution.py:53
  22.6 9.8 %collective-permute-start.1 = (bf16[1,136,256]{2,1,0:T(8,128)(2,1)S(1)}, bf16[1,136,256]{2,1,0:T(8,128)(2,1)S(1)}, u32[]{:S(2)}, u32[]{:S(2)}) collective-permute-start(bf16[1,136,256]{2,1,0:T(8,128)(2,1)S(1)} %get-tuple-element.31), channel_id=1, source_target_pairs={{0,8},{4,12},{8,0},{12,4},{1,9},{5,13},{9,1},{13,5},{2,10},{6,14},... | collective-permute-start | bytes 208904 | tf_op jit(solution)/shard_map/ppermute | solution.py:48

commit v21 on v16

--- a/solution.py
+++ b/solution.py
@@ -54,10 +54,15 @@
 
 
 def messages(count, capacity):
-    half = capacity // 2
     ahead = [(k, 0, capacity) for k in range(count // 2, count)]
-    behind = [(k, first, half) for k in reversed(range(1, count // 2)) for first in (0, half)]
-    return ahead, behind, [(0, 0, capacity)]
+    first = capacity // 2
+    second = (capacity - first) // 2
+    ends = [0, first, first + second, capacity]
+    near = [
+        [(k, start, end - start) for k in reversed(range(1, count // 2)) if end > start]
+        for start, end in zip(ends, ends[1:])
+    ]
+    return ahead, *near, [(0, 0, capacity)]
 
 
 def place_kernel(plan, owner_any, deltas_any, anchors_any, scales_any, *refs):
@@ -373,7 +378,7 @@
     flat_new = new_kv.reshape(rows_dev * 4, HD)
 
     whole = jax.ShapeDtypeStruct((tokens * 2, HD), jnp.bfloat16)
-    ahead, behind, own = messages(senders, blocks // senders)
+    ahead, first, second, third, own = messages(senders, blocks // senders)
     block_rows = tokens * 2 // blocks
 
     def place(plan, deltas):
@@ -434,8 +439,11 @@
     k, count = 1, senders // 2
     send, late_deltas = lax.optimization_barrier((send, late_deltas))
     passed = exchange(send, k)
+    behind = first + second + third
     *sent, mine = place(behind + own, late_deltas)
-    got = got_ahead[1:] + [hand(message, k) for message, (k, _, _) in zip(sent, behind)]
+    later = sent[len(first) : len(first) + len(second)]
+    last = sent[len(first) + len(second) :]
+    got = [hand(message, partner) for message, (partner, _, _) in zip(sent, first)]
     keep = pl.pallas_call(
         second_kernel,
         out_shape=staying(senders),
@@ -453,9 +461,12 @@
             compiler_params=small,
             name="join",
         )(keep, passed)
+        if k == 1:
+            later, send = lax.optimization_barrier((later, send))
+            got += [hand(message, partner) for message, (partner, _, _) in zip(later, second)]
         k, count = 2 * k, count // 2
         passed = exchange(send, k)
-    settled = ahead[:1] + own
+    settled = ahead + first + own
     pages = pl.pallas_call(
         functools.partial(settle_kernel, settled),
         out_shape=whole,
@@ -464,20 +475,22 @@
         scratch_shapes=[pltpu.SemaphoreType.DMA((len(settled),))],
         compiler_params=small,
         name="settle",
-    )(got_ahead[0], mine)
+    )(*got_ahead, *got[: len(first)], mine)
+    last, passed, pages = lax.optimization_barrier((last, passed, pages))
+    got += [hand(message, partner) for message, (partner, _, _) in zip(last, third)]
     attended, pages = pl.pallas_call(
-        functools.partial(finish_kernel, ahead[1:] + behind),
+        functools.partial(finish_kernel, second + third),
         out_shape=[jax.ShapeDtypeStruct((width, HD), jnp.bfloat16), whole],
-        in_specs=[VMEM] * 2 + [HBM] + [ANY] * len(got),
+        in_specs=[VMEM] * 2 + [HBM] + [ANY] * len(second + third),
         out_specs=[HBM, HBM],
         scratch_shapes=[
             pltpu.VMEM((width, HD), jnp.bfloat16),
-            pltpu.SemaphoreType.DMA((len(got) + 1,)),
+            pltpu.SemaphoreType.DMA((len(second + third) + 1,)),
         ],
         input_output_aliases={2: 1},
         compiler_params=small,
         name="finish",
-    )(keep, passed, pages, *got)
+    )(keep, passed, pages, *got[len(first) :])
     pages = pages.reshape(blocks, tokens // blocks, 2, HD)
     attended = (
         attended.reshape(rows_dev, GQ, steps, HD).transpose(0, 2, 1, 3).reshape(rows_dev, steps, GQ * HD)

time: 33.6 us -> 37 us (1.10)
  starting transfers between devices: 10.9 us -> 13.6 us
  waiting for transfers between devices: 8.83 us -> 9.56 us
    ppermute x4 -> x5, starting transfers between devices: 9.09 us -> 11.8 us  [hand(): lax.ppermute(message, 'seq', [(i, partner(i, k, count)) for i in range(co...]
    ppermute x2, waiting for transfers between devices: 5.96 us -> 7.64 us  [exchange(): return lax.ppermute(message, 'seq', [(i, i ^ k) for i in range(count)])]
    ppermute x4 -> x5, waiting for transfers between devices: 2.87 us -> 1.91 us  [hand(): lax.ppermute(message, 'seq', [(i, partner(i, k, count)) for i in range(co...]
  transfers between devices with their start and end apart: 6 -> 7, of which waited for: 4 -> 3; matrix products, arithmetic and copies ran while one was open for 0% -> 0% of each run, Pallas kernels for 31% -> 29%
where the time goes in v21:
time: 37 us; the launch traced here: 36.8 us
  starting transfers between devices  13.6 us (37%)
  Pallas kernels  13 us (35%)
  waiting for transfers between devices  9.56 us (26%)
  between operations  0.68 us (2%)
    ppermute x5, starting transfers between devices, hand(): lax.ppermute(message, 'seq', [(i, partner(i, k, count)) for i in range(co...  11.8 us
    ppermute x2, waiting for transfers between devices, exchange(): return lax.ppermute(message, 'seq', [(i, i ^ k) for i in range(count)])  7.64 us
    pallas_call x1, Pallas kernels, per_device(): pl.pallas_call(first_kernel, out_shape=[leaving(senders), jax.ShapeDtypeS...  5.24 us
    pallas_call x2, Pallas kernels, place(): pl.pallas_call(functools.partial(place_kernel, plan), out_shape=[jax.Shap...  3.19 us
    pallas_call x1, Pallas kernels, per_device(): pl.pallas_call(second_kernel, out_shape=staying(senders), in_specs=[VMEM]...  2.7 us
    ppermute x5, waiting for transfers between devices, hand(): lax.ppermute(message, 'seq', [(i, partner(i, k, count)) for i in range(co...  1.91 us
    ppermute x2, starting transfers between devices, exchange(): return lax.ppermute(message, 'seq', [(i, i ^ k) for i in range(count)])  1.86 us
    pallas_call x1, Pallas kernels, per_device(): pl.pallas_call(functools.partial(settle_kernel, settled), out_shape=whole...  0.97 us
  transfers between devices with their start and end apart: 7, of which 3 were waited for; matrix products, arithmetic and copies ran while one was open for 0% of the time, Pallas kernels for 29%

profile of v21, /device:TPU:0, one launch (start us, length us, event | category | flops | bytes accessed | tf_op | source)
XLA Modules:
  0.0 36.8 jit_solution(2326872193896477414)
XLA Ops:
  0.6 1.6 %place.2 = (bf16[1024,128]{1,0:T(8,128)(2,1)S(1)}, bf16[1024,128]{1,0:T(8,128)(2,1)S(1)}) custom-call(s32[128]{0:T(128)} %owner_any.3, bf16[4096,128]{1,0:T(8,128)(2,1)} %bitcast.14, f32[256,128]{1,0:T(8,128)} %bitcast.18, f32[2,128]{1,0:T(2,128)} %scales_any.3), custom_call_target="tpu_custom_call" | custom-call | tf_op jit(solution)/shard_map/place/pallas_call | solution.py:385
  2.2 3.1 %collective-permute-start.2 = (bf16[1024,128]{1,0:T(8,128)(2,1)S(1)}, bf16[1024,128]{1,0:T(8,128)(2,1)S(1)}, u32[]{:S(2)}, u32[]{:S(2)}) collective-permute-start(bf16[1024,128]{1,0:T(8,128)(2,1)S(1)} %get-tuple-element.42), channel_id=1, source_target_pairs={{0,4},{4,12},{8,0},{12,8},{1,5},{5,13},{9,1},{13,9},{2,6},{6,14},{... | collective-permute-start | bytes 786440 | tf_op jit(solution)/shard_map/ppermute | solution.py:53
  5.3 2.5 %collective-permute-start.3 = (bf16[1024,128]{1,0:T(8,128)(2,1)S(1)}, bf16[1024,128]{1,0:T(8,128)(2,1)S(1)}, u32[]{:S(2)}, u32[]{:S(2)}) collective-permute-start(bf16[1024,128]{1,0:T(8,128)(2,1)S(1)} %get-tuple-element.43), channel_id=1, source_target_pairs={{0,12},{4,8},{8,4},{12,0},{1,13},{5,9},{9,5},{13,1},{2,14},{6,10},... | collective-permute-start | bytes 786440 | tf_op jit(solution)/shard_map/ppermute | solution.py:53
  7.8 5.2 %attend_leaving.1 = (bf16[2,136,256]{2,1,0:T(8,128)(2,1)S(1)}, bf16[2048,256]{1,0:T(8,128)(2,1)S(1)}, bf16[128,2048]{1,0:T(8,128)(2,1)S(1)}, bf16[1024,256]{1,0:T(8,128)(2,1)S(1)}, f32[136,256]{1,0:T(8,128)S(1)}) custom-call(bf16[4096,128]{1,0:T(8,128)(2,1)} %bitcast.15, f32[256,128]{1,0:T(8,128)} %bitcast.19, f32[2,128]{1,0:T(2,128)} %scales_any.3, ...), custom_call_target="tpu_custom_call" | custom-call | tf_op jit(solution)/shard_map/attend_leaving/pallas_call | solution.py:415
  13.1 0.2 collective-permute-start
  13.2 1.6 %place.3 = (bf16[512,128]{1,0:T(8,128)(2,1)S(1)}, bf16[256,128]{1,0:T(8,128)(2,1)S(1)}, bf16[256,128]{1,0:T(8,128)(2,1)S(1)}, bf16[1024,128]{1,0:T(8,128)(2,1)S(1)}) custom-call(s32[128]{0:T(128)} %owner_any.3, bf16[4096,128]{1,0:T(8,128)(2,1)} %bitcast.16, f32[256,128]{1,0:T(8,128)} %bitcast.20, f32[2,128]{1,0:T(2,128)} %scales_any.3), custom_call_target="tpu_custom_call" | custom-call | tf_op jit(solution)/shard_map/place/pallas_call | solution.py:385
  14.8 1.8 %collective-permute-start.4 = (bf16[512,128]{1,0:T(8,128)(2,1)S(1)}, bf16[512,128]{1,0:T(8,128)(2,1)S(1)}, u32[]{:S(2)}, u32[]{:S(2)}) collective-permute-start(bf16[512,128]{1,0:T(8,128)(2,1)S(1)} %get-tuple-element.44), channel_id=1, source_target_pairs={{0,8},{4,0},{8,12},{12,4},{1,9},{5,1},{9,13},{13,5},{2,10},{6,2},{... | collective-permute-start | bytes 393224 | tf_op jit(solution)/shard_map/ppermute | solution.py:53
  16.7 2.7 %attend_staying.1.keep_ref = f32[2,136,256]{2,1,0:T(8,128)S(1)} custom-call(bf16[2048,256]{1,0:T(8,128)(2,1)S(1)} %get-tuple-element.30.keys_ref, bf16[128,2048]{1,0:T(8,128)(2,1)S(1)} %get-tuple-element.31.turned_ref, bf16[1024,256]{1,0:T(8,128)(2,1)S(1)} %get-tuple-element.32.asked_ref, f32[136,256]{1,0:T(8,128)S(1)} %get-tuple-element.33.own_ref), custom_call_target="tpu_custom_call" | custom-call | tf_op jit(solution)/shard_map/attend_staying/pallas_call | solution.py:447
  19.4 3.2 %collective-permute-done.got_ref = bf16[2,136,256]{2,1,0:T(8,128)(2,1)S(1)} collective-permute-done((bf16[2,136,256]{2,1,0:T(8,128)(2,1)S(1)}, bf16[2,136,256]{2,1,0:T(8,128)(2,1)S(1)}, u32[]{:S(2)}, u32[]{:S(2)}) %collective-permute-start) | collective-permute-done | bytes 139296 | tf_op jit(solution)/shard_map/ppermute | solution.py:48
  22.6 0.1 join.1
  22.7 1.7 %collective-permute-start.1 = (bf16[1,136,256]{2,1,0:T(8,128)(2,1)S(1)}, bf16[1,136,256]{2,1,0:T(8,128)(2,1)S(1)}, u32[]{:S(2)}, u32[]{:S(2)}) collective-permute-start(bf16[1,136,256]{2,1,0:T(8,128)(2,1)S(1)} %get-tuple-element.41), channel_id=1, source_target_pairs={{0,8},{4,12},{8,0},{12,4},{1,9},{5,13},{9,1},{13,5},{2,10},{6,14},... | collective-permute-start | bytes 208904 | tf_op jit(solution)/shard_map/ppermute | solution.py:48
  24.4 1.3 %collective-permute-start.5 = (bf16[256,128]{1,0:T(8,128)(2,1)S(1)}, bf16[256,128]{1,0:T(8,128)(2,1)S(1)}, u32[]{:S(2)}, u32[]{:S(2)}) collective-permute-start(bf16[256,128]{1,0:T(8,128)(2,1)S(1)} %get-tuple-element.48), channel_id=1, source_target_pairs={{0,8},{4,0},{8,12},{12,4},{1,9},{5,1},{9,13},{13,5},{2,10},{6,2},{... | collective-permute-start | bytes 196616 | tf_op jit(solution)/shard_map/ppermute | solution.py:53
  25.7 0.0 collective-permute-done.4.refs_2_
  25.7 0.0 collective-permute-done.2.refs_0_
  25.7 0.0 collective-permute-done.3.refs_1_
  25.7 1.0 %settle.1._ = bf16[4096,128]{1,0:T(8,128)(2,1)} custom-call(bf16[1024,128]{1,0:T(8,128)(2,1)S(1)} %collective-permute-done.2.refs_0_, bf16[1024,128]{1,0:T(8,128)(2,1)S(1)} %collective-permute-done.3.refs_1_, bf16[512,128]{1,0:T(8,128)(2,1)S(1)} %collective-permute-done.4.refs_2_, bf16[1024,128]{1,0:T(8,128)(2,1)S(1)} %get-tuple-element.45.refs_3_), custom_call_target="tpu_custom_call" | custom-call | tf_op jit(solution)/shard_map/settle/pallas_call | solution.py:470
  26.7 4.4 %collective-permute-done.1.got_ref = bf16[1,136,256]{2,1,0:T(8,128)(2,1)S(1)} collective-permute-done((bf16[1,136,256]{2,1,0:T(8,128)(2,1)S(1)}, bf16[1,136,256]{2,1,0:T(8,128)(2,1)S(1)}, u32[]{:S(2)}, u32[]{:S(2)}) %collective-permute-start.1) | collective-permute-done | bytes 69664 | tf_op jit(solution)/shard_map/ppermute | solution.py:48
  31.1 3.1 %collective-permute-start.6 = (bf16[256,128]{1,0:T(8,128)(2,1)S(1)}, bf16[256,128]{1,0:T(8,128)(2,1)S(1)}, u32[]{:S(2)}, u32[]{:S(2)}) collective-permute-start(bf16[256,128]{1,0:T(8,128)(2,1)S(1)} %get-tuple-element.49), channel_id=1, source_target_pairs={{0,8},{4,0},{8,12},{12,4},{1,9},{5,1},{9,13},{13,5},{2,10},{6,2},{... | collective-permute-start | bytes 196616 | tf_op jit(solution)/shard_map/ppermute | solution.py:53
  34.1 0.0 collective-permute-done.5.refs_0_
  34.1 1.9 %collective-permute-done.6.refs_1_ = bf16[256,128]{1,0:T(8,128)(2,1)S(1)} collective-permute-done((bf16[256,128]{1,0:T(8,128)(2,1)S(1)}, bf16[256,128]{1,0:T(8,128)(2,1)S(1)}, u32[]{:S(2)}, u32[]{:S(2)}) %collective-permute-start.6) | collective-permute-done | bytes 65568 | tf_op jit(solution)/shard_map/ppermute | solution.py:53
  36.1 0.8 %finish.1 = (bf16[256,128]{1,0:T(8,128)(2,1)}, bf16[4096,128]{1,0:T(8,128)(2,1)}) custom-call(f32[1,136,256]{2,1,0:T(8,128)S(1)} %get-tuple-element.36.keep_ref, bf16[1,136,256]{2,1,0:T(8,128)(2,1)S(1)} %collective-permute-done.1.got_ref, bf16[4096,128]{1,0:T(8,128)(2,1)} %settle.1._, ...), custom_call_target="tpu_custom_call", output_to_operand_aliasing={{1}: (2, {})} | custom-call | tf_op jit(solution)/shard_map/finish/pallas_call | solution.py:481
Async XLA Ops:
  2.2 23.4 %collective-permute-start.2 = (bf16[1024,128]{1,0:T(8,128)(2,1)S(1)}, bf16[1024,128]{1,0:T(8,128)(2,1)S(1)}, u32[]{:S(2)}, u32[]{:S(2)}) collective-permute-start(bf16[1024,128]{1,0:T(8,128)(2,1)S(1)} %get-tuple-element.42), channel_id=1, source_target_pairs={{0,4},{4,12},{8,0},{12,8},{1,5},{5,13},{9,1},{13,9},{2,6},{6,14},{... | collective-permute-start | bytes 786440 | tf_op jit(solution)/shard_map/ppermute | solution.py:53
  5.3 20.4 %collective-permute-start.3 = (bf16[1024,128]{1,0:T(8,128)(2,1)S(1)}, bf16[1024,128]{1,0:T(8,128)(2,1)S(1)}, u32[]{:S(2)}, u32[]{:S(2)}) collective-permute-start(bf16[1024,128]{1,0:T(8,128)(2,1)S(1)} %get-tuple-element.43), channel_id=1, source_target_pairs={{0,12},{4,8},{8,4},{12,0},{1,13},{5,9},{9,5},{13,1},{2,14},{6,10},... | collective-permute-start | bytes 786440 | tf_op jit(solution)/shard_map/ppermute | solution.py:53
  13.1 9.6 %collective-permute-start = (bf16[2,136,256]{2,1,0:T(8,128)(2,1)S(1)}, bf16[2,136,256]{2,1,0:T(8,128)(2,1)S(1)}, u32[]{:S(2)}, u32[]{:S(2)}) collective-permute-start(bf16[2,136,256]{2,1,0:T(8,128)(2,1)S(1)} %get-tuple-element.35), channel_id=1, source_target_pairs={{0,4},{4,0},{8,12},{12,8},{1,5},{5,1},{9,13},{13,9},{2,6},{6,2},{1... | collective-permute-start | bytes 417800 | tf_op jit(solution)/shard_map/ppermute | solution.py:48
  14.8 10.9 %collective-permute-start.4 = (bf16[512,128]{1,0:T(8,128)(2,1)S(1)}, bf16[512,128]{1,0:T(8,128)(2,1)S(1)}, u32[]{:S(2)}, u32[]{:S(2)}) collective-permute-start(bf16[512,128]{1,0:T(8,128)(2,1)S(1)} %get-tuple-element.44), channel_id=1, source_target_pairs={{0,8},{4,0},{8,12},{12,4},{1,9},{5,1},{9,13},{13,5},{2,10},{6,2},{... | collective-permute-start | bytes 393224 | tf_op jit(solution)/shard_map/ppermute | solution.py:53
  22.7 8.4 %collective-permute-start.1 = (bf16[1,136,256]{2,1,0:T(8,128)(2,1)S(1)}, bf16[1,136,256]{2,1,0:T(8,128)(2,1)S(1)}, u32[]{:S(2)}, u32[]{:S(2)}) collective-permute-start(bf16[1,136,256]{2,1,0:T(8,128)(2,1)S(1)} %get-tuple-element.41), channel_id=1, source_target_pairs={{0,8},{4,12},{8,0},{12,4},{1,9},{5,13},{9,1},{13,5},{2,10},{6,14},... | collective-permute-start | bytes 208904 | tf_op jit(solution)/shard_map/ppermute | solution.py:48
  24.4 9.8 %collective-permute-start.5 = (bf16[256,128]{1,0:T(8,128)(2,1)S(1)}, bf16[256,128]{1,0:T(8,128)(2,1)S(1)}, u32[]{:S(2)}, u32[]{:S(2)}) collective-permute-start(bf16[256,128]{1,0:T(8,128)(2,1)S(1)} %get-tuple-element.48), channel_id=1, source_target_pairs={{0,8},{4,0},{8,12},{12,4},{1,9},{5,1},{9,13},{13,5},{2,10},{6,2},{... | collective-permute-start | bytes 196616 | tf_op jit(solution)/shard_map/ppermute | solution.py:53
  31.1 5.0 %collective-permute-start.6 = (bf16[256,128]{1,0:T(8,128)(2,1)S(1)}, bf16[256,128]{1,0:T(8,128)(2,1)S(1)}, u32[]{:S(2)}, u32[]{:S(2)}) collective-permute-start(bf16[256,128]{1,0:T(8,128)(2,1)S(1)} %get-tuple-element.49), channel_id=1, source_target_pairs={{0,8},{4,0},{8,12},{12,4},{1,9},{5,1},{9,13},{13,5},{2,10},{6,2},{... | collective-permute-start | bytes 196616 | tf_op jit(solution)/shard_map/ppermute | solution.py:53

commit v22 on v20

--- a/solution.py
+++ b/solution.py
@@ -165,6 +165,13 @@
     )
 
 
+def difference(index):
+    total = 0
+    while index:
+        total, index = total ^ index, index >> 1
+    return total
+
+
 def attend(parity, width, keys_ref, turned_ref, asked_ref, store):
     me = lax.axis_index("seq")
     asked = asked_ref.shape[0]
@@ -181,7 +188,7 @@
 
     if width % HD == 0:
         for index in range(asked // width // 2):
-            there = (me ^ (2 * index + parity)) * width
+            there = (me ^ difference(2 * index + parity)) * width
             store(index, partial_of(asked_ref[pl.ds(pl.multiple_of(there, width), width), :]))
         return
     tile = min(2 * HD, asked)
@@ -193,10 +200,11 @@
         for part in range(parts):
             lanes = slice(part * width, (part + 1) * width)
             apart = (tile_index * parts + part) ^ me
-
-            @pl.when(apart % 2 == parity)
-            def _(lanes=lanes, apart=apart):
-                store(apart // 2, (summed[:, lanes], top[:, lanes], total[:, lanes]))
+            place = apart ^ (apart >> 1)
+
+            @pl.when(place % 2 == parity)
+            def _(lanes=lanes, place=place):
+                store(place // 2, (summed[:, lanes], top[:, lanes], total[:, lanes]))
 
         return carry
 
@@ -451,7 +459,7 @@
             compiler_params=small,
             name="join",
         )(keep, passed)
-        k, count = 2 * k, count // 2
+        k, count = 2 * k + 1, count // 2
         passed = exchange(send, k)
     settled = ahead[:1] + own
     pages = pl.pallas_call(

time: 33.5 us -> 32.3 us (0.964)
  the two profiles are of different devices: /device:TPU:0 before, /device:TPU:20 now
where the time goes in v22:
time: 32.3 us; the launch traced here: 32.1 us
  Pallas kernels  12.8 us (40%)
  waiting for transfers between devices  11.5 us (36%)
  starting transfers between devices  7.1 us (22%)
  between operations  0.68 us (2%)
    ppermute x2, waiting for transfers between devices, exchange(): return lax.ppermute(message, 'seq', [(i, i ^ k) for i in range(count)])  7.04 us
    ppermute x4, starting transfers between devices, hand(): lax.ppermute(message, 'seq', [(i, partner(i, k, count)) for i in range(co...  6.18 us
    pallas_call x1, Pallas kernels, per_device(): pl.pallas_call(first_kernel, out_shape=[leaving(senders), jax.ShapeDtypeS...  5.24 us
    ppermute x4, waiting for transfers between devices, hand(): lax.ppermute(message, 'seq', [(i, partner(i, k, count)) for i in range(co...  4.48 us
    pallas_call x2, Pallas kernels, place(): pl.pallas_call(functools.partial(place_kernel, plan), out_shape=[jax.Shap...  3.09 us
    pallas_call x1, Pallas kernels, per_device(): pl.pallas_call(second_kernel, out_shape=staying(senders), in_specs=[VMEM]...  2.7 us
    ppermute x2, starting transfers between devices, exchange(): return lax.ppermute(message, 'seq', [(i, i ^ k) for i in range(count)])  0.92 us
    pallas_call x1, Pallas kernels, per_device(): pl.pallas_call(functools.partial(finish_kernel, ahead[1:] + behind), out_...  0.88 us
  transfers between devices with their start and end apart: 6, of which 4 were waited for; matrix products, arithmetic and copies ran while one was open for 0% of the time, Pallas kernels for 32%

profile of v22, /device:TPU:20, one launch (start us, length us, event | category | flops | bytes accessed | tf_op | source)
XLA Modules:
  0.0 32.1 jit_solution(10859762833402707768)
XLA Ops:
  0.6 1.6 %place.2 = (bf16[1024,128]{1,0:T(8,128)(2,1)S(1)}, bf16[1024,128]{1,0:T(8,128)(2,1)S(1)}) custom-call(s32[128]{0:T(128)} %owner_any.3, bf16[4096,128]{1,0:T(8,128)(2,1)} %bitcast.14, f32[256,128]{1,0:T(8,128)} %bitcast.18, f32[2,128]{1,0:T(2,128)} %scales_any.3), custom_call_target="tpu_custom_call" | custom-call | tf_op jit(solution)/shard_map/place/pallas_call | solution.py:386
  2.2 0.4 %collective-permute-start.2 = (bf16[1024,128]{1,0:T(8,128)(2,1)S(1)}, bf16[1024,128]{1,0:T(8,128)(2,1)S(1)}, u32[]{:S(2)}, u32[]{:S(2)}) collective-permute-start(bf16[1024,128]{1,0:T(8,128)(2,1)S(1)} %get-tuple-element.32), channel_id=1, source_target_pairs={{0,4},{4,12},{8,0},{12,8},{1,5},{5,13},{9,1},{13,9},{2,6},{6,14},{... | collective-permute-start | bytes 786440 | tf_op jit(solution)/shard_map/ppermute | solution.py:53
  2.6 2.7 %collective-permute-start.3 = (bf16[1024,128]{1,0:T(8,128)(2,1)S(1)}, bf16[1024,128]{1,0:T(8,128)(2,1)S(1)}, u32[]{:S(2)}, u32[]{:S(2)}) collective-permute-start(bf16[1024,128]{1,0:T(8,128)(2,1)S(1)} %get-tuple-element.35), channel_id=1, source_target_pairs={{0,12},{4,8},{8,4},{12,0},{1,13},{5,9},{9,5},{13,1},{2,14},{6,10},... | collective-permute-start | bytes 786440 | tf_op jit(solution)/shard_map/ppermute | solution.py:53
  5.3 5.2 %attend_leaving.1 = (bf16[2,136,256]{2,1,0:T(8,128)(2,1)S(1)}, bf16[2048,256]{1,0:T(8,128)(2,1)S(1)}, bf16[128,2048]{1,0:T(8,128)(2,1)S(1)}, bf16[1024,256]{1,0:T(8,128)(2,1)S(1)}, f32[136,256]{1,0:T(8,128)S(1)}) custom-call(bf16[4096,128]{1,0:T(8,128)(2,1)} %bitcast.15, f32[256,128]{1,0:T(8,128)} %bitcast.19, f32[2,128]{1,0:T(2,128)} %scales_any.3, ...), custom_call_target="tpu_custom_call" | custom-call | tf_op jit(solution)/shard_map/attend_leaving/pallas_call | solution.py:416
  10.5 0.4 %collective-permute-start = (bf16[2,136,256]{2,1,0:T(8,128)(2,1)S(1)}, bf16[2,136,256]{2,1,0:T(8,128)(2,1)S(1)}, u32[]{:S(2)}, u32[]{:S(2)}) collective-permute-start(bf16[2,136,256]{2,1,0:T(8,128)(2,1)S(1)} %get-tuple-element.29), channel_id=1, source_target_pairs={{0,4},{4,0},{8,12},{12,8},{1,5},{5,1},{9,13},{13,9},{2,6},{6,2},{1... | collective-permute-start | bytes 417800 | tf_op jit(solution)/shard_map/ppermute | solution.py:48
  11.0 1.5 %place.3 = (bf16[512,128]{1,0:T(8,128)(2,1)S(1)}, bf16[512,128]{1,0:T(8,128)(2,1)S(1)}, bf16[1024,128]{1,0:T(8,128)(2,1)S(1)}) custom-call(s32[128]{0:T(128)} %owner_any.3, bf16[4096,128]{1,0:T(8,128)(2,1)} %bitcast.16, f32[256,128]{1,0:T(8,128)} %bitcast.20, f32[2,128]{1,0:T(2,128)} %scales_any.3), custom_call_target="tpu_custom_call" | custom-call | tf_op jit(solution)/shard_map/place/pallas_call | solution.py:386
  12.5 1.7 %collective-permute-start.4 = (bf16[512,128]{1,0:T(8,128)(2,1)S(1)}, bf16[512,128]{1,0:T(8,128)(2,1)S(1)}, u32[]{:S(2)}, u32[]{:S(2)}) collective-permute-start(bf16[512,128]{1,0:T(8,128)(2,1)S(1)} %get-tuple-element.36), channel_id=1, source_target_pairs={{0,8},{4,0},{8,12},{12,4},{1,9},{5,1},{9,13},{13,5},{2,10},{6,2},{... | collective-permute-start | bytes 393224 | tf_op jit(solution)/shard_map/ppermute | solution.py:53
  14.2 1.4 %collective-permute-start.5 = (bf16[512,128]{1,0:T(8,128)(2,1)S(1)}, bf16[512,128]{1,0:T(8,128)(2,1)S(1)}, u32[]{:S(2)}, u32[]{:S(2)}) collective-permute-start(bf16[512,128]{1,0:T(8,128)(2,1)S(1)} %get-tuple-element.37), channel_id=1, source_target_pairs={{0,8},{4,0},{8,12},{12,4},{1,9},{5,1},{9,13},{13,5},{2,10},{6,2},{... | collective-permute-start | bytes 393224 | tf_op jit(solution)/shard_map/ppermute | solution.py:53
  15.6 2.7 %attend_staying.1.keep_ref = f32[2,136,256]{2,1,0:T(8,128)S(1)} custom-call(bf16[2048,256]{1,0:T(8,128)(2,1)S(1)} %get-tuple-element.24.keys_ref, bf16[128,2048]{1,0:T(8,128)(2,1)S(1)} %get-tuple-element.25.turned_ref, bf16[1024,256]{1,0:T(8,128)(2,1)S(1)} %get-tuple-element.26.asked_ref, f32[136,256]{1,0:T(8,128)S(1)} %get-tuple-element.27.own_ref), custom_call_target="tpu_custom_call" | custom-call | tf_op jit(solution)/shard_map/attend_staying/pallas_call | solution.py:445
  18.3 1.9 %collective-permute-done.got_ref = bf16[2,136,256]{2,1,0:T(8,128)(2,1)S(1)} collective-permute-done((bf16[2,136,256]{2,1,0:T(8,128)(2,1)S(1)}, bf16[2,136,256]{2,1,0:T(8,128)(2,1)S(1)}, u32[]{:S(2)}, u32[]{:S(2)}) %collective-permute-start) | collective-permute-done | bytes 139296 | tf_op jit(solution)/shard_map/ppermute | solution.py:48
  20.1 0.1 join.1
  20.2 0.5 %collective-permute-start.1 = (bf16[1,136,256]{2,1,0:T(8,128)(2,1)S(1)}, bf16[1,136,256]{2,1,0:T(8,128)(2,1)S(1)}, u32[]{:S(2)}, u32[]{:S(2)}) collective-permute-start(bf16[1,136,256]{2,1,0:T(8,128)(2,1)S(1)} %get-tuple-element.31), channel_id=1, source_target_pairs={{0,12},{4,8},{8,4},{12,0},{1,13},{5,9},{9,5},{13,1},{2,14},{6,10},... | collective-permute-start | bytes 208904 | tf_op jit(solution)/shard_map/ppermute | solution.py:48
  20.7 0.0 collective-permute-done.2.refs_0_
  20.7 0.8 %settle.1._ = bf16[4096,128]{1,0:T(8,128)(2,1)} custom-call(bf16[1024,128]{1,0:T(8,128)(2,1)S(1)} %collective-permute-done.2.refs_0_, bf16[1024,128]{1,0:T(8,128)(2,1)S(1)} %get-tuple-element.34.refs_1_), custom_call_target="tpu_custom_call" | custom-call | tf_op jit(solution)/shard_map/settle/pallas_call | solution.py:465
  21.6 1.4 %collective-permute-done.4.refs_1_ = bf16[512,128]{1,0:T(8,128)(2,1)S(1)} collective-permute-done((bf16[512,128]{1,0:T(8,128)(2,1)S(1)}, bf16[512,128]{1,0:T(8,128)(2,1)S(1)}, u32[]{:S(2)}, u32[]{:S(2)}) %collective-permute-start.4) | collective-permute-done | bytes 131104 | tf_op jit(solution)/shard_map/ppermute | solution.py:53
  22.9 3.1 %collective-permute-done.5.refs_2_ = bf16[512,128]{1,0:T(8,128)(2,1)S(1)} collective-permute-done((bf16[512,128]{1,0:T(8,128)(2,1)S(1)}, bf16[512,128]{1,0:T(8,128)(2,1)S(1)}, u32[]{:S(2)}, u32[]{:S(2)}) %collective-permute-start.5) | collective-permute-done | bytes 131104 | tf_op jit(solution)/shard_map/ppermute | solution.py:53
  26.0 5.2 %collective-permute-done.1.got_ref = bf16[1,136,256]{2,1,0:T(8,128)(2,1)S(1)} collective-permute-done((bf16[1,136,256]{2,1,0:T(8,128)(2,1)S(1)}, bf16[1,136,256]{2,1,0:T(8,128)(2,1)S(1)}, u32[]{:S(2)}, u32[]{:S(2)}) %collective-permute-start.1) | collective-permute-done | bytes 69664 | tf_op jit(solution)/shard_map/ppermute | solution.py:48
  31.2 0.0 collective-permute-done.3.refs_0_
  31.2 0.9 %finish.1 = (bf16[256,128]{1,0:T(8,128)(2,1)}, bf16[4096,128]{1,0:T(8,128)(2,1)}) custom-call(f32[1,136,256]{2,1,0:T(8,128)S(1)} %get-tuple-element.30.keep_ref, bf16[1,136,256]{2,1,0:T(8,128)(2,1)S(1)} %collective-permute-done.1.got_ref, bf16[4096,128]{1,0:T(8,128)(2,1)} %settle.1._, ...), custom_call_target="tpu_custom_call", output_to_operand_aliasing={{1}: (2, {})} | custom-call | tf_op jit(solution)/shard_map/finish/pallas_call | solution.py:474
Async XLA Ops:
  2.2 18.5 %collective-permute-start.2 = (bf16[1024,128]{1,0:T(8,128)(2,1)S(1)}, bf16[1024,128]{1,0:T(8,128)(2,1)S(1)}, u32[]{:S(2)}, u32[]{:S(2)}) collective-permute-start(bf16[1024,128]{1,0:T(8,128)(2,1)S(1)} %get-tuple-element.32), channel_id=1, source_target_pairs={{0,4},{4,12},{8,0},{12,8},{1,5},{5,13},{9,1},{13,9},{2,6},{6,14},{... | collective-permute-start | bytes 786440 | tf_op jit(solution)/shard_map/ppermute | solution.py:53
  2.6 28.6 %collective-permute-start.3 = (bf16[1024,128]{1,0:T(8,128)(2,1)S(1)}, bf16[1024,128]{1,0:T(8,128)(2,1)S(1)}, u32[]{:S(2)}, u32[]{:S(2)}) collective-permute-start(bf16[1024,128]{1,0:T(8,128)(2,1)S(1)} %get-tuple-element.35), channel_id=1, source_target_pairs={{0,12},{4,8},{8,4},{12,0},{1,13},{5,9},{9,5},{13,1},{2,14},{6,10},... | collective-permute-start | bytes 786440 | tf_op jit(solution)/shard_map/ppermute | solution.py:53
  10.5 9.6 %collective-permute-start = (bf16[2,136,256]{2,1,0:T(8,128)(2,1)S(1)}, bf16[2,136,256]{2,1,0:T(8,128)(2,1)S(1)}, u32[]{:S(2)}, u32[]{:S(2)}) collective-permute-start(bf16[2,136,256]{2,1,0:T(8,128)(2,1)S(1)} %get-tuple-element.29), channel_id=1, source_target_pairs={{0,4},{4,0},{8,12},{12,8},{1,5},{5,1},{9,13},{13,9},{2,6},{6,2},{1... | collective-permute-start | bytes 417800 | tf_op jit(solution)/shard_map/ppermute | solution.py:48
  12.5 10.5 %collective-permute-start.4 = (bf16[512,128]{1,0:T(8,128)(2,1)S(1)}, bf16[512,128]{1,0:T(8,128)(2,1)S(1)}, u32[]{:S(2)}, u32[]{:S(2)}) collective-permute-start(bf16[512,128]{1,0:T(8,128)(2,1)S(1)} %get-tuple-element.36), channel_id=1, source_target_pairs={{0,8},{4,0},{8,12},{12,4},{1,9},{5,1},{9,13},{13,5},{2,10},{6,2},{... | collective-permute-start | bytes 393224 | tf_op jit(solution)/shard_map/ppermute | solution.py:53
  14.2 11.8 %collective-permute-start.5 = (bf16[512,128]{1,0:T(8,128)(2,1)S(1)}, bf16[512,128]{1,0:T(8,128)(2,1)S(1)}, u32[]{:S(2)}, u32[]{:S(2)}) collective-permute-start(bf16[512,128]{1,0:T(8,128)(2,1)S(1)} %get-tuple-element.37), channel_id=1, source_target_pairs={{0,8},{4,0},{8,12},{12,4},{1,9},{5,1},{9,13},{13,5},{2,10},{6,2},{... | collective-permute-start | bytes 393224 | tf_op jit(solution)/shard_map/ppermute | solution.py:53
  20.2 11.0 %collective-permute-start.1 = (bf16[1,136,256]{2,1,0:T(8,128)(2,1)S(1)}, bf16[1,136,256]{2,1,0:T(8,128)(2,1)S(1)}, u32[]{:S(2)}, u32[]{:S(2)}) collective-permute-start(bf16[1,136,256]{2,1,0:T(8,128)(2,1)S(1)} %get-tuple-element.31), channel_id=1, source_target_pairs={{0,12},{4,8},{8,4},{12,0},{1,13},{5,9},{9,5},{13,1},{2,14},{6,10},... | collective-permute-start | bytes 208904 | tf_op jit(solution)/shard_map/ppermute | solution.py:48

commit v23 on v22

--- a/solution.py
+++ b/solution.py
@@ -21,25 +21,23 @@
 SMEM = pl.BlockSpec(memory_space=pltpu.SMEM)
 
 
-def inner(device, count):
-    return (device ^ (device // (count // 2))) & 1
-
-
 def partner(device, k, count):
     far = count // 2
+    upper = device // far
     if k == far:
-        return device ^ (1 + inner(device, count) * (far - 1))
-    if k == 1:
-        return device ^ (far - inner(device, count) * (far - 1))
+        return device ^ (far + upper)
+    if k == far + 1:
+        return device ^ (far + 1 - upper)
     return device ^ k
 
 
 def source(device, k, count):
     far = count // 2
+    upper = device // far
     if k == far:
-        return device ^ (far - inner(device, count) * (far - 1))
-    if k == 1:
-        return device ^ (1 + inner(device, count) * (far - 1))
+        return device ^ (far + 1 - upper)
+    if k == far + 1:
+        return device ^ (far + upper)
     return device ^ k
 
 
@@ -55,7 +53,7 @@
 
 def messages(count, capacity):
     half = capacity // 2
-    ahead = [(k, 0, capacity) for k in range(count // 2, count)]
+    ahead = [(k, 0, capacity) for k in reversed(range(count // 2, count))]
     behind = [(k, first, half) for k in reversed(range(1, count // 2)) for first in (0, half)]
     return ahead, behind, [(0, 0, capacity)]
 

time: 32.3 us -> 35 us (1.084)
  the two profiles are of different devices: /device:TPU:20 before, /device:TPU:0 now
where the time goes in v23:
time: 35 us; the launch traced here: 34.8 us
  waiting for transfers between devices  13 us (37%)
  Pallas kernels  12.8 us (37%)
  starting transfers between devices  8.23 us (24%)
  between operations  0.69 us (2%)
    ppermute x4, starting transfers between devices, hand(): lax.ppermute(message, 'seq', [(i, partner(i, k, count)) for i in range(co...  7.19 us
    ppermute x2, waiting for transfers between devices, exchange(): return lax.ppermute(message, 'seq', [(i, i ^ k) for i in range(count)])  7.06 us
    ppermute x4, waiting for transfers between devices, hand(): lax.ppermute(message, 'seq', [(i, partner(i, k, count)) for i in range(co...  5.98 us
    pallas_call x1, Pallas kernels, per_device(): pl.pallas_call(first_kernel, out_shape=[leaving(senders), jax.ShapeDtypeS...  5.25 us
    pallas_call x2, Pallas kernels, place(): pl.pallas_call(functools.partial(place_kernel, plan), out_shape=[jax.Shap...  3.09 us
    pallas_call x1, Pallas kernels, per_device(): pl.pallas_call(second_kernel, out_shape=staying(senders), in_specs=[VMEM]...  2.7 us
    ppermute x2, starting transfers between devices, exchange(): return lax.ppermute(message, 'seq', [(i, i ^ k) for i in range(count)])  1.03 us
    pallas_call x1, Pallas kernels, per_device(): pl.pallas_call(functools.partial(finish_kernel, ahead[1:] + behind), out_...  0.89 us
  transfers between devices with their start and end apart: 6, of which 3 were waited for; matrix products, arithmetic and copies ran while one was open for 0% of the time, Pallas kernels for 30%

profile of v23, /device:TPU:0, one launch (start us, length us, event | category | flops | bytes accessed | tf_op | source)
XLA Modules:
  0.0 34.8 jit_solution(10598942694514834257)
XLA Ops:
  0.6 1.6 %place.2 = (bf16[1024,128]{1,0:T(8,128)(2,1)S(1)}, bf16[1024,128]{1,0:T(8,128)(2,1)S(1)}) custom-call(s32[128]{0:T(128)} %owner_any.3, bf16[4096,128]{1,0:T(8,128)(2,1)} %bitcast.14, f32[256,128]{1,0:T(8,128)} %bitcast.18, f32[2,128]{1,0:T(2,128)} %scales_any.3), custom_call_target="tpu_custom_call" | custom-call | tf_op jit(solution)/shard_map/place/pallas_call | solution.py:384
  2.2 5.1 %collective-permute-start.2 = (bf16[1024,128]{1,0:T(8,128)(2,1)S(1)}, bf16[1024,128]{1,0:T(8,128)(2,1)S(1)}, u32[]{:S(2)}, u32[]{:S(2)}) collective-permute-start(bf16[1024,128]{1,0:T(8,128)(2,1)S(1)} %get-tuple-element.32), channel_id=1, source_target_pairs={{0,12},{4,8},{8,0},{12,4},{1,13},{5,9},{9,1},{13,5},{2,14},{6,10},... | collective-permute-start | bytes 786440 | tf_op jit(solution)/shard_map/ppermute | solution.py:51
  7.3 0.0 collective-permute-start.3
  7.3 5.2 %attend_leaving.1 = (bf16[2,136,256]{2,1,0:T(8,128)(2,1)S(1)}, bf16[2048,256]{1,0:T(8,128)(2,1)S(1)}, bf16[128,2048]{1,0:T(8,128)(2,1)S(1)}, bf16[1024,256]{1,0:T(8,128)(2,1)S(1)}, f32[136,256]{1,0:T(8,128)S(1)}) custom-call(bf16[4096,128]{1,0:T(8,128)(2,1)} %bitcast.15, f32[256,128]{1,0:T(8,128)} %bitcast.19, f32[2,128]{1,0:T(2,128)} %scales_any.3, ...), custom_call_target="tpu_custom_call" | custom-call | tf_op jit(solution)/shard_map/attend_leaving/pallas_call | solution.py:414
  12.6 1.0 %collective-permute-start = (bf16[2,136,256]{2,1,0:T(8,128)(2,1)S(1)}, bf16[2,136,256]{2,1,0:T(8,128)(2,1)S(1)}, u32[]{:S(2)}, u32[]{:S(2)}) collective-permute-start(bf16[2,136,256]{2,1,0:T(8,128)(2,1)S(1)} %get-tuple-element.29), channel_id=1, source_target_pairs={{0,4},{4,0},{8,12},{12,8},{1,5},{5,1},{9,13},{13,9},{2,6},{6,2},{1... | collective-permute-start | bytes 417800 | tf_op jit(solution)/shard_map/ppermute | solution.py:46
  13.5 1.5 %place.3 = (bf16[512,128]{1,0:T(8,128)(2,1)S(1)}, bf16[512,128]{1,0:T(8,128)(2,1)S(1)}, bf16[1024,128]{1,0:T(8,128)(2,1)S(1)}) custom-call(s32[128]{0:T(128)} %owner_any.3, bf16[4096,128]{1,0:T(8,128)(2,1)} %bitcast.16, f32[256,128]{1,0:T(8,128)} %bitcast.20, f32[2,128]{1,0:T(2,128)} %scales_any.3), custom_call_target="tpu_custom_call" | custom-call | tf_op jit(solution)/shard_map/place/pallas_call | solution.py:384
  15.1 1.2 %collective-permute-start.4 = (bf16[512,128]{1,0:T(8,128)(2,1)S(1)}, bf16[512,128]{1,0:T(8,128)(2,1)S(1)}, u32[]{:S(2)}, u32[]{:S(2)}) collective-permute-start(bf16[512,128]{1,0:T(8,128)(2,1)S(1)} %get-tuple-element.36), channel_id=1, source_target_pairs={{0,4},{4,0},{8,12},{12,8},{1,5},{5,1},{9,13},{13,9},{2,6},{6,2},{1... | collective-permute-start | bytes 393224 | tf_op jit(solution)/shard_map/ppermute | solution.py:51
  16.2 0.9 %collective-permute-start.5 = (bf16[512,128]{1,0:T(8,128)(2,1)S(1)}, bf16[512,128]{1,0:T(8,128)(2,1)S(1)}, u32[]{:S(2)}, u32[]{:S(2)}) collective-permute-start(bf16[512,128]{1,0:T(8,128)(2,1)S(1)} %get-tuple-element.37), channel_id=1, source_target_pairs={{0,4},{4,0},{8,12},{12,8},{1,5},{5,1},{9,13},{13,9},{2,6},{6,2},{1... | collective-permute-start | bytes 393224 | tf_op jit(solution)/shard_map/ppermute | solution.py:51
  17.1 2.7 %attend_staying.1.keep_ref = f32[2,136,256]{2,1,0:T(8,128)S(1)} custom-call(bf16[2048,256]{1,0:T(8,128)(2,1)S(1)} %get-tuple-element.24.keys_ref, bf16[128,2048]{1,0:T(8,128)(2,1)S(1)} %get-tuple-element.25.turned_ref, bf16[1024,256]{1,0:T(8,128)(2,1)S(1)} %get-tuple-element.26.asked_ref, f32[136,256]{1,0:T(8,128)S(1)} %get-tuple-element.27.own_ref), custom_call_target="tpu_custom_call" | custom-call | tf_op jit(solution)/shard_map/attend_staying/pallas_call | solution.py:443
  19.9 7.1 %collective-permute-done.got_ref = bf16[2,136,256]{2,1,0:T(8,128)(2,1)S(1)} collective-permute-done((bf16[2,136,256]{2,1,0:T(8,128)(2,1)S(1)}, bf16[2,136,256]{2,1,0:T(8,128)(2,1)S(1)}, u32[]{:S(2)}, u32[]{:S(2)}) %collective-permute-start) | collective-permute-done | bytes 139296 | tf_op jit(solution)/shard_map/ppermute | solution.py:46
  26.9 0.1 join.1
  27.0 0.1 collective-permute-start.1
  27.1 0.0 collective-permute-done.2.refs_0_
  27.1 0.8 %settle.1._ = bf16[4096,128]{1,0:T(8,128)(2,1)} custom-call(bf16[1024,128]{1,0:T(8,128)(2,1)S(1)} %collective-permute-done.2.refs_0_, bf16[1024,128]{1,0:T(8,128)(2,1)S(1)} %get-tuple-element.34.refs_1_), custom_call_target="tpu_custom_call" | custom-call | tf_op jit(solution)/shard_map/settle/pallas_call | solution.py:463
  27.9 1.8 %collective-permute-done.4.refs_1_ = bf16[512,128]{1,0:T(8,128)(2,1)S(1)} collective-permute-done((bf16[512,128]{1,0:T(8,128)(2,1)S(1)}, bf16[512,128]{1,0:T(8,128)(2,1)S(1)}, u32[]{:S(2)}, u32[]{:S(2)}) %collective-permute-start.4) | collective-permute-done | bytes 131104 | tf_op jit(solution)/shard_map/ppermute | solution.py:51
  29.7 4.2 %collective-permute-done.5.refs_2_ = bf16[512,128]{1,0:T(8,128)(2,1)S(1)} collective-permute-done((bf16[512,128]{1,0:T(8,128)(2,1)S(1)}, bf16[512,128]{1,0:T(8,128)(2,1)S(1)}, u32[]{:S(2)}, u32[]{:S(2)}) %collective-permute-start.5) | collective-permute-done | bytes 131104 | tf_op jit(solution)/shard_map/ppermute | solution.py:51
  33.9 0.0 collective-permute-done.1.got_ref
  33.9 0.0 collective-permute-done.3.refs_0_
  33.9 0.9 %finish.1 = (bf16[256,128]{1,0:T(8,128)(2,1)}, bf16[4096,128]{1,0:T(8,128)(2,1)}) custom-call(f32[1,136,256]{2,1,0:T(8,128)S(1)} %get-tuple-element.30.keep_ref, bf16[1,136,256]{2,1,0:T(8,128)(2,1)S(1)} %collective-permute-done.1.got_ref, bf16[4096,128]{1,0:T(8,128)(2,1)} %settle.1._, ...), custom_call_target="tpu_custom_call", output_to_operand_aliasing={{1}: (2, {})} | custom-call | tf_op jit(solution)/shard_map/finish/pallas_call | solution.py:472
Async XLA Ops:
  2.2 24.9 %collective-permute-start.2 = (bf16[1024,128]{1,0:T(8,128)(2,1)S(1)}, bf16[1024,128]{1,0:T(8,128)(2,1)S(1)}, u32[]{:S(2)}, u32[]{:S(2)}) collective-permute-start(bf16[1024,128]{1,0:T(8,128)(2,1)S(1)} %get-tuple-element.32), channel_id=1, source_target_pairs={{0,12},{4,8},{8,0},{12,4},{1,13},{5,9},{9,1},{13,5},{2,14},{6,10},... | collective-permute-start | bytes 786440 | tf_op jit(solution)/shard_map/ppermute | solution.py:51
  7.3 26.6 %collective-permute-start.3 = (bf16[1024,128]{1,0:T(8,128)(2,1)S(1)}, bf16[1024,128]{1,0:T(8,128)(2,1)S(1)}, u32[]{:S(2)}, u32[]{:S(2)}) collective-permute-start(bf16[1024,128]{1,0:T(8,128)(2,1)S(1)} %get-tuple-element.35), channel_id=1, source_target_pairs={{0,8},{4,12},{8,4},{12,0},{1,9},{5,13},{9,5},{13,1},{2,10},{6,14},... | collective-permute-start | bytes 786440 | tf_op jit(solution)/shard_map/ppermute | solution.py:51
  12.6 14.4 %collective-permute-start = (bf16[2,136,256]{2,1,0:T(8,128)(2,1)S(1)}, bf16[2,136,256]{2,1,0:T(8,128)(2,1)S(1)}, u32[]{:S(2)}, u32[]{:S(2)}) collective-permute-start(bf16[2,136,256]{2,1,0:T(8,128)(2,1)S(1)} %get-tuple-element.29), channel_id=1, source_target_pairs={{0,4},{4,0},{8,12},{12,8},{1,5},{5,1},{9,13},{13,9},{2,6},{6,2},{1... | collective-permute-start | bytes 417800 | tf_op jit(solution)/shard_map/ppermute | solution.py:46
  15.1 14.7 %collective-permute-start.4 = (bf16[512,128]{1,0:T(8,128)(2,1)S(1)}, bf16[512,128]{1,0:T(8,128)(2,1)S(1)}, u32[]{:S(2)}, u32[]{:S(2)}) collective-permute-start(bf16[512,128]{1,0:T(8,128)(2,1)S(1)} %get-tuple-element.36), channel_id=1, source_target_pairs={{0,4},{4,0},{8,12},{12,8},{1,5},{5,1},{9,13},{13,9},{2,6},{6,2},{1... | collective-permute-start | bytes 393224 | tf_op jit(solution)/shard_map/ppermute | solution.py:51
  16.2 17.6 %collective-permute-start.5 = (bf16[512,128]{1,0:T(8,128)(2,1)S(1)}, bf16[512,128]{1,0:T(8,128)(2,1)S(1)}, u32[]{:S(2)}, u32[]{:S(2)}) collective-permute-start(bf16[512,128]{1,0:T(8,128)(2,1)S(1)} %get-tuple-element.37), channel_id=1, source_target_pairs={{0,4},{4,0},{8,12},{12,8},{1,5},{5,1},{9,13},{13,9},{2,6},{6,2},{1... | collective-permute-start | bytes 393224 | tf_op jit(solution)/shard_map/ppermute | solution.py:51
  27.0 6.9 %collective-permute-start.1 = (bf16[1,136,256]{2,1,0:T(8,128)(2,1)S(1)}, bf16[1,136,256]{2,1,0:T(8,128)(2,1)S(1)}, u32[]{:S(2)}, u32[]{:S(2)}) collective-permute-start(bf16[1,136,256]{2,1,0:T(8,128)(2,1)S(1)} %get-tuple-element.31), channel_id=1, source_target_pairs={{0,12},{4,8},{8,4},{12,0},{1,13},{5,9},{9,5},{13,1},{2,14},{6,10},... | collective-permute-start | bytes 208904 | tf_op jit(solution)/shard_map/ppermute | solution.py:46

commit v24 on v22

--- a/solution.py
+++ b/solution.py
@@ -55,7 +55,7 @@
 
 def messages(count, capacity):
     half = capacity // 2
-    ahead = [(k, 0, capacity) for k in range(count // 2, count)]
+    ahead = [(k, 0, capacity) for k in reversed(range(count // 2, count))]
     behind = [(k, first, half) for k in reversed(range(1, count // 2)) for first in (0, half)]
     return ahead, behind, [(0, 0, capacity)]
 

time: 32.3 us -> 33 us (1.022)
  the two profiles are of different devices: /device:TPU:20 before, /device:TPU:0 now
where the time goes in v24:
time: 33 us; the launch traced here: 32.8 us
  starting transfers between devices  13.3 us (40%)
  Pallas kernels  12.8 us (39%)
  waiting for transfers between devices  6.02 us (18%)
  between operations  0.68 us (2%)
    ppermute x4, starting transfers between devices, hand(): lax.ppermute(message, 'seq', [(i, partner(i, k, count)) for i in range(co...  9.49 us
    pallas_call x1, Pallas kernels, per_device(): pl.pallas_call(first_kernel, out_shape=[leaving(senders), jax.ShapeDtypeS...  5.24 us
    ppermute x2, starting transfers between devices, exchange(): return lax.ppermute(message, 'seq', [(i, i ^ k) for i in range(count)])  3.82 us
    ppermute x4, waiting for transfers between devices, hand(): lax.ppermute(message, 'seq', [(i, partner(i, k, count)) for i in range(co...  3.72 us
    pallas_call x2, Pallas kernels, place(): pl.pallas_call(functools.partial(place_kernel, plan), out_shape=[jax.Shap...  3.1 us
    pallas_call x1, Pallas kernels, per_device(): pl.pallas_call(second_kernel, out_shape=staying(senders), in_specs=[VMEM]...  2.7 us
    ppermute x2, waiting for transfers between devices, exchange(): return lax.ppermute(message, 'seq', [(i, i ^ k) for i in range(count)])  2.3 us
    pallas_call x1, Pallas kernels, per_device(): pl.pallas_call(functools.partial(finish_kernel, ahead[1:] + behind), out_...  0.89 us
  transfers between devices with their start and end apart: 6, of which 4 were waited for; matrix products, arithmetic and copies ran while one was open for 0% of the time, Pallas kernels for 32%

profile of v24, /device:TPU:0, one launch (start us, length us, event | category | flops | bytes accessed | tf_op | source)
XLA Modules:
  0.0 32.8 jit_solution(4827955118253159947)
XLA Ops:
  0.6 1.6 %place.2 = (bf16[1024,128]{1,0:T(8,128)(2,1)S(1)}, bf16[1024,128]{1,0:T(8,128)(2,1)S(1)}) custom-call(s32[128]{0:T(128)} %owner_any.3, bf16[4096,128]{1,0:T(8,128)(2,1)} %bitcast.14, f32[256,128]{1,0:T(8,128)} %bitcast.18, f32[2,128]{1,0:T(2,128)} %scales_any.3), custom_call_target="tpu_custom_call" | custom-call | tf_op jit(solution)/shard_map/place/pallas_call | solution.py:386
  2.2 5.1 %collective-permute-start.2 = (bf16[1024,128]{1,0:T(8,128)(2,1)S(1)}, bf16[1024,128]{1,0:T(8,128)(2,1)S(1)}, u32[]{:S(2)}, u32[]{:S(2)}) collective-permute-start(bf16[1024,128]{1,0:T(8,128)(2,1)S(1)} %get-tuple-element.32), channel_id=1, source_target_pairs={{0,12},{4,8},{8,4},{12,0},{1,13},{5,9},{9,5},{13,1},{2,14},{6,10},... | collective-permute-start | bytes 786440 | tf_op jit(solution)/shard_map/ppermute | solution.py:53
  7.3 0.0 collective-permute-start.3
  7.3 5.2 %attend_leaving.1 = (bf16[2,136,256]{2,1,0:T(8,128)(2,1)S(1)}, bf16[2048,256]{1,0:T(8,128)(2,1)S(1)}, bf16[128,2048]{1,0:T(8,128)(2,1)S(1)}, bf16[1024,256]{1,0:T(8,128)(2,1)S(1)}, f32[136,256]{1,0:T(8,128)S(1)}) custom-call(bf16[4096,128]{1,0:T(8,128)(2,1)} %bitcast.15, f32[256,128]{1,0:T(8,128)} %bitcast.19, f32[2,128]{1,0:T(2,128)} %scales_any.3, ...), custom_call_target="tpu_custom_call" | custom-call | tf_op jit(solution)/shard_map/attend_leaving/pallas_call | solution.py:416
  12.6 0.7 %collective-permute-start = (bf16[2,136,256]{2,1,0:T(8,128)(2,1)S(1)}, bf16[2,136,256]{2,1,0:T(8,128)(2,1)S(1)}, u32[]{:S(2)}, u32[]{:S(2)}) collective-permute-start(bf16[2,136,256]{2,1,0:T(8,128)(2,1)S(1)} %get-tuple-element.29), channel_id=1, source_target_pairs={{0,4},{4,0},{8,12},{12,8},{1,5},{5,1},{9,13},{13,9},{2,6},{6,2},{1... | collective-permute-start | bytes 417800 | tf_op jit(solution)/shard_map/ppermute | solution.py:48
  13.3 1.5 %place.3 = (bf16[512,128]{1,0:T(8,128)(2,1)S(1)}, bf16[512,128]{1,0:T(8,128)(2,1)S(1)}, bf16[1024,128]{1,0:T(8,128)(2,1)S(1)}) custom-call(s32[128]{0:T(128)} %owner_any.3, bf16[4096,128]{1,0:T(8,128)(2,1)} %bitcast.16, f32[256,128]{1,0:T(8,128)} %bitcast.20, f32[2,128]{1,0:T(2,128)} %scales_any.3), custom_call_target="tpu_custom_call" | custom-call | tf_op jit(solution)/shard_map/place/pallas_call | solution.py:386
  14.8 2.4 %collective-permute-start.4 = (bf16[512,128]{1,0:T(8,128)(2,1)S(1)}, bf16[512,128]{1,0:T(8,128)(2,1)S(1)}, u32[]{:S(2)}, u32[]{:S(2)}) collective-permute-start(bf16[512,128]{1,0:T(8,128)(2,1)S(1)} %get-tuple-element.36), channel_id=1, source_target_pairs={{0,8},{4,0},{8,12},{12,4},{1,9},{5,1},{9,13},{13,5},{2,10},{6,2},{... | collective-permute-start | bytes 393224 | tf_op jit(solution)/shard_map/ppermute | solution.py:53
  17.2 2.0 %collective-permute-start.5 = (bf16[512,128]{1,0:T(8,128)(2,1)S(1)}, bf16[512,128]{1,0:T(8,128)(2,1)S(1)}, u32[]{:S(2)}, u32[]{:S(2)}) collective-permute-start(bf16[512,128]{1,0:T(8,128)(2,1)S(1)} %get-tuple-element.37), channel_id=1, source_target_pairs={{0,8},{4,0},{8,12},{12,4},{1,9},{5,1},{9,13},{13,5},{2,10},{6,2},{... | collective-permute-start | bytes 393224 | tf_op jit(solution)/shard_map/ppermute | solution.py:53
  19.2 2.7 %attend_staying.1.keep_ref = f32[2,136,256]{2,1,0:T(8,128)S(1)} custom-call(bf16[2048,256]{1,0:T(8,128)(2,1)S(1)} %get-tuple-element.24.keys_ref, bf16[128,2048]{1,0:T(8,128)(2,1)S(1)} %get-tuple-element.25.turned_ref, bf16[1024,256]{1,0:T(8,128)(2,1)S(1)} %get-tuple-element.26.asked_ref, f32[136,256]{1,0:T(8,128)S(1)} %get-tuple-element.27.own_ref), custom_call_target="tpu_custom_call" | custom-call | tf_op jit(solution)/shard_map/attend_staying/pallas_call | solution.py:445
  21.9 0.8 %collective-permute-done.got_ref = bf16[2,136,256]{2,1,0:T(8,128)(2,1)S(1)} collective-permute-done((bf16[2,136,256]{2,1,0:T(8,128)(2,1)S(1)}, bf16[2,136,256]{2,1,0:T(8,128)(2,1)S(1)}, u32[]{:S(2)}, u32[]{:S(2)}) %collective-permute-start) | collective-permute-done | bytes 139296 | tf_op jit(solution)/shard_map/ppermute | solution.py:48
  22.6 0.1 join.1
  22.7 3.1 %collective-permute-start.1 = (bf16[1,136,256]{2,1,0:T(8,128)(2,1)S(1)}, bf16[1,136,256]{2,1,0:T(8,128)(2,1)S(1)}, u32[]{:S(2)}, u32[]{:S(2)}) collective-permute-start(bf16[1,136,256]{2,1,0:T(8,128)(2,1)S(1)} %get-tuple-element.31), channel_id=1, source_target_pairs={{0,12},{4,8},{8,4},{12,0},{1,13},{5,9},{9,5},{13,1},{2,14},{6,10},... | collective-permute-start | bytes 208904 | tf_op jit(solution)/shard_map/ppermute | solution.py:48
  25.8 0.0 collective-permute-done.2.refs_0_
  25.8 0.8 %settle.1._ = bf16[4096,128]{1,0:T(8,128)(2,1)} custom-call(bf16[1024,128]{1,0:T(8,128)(2,1)S(1)} %collective-permute-done.2.refs_0_, bf16[1024,128]{1,0:T(8,128)(2,1)S(1)} %get-tuple-element.34.refs_1_), custom_call_target="tpu_custom_call" | custom-call | tf_op jit(solution)/shard_map/settle/pallas_call | solution.py:465
  26.7 0.0 collective-permute-done.4.refs_1_
  26.7 1.3 %collective-permute-done.5.refs_2_ = bf16[512,128]{1,0:T(8,128)(2,1)S(1)} collective-permute-done((bf16[512,128]{1,0:T(8,128)(2,1)S(1)}, bf16[512,128]{1,0:T(8,128)(2,1)S(1)}, u32[]{:S(2)}, u32[]{:S(2)}) %collective-permute-start.5) | collective-permute-done | bytes 131104 | tf_op jit(solution)/shard_map/ppermute | solution.py:53
  27.9 1.5 %collective-permute-done.1.got_ref = bf16[1,136,256]{2,1,0:T(8,128)(2,1)S(1)} collective-permute-done((bf16[1,136,256]{2,1,0:T(8,128)(2,1)S(1)}, bf16[1,136,256]{2,1,0:T(8,128)(2,1)S(1)}, u32[]{:S(2)}, u32[]{:S(2)}) %collective-permute-start.1) | collective-permute-done | bytes 69664 | tf_op jit(solution)/shard_map/ppermute | solution.py:48
  29.5 2.4 %collective-permute-done.3.refs_0_ = bf16[1024,128]{1,0:T(8,128)(2,1)S(1)} collective-permute-done((bf16[1024,128]{1,0:T(8,128)(2,1)S(1)}, bf16[1024,128]{1,0:T(8,128)(2,1)S(1)}, u32[]{:S(2)}, u32[]{:S(2)}) %collective-permute-start.3) | collective-permute-done | bytes 262176 | tf_op jit(solution)/shard_map/ppermute | solution.py:53
  31.9 0.9 %finish.1 = (bf16[256,128]{1,0:T(8,128)(2,1)}, bf16[4096,128]{1,0:T(8,128)(2,1)}) custom-call(f32[1,136,256]{2,1,0:T(8,128)S(1)} %get-tuple-element.30.keep_ref, bf16[1,136,256]{2,1,0:T(8,128)(2,1)S(1)} %collective-permute-done.1.got_ref, bf16[4096,128]{1,0:T(8,128)(2,1)} %settle.1._, ...), custom_call_target="tpu_custom_call", output_to_operand_aliasing={{1}: (2, {})} | custom-call | tf_op jit(solution)/shard_map/finish/pallas_call | solution.py:474
Async XLA Ops:
  2.2 23.6 %collective-permute-start.2 = (bf16[1024,128]{1,0:T(8,128)(2,1)S(1)}, bf16[1024,128]{1,0:T(8,128)(2,1)S(1)}, u32[]{:S(2)}, u32[]{:S(2)}) collective-permute-start(bf16[1024,128]{1,0:T(8,128)(2,1)S(1)} %get-tuple-element.32), channel_id=1, source_target_pairs={{0,12},{4,8},{8,4},{12,0},{1,13},{5,9},{9,5},{13,1},{2,14},{6,10},... | collective-permute-start | bytes 786440 | tf_op jit(solution)/shard_map/ppermute | solution.py:53
  7.3 24.6 %collective-permute-start.3 = (bf16[1024,128]{1,0:T(8,128)(2,1)S(1)}, bf16[1024,128]{1,0:T(8,128)(2,1)S(1)}, u32[]{:S(2)}, u32[]{:S(2)}) collective-permute-start(bf16[1024,128]{1,0:T(8,128)(2,1)S(1)} %get-tuple-element.35), channel_id=1, source_target_pairs={{0,4},{4,12},{8,0},{12,8},{1,5},{5,13},{9,1},{13,9},{2,6},{6,14},{... | collective-permute-start | bytes 786440 | tf_op jit(solution)/shard_map/ppermute | solution.py:53
  12.6 10.1 %collective-permute-start = (bf16[2,136,256]{2,1,0:T(8,128)(2,1)S(1)}, bf16[2,136,256]{2,1,0:T(8,128)(2,1)S(1)}, u32[]{:S(2)}, u32[]{:S(2)}) collective-permute-start(bf16[2,136,256]{2,1,0:T(8,128)(2,1)S(1)} %get-tuple-element.29), channel_id=1, source_target_pairs={{0,4},{4,0},{8,12},{12,8},{1,5},{5,1},{9,13},{13,9},{2,6},{6,2},{1... | collective-permute-start | bytes 417800 | tf_op jit(solution)/shard_map/ppermute | solution.py:48
  14.8 11.9 %collective-permute-start.4 = (bf16[512,128]{1,0:T(8,128)(2,1)S(1)}, bf16[512,128]{1,0:T(8,128)(2,1)S(1)}, u32[]{:S(2)}, u32[]{:S(2)}) collective-permute-start(bf16[512,128]{1,0:T(8,128)(2,1)S(1)} %get-tuple-element.36), channel_id=1, source_target_pairs={{0,8},{4,0},{8,12},{12,4},{1,9},{5,1},{9,13},{13,5},{2,10},{6,2},{... | collective-permute-start | bytes 393224 | tf_op jit(solution)/shard_map/ppermute | solution.py:53
  17.2 10.8 %collective-permute-start.5 = (bf16[512,128]{1,0:T(8,128)(2,1)S(1)}, bf16[512,128]{1,0:T(8,128)(2,1)S(1)}, u32[]{:S(2)}, u32[]{:S(2)}) collective-permute-start(bf16[512,128]{1,0:T(8,128)(2,1)S(1)} %get-tuple-element.37), channel_id=1, source_target_pairs={{0,8},{4,0},{8,12},{12,4},{1,9},{5,1},{9,13},{13,5},{2,10},{6,2},{... | collective-permute-start | bytes 393224 | tf_op jit(solution)/shard_map/ppermute | solution.py:53
  22.7 6.8 %collective-permute-start.1 = (bf16[1,136,256]{2,1,0:T(8,128)(2,1)S(1)}, bf16[1,136,256]{2,1,0:T(8,128)(2,1)S(1)}, u32[]{:S(2)}, u32[]{:S(2)}) collective-permute-start(bf16[1,136,256]{2,1,0:T(8,128)(2,1)S(1)} %get-tuple-element.31), channel_id=1, source_target_pairs={{0,12},{4,8},{8,4},{12,0},{1,13},{5,9},{9,5},{13,1},{2,14},{6,10},... | collective-permute-start | bytes 208904 | tf_op jit(solution)/shard_map/ppermute | solution.py:48

commit v25 on v24

--- a/solution.py
+++ b/solution.py
@@ -21,25 +21,23 @@
 SMEM = pl.BlockSpec(memory_space=pltpu.SMEM)
 
 
-def inner(device, count):
-    return (device ^ (device // (count // 2))) & 1
-
-
 def partner(device, k, count):
     far = count // 2
-    if k == far:
-        return device ^ (1 + inner(device, count) * (far - 1))
+    odd = device & 1
+    if k == far + 1:
+        return device ^ (1 + odd * far)
     if k == 1:
-        return device ^ (far - inner(device, count) * (far - 1))
+        return device ^ (1 + (1 - odd) * far)
     return device ^ k
 
 
 def source(device, k, count):
     far = count // 2
-    if k == far:
-        return device ^ (far - inner(device, count) * (far - 1))
+    odd = device & 1
+    if k == far + 1:
+        return device ^ (1 + (1 - odd) * far)
     if k == 1:
-        return device ^ (1 + inner(device, count) * (far - 1))
+        return device ^ (1 + odd * far)
     return device ^ k
 
 

time: 33 us -> 32.7 us (level)
  starting transfers between devices: 13.3 us -> 9.23 us
  waiting for transfers between devices: 6.02 us -> 9.76 us
    ppermute x2, waiting for transfers between devices: 2.3 us -> 5.9 us  [exchange(): return lax.ppermute(message, 'seq', [(i, i ^ k) for i in range(count)])]
    ppermute x2, starting transfers between devices: 3.82 us -> 0.21 us  [exchange(): return lax.ppermute(message, 'seq', [(i, i ^ k) for i in range(count)])]
    ppermute x4, starting transfers between devices: 9.49 us -> 9.01 us  [hand(): lax.ppermute(message, 'seq', [(i, partner(i, k, count)) for i in range(co...]
where the time goes in v25:
time: 32.7 us; the launch traced here: 32.5 us
  Pallas kernels  12.8 us (39%)
  waiting for transfers between devices  9.76 us (30%)
  starting transfers between devices  9.23 us (28%)
  between operations  0.69 us (2%)
    ppermute x4, starting transfers between devices, hand(): lax.ppermute(message, 'seq', [(i, partner(i, k, count)) for i in range(co...  9.01 us
    ppermute x2, waiting for transfers between devices, exchange(): return lax.ppermute(message, 'seq', [(i, i ^ k) for i in range(count)])  5.9 us
    pallas_call x1, Pallas kernels, per_device(): pl.pallas_call(first_kernel, out_shape=[leaving(senders), jax.ShapeDtypeS...  5.24 us
    ppermute x4, waiting for transfers between devices, hand(): lax.ppermute(message, 'seq', [(i, partner(i, k, count)) for i in range(co...  3.86 us
    pallas_call x2, Pallas kernels, place(): pl.pallas_call(functools.partial(place_kernel, plan), out_shape=[jax.Shap...  3.09 us
    pallas_call x1, Pallas kernels, per_device(): pl.pallas_call(second_kernel, out_shape=staying(senders), in_specs=[VMEM]...  2.7 us
    pallas_call x1, Pallas kernels, per_device(): pl.pallas_call(functools.partial(finish_kernel, ahead[1:] + behind), out_...  0.88 us
    pallas_call x1, Pallas kernels, per_device(): pl.pallas_call(functools.partial(settle_kernel, settled), out_shape=whole...  0.82 us
  transfers between devices with their start and end apart: 6, of which 4 were waited for; matrix products, arithmetic and copies ran while one was open for 0% of the time, Pallas kernels for 32%

profile of v25, /device:TPU:0, one launch (start us, length us, event | category | flops | bytes accessed | tf_op | source)
XLA Modules:
  0.0 32.5 jit_solution(8545445183167532155)
XLA Ops:
  0.6 1.6 %place.2 = (bf16[1024,128]{1,0:T(8,128)(2,1)S(1)}, bf16[1024,128]{1,0:T(8,128)(2,1)S(1)}) custom-call(s32[128]{0:T(128)} %owner_any.3, bf16[4096,128]{1,0:T(8,128)(2,1)} %bitcast.14, f32[256,128]{1,0:T(8,128)} %bitcast.18, f32[2,128]{1,0:T(2,128)} %scales_any.3), custom_call_target="tpu_custom_call" | custom-call | tf_op jit(solution)/shard_map/place/pallas_call | solution.py:384
  2.2 3.1 %collective-permute-start.2 = (bf16[1024,128]{1,0:T(8,128)(2,1)S(1)}, bf16[1024,128]{1,0:T(8,128)(2,1)S(1)}, u32[]{:S(2)}, u32[]{:S(2)}) collective-permute-start(bf16[1024,128]{1,0:T(8,128)(2,1)S(1)} %get-tuple-element.32), channel_id=1, source_target_pairs={{0,4},{4,8},{8,12},{12,0},{1,5},{5,9},{9,13},{13,1},{2,6},{6,10},{... | collective-permute-start | bytes 786440 | tf_op jit(solution)/shard_map/ppermute | solution.py:51
  5.3 2.6 %collective-permute-start.3 = (bf16[1024,128]{1,0:T(8,128)(2,1)S(1)}, bf16[1024,128]{1,0:T(8,128)(2,1)S(1)}, u32[]{:S(2)}, u32[]{:S(2)}) collective-permute-start(bf16[1024,128]{1,0:T(8,128)(2,1)S(1)} %get-tuple-element.35), channel_id=1, source_target_pairs={{0,8},{4,12},{8,0},{12,4},{1,9},{5,13},{9,1},{13,5},{2,10},{6,14},... | collective-permute-start | bytes 786440 | tf_op jit(solution)/shard_map/ppermute | solution.py:51
  7.9 5.2 %attend_leaving.1 = (bf16[2,136,256]{2,1,0:T(8,128)(2,1)S(1)}, bf16[2048,256]{1,0:T(8,128)(2,1)S(1)}, bf16[128,2048]{1,0:T(8,128)(2,1)S(1)}, bf16[1024,256]{1,0:T(8,128)(2,1)S(1)}, f32[136,256]{1,0:T(8,128)S(1)}) custom-call(bf16[4096,128]{1,0:T(8,128)(2,1)} %bitcast.15, f32[256,128]{1,0:T(8,128)} %bitcast.19, f32[2,128]{1,0:T(2,128)} %scales_any.3, ...), custom_call_target="tpu_custom_call" | custom-call | tf_op jit(solution)/shard_map/attend_leaving/pallas_call | solution.py:414
  13.1 0.1 collective-permute-start
  13.3 1.5 %place.3 = (bf16[512,128]{1,0:T(8,128)(2,1)S(1)}, bf16[512,128]{1,0:T(8,128)(2,1)S(1)}, bf16[1024,128]{1,0:T(8,128)(2,1)S(1)}) custom-call(s32[128]{0:T(128)} %owner_any.3, bf16[4096,128]{1,0:T(8,128)(2,1)} %bitcast.16, f32[256,128]{1,0:T(8,128)} %bitcast.20, f32[2,128]{1,0:T(2,128)} %scales_any.3), custom_call_target="tpu_custom_call" | custom-call | tf_op jit(solution)/shard_map/place/pallas_call | solution.py:384
  14.8 1.8 %collective-permute-start.4 = (bf16[512,128]{1,0:T(8,128)(2,1)S(1)}, bf16[512,128]{1,0:T(8,128)(2,1)S(1)}, u32[]{:S(2)}, u32[]{:S(2)}) collective-permute-start(bf16[512,128]{1,0:T(8,128)(2,1)S(1)} %get-tuple-element.36), channel_id=1, source_target_pairs={{0,12},{4,0},{8,4},{12,8},{1,13},{5,1},{9,5},{13,9},{2,14},{6,2},{... | collective-permute-start | bytes 393224 | tf_op jit(solution)/shard_map/ppermute | solution.py:51
  16.6 1.6 %collective-permute-start.5 = (bf16[512,128]{1,0:T(8,128)(2,1)S(1)}, bf16[512,128]{1,0:T(8,128)(2,1)S(1)}, u32[]{:S(2)}, u32[]{:S(2)}) collective-permute-start(bf16[512,128]{1,0:T(8,128)(2,1)S(1)} %get-tuple-element.37), channel_id=1, source_target_pairs={{0,12},{4,0},{8,4},{12,8},{1,13},{5,1},{9,5},{13,9},{2,14},{6,2},{... | collective-permute-start | bytes 393224 | tf_op jit(solution)/shard_map/ppermute | solution.py:51
  18.1 2.7 %attend_staying.1.keep_ref = f32[2,136,256]{2,1,0:T(8,128)S(1)} custom-call(bf16[2048,256]{1,0:T(8,128)(2,1)S(1)} %get-tuple-element.24.keys_ref, bf16[128,2048]{1,0:T(8,128)(2,1)S(1)} %get-tuple-element.25.turned_ref, bf16[1024,256]{1,0:T(8,128)(2,1)S(1)} %get-tuple-element.26.asked_ref, f32[136,256]{1,0:T(8,128)S(1)} %get-tuple-element.27.own_ref), custom_call_target="tpu_custom_call" | custom-call | tf_op jit(solution)/shard_map/attend_staying/pallas_call | solution.py:443
  20.9 4.4 %collective-permute-done.got_ref = bf16[2,136,256]{2,1,0:T(8,128)(2,1)S(1)} collective-permute-done((bf16[2,136,256]{2,1,0:T(8,128)(2,1)S(1)}, bf16[2,136,256]{2,1,0:T(8,128)(2,1)S(1)}, u32[]{:S(2)}, u32[]{:S(2)}) %collective-permute-start) | collective-permute-done | bytes 139296 | tf_op jit(solution)/shard_map/ppermute | solution.py:46
  25.2 0.1 join.1
  25.3 0.1 collective-permute-start.1
  25.4 0.0 collective-permute-done.2.refs_0_
  25.4 0.8 %settle.1._ = bf16[4096,128]{1,0:T(8,128)(2,1)} custom-call(bf16[1024,128]{1,0:T(8,128)(2,1)S(1)} %collective-permute-done.2.refs_0_, bf16[1024,128]{1,0:T(8,128)(2,1)S(1)} %get-tuple-element.34.refs_1_), custom_call_target="tpu_custom_call" | custom-call | tf_op jit(solution)/shard_map/settle/pallas_call | solution.py:463
  26.2 2.4 %collective-permute-done.4.refs_1_ = bf16[512,128]{1,0:T(8,128)(2,1)S(1)} collective-permute-done((bf16[512,128]{1,0:T(8,128)(2,1)S(1)}, bf16[512,128]{1,0:T(8,128)(2,1)S(1)}, u32[]{:S(2)}, u32[]{:S(2)}) %collective-permute-start.4) | collective-permute-done | bytes 131104 | tf_op jit(solution)/shard_map/ppermute | solution.py:51
  28.7 1.4 %collective-permute-done.5.refs_2_ = bf16[512,128]{1,0:T(8,128)(2,1)S(1)} collective-permute-done((bf16[512,128]{1,0:T(8,128)(2,1)S(1)}, bf16[512,128]{1,0:T(8,128)(2,1)S(1)}, u32[]{:S(2)}, u32[]{:S(2)}) %collective-permute-start.5) | collective-permute-done | bytes 131104 | tf_op jit(solution)/shard_map/ppermute | solution.py:51
  30.1 1.5 %collective-permute-done.1.got_ref = bf16[1,136,256]{2,1,0:T(8,128)(2,1)S(1)} collective-permute-done((bf16[1,136,256]{2,1,0:T(8,128)(2,1)S(1)}, bf16[1,136,256]{2,1,0:T(8,128)(2,1)S(1)}, u32[]{:S(2)}, u32[]{:S(2)}) %collective-permute-start.1) | collective-permute-done | bytes 69664 | tf_op jit(solution)/shard_map/ppermute | solution.py:46
  31.6 0.0 collective-permute-done.3.refs_0_
  31.6 0.9 %finish.1 = (bf16[256,128]{1,0:T(8,128)(2,1)}, bf16[4096,128]{1,0:T(8,128)(2,1)}) custom-call(f32[1,136,256]{2,1,0:T(8,128)S(1)} %get-tuple-element.30.keep_ref, bf16[1,136,256]{2,1,0:T(8,128)(2,1)S(1)} %collective-permute-done.1.got_ref, bf16[4096,128]{1,0:T(8,128)(2,1)} %settle.1._, ...), custom_call_target="tpu_custom_call", output_to_operand_aliasing={{1}: (2, {})} | custom-call | tf_op jit(solution)/shard_map/finish/pallas_call | solution.py:472
Async XLA Ops:
  2.2 23.2 %collective-permute-start.2 = (bf16[1024,128]{1,0:T(8,128)(2,1)S(1)}, bf16[1024,128]{1,0:T(8,128)(2,1)S(1)}, u32[]{:S(2)}, u32[]{:S(2)}) collective-permute-start(bf16[1024,128]{1,0:T(8,128)(2,1)S(1)} %get-tuple-element.32), channel_id=1, source_target_pairs={{0,4},{4,8},{8,12},{12,0},{1,5},{5,9},{9,13},{13,1},{2,6},{6,10},{... | collective-permute-start | bytes 786440 | tf_op jit(solution)/shard_map/ppermute | solution.py:51
  5.3 26.3 %collective-permute-start.3 = (bf16[1024,128]{1,0:T(8,128)(2,1)S(1)}, bf16[1024,128]{1,0:T(8,128)(2,1)S(1)}, u32[]{:S(2)}, u32[]{:S(2)}) collective-permute-start(bf16[1024,128]{1,0:T(8,128)(2,1)S(1)} %get-tuple-element.35), channel_id=1, source_target_pairs={{0,8},{4,12},{8,0},{12,4},{1,9},{5,13},{9,1},{13,5},{2,10},{6,14},... | collective-permute-start | bytes 786440 | tf_op jit(solution)/shard_map/ppermute | solution.py:51
  13.1 12.1 %collective-permute-start = (bf16[2,136,256]{2,1,0:T(8,128)(2,1)S(1)}, bf16[2,136,256]{2,1,0:T(8,128)(2,1)S(1)}, u32[]{:S(2)}, u32[]{:S(2)}) collective-permute-start(bf16[2,136,256]{2,1,0:T(8,128)(2,1)S(1)} %get-tuple-element.29), channel_id=1, source_target_pairs={{0,4},{4,0},{8,12},{12,8},{1,5},{5,1},{9,13},{13,9},{2,6},{6,2},{1... | collective-permute-start | bytes 417800 | tf_op jit(solution)/shard_map/ppermute | solution.py:46
  14.8 13.9 %collective-permute-start.4 = (bf16[512,128]{1,0:T(8,128)(2,1)S(1)}, bf16[512,128]{1,0:T(8,128)(2,1)S(1)}, u32[]{:S(2)}, u32[]{:S(2)}) collective-permute-start(bf16[512,128]{1,0:T(8,128)(2,1)S(1)} %get-tuple-element.36), channel_id=1, source_target_pairs={{0,12},{4,0},{8,4},{12,8},{1,13},{5,1},{9,5},{13,9},{2,14},{6,2},{... | collective-permute-start | bytes 393224 | tf_op jit(solution)/shard_map/ppermute | solution.py:51
  16.6 13.5 %collective-permute-start.5 = (bf16[512,128]{1,0:T(8,128)(2,1)S(1)}, bf16[512,128]{1,0:T(8,128)(2,1)S(1)}, u32[]{:S(2)}, u32[]{:S(2)}) collective-permute-start(bf16[512,128]{1,0:T(8,128)(2,1)S(1)} %get-tuple-element.37), channel_id=1, source_target_pairs={{0,12},{4,0},{8,4},{12,8},{1,13},{5,1},{9,5},{13,9},{2,14},{6,2},{... | collective-permute-start | bytes 393224 | tf_op jit(solution)/shard_map/ppermute | solution.py:51
  25.3 6.3 %collective-permute-start.1 = (bf16[1,136,256]{2,1,0:T(8,128)(2,1)S(1)}, bf16[1,136,256]{2,1,0:T(8,128)(2,1)S(1)}, u32[]{:S(2)}, u32[]{:S(2)}) collective-permute-start(bf16[1,136,256]{2,1,0:T(8,128)(2,1)S(1)} %get-tuple-element.31), channel_id=1, source_target_pairs={{0,12},{4,8},{8,4},{12,0},{1,13},{5,9},{9,5},{13,1},{2,14},{6,10},... | collective-permute-start | bytes 208904 | tf_op jit(solution)/shard_map/ppermute | solution.py:46

commit v26 on v22

--- a/solution.py
+++ b/solution.py
@@ -10,7 +10,7 @@
 HD = 128
 GQ = 8
 STEPS = 2
-STAT_ROWS = 8
+STAT_ROWS = 16
 KEEP_ROWS = 8
 FAR = -1e30
 RATE = HD ** (-0.5) * 1.4426950408889634
@@ -288,7 +288,7 @@
 
     for load in loads[:2]:
         load.wait()
-    wide_ref[...] = deltas_ref[...].astype(jnp.float32)
+    wide_ref[0 : blocks * rows, :] = deltas_ref[...].astype(jnp.float32)
     scale_key = scales_ref[0:1, :]
     scale_value = scales_ref[1:2, :]
 
@@ -429,7 +429,7 @@
             for array in needed
         ]
         + [
-            pltpu.VMEM((tokens * 2, HD), jnp.float32),
+            pltpu.VMEM((tokens * 2 + 16, HD), jnp.float32),
             pltpu.VMEM((tokens, HD), jnp.bfloat16),
             pltpu.SemaphoreType.DMA((len(needed),)),
         ],

time: 32.3 us -> 32.4 us (level)
  the two profiles are of different devices: /device:TPU:20 before, /device:TPU:16 now
where the time goes in v26:
time: 32.4 us; the launch traced here: 32.3 us
  Pallas kernels  12.7 us (39%)
  waiting for transfers between devices  11.7 us (36%)
  starting transfers between devices  7.13 us (22%)
  between operations  0.68 us (2%)
    ppermute x2, waiting for transfers between devices, exchange(): return lax.ppermute(message, 'seq', [(i, i ^ k) for i in range(count)])  7.12 us
    ppermute x4, starting transfers between devices, hand(): lax.ppermute(message, 'seq', [(i, partner(i, k, count)) for i in range(co...  6.18 us
    pallas_call x1, Pallas kernels, per_device(): pl.pallas_call(first_kernel, out_shape=[leaving(senders), jax.ShapeDtypeS...  5.23 us
    ppermute x4, waiting for transfers between devices, hand(): lax.ppermute(message, 'seq', [(i, partner(i, k, count)) for i in range(co...  4.57 us
    pallas_call x2, Pallas kernels, place(): pl.pallas_call(functools.partial(place_kernel, plan), out_shape=[jax.Shap...  3.09 us
    pallas_call x1, Pallas kernels, per_device(): pl.pallas_call(second_kernel, out_shape=staying(senders), in_specs=[VMEM]...  2.67 us
    ppermute x2, starting transfers between devices, exchange(): return lax.ppermute(message, 'seq', [(i, i ^ k) for i in range(count)])  0.96 us
    pallas_call x1, Pallas kernels, per_device(): pl.pallas_call(functools.partial(finish_kernel, ahead[1:] + behind), out_...  0.88 us
  transfers between devices with their start and end apart: 6, of which 4 were waited for; matrix products, arithmetic and copies ran while one was open for 0% of the time, Pallas kernels for 32%

profile of v26, /device:TPU:16, one launch (start us, length us, event | category | flops | bytes accessed | tf_op | source)
XLA Modules:
  0.0 32.3 jit_solution(5983528727620491114)
XLA Ops:
  0.6 1.6 %place.2 = (bf16[1024,128]{1,0:T(8,128)(2,1)S(1)}, bf16[1024,128]{1,0:T(8,128)(2,1)S(1)}) custom-call(s32[128]{0:T(128)} %owner_any.3, bf16[4096,128]{1,0:T(8,128)(2,1)} %bitcast.14, f32[256,128]{1,0:T(8,128)} %bitcast.18, f32[2,128]{1,0:T(2,128)} %scales_any.3), custom_call_target="tpu_custom_call" | custom-call | tf_op jit(solution)/shard_map/place/pallas_call | solution.py:386
  2.2 0.1 collective-permute-start.2
  2.3 3.0 %collective-permute-start.3 = (bf16[1024,128]{1,0:T(8,128)(2,1)S(1)}, bf16[1024,128]{1,0:T(8,128)(2,1)S(1)}, u32[]{:S(2)}, u32[]{:S(2)}) collective-permute-start(bf16[1024,128]{1,0:T(8,128)(2,1)S(1)} %get-tuple-element.35), channel_id=1, source_target_pairs={{0,12},{4,8},{8,4},{12,0},{1,13},{5,9},{9,5},{13,1},{2,14},{6,10},... | collective-permute-start | bytes 786440 | tf_op jit(solution)/shard_map/ppermute | solution.py:53
  5.3 5.2 %attend_leaving.1 = (bf16[2,144,256]{2,1,0:T(8,128)(2,1)S(1)}, bf16[2048,256]{1,0:T(8,128)(2,1)S(1)}, bf16[128,2048]{1,0:T(8,128)(2,1)S(1)}, bf16[1024,256]{1,0:T(8,128)(2,1)S(1)}, f32[136,256]{1,0:T(8,128)S(1)}) custom-call(bf16[4096,128]{1,0:T(8,128)(2,1)} %bitcast.15, f32[256,128]{1,0:T(8,128)} %bitcast.19, f32[2,128]{1,0:T(2,128)} %scales_any.3, ...), custom_call_target="tpu_custom_call" | custom-call | tf_op jit(solution)/shard_map/attend_leaving/pallas_call | solution.py:416
  10.5 0.4 %collective-permute-start = (bf16[2,144,256]{2,1,0:T(8,128)(2,1)S(1)}, bf16[2,144,256]{2,1,0:T(8,128)(2,1)S(1)}, u32[]{:S(2)}, u32[]{:S(2)}) collective-permute-start(bf16[2,144,256]{2,1,0:T(8,128)(2,1)S(1)} %get-tuple-element.29), channel_id=1, source_target_pairs={{0,4},{4,0},{8,12},{12,8},{1,5},{5,1},{9,13},{13,9},{2,6},{6,2},{1... | collective-permute-start | bytes 442376 | tf_op jit(solution)/shard_map/ppermute | solution.py:48
  10.9 1.5 %place.3 = (bf16[512,128]{1,0:T(8,128)(2,1)S(1)}, bf16[512,128]{1,0:T(8,128)(2,1)S(1)}, bf16[1024,128]{1,0:T(8,128)(2,1)S(1)}) custom-call(s32[128]{0:T(128)} %owner_any.3, bf16[4096,128]{1,0:T(8,128)(2,1)} %bitcast.16, f32[256,128]{1,0:T(8,128)} %bitcast.20, f32[2,128]{1,0:T(2,128)} %scales_any.3), custom_call_target="tpu_custom_call" | custom-call | tf_op jit(solution)/shard_map/place/pallas_call | solution.py:386
  12.5 1.7 %collective-permute-start.4 = (bf16[512,128]{1,0:T(8,128)(2,1)S(1)}, bf16[512,128]{1,0:T(8,128)(2,1)S(1)}, u32[]{:S(2)}, u32[]{:S(2)}) collective-permute-start(bf16[512,128]{1,0:T(8,128)(2,1)S(1)} %get-tuple-element.36), channel_id=1, source_target_pairs={{0,8},{4,0},{8,12},{12,4},{1,9},{5,1},{9,13},{13,5},{2,10},{6,2},{... | collective-permute-start | bytes 393224 | tf_op jit(solution)/shard_map/ppermute | solution.py:53
  14.2 1.3 %collective-permute-start.5 = (bf16[512,128]{1,0:T(8,128)(2,1)S(1)}, bf16[512,128]{1,0:T(8,128)(2,1)S(1)}, u32[]{:S(2)}, u32[]{:S(2)}) collective-permute-start(bf16[512,128]{1,0:T(8,128)(2,1)S(1)} %get-tuple-element.37), channel_id=1, source_target_pairs={{0,8},{4,0},{8,12},{12,4},{1,9},{5,1},{9,13},{13,5},{2,10},{6,2},{... | collective-permute-start | bytes 393224 | tf_op jit(solution)/shard_map/ppermute | solution.py:53
  15.6 2.7 %attend_staying.1.keep_ref = f32[2,136,256]{2,1,0:T(8,128)S(1)} custom-call(bf16[2048,256]{1,0:T(8,128)(2,1)S(1)} %get-tuple-element.24.keys_ref, bf16[128,2048]{1,0:T(8,128)(2,1)S(1)} %get-tuple-element.25.turned_ref, bf16[1024,256]{1,0:T(8,128)(2,1)S(1)} %get-tuple-element.26.asked_ref, f32[136,256]{1,0:T(8,128)S(1)} %get-tuple-element.27.own_ref), custom_call_target="tpu_custom_call" | custom-call | tf_op jit(solution)/shard_map/attend_staying/pallas_call | solution.py:445
  18.2 2.0 %collective-permute-done.got_ref = bf16[2,144,256]{2,1,0:T(8,128)(2,1)S(1)} collective-permute-done((bf16[2,144,256]{2,1,0:T(8,128)(2,1)S(1)}, bf16[2,144,256]{2,1,0:T(8,128)(2,1)S(1)}, u32[]{:S(2)}, u32[]{:S(2)}) %collective-permute-start) | collective-permute-done | bytes 147488 | tf_op jit(solution)/shard_map/ppermute | solution.py:48
  20.3 0.1 join.1
  20.3 0.6 %collective-permute-start.1 = (bf16[1,144,256]{2,1,0:T(8,128)(2,1)S(1)}, bf16[1,144,256]{2,1,0:T(8,128)(2,1)S(1)}, u32[]{:S(2)}, u32[]{:S(2)}) collective-permute-start(bf16[1,144,256]{2,1,0:T(8,128)(2,1)S(1)} %get-tuple-element.31), channel_id=1, source_target_pairs={{0,12},{4,8},{8,4},{12,0},{1,13},{5,9},{9,5},{13,1},{2,14},{6,10},... | collective-permute-start | bytes 221192 | tf_op jit(solution)/shard_map/ppermute | solution.py:48
  20.9 0.0 collective-permute-done.2.refs_0_
  20.9 0.8 %settle.1._ = bf16[4096,128]{1,0:T(8,128)(2,1)} custom-call(bf16[1024,128]{1,0:T(8,128)(2,1)S(1)} %collective-permute-done.2.refs_0_, bf16[1024,128]{1,0:T(8,128)(2,1)S(1)} %get-tuple-element.34.refs_1_), custom_call_target="tpu_custom_call" | custom-call | tf_op jit(solution)/shard_map/settle/pallas_call | solution.py:465
  21.7 1.4 %collective-permute-done.4.refs_1_ = bf16[512,128]{1,0:T(8,128)(2,1)S(1)} collective-permute-done((bf16[512,128]{1,0:T(8,128)(2,1)S(1)}, bf16[512,128]{1,0:T(8,128)(2,1)S(1)}, u32[]{:S(2)}, u32[]{:S(2)}) %collective-permute-start.4) | collective-permute-done | bytes 131104 | tf_op jit(solution)/shard_map/ppermute | solution.py:53
  23.1 3.2 %collective-permute-done.5.refs_2_ = bf16[512,128]{1,0:T(8,128)(2,1)S(1)} collective-permute-done((bf16[512,128]{1,0:T(8,128)(2,1)S(1)}, bf16[512,128]{1,0:T(8,128)(2,1)S(1)}, u32[]{:S(2)}, u32[]{:S(2)}) %collective-permute-start.5) | collective-permute-done | bytes 131104 | tf_op jit(solution)/shard_map/ppermute | solution.py:53
  26.3 5.1 %collective-permute-done.1.got_ref = bf16[1,144,256]{2,1,0:T(8,128)(2,1)S(1)} collective-permute-done((bf16[1,144,256]{2,1,0:T(8,128)(2,1)S(1)}, bf16[1,144,256]{2,1,0:T(8,128)(2,1)S(1)}, u32[]{:S(2)}, u32[]{:S(2)}) %collective-permute-start.1) | collective-permute-done | bytes 73760 | tf_op jit(solution)/shard_map/ppermute | solution.py:48
  31.4 0.0 collective-permute-done.3.refs_0_
  31.4 0.9 %finish.1 = (bf16[256,128]{1,0:T(8,128)(2,1)}, bf16[4096,128]{1,0:T(8,128)(2,1)}) custom-call(f32[1,136,256]{2,1,0:T(8,128)S(1)} %get-tuple-element.30.keep_ref, bf16[1,144,256]{2,1,0:T(8,128)(2,1)S(1)} %collective-permute-done.1.got_ref, bf16[4096,128]{1,0:T(8,128)(2,1)} %settle.1._, ...), custom_call_target="tpu_custom_call", output_to_operand_aliasing={{1}: (2, {})} | custom-call | tf_op jit(solution)/shard_map/finish/pallas_call | solution.py:474
Async XLA Ops:
  2.2 18.7 %collective-permute-start.2 = (bf16[1024,128]{1,0:T(8,128)(2,1)S(1)}, bf16[1024,128]{1,0:T(8,128)(2,1)S(1)}, u32[]{:S(2)}, u32[]{:S(2)}) collective-permute-start(bf16[1024,128]{1,0:T(8,128)(2,1)S(1)} %get-tuple-element.32), channel_id=1, source_target_pairs={{0,4},{4,12},{8,0},{12,8},{1,5},{5,13},{9,1},{13,9},{2,6},{6,14},{... | collective-permute-start | bytes 786440 | tf_op jit(solution)/shard_map/ppermute | solution.py:53
  2.3 29.1 %collective-permute-start.3 = (bf16[1024,128]{1,0:T(8,128)(2,1)S(1)}, bf16[1024,128]{1,0:T(8,128)(2,1)S(1)}, u32[]{:S(2)}, u32[]{:S(2)}) collective-permute-start(bf16[1024,128]{1,0:T(8,128)(2,1)S(1)} %get-tuple-element.35), channel_id=1, source_target_pairs={{0,12},{4,8},{8,4},{12,0},{1,13},{5,9},{9,5},{13,1},{2,14},{6,10},... | collective-permute-start | bytes 786440 | tf_op jit(solution)/shard_map/ppermute | solution.py:53
  10.5 9.7 %collective-permute-start = (bf16[2,144,256]{2,1,0:T(8,128)(2,1)S(1)}, bf16[2,144,256]{2,1,0:T(8,128)(2,1)S(1)}, u32[]{:S(2)}, u32[]{:S(2)}) collective-permute-start(bf16[2,144,256]{2,1,0:T(8,128)(2,1)S(1)} %get-tuple-element.29), channel_id=1, source_target_pairs={{0,4},{4,0},{8,12},{12,8},{1,5},{5,1},{9,13},{13,9},{2,6},{6,2},{1... | collective-permute-start | bytes 442376 | tf_op jit(solution)/shard_map/ppermute | solution.py:48
  12.5 10.6 %collective-permute-start.4 = (bf16[512,128]{1,0:T(8,128)(2,1)S(1)}, bf16[512,128]{1,0:T(8,128)(2,1)S(1)}, u32[]{:S(2)}, u32[]{:S(2)}) collective-permute-start(bf16[512,128]{1,0:T(8,128)(2,1)S(1)} %get-tuple-element.36), channel_id=1, source_target_pairs={{0,8},{4,0},{8,12},{12,4},{1,9},{5,1},{9,13},{13,5},{2,10},{6,2},{... | collective-permute-start | bytes 393224 | tf_op jit(solution)/shard_map/ppermute | solution.py:53
  14.2 12.1 %collective-permute-start.5 = (bf16[512,128]{1,0:T(8,128)(2,1)S(1)}, bf16[512,128]{1,0:T(8,128)(2,1)S(1)}, u32[]{:S(2)}, u32[]{:S(2)}) collective-permute-start(bf16[512,128]{1,0:T(8,128)(2,1)S(1)} %get-tuple-element.37), channel_id=1, source_target_pairs={{0,8},{4,0},{8,12},{12,4},{1,9},{5,1},{9,13},{13,5},{2,10},{6,2},{... | collective-permute-start | bytes 393224 | tf_op jit(solution)/shard_map/ppermute | solution.py:53
  20.3 11.0 %collective-permute-start.1 = (bf16[1,144,256]{2,1,0:T(8,128)(2,1)S(1)}, bf16[1,144,256]{2,1,0:T(8,128)(2,1)S(1)}, u32[]{:S(2)}, u32[]{:S(2)}) collective-permute-start(bf16[1,144,256]{2,1,0:T(8,128)(2,1)S(1)} %get-tuple-element.31), channel_id=1, source_target_pairs={{0,12},{4,8},{8,4},{12,0},{1,13},{5,9},{9,5},{13,1},{2,14},{6,10},... | collective-permute-start | bytes 221192 | tf_op jit(solution)/shard_map/ppermute | solution.py:48

commit v27 on v26

--- a/solution.py
+++ b/solution.py
@@ -10,7 +10,7 @@
 HD = 128
 GQ = 8
 STEPS = 2
-STAT_ROWS = 16
+STAT_ROWS = 6
 KEEP_ROWS = 8
 FAR = -1e30
 RATE = HD ** (-0.5) * 1.4426950408889634
@@ -130,18 +130,35 @@
     return [high, middle, low]
 
 
+def message_shape(width):
+    parts = max(1, width // HD)
+    return parts * HD + -(-parts * STAT_ROWS // 16) * 16, width // parts
+
+
 def packed(partial):
     summed, top, total = partial
+    rows, lanes = message_shape(top.shape[1])
+    sums = summed.astype(jnp.bfloat16)
     stats = pieces(top) + pieces(total)
-    rest = jnp.zeros((STAT_ROWS - len(stats), top.shape[1]), jnp.bfloat16)
-    return jnp.concatenate([summed.astype(jnp.bfloat16)] + stats + [rest], axis=0)
+    here = [slice(first, first + lanes) for first in range(0, top.shape[1], lanes)]
+    filled = [sums[:, part] for part in here] + [row[:, part] for part in here for row in stats]
+    rest = rows - len(here) * (HD + STAT_ROWS)
+    return jnp.concatenate(filled + [jnp.zeros((rest, lanes), jnp.bfloat16)], axis=0)
 
 
 def unpacked(block):
-    stats = block[HD:, :].astype(jnp.float32)
-    top = stats[0:1] + stats[1:2] + stats[2:3]
-    total = stats[3:4] + stats[4:5] + stats[5:6]
-    return block[0:HD, :].astype(jnp.float32), top, total
+    parts = block.shape[0] // HD
+    sums = [block[part * HD : (part + 1) * HD, :] for part in range(parts)]
+    stats = block[parts * HD :, :].astype(jnp.float32)
+
+    def row(first):
+        found = []
+        for part in range(parts):
+            at = part * STAT_ROWS + first
+            found.append(stats[at : at + 1] + stats[at + 1 : at + 2] + stats[at + 2 : at + 3])
+        return jnp.concatenate(found, axis=1)
+
+    return jnp.concatenate(sums, axis=1).astype(jnp.float32), row(0), row(3)
 
 
 def held(partial):
@@ -228,7 +245,7 @@
     requests = lengths_ref.shape[0]
     asked = queries_ref.shape[0]
     per_row = asked // request_ref.shape[0]
-    width = send_ref.shape[2]
+    width = own_ref.shape[1]
     for load in loads[2:]:
         load.wait()
 
@@ -406,7 +423,7 @@
     got_ahead = [hand(message, k) for message, (k, _, _) in zip(sent, ahead)]
 
     def leaving(count):
-        return jax.ShapeDtypeStruct((count // 2, HD + STAT_ROWS, width), jnp.bfloat16)
+        return jax.ShapeDtypeStruct((count // 2, *message_shape(width)), jnp.bfloat16)
 
     def staying(count):
         return jax.ShapeDtypeStruct((count // 2, HD + KEEP_ROWS, width), jnp.float32)

time: 32.4 us -> 32.3 us (level)
  no operation moved by 1% of the time
where the time goes in v27:
time: 32.3 us; the launch traced here: 32.1 us
  Pallas kernels  12.8 us (40%)
  waiting for transfers between devices  11.5 us (36%)
  starting transfers between devices  7.09 us (22%)
  between operations  0.68 us (2%)
    ppermute x2, waiting for transfers between devices, exchange(): return lax.ppermute(message, 'seq', [(i, i ^ k) for i in range(count)])  7.04 us
    ppermute x4, starting transfers between devices, hand(): lax.ppermute(message, 'seq', [(i, partner(i, k, count)) for i in range(co...  6.17 us
    pallas_call x1, Pallas kernels, per_device(): pl.pallas_call(first_kernel, out_shape=[leaving(senders), jax.ShapeDtypeS...  5.23 us
    ppermute x4, waiting for transfers between devices, hand(): lax.ppermute(message, 'seq', [(i, partner(i, k, count)) for i in range(co...  4.47 us
    pallas_call x2, Pallas kernels, place(): pl.pallas_call(functools.partial(place_kernel, plan), out_shape=[jax.Shap...  3.09 us
    pallas_call x1, Pallas kernels, per_device(): pl.pallas_call(second_kernel, out_shape=staying(senders), in_specs=[VMEM]...  2.7 us
    ppermute x2, starting transfers between devices, exchange(): return lax.ppermute(message, 'seq', [(i, i ^ k) for i in range(count)])  0.92 us
    pallas_call x1, Pallas kernels, per_device(): pl.pallas_call(functools.partial(finish_kernel, ahead[1:] + behind), out_...  0.88 us
  transfers between devices with their start and end apart: 6, of which 4 were waited for; matrix products, arithmetic and copies ran while one was open for 0% of the time, Pallas kernels for 32%

profile of v27, /device:TPU:16, one launch (start us, length us, event | category | flops | bytes accessed | tf_op | source)
XLA Modules:
  0.0 32.1 jit_solution(7829181451863559646)
XLA Ops:
  0.6 1.6 %place.2 = (bf16[1024,128]{1,0:T(8,128)(2,1)S(1)}, bf16[1024,128]{1,0:T(8,128)(2,1)S(1)}) custom-call(s32[128]{0:T(128)} %owner_any.3, bf16[4096,128]{1,0:T(8,128)(2,1)} %bitcast.14, f32[256,128]{1,0:T(8,128)} %bitcast.18, f32[2,128]{1,0:T(2,128)} %scales_any.3), custom_call_target="tpu_custom_call" | custom-call | tf_op jit(solution)/shard_map/place/pallas_call | solution.py:403
  2.2 0.1 collective-permute-start.2
  2.3 3.0 %collective-permute-start.3 = (bf16[1024,128]{1,0:T(8,128)(2,1)S(1)}, bf16[1024,128]{1,0:T(8,128)(2,1)S(1)}, u32[]{:S(2)}, u32[]{:S(2)}) collective-permute-start(bf16[1024,128]{1,0:T(8,128)(2,1)S(1)} %get-tuple-element.35), channel_id=1, source_target_pairs={{0,12},{4,8},{8,4},{12,0},{1,13},{5,9},{9,5},{13,1},{2,14},{6,10},... | collective-permute-start | bytes 786440 | tf_op jit(solution)/shard_map/ppermute | solution.py:53
  5.3 5.2 %attend_leaving.1 = (bf16[2,272,128]{2,1,0:T(8,128)(2,1)S(1)}, bf16[2048,256]{1,0:T(8,128)(2,1)S(1)}, bf16[128,2048]{1,0:T(8,128)(2,1)S(1)}, bf16[1024,256]{1,0:T(8,128)(2,1)S(1)}, f32[136,256]{1,0:T(8,128)S(1)}) custom-call(bf16[4096,128]{1,0:T(8,128)(2,1)} %bitcast.15, f32[256,128]{1,0:T(8,128)} %bitcast.19, f32[2,128]{1,0:T(2,128)} %scales_any.3, ...), custom_call_target="tpu_custom_call" | custom-call | tf_op jit(solution)/shard_map/attend_leaving/pallas_call | solution.py:433
  10.5 0.4 %collective-permute-start = (bf16[2,272,128]{2,1,0:T(8,128)(2,1)S(1)}, bf16[2,272,128]{2,1,0:T(8,128)(2,1)S(1)}, u32[]{:S(2)}, u32[]{:S(2)}) collective-permute-start(bf16[2,272,128]{2,1,0:T(8,128)(2,1)S(1)} %get-tuple-element.29), channel_id=1, source_target_pairs={{0,4},{4,0},{8,12},{12,8},{1,5},{5,1},{9,13},{13,9},{2,6},{6,2},{1... | collective-permute-start | bytes 417800 | tf_op jit(solution)/shard_map/ppermute | solution.py:48
  10.9 1.5 %place.3 = (bf16[512,128]{1,0:T(8,128)(2,1)S(1)}, bf16[512,128]{1,0:T(8,128)(2,1)S(1)}, bf16[1024,128]{1,0:T(8,128)(2,1)S(1)}) custom-call(s32[128]{0:T(128)} %owner_any.3, bf16[4096,128]{1,0:T(8,128)(2,1)} %bitcast.16, f32[256,128]{1,0:T(8,128)} %bitcast.20, f32[2,128]{1,0:T(2,128)} %scales_any.3), custom_call_target="tpu_custom_call" | custom-call | tf_op jit(solution)/shard_map/place/pallas_call | solution.py:403
  12.5 1.7 %collective-permute-start.4 = (bf16[512,128]{1,0:T(8,128)(2,1)S(1)}, bf16[512,128]{1,0:T(8,128)(2,1)S(1)}, u32[]{:S(2)}, u32[]{:S(2)}) collective-permute-start(bf16[512,128]{1,0:T(8,128)(2,1)S(1)} %get-tuple-element.36), channel_id=1, source_target_pairs={{0,8},{4,0},{8,12},{12,4},{1,9},{5,1},{9,13},{13,5},{2,10},{6,2},{... | collective-permute-start | bytes 393224 | tf_op jit(solution)/shard_map/ppermute | solution.py:53
  14.2 1.4 %collective-permute-start.5 = (bf16[512,128]{1,0:T(8,128)(2,1)S(1)}, bf16[512,128]{1,0:T(8,128)(2,1)S(1)}, u32[]{:S(2)}, u32[]{:S(2)}) collective-permute-start(bf16[512,128]{1,0:T(8,128)(2,1)S(1)} %get-tuple-element.37), channel_id=1, source_target_pairs={{0,8},{4,0},{8,12},{12,4},{1,9},{5,1},{9,13},{13,5},{2,10},{6,2},{... | collective-permute-start | bytes 393224 | tf_op jit(solution)/shard_map/ppermute | solution.py:53
  15.6 2.7 %attend_staying.1.keep_ref = f32[2,136,256]{2,1,0:T(8,128)S(1)} custom-call(bf16[2048,256]{1,0:T(8,128)(2,1)S(1)} %get-tuple-element.24.keys_ref, bf16[128,2048]{1,0:T(8,128)(2,1)S(1)} %get-tuple-element.25.turned_ref, bf16[1024,256]{1,0:T(8,128)(2,1)S(1)} %get-tuple-element.26.asked_ref, f32[136,256]{1,0:T(8,128)S(1)} %get-tuple-element.27.own_ref), custom_call_target="tpu_custom_call" | custom-call | tf_op jit(solution)/shard_map/attend_staying/pallas_call | solution.py:462
  18.3 1.9 %collective-permute-done.got_ref = bf16[2,272,128]{2,1,0:T(8,128)(2,1)S(1)} collective-permute-done((bf16[2,272,128]{2,1,0:T(8,128)(2,1)S(1)}, bf16[2,272,128]{2,1,0:T(8,128)(2,1)S(1)}, u32[]{:S(2)}, u32[]{:S(2)}) %collective-permute-start) | collective-permute-done | bytes 139296 | tf_op jit(solution)/shard_map/ppermute | solution.py:48
  20.1 0.1 join.1
  20.2 0.5 %collective-permute-start.1 = (bf16[1,272,128]{2,1,0:T(8,128)(2,1)S(1)}, bf16[1,272,128]{2,1,0:T(8,128)(2,1)S(1)}, u32[]{:S(2)}, u32[]{:S(2)}) collective-permute-start(bf16[1,272,128]{2,1,0:T(8,128)(2,1)S(1)} %get-tuple-element.31), channel_id=1, source_target_pairs={{0,12},{4,8},{8,4},{12,0},{1,13},{5,9},{9,5},{13,1},{2,14},{6,10},... | collective-permute-start | bytes 208904 | tf_op jit(solution)/shard_map/ppermute | solution.py:48
  20.7 0.0 collective-permute-done.2.refs_0_
  20.7 0.8 %settle.1._ = bf16[4096,128]{1,0:T(8,128)(2,1)} custom-call(bf16[1024,128]{1,0:T(8,128)(2,1)S(1)} %collective-permute-done.2.refs_0_, bf16[1024,128]{1,0:T(8,128)(2,1)S(1)} %get-tuple-element.34.refs_1_), custom_call_target="tpu_custom_call" | custom-call | tf_op jit(solution)/shard_map/settle/pallas_call | solution.py:482
  21.6 1.4 %collective-permute-done.4.refs_1_ = bf16[512,128]{1,0:T(8,128)(2,1)S(1)} collective-permute-done((bf16[512,128]{1,0:T(8,128)(2,1)S(1)}, bf16[512,128]{1,0:T(8,128)(2,1)S(1)}, u32[]{:S(2)}, u32[]{:S(2)}) %collective-permute-start.4) | collective-permute-done | bytes 131104 | tf_op jit(solution)/shard_map/ppermute | solution.py:53
  22.9 3.1 %collective-permute-done.5.refs_2_ = bf16[512,128]{1,0:T(8,128)(2,1)S(1)} collective-permute-done((bf16[512,128]{1,0:T(8,128)(2,1)S(1)}, bf16[512,128]{1,0:T(8,128)(2,1)S(1)}, u32[]{:S(2)}, u32[]{:S(2)}) %collective-permute-start.5) | collective-permute-done | bytes 131104 | tf_op jit(solution)/shard_map/ppermute | solution.py:53
  26.0 5.2 %collective-permute-done.1.got_ref = bf16[1,272,128]{2,1,0:T(8,128)(2,1)S(1)} collective-permute-done((bf16[1,272,128]{2,1,0:T(8,128)(2,1)S(1)}, bf16[1,272,128]{2,1,0:T(8,128)(2,1)S(1)}, u32[]{:S(2)}, u32[]{:S(2)}) %collective-permute-start.1) | collective-permute-done | bytes 69664 | tf_op jit(solution)/shard_map/ppermute | solution.py:48
  31.2 0.0 collective-permute-done.3.refs_0_
  31.2 0.9 %finish.1 = (bf16[256,128]{1,0:T(8,128)(2,1)}, bf16[4096,128]{1,0:T(8,128)(2,1)}) custom-call(f32[1,136,256]{2,1,0:T(8,128)S(1)} %get-tuple-element.30.keep_ref, bf16[1,272,128]{2,1,0:T(8,128)(2,1)S(1)} %collective-permute-done.1.got_ref, bf16[4096,128]{1,0:T(8,128)(2,1)} %settle.1._, ...), custom_call_target="tpu_custom_call", output_to_operand_aliasing={{1}: (2, {})} | custom-call | tf_op jit(solution)/shard_map/finish/pallas_call | solution.py:491
Async XLA Ops:
  2.2 18.5 %collective-permute-start.2 = (bf16[1024,128]{1,0:T(8,128)(2,1)S(1)}, bf16[1024,128]{1,0:T(8,128)(2,1)S(1)}, u32[]{:S(2)}, u32[]{:S(2)}) collective-permute-start(bf16[1024,128]{1,0:T(8,128)(2,1)S(1)} %get-tuple-element.32), channel_id=1, source_target_pairs={{0,4},{4,12},{8,0},{12,8},{1,5},{5,13},{9,1},{13,9},{2,6},{6,14},{... | collective-permute-start | bytes 786440 | tf_op jit(solution)/shard_map/ppermute | solution.py:53
  2.3 28.9 %collective-permute-start.3 = (bf16[1024,128]{1,0:T(8,128)(2,1)S(1)}, bf16[1024,128]{1,0:T(8,128)(2,1)S(1)}, u32[]{:S(2)}, u32[]{:S(2)}) collective-permute-start(bf16[1024,128]{1,0:T(8,128)(2,1)S(1)} %get-tuple-element.35), channel_id=1, source_target_pairs={{0,12},{4,8},{8,4},{12,0},{1,13},{5,9},{9,5},{13,1},{2,14},{6,10},... | collective-permute-start | bytes 786440 | tf_op jit(solution)/shard_map/ppermute | solution.py:53
  10.5 9.6 %collective-permute-start = (bf16[2,272,128]{2,1,0:T(8,128)(2,1)S(1)}, bf16[2,272,128]{2,1,0:T(8,128)(2,1)S(1)}, u32[]{:S(2)}, u32[]{:S(2)}) collective-permute-start(bf16[2,272,128]{2,1,0:T(8,128)(2,1)S(1)} %get-tuple-element.29), channel_id=1, source_target_pairs={{0,4},{4,0},{8,12},{12,8},{1,5},{5,1},{9,13},{13,9},{2,6},{6,2},{1... | collective-permute-start | bytes 417800 | tf_op jit(solution)/shard_map/ppermute | solution.py:48
  12.5 10.5 %collective-permute-start.4 = (bf16[512,128]{1,0:T(8,128)(2,1)S(1)}, bf16[512,128]{1,0:T(8,128)(2,1)S(1)}, u32[]{:S(2)}, u32[]{:S(2)}) collective-permute-start(bf16[512,128]{1,0:T(8,128)(2,1)S(1)} %get-tuple-element.36), channel_id=1, source_target_pairs={{0,8},{4,0},{8,12},{12,4},{1,9},{5,1},{9,13},{13,5},{2,10},{6,2},{... | collective-permute-start | bytes 393224 | tf_op jit(solution)/shard_map/ppermute | solution.py:53
  14.2 11.8 %collective-permute-start.5 = (bf16[512,128]{1,0:T(8,128)(2,1)S(1)}, bf16[512,128]{1,0:T(8,128)(2,1)S(1)}, u32[]{:S(2)}, u32[]{:S(2)}) collective-permute-start(bf16[512,128]{1,0:T(8,128)(2,1)S(1)} %get-tuple-element.37), channel_id=1, source_target_pairs={{0,8},{4,0},{8,12},{12,4},{1,9},{5,1},{9,13},{13,5},{2,10},{6,2},{... | collective-permute-start | bytes 393224 | tf_op jit(solution)/shard_map/ppermute | solution.py:53
  20.2 11.0 %collective-permute-start.1 = (bf16[1,272,128]{2,1,0:T(8,128)(2,1)S(1)}, bf16[1,272,128]{2,1,0:T(8,128)(2,1)S(1)}, u32[]{:S(2)}, u32[]{:S(2)}) collective-permute-start(bf16[1,272,128]{2,1,0:T(8,128)(2,1)S(1)} %get-tuple-element.31), channel_id=1, source_target_pairs={{0,12},{4,8},{8,4},{12,0},{1,13},{5,9},{9,5},{13,1},{2,14},{6,10},... | collective-permute-start | bytes 208904 | tf_op jit(solution)/shard_map/ppermute | solution.py:48

commit v28 on v27

--- a/solution.py
+++ b/solution.py
@@ -45,7 +45,8 @@
 
 def exchange(message, k):
     count = lax.axis_size("seq")
-    return lax.ppermute(message, "seq", [(i, i ^ k) for i in range(count)])
+    last = k == count - 1
+    return lax.ppermute(message, "seq", [(i, i ^ k ^ (last and i < count // 2)) for i in range(count)])
 
 
 def hand(message, k):
@@ -191,6 +192,8 @@
 
 def attend(parity, width, keys_ref, turned_ref, asked_ref, store):
     me = lax.axis_index("seq")
+    far = lax.axis_size("seq") // 2
+    lower = 1 - me // far
     asked = asked_ref.shape[0]
 
     def partial_of(here):
@@ -205,7 +208,8 @@
 
     if width % HD == 0:
         for index in range(asked // width // 2):
-            there = (me ^ difference(2 * index + parity)) * width
+            place = 2 * index + parity
+            there = (me ^ difference(place) ^ (lower if place >= far else 0)) * width
             store(index, partial_of(asked_ref[pl.ds(pl.multiple_of(there, width), width), :]))
         return
     tile = min(2 * HD, asked)
@@ -217,6 +221,7 @@
         for part in range(parts):
             lanes = slice(part * width, (part + 1) * width)
             apart = (tile_index * parts + part) ^ me
+            apart = apart ^ (apart // far * lower)
             place = apart ^ (apart >> 1)
 
             @pl.when(place % 2 == parity)

time: 32.3 us -> 32.2 us (level)
  the two profiles are of different devices: /device:TPU:16 before, /device:TPU:24 now
where the time goes in v28:
time: 32.2 us; the launch traced here: 32 us
  Pallas kernels  12.8 us (40%)
  waiting for transfers between devices  11.9 us (37%)
  starting transfers between devices  6.56 us (20%)
  between operations  0.68 us (2%)
    ppermute x2, waiting for transfers between devices, exchange(): lax.ppermute(message, 'seq', [(i, i ^ k ^ (last and i < count // 2)) for...  8.8 us
    pallas_call x1, Pallas kernels, per_device(): pl.pallas_call(first_kernel, out_shape=[leaving(senders), jax.ShapeDtypeS...  5.23 us
    ppermute x4, starting transfers between devices, hand(): lax.ppermute(message, 'seq', [(i, partner(i, k, count)) for i in range(co...  3.37 us
    ppermute x2, starting transfers between devices, exchange(): lax.ppermute(message, 'seq', [(i, i ^ k ^ (last and i < count // 2)) for...  3.2 us
    ppermute x4, waiting for transfers between devices, hand(): lax.ppermute(message, 'seq', [(i, partner(i, k, count)) for i in range(co...  3.14 us
    pallas_call x2, Pallas kernels, place(): pl.pallas_call(functools.partial(place_kernel, plan), out_shape=[jax.Shap...  3.09 us
    pallas_call x1, Pallas kernels, per_device(): pl.pallas_call(second_kernel, out_shape=staying(senders), in_specs=[VMEM]...  2.7 us
    pallas_call x1, Pallas kernels, per_device(): pl.pallas_call(functools.partial(finish_kernel, ahead[1:] + behind), out_...  0.88 us
  transfers between devices with their start and end apart: 6, of which 4 were waited for; matrix products, arithmetic and copies ran while one was open for 0% of the time, Pallas kernels for 32%

profile of v28, /device:TPU:24, one launch (start us, length us, event | category | flops | bytes accessed | tf_op | source)
XLA Modules:
  0.0 32.0 jit_solution(5305798590606854284)
XLA Ops:
  0.6 1.6 %place.2 = (bf16[1024,128]{1,0:T(8,128)(2,1)S(1)}, bf16[1024,128]{1,0:T(8,128)(2,1)S(1)}) custom-call(s32[128]{0:T(128)} %owner_any.3, bf16[4096,128]{1,0:T(8,128)(2,1)} %bitcast.14, f32[256,128]{1,0:T(8,128)} %bitcast.18, f32[2,128]{1,0:T(2,128)} %scales_any.3), custom_call_target="tpu_custom_call" | custom-call | tf_op jit(solution)/shard_map/place/pallas_call | solution.py:408
  2.2 0.5 %collective-permute-start.2 = (bf16[1024,128]{1,0:T(8,128)(2,1)S(1)}, bf16[1024,128]{1,0:T(8,128)(2,1)S(1)}, u32[]{:S(2)}, u32[]{:S(2)}) collective-permute-start(bf16[1024,128]{1,0:T(8,128)(2,1)S(1)} %get-tuple-element.32), channel_id=1, source_target_pairs={{0,4},{4,12},{8,0},{12,8},{1,5},{5,13},{9,1},{13,9},{2,6},{6,14},{... | collective-permute-start | bytes 786440 | tf_op jit(solution)/shard_map/ppermute | solution.py:54
  2.7 1.3 %collective-permute-start.3 = (bf16[1024,128]{1,0:T(8,128)(2,1)S(1)}, bf16[1024,128]{1,0:T(8,128)(2,1)S(1)}, u32[]{:S(2)}, u32[]{:S(2)}) collective-permute-start(bf16[1024,128]{1,0:T(8,128)(2,1)S(1)} %get-tuple-element.35), channel_id=1, source_target_pairs={{0,12},{4,8},{8,4},{12,0},{1,13},{5,9},{9,5},{13,1},{2,14},{6,10},... | collective-permute-start | bytes 786440 | tf_op jit(solution)/shard_map/ppermute | solution.py:54
  4.1 5.2 %attend_leaving.1 = (bf16[2,272,128]{2,1,0:T(8,128)(2,1)S(1)}, bf16[2048,256]{1,0:T(8,128)(2,1)S(1)}, bf16[128,2048]{1,0:T(8,128)(2,1)S(1)}, bf16[1024,256]{1,0:T(8,128)(2,1)S(1)}, f32[136,256]{1,0:T(8,128)S(1)}) custom-call(bf16[4096,128]{1,0:T(8,128)(2,1)} %bitcast.15, f32[256,128]{1,0:T(8,128)} %bitcast.19, f32[2,128]{1,0:T(2,128)} %scales_any.3, ...), custom_call_target="tpu_custom_call" | custom-call | tf_op jit(solution)/shard_map/attend_leaving/pallas_call | solution.py:438
  9.3 1.8 %collective-permute-start = (bf16[2,272,128]{2,1,0:T(8,128)(2,1)S(1)}, bf16[2,272,128]{2,1,0:T(8,128)(2,1)S(1)}, u32[]{:S(2)}, u32[]{:S(2)}) collective-permute-start(bf16[2,272,128]{2,1,0:T(8,128)(2,1)S(1)} %get-tuple-element.29), channel_id=1, source_target_pairs={{0,4},{4,0},{8,12},{12,8},{1,5},{5,1},{9,13},{13,9},{2,6},{6,2},{1... | collective-permute-start | bytes 417800 | tf_op jit(solution)/shard_map/ppermute | solution.py:49
  11.1 1.5 %place.3 = (bf16[512,128]{1,0:T(8,128)(2,1)S(1)}, bf16[512,128]{1,0:T(8,128)(2,1)S(1)}, bf16[1024,128]{1,0:T(8,128)(2,1)S(1)}) custom-call(s32[128]{0:T(128)} %owner_any.3, bf16[4096,128]{1,0:T(8,128)(2,1)} %bitcast.16, f32[256,128]{1,0:T(8,128)} %bitcast.20, f32[2,128]{1,0:T(2,128)} %scales_any.3), custom_call_target="tpu_custom_call" | custom-call | tf_op jit(solution)/shard_map/place/pallas_call | solution.py:408
  12.6 1.4 %collective-permute-start.4 = (bf16[512,128]{1,0:T(8,128)(2,1)S(1)}, bf16[512,128]{1,0:T(8,128)(2,1)S(1)}, u32[]{:S(2)}, u32[]{:S(2)}) collective-permute-start(bf16[512,128]{1,0:T(8,128)(2,1)S(1)} %get-tuple-element.36), channel_id=1, source_target_pairs={{0,8},{4,0},{8,12},{12,4},{1,9},{5,1},{9,13},{13,5},{2,10},{6,2},{... | collective-permute-start | bytes 393224 | tf_op jit(solution)/shard_map/ppermute | solution.py:54
  14.0 0.1 collective-permute-start.5
  14.1 2.7 %attend_staying.1.keep_ref = f32[2,136,256]{2,1,0:T(8,128)S(1)} custom-call(bf16[2048,256]{1,0:T(8,128)(2,1)S(1)} %get-tuple-element.24.keys_ref, bf16[128,2048]{1,0:T(8,128)(2,1)S(1)} %get-tuple-element.25.turned_ref, bf16[1024,256]{1,0:T(8,128)(2,1)S(1)} %get-tuple-element.26.asked_ref, f32[136,256]{1,0:T(8,128)S(1)} %get-tuple-element.27.own_ref), custom_call_target="tpu_custom_call" | custom-call | tf_op jit(solution)/shard_map/attend_staying/pallas_call | solution.py:467
  16.8 3.2 %collective-permute-done.got_ref = bf16[2,272,128]{2,1,0:T(8,128)(2,1)S(1)} collective-permute-done((bf16[2,272,128]{2,1,0:T(8,128)(2,1)S(1)}, bf16[2,272,128]{2,1,0:T(8,128)(2,1)S(1)}, u32[]{:S(2)}, u32[]{:S(2)}) %collective-permute-start) | collective-permute-done | bytes 139296 | tf_op jit(solution)/shard_map/ppermute | solution.py:49
  20.0 0.1 join.1
  20.0 1.4 %collective-permute-start.1 = (bf16[1,272,128]{2,1,0:T(8,128)(2,1)S(1)}, bf16[1,272,128]{2,1,0:T(8,128)(2,1)S(1)}, u32[]{:S(2)}, u32[]{:S(2)}) collective-permute-start(bf16[1,272,128]{2,1,0:T(8,128)(2,1)S(1)} %get-tuple-element.31), channel_id=1, source_target_pairs={{0,8},{4,12},{8,4},{12,0},{1,9},{5,13},{9,5},{13,1},{2,10},{6,14},... | collective-permute-start | bytes 208904 | tf_op jit(solution)/shard_map/ppermute | solution.py:49
  21.5 0.0 collective-permute-done.2.refs_0_
  21.5 0.8 %settle.1._ = bf16[4096,128]{1,0:T(8,128)(2,1)} custom-call(bf16[1024,128]{1,0:T(8,128)(2,1)S(1)} %collective-permute-done.2.refs_0_, bf16[1024,128]{1,0:T(8,128)(2,1)S(1)} %get-tuple-element.34.refs_1_), custom_call_target="tpu_custom_call" | custom-call | tf_op jit(solution)/shard_map/settle/pallas_call | solution.py:487
  22.3 0.5 %collective-permute-done.4.refs_1_ = bf16[512,128]{1,0:T(8,128)(2,1)S(1)} collective-permute-done((bf16[512,128]{1,0:T(8,128)(2,1)S(1)}, bf16[512,128]{1,0:T(8,128)(2,1)S(1)}, u32[]{:S(2)}, u32[]{:S(2)}) %collective-permute-start.4) | collective-permute-done | bytes 131104 | tf_op jit(solution)/shard_map/ppermute | solution.py:54
  22.8 2.7 %collective-permute-done.5.refs_2_ = bf16[512,128]{1,0:T(8,128)(2,1)S(1)} collective-permute-done((bf16[512,128]{1,0:T(8,128)(2,1)S(1)}, bf16[512,128]{1,0:T(8,128)(2,1)S(1)}, u32[]{:S(2)}, u32[]{:S(2)}) %collective-permute-start.5) | collective-permute-done | bytes 131104 | tf_op jit(solution)/shard_map/ppermute | solution.py:54
  25.4 5.6 %collective-permute-done.1.got_ref = bf16[1,272,128]{2,1,0:T(8,128)(2,1)S(1)} collective-permute-done((bf16[1,272,128]{2,1,0:T(8,128)(2,1)S(1)}, bf16[1,272,128]{2,1,0:T(8,128)(2,1)S(1)}, u32[]{:S(2)}, u32[]{:S(2)}) %collective-permute-start.1) | collective-permute-done | bytes 69664 | tf_op jit(solution)/shard_map/ppermute | solution.py:49
  31.1 0.0 collective-permute-done.3.refs_0_
  31.1 0.9 %finish.1 = (bf16[256,128]{1,0:T(8,128)(2,1)}, bf16[4096,128]{1,0:T(8,128)(2,1)}) custom-call(f32[1,136,256]{2,1,0:T(8,128)S(1)} %get-tuple-element.30.keep_ref, bf16[1,272,128]{2,1,0:T(8,128)(2,1)S(1)} %collective-permute-done.1.got_ref, bf16[4096,128]{1,0:T(8,128)(2,1)} %settle.1._, ...), custom_call_target="tpu_custom_call", output_to_operand_aliasing={{1}: (2, {})} | custom-call | tf_op jit(solution)/shard_map/finish/pallas_call | solution.py:496
Async XLA Ops:
  2.2 19.3 %collective-permute-start.2 = (bf16[1024,128]{1,0:T(8,128)(2,1)S(1)}, bf16[1024,128]{1,0:T(8,128)(2,1)S(1)}, u32[]{:S(2)}, u32[]{:S(2)}) collective-permute-start(bf16[1024,128]{1,0:T(8,128)(2,1)S(1)} %get-tuple-element.32), channel_id=1, source_target_pairs={{0,4},{4,12},{8,0},{12,8},{1,5},{5,13},{9,1},{13,9},{2,6},{6,14},{... | collective-permute-start | bytes 786440 | tf_op jit(solution)/shard_map/ppermute | solution.py:54
  2.7 28.4 %collective-permute-start.3 = (bf16[1024,128]{1,0:T(8,128)(2,1)S(1)}, bf16[1024,128]{1,0:T(8,128)(2,1)S(1)}, u32[]{:S(2)}, u32[]{:S(2)}) collective-permute-start(bf16[1024,128]{1,0:T(8,128)(2,1)S(1)} %get-tuple-element.35), channel_id=1, source_target_pairs={{0,12},{4,8},{8,4},{12,0},{1,13},{5,9},{9,5},{13,1},{2,14},{6,10},... | collective-permute-start | bytes 786440 | tf_op jit(solution)/shard_map/ppermute | solution.py:54
  9.3 10.7 %collective-permute-start = (bf16[2,272,128]{2,1,0:T(8,128)(2,1)S(1)}, bf16[2,272,128]{2,1,0:T(8,128)(2,1)S(1)}, u32[]{:S(2)}, u32[]{:S(2)}) collective-permute-start(bf16[2,272,128]{2,1,0:T(8,128)(2,1)S(1)} %get-tuple-element.29), channel_id=1, source_target_pairs={{0,4},{4,0},{8,12},{12,8},{1,5},{5,1},{9,13},{13,9},{2,6},{6,2},{1... | collective-permute-start | bytes 417800 | tf_op jit(solution)/shard_map/ppermute | solution.py:49
  12.6 10.2 %collective-permute-start.4 = (bf16[512,128]{1,0:T(8,128)(2,1)S(1)}, bf16[512,128]{1,0:T(8,128)(2,1)S(1)}, u32[]{:S(2)}, u32[]{:S(2)}) collective-permute-start(bf16[512,128]{1,0:T(8,128)(2,1)S(1)} %get-tuple-element.36), channel_id=1, source_target_pairs={{0,8},{4,0},{8,12},{12,4},{1,9},{5,1},{9,13},{13,5},{2,10},{6,2},{... | collective-permute-start | bytes 393224 | tf_op jit(solution)/shard_map/ppermute | solution.py:54
  14.0 11.4 %collective-permute-start.5 = (bf16[512,128]{1,0:T(8,128)(2,1)S(1)}, bf16[512,128]{1,0:T(8,128)(2,1)S(1)}, u32[]{:S(2)}, u32[]{:S(2)}) collective-permute-start(bf16[512,128]{1,0:T(8,128)(2,1)S(1)} %get-tuple-element.37), channel_id=1, source_target_pairs={{0,8},{4,0},{8,12},{12,4},{1,9},{5,1},{9,13},{13,5},{2,10},{6,2},{... | collective-permute-start | bytes 393224 | tf_op jit(solution)/shard_map/ppermute | solution.py:54
  20.0 11.0 %collective-permute-start.1 = (bf16[1,272,128]{2,1,0:T(8,128)(2,1)S(1)}, bf16[1,272,128]{2,1,0:T(8,128)(2,1)S(1)}, u32[]{:S(2)}, u32[]{:S(2)}) collective-permute-start(bf16[1,272,128]{2,1,0:T(8,128)(2,1)S(1)} %get-tuple-element.31), channel_id=1, source_target_pairs={{0,8},{4,12},{8,4},{12,0},{1,9},{5,13},{9,5},{13,1},{2,10},{6,14},... | collective-permute-start | bytes 208904 | tf_op jit(solution)/shard_map/ppermute | solution.py:49

commit v29 on v27

--- a/solution.py
+++ b/solution.py
@@ -345,35 +345,28 @@
             next_ref[index // 2] = held(partial)
 
 
-def settle(plan, handed, pages, sems):
+def settle_kernel(plan, *refs):
+    pages, sems = refs[-2:]
     receivers = lax.axis_size("seq")
     me = lax.axis_index("seq")
     rows = pages.shape[0] // receivers
     copies = []
-    for index, (k, start, slots) in enumerate(plan):
-        size = handed[index].shape[0]
+    for index, ((k, start, slots), handed) in enumerate(zip(plan, refs)):
+        size = handed.shape[0]
         sender = source(me, k, receivers) if k else me
         first = pl.multiple_of(sender * rows + start * (size // slots), size)
-        copies.append(pltpu.make_async_copy(handed[index], pages.at[pl.ds(first, size), :], sems.at[index]))
+        copies.append(pltpu.make_async_copy(handed, pages.at[pl.ds(first, size), :], sems.at[index]))
         copies[-1].start()
-    return copies
-
-
-def settle_kernel(plan, *refs):
-    *handed, pages, sems = refs
-    for copy in settle(plan, handed, pages, sems):
+    for copy in copies:
         copy.wait()
 
 
-def finish_kernel(plan, keep_ref, got_ref, _, *refs):
-    *handed, out_any, pages, out_ref, sems = refs
-    copies = settle(plan, handed, pages, sems)
+def finish_kernel(keep_ref, got_ref, out_any, out_ref, sem):
     summed, _, total = joined(taken(keep_ref[0]), unpacked(got_ref[0]))
     out_ref[...] = (summed / total).T.astype(jnp.bfloat16)
-    copies.append(pltpu.make_async_copy(out_ref, out_any, sems.at[len(copies)]))
-    copies[-1].start()
-    for copy in copies:
-        copy.wait()
+    store = pltpu.make_async_copy(out_ref, out_any, sem)
+    store.start()
+    store.wait()
 
 
 def in_hbm(arrays):
@@ -478,29 +471,31 @@
         )(keep, passed)
         k, count = 2 * k + 1, count // 2
         passed = exchange(send, k)
-    settled = ahead[:1] + own
-    pages = pl.pallas_call(
-        functools.partial(settle_kernel, settled),
-        out_shape=whole,
-        in_specs=[ANY] * len(settled),
+    def settle(plan, handed, pages=None):
+        before = [] if pages is None else [pages]
+        return pl.pallas_call(
+            functools.partial(settle_kernel, plan),
+            out_shape=whole,
+            in_specs=[ANY] * len(plan) + [HBM] * len(before),
+            out_specs=HBM,
+            scratch_shapes=[pltpu.SemaphoreType.DMA((len(plan),))],
+            input_output_aliases={len(plan): 0} if before else {},
+            compiler_params=small,
+            name="settle",
+        )(*handed, *before)
+
+    pages = settle(ahead[:1] + own, [got_ahead[0], mine])
+    pages = settle(ahead[1:] + behind, got, pages)
+    keep, pages = lax.optimization_barrier((keep, pages))
+    attended = pl.pallas_call(
+        finish_kernel,
+        out_shape=jax.ShapeDtypeStruct((width, HD), jnp.bfloat16),
+        in_specs=[VMEM] * 2,
         out_specs=HBM,
-        scratch_shapes=[pltpu.SemaphoreType.DMA((len(settled),))],
-        compiler_params=small,
-        name="settle",
-    )(got_ahead[0], mine)
-    attended, pages = pl.pallas_call(
-        functools.partial(finish_kernel, ahead[1:] + behind),
-        out_shape=[jax.ShapeDtypeStruct((width, HD), jnp.bfloat16), whole],
-        in_specs=[VMEM] * 2 + [HBM] + [ANY] * len(got),
-        out_specs=[HBM, HBM],
-        scratch_shapes=[
-            pltpu.VMEM((width, HD), jnp.bfloat16),
-            pltpu.SemaphoreType.DMA((len(got) + 1,)),
-        ],
-        input_output_aliases={2: 1},
+        scratch_shapes=[pltpu.VMEM((width, HD), jnp.bfloat16), pltpu.SemaphoreType.DMA],
         compiler_params=small,
         name="finish",
-    )(keep, passed, pages, *got)
+    )(keep, passed)
     pages = pages.reshape(blocks, tokens // blocks, 2, HD)
     attended = (
         attended.reshape(rows_dev, GQ, steps, HD).transpose(0, 2, 1, 3).reshape(rows_dev, steps, GQ * HD)

time: 32.3 us -> 32.2 us (level)
  Pallas kernels: 12.8 us -> 13.5 us
  waiting for transfers between devices: 11.5 us -> 10.8 us
    ppermute x2, waiting for transfers between devices: 7.04 us -> 1.88 us  [exchange(): return lax.ppermute(message, 'seq', [(i, i ^ k) for i in range(count)])]
    ppermute x4, waiting for transfers between devices: 4.47 us -> 8.89 us  [hand(): lax.ppermute(message, 'seq', [(i, partner(i, k, count)) for i in range(co...]
    pallas_call x2 -> x3, Pallas kernels: 1.69 us -> 2.38 us  [the longest x2 1.61 us: settle(): pl.pallas_call(functools.partial(settle_kernel, plan), out_shape=whole, i...]
  transfers between devices with their start and end apart: 6 -> 6, of which waited for: 4 -> 4; matrix products, arithmetic and copies ran while one was open for 0% -> 0% of each run, Pallas kernels for 32% -> 35%
where the time goes in v29:
time: 32.2 us; the launch traced here: 32 us
  Pallas kernels  13.5 us (42%)
  waiting for transfers between devices  10.8 us (34%)
  starting transfers between devices  7.09 us (22%)
  between operations  0.7 us (2%)
    ppermute x4, waiting for transfers between devices, hand(): lax.ppermute(message, 'seq', [(i, partner(i, k, count)) for i in range(co...  8.89 us
    ppermute x4, starting transfers between devices, hand(): lax.ppermute(message, 'seq', [(i, partner(i, k, count)) for i in range(co...  6.17 us
    pallas_call x1, Pallas kernels, per_device(): pl.pallas_call(first_kernel, out_shape=[leaving(senders), jax.ShapeDtypeS...  5.23 us
    pallas_call x2, Pallas kernels, place(): pl.pallas_call(functools.partial(place_kernel, plan), out_shape=[jax.Shap...  3.09 us
    pallas_call x1, Pallas kernels, per_device(): pl.pallas_call(second_kernel, out_shape=staying(senders), in_specs=[VMEM]...  2.7 us
    ppermute x2, waiting for transfers between devices, exchange(): return lax.ppermute(message, 'seq', [(i, i ^ k) for i in range(count)])  1.88 us
    pallas_call x2, Pallas kernels, settle(): pl.pallas_call(functools.partial(settle_kernel, plan), out_shape=whole, i...  1.61 us
    ppermute x2, starting transfers between devices, exchange(): return lax.ppermute(message, 'seq', [(i, i ^ k) for i in range(count)])  0.92 us
  transfers between devices with their start and end apart: 6, of which 4 were waited for; matrix products, arithmetic and copies ran while one was open for 0% of the time, Pallas kernels for 35%

profile of v29, /device:TPU:16, one launch (start us, length us, event | category | flops | bytes accessed | tf_op | source)
XLA Modules:
  0.0 32.0 jit_solution(9718159358187137065)
XLA Ops:
  0.6 1.6 %place.2 = (bf16[1024,128]{1,0:T(8,128)(2,1)S(1)}, bf16[1024,128]{1,0:T(8,128)(2,1)S(1)}) custom-call(s32[128]{0:T(128)} %owner_any.3, bf16[4096,128]{1,0:T(8,128)(2,1)} %bitcast.14, f32[256,128]{1,0:T(8,128)} %bitcast.18, f32[2,128]{1,0:T(2,128)} %scales_any.3), custom_call_target="tpu_custom_call" | custom-call | tf_op jit(solution)/shard_map/place/pallas_call | solution.py:396
  2.2 0.1 collective-permute-start.4
  2.3 3.0 %collective-permute-start.1 = (bf16[1024,128]{1,0:T(8,128)(2,1)S(1)}, bf16[1024,128]{1,0:T(8,128)(2,1)S(1)}, u32[]{:S(2)}, u32[]{:S(2)}) collective-permute-start(bf16[1024,128]{1,0:T(8,128)(2,1)S(1)} %get-tuple-element.31), channel_id=1, source_target_pairs={{0,12},{4,8},{8,4},{12,0},{1,13},{5,9},{9,5},{13,1},{2,14},{6,10},... | collective-permute-start | bytes 786440 | tf_op jit(solution)/shard_map/ppermute | solution.py:53
  5.3 5.2 %attend_leaving.1 = (bf16[2,272,128]{2,1,0:T(8,128)(2,1)S(1)}, bf16[2048,256]{1,0:T(8,128)(2,1)S(1)}, bf16[128,2048]{1,0:T(8,128)(2,1)S(1)}, bf16[1024,256]{1,0:T(8,128)(2,1)S(1)}, f32[136,256]{1,0:T(8,128)S(1)}) custom-call(bf16[4096,128]{1,0:T(8,128)(2,1)} %bitcast.15, f32[256,128]{1,0:T(8,128)} %bitcast.19, f32[2,128]{1,0:T(2,128)} %scales_any.3, ...), custom_call_target="tpu_custom_call" | custom-call | tf_op jit(solution)/shard_map/attend_leaving/pallas_call | solution.py:426
  10.5 0.4 %collective-permute-start = (bf16[2,272,128]{2,1,0:T(8,128)(2,1)S(1)}, bf16[2,272,128]{2,1,0:T(8,128)(2,1)S(1)}, u32[]{:S(2)}, u32[]{:S(2)}) collective-permute-start(bf16[2,272,128]{2,1,0:T(8,128)(2,1)S(1)} %get-tuple-element.29), channel_id=1, source_target_pairs={{0,4},{4,0},{8,12},{12,8},{1,5},{5,1},{9,13},{13,9},{2,6},{6,2},{1... | collective-permute-start | bytes 417800 | tf_op jit(solution)/shard_map/ppermute | solution.py:48
  10.9 1.5 %place.3 = (bf16[512,128]{1,0:T(8,128)(2,1)S(1)}, bf16[512,128]{1,0:T(8,128)(2,1)S(1)}, bf16[1024,128]{1,0:T(8,128)(2,1)S(1)}) custom-call(s32[128]{0:T(128)} %owner_any.3, bf16[4096,128]{1,0:T(8,128)(2,1)} %bitcast.16, f32[256,128]{1,0:T(8,128)} %bitcast.20, f32[2,128]{1,0:T(2,128)} %scales_any.3), custom_call_target="tpu_custom_call" | custom-call | tf_op jit(solution)/shard_map/place/pallas_call | solution.py:396
  12.5 1.7 %collective-permute-start.2 = (bf16[512,128]{1,0:T(8,128)(2,1)S(1)}, bf16[512,128]{1,0:T(8,128)(2,1)S(1)}, u32[]{:S(2)}, u32[]{:S(2)}) collective-permute-start(bf16[512,128]{1,0:T(8,128)(2,1)S(1)} %get-tuple-element.33), channel_id=1, source_target_pairs={{0,8},{4,0},{8,12},{12,4},{1,9},{5,1},{9,13},{13,5},{2,10},{6,2},{... | collective-permute-start | bytes 393224 | tf_op jit(solution)/shard_map/ppermute | solution.py:53
  14.2 1.4 %collective-permute-start.3 = (bf16[512,128]{1,0:T(8,128)(2,1)S(1)}, bf16[512,128]{1,0:T(8,128)(2,1)S(1)}, u32[]{:S(2)}, u32[]{:S(2)}) collective-permute-start(bf16[512,128]{1,0:T(8,128)(2,1)S(1)} %get-tuple-element.34), channel_id=1, source_target_pairs={{0,8},{4,0},{8,12},{12,4},{1,9},{5,1},{9,13},{13,5},{2,10},{6,2},{... | collective-permute-start | bytes 393224 | tf_op jit(solution)/shard_map/ppermute | solution.py:53
  15.6 2.7 %attend_staying.1.keep_ref = f32[2,136,256]{2,1,0:T(8,128)S(1)} custom-call(bf16[2048,256]{1,0:T(8,128)(2,1)S(1)} %get-tuple-element.24.keys_ref, bf16[128,2048]{1,0:T(8,128)(2,1)S(1)} %get-tuple-element.25.turned_ref, bf16[1024,256]{1,0:T(8,128)(2,1)S(1)} %get-tuple-element.26.asked_ref, f32[136,256]{1,0:T(8,128)S(1)} %get-tuple-element.27.own_ref), custom_call_target="tpu_custom_call" | custom-call | tf_op jit(solution)/shard_map/attend_staying/pallas_call | solution.py:455
  18.3 1.9 %collective-permute-done.got_ref = bf16[2,272,128]{2,1,0:T(8,128)(2,1)S(1)} collective-permute-done((bf16[2,272,128]{2,1,0:T(8,128)(2,1)S(1)}, bf16[2,272,128]{2,1,0:T(8,128)(2,1)S(1)}, u32[]{:S(2)}, u32[]{:S(2)}) %collective-permute-start) | collective-permute-done | bytes 139296 | tf_op jit(solution)/shard_map/ppermute | solution.py:48
  20.1 0.1 join.1
  20.2 0.5 %collective-permute-start.5 = (bf16[1,272,128]{2,1,0:T(8,128)(2,1)S(1)}, bf16[1,272,128]{2,1,0:T(8,128)(2,1)S(1)}, u32[]{:S(2)}, u32[]{:S(2)}) collective-permute-start(bf16[1,272,128]{2,1,0:T(8,128)(2,1)S(1)} %get-tuple-element.39), channel_id=1, source_target_pairs={{0,12},{4,8},{8,4},{12,0},{1,13},{5,9},{9,5},{13,1},{2,14},{6,10},... | collective-permute-start | bytes 208904 | tf_op jit(solution)/shard_map/ppermute | solution.py:48
  20.7 0.0 collective-permute-done.4.refs_0_
  20.7 0.8 %settle.2.refs_3_ = bf16[4096,128]{1,0:T(8,128)(2,1)} custom-call(bf16[1024,128]{1,0:T(8,128)(2,1)S(1)} %collective-permute-done.4.refs_0_, bf16[1024,128]{1,0:T(8,128)(2,1)S(1)} %get-tuple-element.36.refs_1_), custom_call_target="tpu_custom_call" | custom-call | tf_op jit(solution)/shard_map/settle/pallas_call | solution.py:476
  21.6 1.4 %collective-permute-done.2.refs_1_ = bf16[512,128]{1,0:T(8,128)(2,1)S(1)} collective-permute-done((bf16[512,128]{1,0:T(8,128)(2,1)S(1)}, bf16[512,128]{1,0:T(8,128)(2,1)S(1)}, u32[]{:S(2)}, u32[]{:S(2)}) %collective-permute-start.2) | collective-permute-done | bytes 131104 | tf_op jit(solution)/shard_map/ppermute | solution.py:53
  22.9 3.1 %collective-permute-done.3.refs_2_ = bf16[512,128]{1,0:T(8,128)(2,1)S(1)} collective-permute-done((bf16[512,128]{1,0:T(8,128)(2,1)S(1)}, bf16[512,128]{1,0:T(8,128)(2,1)S(1)}, u32[]{:S(2)}, u32[]{:S(2)}) %collective-permute-start.3) | collective-permute-done | bytes 131104 | tf_op jit(solution)/shard_map/ppermute | solution.py:53
  26.0 4.4 %collective-permute-done.1.refs_0_ = bf16[1024,128]{1,0:T(8,128)(2,1)S(1)} collective-permute-done((bf16[1024,128]{1,0:T(8,128)(2,1)S(1)}, bf16[1024,128]{1,0:T(8,128)(2,1)S(1)}, u32[]{:S(2)}, u32[]{:S(2)}) %collective-permute-start.1) | collective-permute-done | bytes 262176 | tf_op jit(solution)/shard_map/ppermute | solution.py:53
  30.4 0.8 %settle.3 = bf16[4096,128]{1,0:T(8,128)(2,1)} custom-call(bf16[1024,128]{1,0:T(8,128)(2,1)S(1)} %collective-permute-done.1.refs_0_, bf16[512,128]{1,0:T(8,128)(2,1)S(1)} %collective-permute-done.2.refs_1_, bf16[512,128]{1,0:T(8,128)(2,1)S(1)} %collective-permute-done.3.refs_2_, bf16[4096,128]{1,0:T(8,128)(2,1)} %settle.2.refs_3_), custom_call_target="tpu_custom_call", output_to_operand_aliasing={{}: (3, {})} | custom-call | tf_op jit(solution)/shard_map/settle/pallas_call | solution.py:476
  31.3 0.0 collective-permute-done.5.got_ref
  31.3 0.8 %finish.1 = bf16[256,128]{1,0:T(8,128)(2,1)} custom-call(f32[1,136,256]{2,1,0:T(8,128)S(1)} %get-tuple-element.38.keep_ref, bf16[1,272,128]{2,1,0:T(8,128)(2,1)S(1)} %collective-permute-done.5.got_ref), custom_call_target="tpu_custom_call" | custom-call | tf_op jit(solution)/shard_map/finish/pallas_call | solution.py:490
Async XLA Ops:
  2.2 18.5 %collective-permute-start.4 = (bf16[1024,128]{1,0:T(8,128)(2,1)S(1)}, bf16[1024,128]{1,0:T(8,128)(2,1)S(1)}, u32[]{:S(2)}, u32[]{:S(2)}) collective-permute-start(bf16[1024,128]{1,0:T(8,128)(2,1)S(1)} %get-tuple-element.35), channel_id=1, source_target_pairs={{0,4},{4,12},{8,0},{12,8},{1,5},{5,13},{9,1},{13,9},{2,6},{6,14},{... | collective-permute-start | bytes 786440 | tf_op jit(solution)/shard_map/ppermute | solution.py:53
  2.3 28.2 %collective-permute-start.1 = (bf16[1024,128]{1,0:T(8,128)(2,1)S(1)}, bf16[1024,128]{1,0:T(8,128)(2,1)S(1)}, u32[]{:S(2)}, u32[]{:S(2)}) collective-permute-start(bf16[1024,128]{1,0:T(8,128)(2,1)S(1)} %get-tuple-element.31), channel_id=1, source_target_pairs={{0,12},{4,8},{8,4},{12,0},{1,13},{5,9},{9,5},{13,1},{2,14},{6,10},... | collective-permute-start | bytes 786440 | tf_op jit(solution)/shard_map/ppermute | solution.py:53
  10.5 9.6 %collective-permute-start = (bf16[2,272,128]{2,1,0:T(8,128)(2,1)S(1)}, bf16[2,272,128]{2,1,0:T(8,128)(2,1)S(1)}, u32[]{:S(2)}, u32[]{:S(2)}) collective-permute-start(bf16[2,272,128]{2,1,0:T(8,128)(2,1)S(1)} %get-tuple-element.29), channel_id=1, source_target_pairs={{0,4},{4,0},{8,12},{12,8},{1,5},{5,1},{9,13},{13,9},{2,6},{6,2},{1... | collective-permute-start | bytes 417800 | tf_op jit(solution)/shard_map/ppermute | solution.py:48
  12.5 10.5 %collective-permute-start.2 = (bf16[512,128]{1,0:T(8,128)(2,1)S(1)}, bf16[512,128]{1,0:T(8,128)(2,1)S(1)}, u32[]{:S(2)}, u32[]{:S(2)}) collective-permute-start(bf16[512,128]{1,0:T(8,128)(2,1)S(1)} %get-tuple-element.33), channel_id=1, source_target_pairs={{0,8},{4,0},{8,12},{12,4},{1,9},{5,1},{9,13},{13,5},{2,10},{6,2},{... | collective-permute-start | bytes 393224 | tf_op jit(solution)/shard_map/ppermute | solution.py:53
  14.2 11.8 %collective-permute-start.3 = (bf16[512,128]{1,0:T(8,128)(2,1)S(1)}, bf16[512,128]{1,0:T(8,128)(2,1)S(1)}, u32[]{:S(2)}, u32[]{:S(2)}) collective-permute-start(bf16[512,128]{1,0:T(8,128)(2,1)S(1)} %get-tuple-element.34), channel_id=1, source_target_pairs={{0,8},{4,0},{8,12},{12,4},{1,9},{5,1},{9,13},{13,5},{2,10},{6,2},{... | collective-permute-start | bytes 393224 | tf_op jit(solution)/shard_map/ppermute | solution.py:53
  20.2 11.0 %collective-permute-start.5 = (bf16[1,272,128]{2,1,0:T(8,128)(2,1)S(1)}, bf16[1,272,128]{2,1,0:T(8,128)(2,1)S(1)}, u32[]{:S(2)}, u32[]{:S(2)}) collective-permute-start(bf16[1,272,128]{2,1,0:T(8,128)(2,1)S(1)} %get-tuple-element.39), channel_id=1, source_target_pairs={{0,12},{4,8},{8,4},{12,0},{1,13},{5,9},{9,5},{13,1},{2,14},{6,10},... | collective-permute-start | bytes 208904 | tf_op jit(solution)/shard_map/ppermute | solution.py:48

commit v30 on v27

--- a/solution.py
+++ b/solution.py
@@ -55,7 +55,7 @@
 
 def messages(count, capacity):
     half = capacity // 2
-    ahead = [(k, 0, capacity) for k in range(count // 2, count)]
+    ahead = [(k, 0, capacity) for k in reversed(range(count // 2, count))]
     behind = [(k, first, half) for k in reversed(range(1, count // 2)) for first in (0, half)]
     return ahead, behind, [(0, 0, capacity)]
 
@@ -458,7 +458,6 @@
     send, late_deltas = lax.optimization_barrier((send, late_deltas))
     passed = exchange(send, k)
     *sent, mine = place(behind + own, late_deltas)
-    got = got_ahead[1:] + [hand(message, k) for message, (k, _, _) in zip(sent, behind)]
     keep = pl.pallas_call(
         second_kernel,
         out_shape=staying(senders),
@@ -467,6 +466,8 @@
         compiler_params=roomy,
         name="attend_staying",
     )(*common)
+    sent, keep = lax.optimization_barrier((sent, keep))
+    got = got_ahead[1:] + [hand(message, partner) for message, (partner, _, _) in zip(sent, behind)]
     while count > 1:
         send, keep = pl.pallas_call(
             join_kernel,

time: 32.3 us -> 33 us (1.022)
  the two profiles are of different devices: /device:TPU:16 before, /device:TPU:0 now
where the time goes in v30:
time: 33 us; the launch traced here: 32.8 us
  Pallas kernels  12.8 us (39%)
  starting transfers between devices  10.3 us (31%)
  waiting for transfers between devices  9.05 us (27%)
  between operations  0.69 us (2%)
    ppermute x4, starting transfers between devices, hand(): lax.ppermute(message, 'seq', [(i, partner(i, k, count)) for i in range(co...  9.49 us
    ppermute x4, waiting for transfers between devices, hand(): lax.ppermute(message, 'seq', [(i, partner(i, k, count)) for i in range(co...  7.49 us
    pallas_call x1, Pallas kernels, per_device(): pl.pallas_call(first_kernel, out_shape=[leaving(senders), jax.ShapeDtypeS...  5.23 us
    pallas_call x2, Pallas kernels, place(): pl.pallas_call(functools.partial(place_kernel, plan), out_shape=[jax.Shap...  3.1 us
    pallas_call x1, Pallas kernels, per_device(): pl.pallas_call(second_kernel, out_shape=staying(senders), in_specs=[VMEM]...  2.71 us
    ppermute x2, waiting for transfers between devices, exchange(): return lax.ppermute(message, 'seq', [(i, i ^ k) for i in range(count)])  1.55 us
    pallas_call x1, Pallas kernels, per_device(): pl.pallas_call(functools.partial(finish_kernel, ahead[1:] + behind), out_...  0.89 us
    pallas_call x1, Pallas kernels, per_device(): pl.pallas_call(functools.partial(settle_kernel, settled), out_shape=whole...  0.82 us
  transfers between devices with their start and end apart: 6, of which 5 were waited for; matrix products, arithmetic and copies ran while one was open for 0% of the time, Pallas kernels for 32%

profile of v30, /device:TPU:0, one launch (start us, length us, event | category | flops | bytes accessed | tf_op | source)
XLA Modules:
  0.0 32.8 jit_solution(15633403299374844916)
XLA Ops:
  0.6 1.6 %place.2 = (bf16[1024,128]{1,0:T(8,128)(2,1)S(1)}, bf16[1024,128]{1,0:T(8,128)(2,1)S(1)}) custom-call(s32[128]{0:T(128)} %owner_any.3, bf16[4096,128]{1,0:T(8,128)(2,1)} %bitcast.14, f32[256,128]{1,0:T(8,128)} %bitcast.18, f32[2,128]{1,0:T(2,128)} %scales_any.3), custom_call_target="tpu_custom_call" | custom-call | tf_op jit(solution)/shard_map/place/pallas_call | solution.py:403
  2.2 5.1 %collective-permute-start.2 = (bf16[1024,128]{1,0:T(8,128)(2,1)S(1)}, bf16[1024,128]{1,0:T(8,128)(2,1)S(1)}, u32[]{:S(2)}, u32[]{:S(2)}) collective-permute-start(bf16[1024,128]{1,0:T(8,128)(2,1)S(1)} %get-tuple-element.39), channel_id=1, source_target_pairs={{0,12},{4,8},{8,4},{12,0},{1,13},{5,9},{9,5},{13,1},{2,14},{6,10},... | collective-permute-start | bytes 786440 | tf_op jit(solution)/shard_map/ppermute | solution.py:53
  7.3 0.0 collective-permute-start.3
  7.3 5.2 %attend_leaving.1 = (bf16[2,272,128]{2,1,0:T(8,128)(2,1)S(1)}, bf16[2048,256]{1,0:T(8,128)(2,1)S(1)}, bf16[128,2048]{1,0:T(8,128)(2,1)S(1)}, bf16[1024,256]{1,0:T(8,128)(2,1)S(1)}, f32[136,256]{1,0:T(8,128)S(1)}) custom-call(bf16[4096,128]{1,0:T(8,128)(2,1)} %bitcast.15, f32[256,128]{1,0:T(8,128)} %bitcast.19, f32[2,128]{1,0:T(2,128)} %scales_any.3, ...), custom_call_target="tpu_custom_call" | custom-call | tf_op jit(solution)/shard_map/attend_leaving/pallas_call | solution.py:433
  12.6 0.7 %collective-permute-start = (bf16[2,272,128]{2,1,0:T(8,128)(2,1)S(1)}, bf16[2,272,128]{2,1,0:T(8,128)(2,1)S(1)}, u32[]{:S(2)}, u32[]{:S(2)}) collective-permute-start(bf16[2,272,128]{2,1,0:T(8,128)(2,1)S(1)} %get-tuple-element.36), channel_id=1, source_target_pairs={{0,4},{4,0},{8,12},{12,8},{1,5},{5,1},{9,13},{13,9},{2,6},{6,2},{1... | collective-permute-start | bytes 417800 | tf_op jit(solution)/shard_map/ppermute | solution.py:48
  13.3 1.5 %place.3 = (bf16[512,128]{1,0:T(8,128)(2,1)S(1)}, bf16[512,128]{1,0:T(8,128)(2,1)S(1)}, bf16[1024,128]{1,0:T(8,128)(2,1)S(1)}) custom-call(s32[128]{0:T(128)} %owner_any.3, bf16[4096,128]{1,0:T(8,128)(2,1)} %bitcast.16, f32[256,128]{1,0:T(8,128)} %bitcast.20, f32[2,128]{1,0:T(2,128)} %scales_any.3), custom_call_target="tpu_custom_call" | custom-call | tf_op jit(solution)/shard_map/place/pallas_call | solution.py:403
  14.8 2.7 %attend_staying.1.keep_ref = f32[2,136,256]{2,1,0:T(8,128)S(1)} custom-call(bf16[2048,256]{1,0:T(8,128)(2,1)S(1)} %get-tuple-element.31.keys_ref, bf16[128,2048]{1,0:T(8,128)(2,1)S(1)} %get-tuple-element.32.turned_ref, bf16[1024,256]{1,0:T(8,128)(2,1)S(1)} %get-tuple-element.33.asked_ref, f32[136,256]{1,0:T(8,128)S(1)} %get-tuple-element.34.own_ref), custom_call_target="tpu_custom_call" | custom-call | tf_op jit(solution)/shard_map/attend_staying/pallas_call | solution.py:461
  17.5 2.4 %collective-permute-start.4 = (bf16[512,128]{1,0:T(8,128)(2,1)S(1)}, bf16[512,128]{1,0:T(8,128)(2,1)S(1)}, u32[]{:S(2)}, u32[]{:S(2)}) collective-permute-start(bf16[512,128]{1,0:T(8,128)(2,1)S(1)} %get-tuple-element.42), channel_id=1, source_target_pairs={{0,8},{4,0},{8,12},{12,4},{1,9},{5,1},{9,13},{13,5},{2,10},{6,2},{... | collective-permute-start | bytes 393224 | tf_op jit(solution)/shard_map/ppermute | solution.py:53
  19.9 2.0 %collective-permute-start.5 = (bf16[512,128]{1,0:T(8,128)(2,1)S(1)}, bf16[512,128]{1,0:T(8,128)(2,1)S(1)}, u32[]{:S(2)}, u32[]{:S(2)}) collective-permute-start(bf16[512,128]{1,0:T(8,128)(2,1)S(1)} %get-tuple-element.43), channel_id=1, source_target_pairs={{0,8},{4,0},{8,12},{12,4},{1,9},{5,1},{9,13},{13,5},{2,10},{6,2},{... | collective-permute-start | bytes 393224 | tf_op jit(solution)/shard_map/ppermute | solution.py:53
  21.9 0.8 %collective-permute-done.got_ref = bf16[2,272,128]{2,1,0:T(8,128)(2,1)S(1)} collective-permute-done((bf16[2,272,128]{2,1,0:T(8,128)(2,1)S(1)}, bf16[2,272,128]{2,1,0:T(8,128)(2,1)S(1)}, u32[]{:S(2)}, u32[]{:S(2)}) %collective-permute-start) | collective-permute-done | bytes 139296 | tf_op jit(solution)/shard_map/ppermute | solution.py:48
  22.6 0.1 join.1
  22.7 0.1 collective-permute-start.1
  22.8 0.0 collective-permute-done.2.refs_0_
  22.8 0.8 %settle.1._ = bf16[4096,128]{1,0:T(8,128)(2,1)} custom-call(bf16[1024,128]{1,0:T(8,128)(2,1)S(1)} %collective-permute-done.2.refs_0_, bf16[1024,128]{1,0:T(8,128)(2,1)S(1)} %get-tuple-element.40.refs_1_), custom_call_target="tpu_custom_call" | custom-call | tf_op jit(solution)/shard_map/settle/pallas_call | solution.py:483
  23.6 1.9 %collective-permute-done.4.refs_1_ = bf16[512,128]{1,0:T(8,128)(2,1)S(1)} collective-permute-done((bf16[512,128]{1,0:T(8,128)(2,1)S(1)}, bf16[512,128]{1,0:T(8,128)(2,1)S(1)}, u32[]{:S(2)}, u32[]{:S(2)}) %collective-permute-start.4) | collective-permute-done | bytes 131104 | tf_op jit(solution)/shard_map/ppermute | solution.py:53
  25.5 3.2 %collective-permute-done.5.refs_2_ = bf16[512,128]{1,0:T(8,128)(2,1)S(1)} collective-permute-done((bf16[512,128]{1,0:T(8,128)(2,1)S(1)}, bf16[512,128]{1,0:T(8,128)(2,1)S(1)}, u32[]{:S(2)}, u32[]{:S(2)}) %collective-permute-start.5) | collective-permute-done | bytes 131104 | tf_op jit(solution)/shard_map/ppermute | solution.py:53
  28.7 0.8 %collective-permute-done.1.got_ref = bf16[1,272,128]{2,1,0:T(8,128)(2,1)S(1)} collective-permute-done((bf16[1,272,128]{2,1,0:T(8,128)(2,1)S(1)}, bf16[1,272,128]{2,1,0:T(8,128)(2,1)S(1)}, u32[]{:S(2)}, u32[]{:S(2)}) %collective-permute-start.1) | collective-permute-done | bytes 69664 | tf_op jit(solution)/shard_map/ppermute | solution.py:48
  29.5 2.4 %collective-permute-done.3.refs_0_ = bf16[1024,128]{1,0:T(8,128)(2,1)S(1)} collective-permute-done((bf16[1024,128]{1,0:T(8,128)(2,1)S(1)}, bf16[1024,128]{1,0:T(8,128)(2,1)S(1)}, u32[]{:S(2)}, u32[]{:S(2)}) %collective-permute-start.3) | collective-permute-done | bytes 262176 | tf_op jit(solution)/shard_map/ppermute | solution.py:53
  31.9 0.9 %finish.1 = (bf16[256,128]{1,0:T(8,128)(2,1)}, bf16[4096,128]{1,0:T(8,128)(2,1)}) custom-call(f32[1,136,256]{2,1,0:T(8,128)S(1)} %get-tuple-element.37.keep_ref, bf16[1,272,128]{2,1,0:T(8,128)(2,1)S(1)} %collective-permute-done.1.got_ref, bf16[4096,128]{1,0:T(8,128)(2,1)} %settle.1._, ...), custom_call_target="tpu_custom_call", output_to_operand_aliasing={{1}: (2, {})} | custom-call | tf_op jit(solution)/shard_map/finish/pallas_call | solution.py:492
Async XLA Ops:
  2.2 20.6 %collective-permute-start.2 = (bf16[1024,128]{1,0:T(8,128)(2,1)S(1)}, bf16[1024,128]{1,0:T(8,128)(2,1)S(1)}, u32[]{:S(2)}, u32[]{:S(2)}) collective-permute-start(bf16[1024,128]{1,0:T(8,128)(2,1)S(1)} %get-tuple-element.39), channel_id=1, source_target_pairs={{0,12},{4,8},{8,4},{12,0},{1,13},{5,9},{9,5},{13,1},{2,14},{6,10},... | collective-permute-start | bytes 786440 | tf_op jit(solution)/shard_map/ppermute | solution.py:53
  7.3 24.6 %collective-permute-start.3 = (bf16[1024,128]{1,0:T(8,128)(2,1)S(1)}, bf16[1024,128]{1,0:T(8,128)(2,1)S(1)}, u32[]{:S(2)}, u32[]{:S(2)}) collective-permute-start(bf16[1024,128]{1,0:T(8,128)(2,1)S(1)} %get-tuple-element.41), channel_id=1, source_target_pairs={{0,4},{4,12},{8,0},{12,8},{1,5},{5,13},{9,1},{13,9},{2,6},{6,14},{... | collective-permute-start | bytes 786440 | tf_op jit(solution)/shard_map/ppermute | solution.py:53
  12.6 10.1 %collective-permute-start = (bf16[2,272,128]{2,1,0:T(8,128)(2,1)S(1)}, bf16[2,272,128]{2,1,0:T(8,128)(2,1)S(1)}, u32[]{:S(2)}, u32[]{:S(2)}) collective-permute-start(bf16[2,272,128]{2,1,0:T(8,128)(2,1)S(1)} %get-tuple-element.36), channel_id=1, source_target_pairs={{0,4},{4,0},{8,12},{12,8},{1,5},{5,1},{9,13},{13,9},{2,6},{6,2},{1... | collective-permute-start | bytes 417800 | tf_op jit(solution)/shard_map/ppermute | solution.py:48
  17.5 8.0 %collective-permute-start.4 = (bf16[512,128]{1,0:T(8,128)(2,1)S(1)}, bf16[512,128]{1,0:T(8,128)(2,1)S(1)}, u32[]{:S(2)}, u32[]{:S(2)}) collective-permute-start(bf16[512,128]{1,0:T(8,128)(2,1)S(1)} %get-tuple-element.42), channel_id=1, source_target_pairs={{0,8},{4,0},{8,12},{12,4},{1,9},{5,1},{9,13},{13,5},{2,10},{6,2},{... | collective-permute-start | bytes 393224 | tf_op jit(solution)/shard_map/ppermute | solution.py:53
  19.9 8.8 %collective-permute-start.5 = (bf16[512,128]{1,0:T(8,128)(2,1)S(1)}, bf16[512,128]{1,0:T(8,128)(2,1)S(1)}, u32[]{:S(2)}, u32[]{:S(2)}) collective-permute-start(bf16[512,128]{1,0:T(8,128)(2,1)S(1)} %get-tuple-element.43), channel_id=1, source_target_pairs={{0,8},{4,0},{8,12},{12,4},{1,9},{5,1},{9,13},{13,5},{2,10},{6,2},{... | collective-permute-start | bytes 393224 | tf_op jit(solution)/shard_map/ppermute | solution.py:53
  22.7 6.8 %collective-permute-start.1 = (bf16[1,272,128]{2,1,0:T(8,128)(2,1)S(1)}, bf16[1,272,128]{2,1,0:T(8,128)(2,1)S(1)}, u32[]{:S(2)}, u32[]{:S(2)}) collective-permute-start(bf16[1,272,128]{2,1,0:T(8,128)(2,1)S(1)} %get-tuple-element.38), channel_id=1, source_target_pairs={{0,12},{4,8},{8,4},{12,0},{1,13},{5,9},{9,5},{13,1},{2,14},{6,10},... | collective-permute-start | bytes 208904 | tf_op jit(solution)/shard_map/ppermute | solution.py:48

commit v31 on v30

--- a/solution.py
+++ b/solution.py
@@ -55,7 +55,7 @@
 
 def messages(count, capacity):
     half = capacity // 2
-    ahead = [(k, 0, capacity) for k in reversed(range(count // 2, count))]
+    ahead = [(k, 0, capacity) for k in range(count // 2, count)]
     behind = [(k, first, half) for k in reversed(range(1, count // 2)) for first in (0, half)]
     return ahead, behind, [(0, 0, capacity)]
 

time: 33 us -> 32.3 us (0.979)
  the two profiles are of different devices: /device:TPU:0 before, /device:TPU:16 now
where the time goes in v31:
time: 32.3 us; the launch traced here: 32.1 us
  Pallas kernels  12.8 us (40%)
  waiting for transfers between devices  11.5 us (36%)
  starting transfers between devices  7.09 us (22%)
  between operations  0.68 us (2%)
    ppermute x2, waiting for transfers between devices, exchange(): return lax.ppermute(message, 'seq', [(i, i ^ k) for i in range(count)])  7.04 us
    ppermute x4, starting transfers between devices, hand(): lax.ppermute(message, 'seq', [(i, partner(i, k, count)) for i in range(co...  6.17 us
    pallas_call x1, Pallas kernels, per_device(): pl.pallas_call(first_kernel, out_shape=[leaving(senders), jax.ShapeDtypeS...  5.23 us
    ppermute x4, waiting for transfers between devices, hand(): lax.ppermute(message, 'seq', [(i, partner(i, k, count)) for i in range(co...  4.47 us
    pallas_call x2, Pallas kernels, place(): pl.pallas_call(functools.partial(place_kernel, plan), out_shape=[jax.Shap...  3.09 us
    pallas_call x1, Pallas kernels, per_device(): pl.pallas_call(second_kernel, out_shape=staying(senders), in_specs=[VMEM]...  2.71 us
    ppermute x2, starting transfers between devices, exchange(): return lax.ppermute(message, 'seq', [(i, i ^ k) for i in range(count)])  0.92 us
    pallas_call x1, Pallas kernels, per_device(): pl.pallas_call(functools.partial(finish_kernel, ahead[1:] + behind), out_...  0.88 us
  transfers between devices with their start and end apart: 6, of which 4 were waited for; matrix products, arithmetic and copies ran while one was open for 0% of the time, Pallas kernels for 32%

profile of v31, /device:TPU:16, one launch (start us, length us, event | category | flops | bytes accessed | tf_op | source)
XLA Modules:
  0.0 32.1 jit_solution(3490296969562316813)
XLA Ops:
  0.6 1.6 %place.2 = (bf16[1024,128]{1,0:T(8,128)(2,1)S(1)}, bf16[1024,128]{1,0:T(8,128)(2,1)S(1)}) custom-call(s32[128]{0:T(128)} %owner_any.3, bf16[4096,128]{1,0:T(8,128)(2,1)} %bitcast.14, f32[256,128]{1,0:T(8,128)} %bitcast.18, f32[2,128]{1,0:T(2,128)} %scales_any.3), custom_call_target="tpu_custom_call" | custom-call | tf_op jit(solution)/shard_map/place/pallas_call | solution.py:403
  2.2 0.1 collective-permute-start.2
  2.3 3.0 %collective-permute-start.3 = (bf16[1024,128]{1,0:T(8,128)(2,1)S(1)}, bf16[1024,128]{1,0:T(8,128)(2,1)S(1)}, u32[]{:S(2)}, u32[]{:S(2)}) collective-permute-start(bf16[1024,128]{1,0:T(8,128)(2,1)S(1)} %get-tuple-element.41), channel_id=1, source_target_pairs={{0,12},{4,8},{8,4},{12,0},{1,13},{5,9},{9,5},{13,1},{2,14},{6,10},... | collective-permute-start | bytes 786440 | tf_op jit(solution)/shard_map/ppermute | solution.py:53
  5.3 5.2 %attend_leaving.1 = (bf16[2,272,128]{2,1,0:T(8,128)(2,1)S(1)}, bf16[2048,256]{1,0:T(8,128)(2,1)S(1)}, bf16[128,2048]{1,0:T(8,128)(2,1)S(1)}, bf16[1024,256]{1,0:T(8,128)(2,1)S(1)}, f32[136,256]{1,0:T(8,128)S(1)}) custom-call(bf16[4096,128]{1,0:T(8,128)(2,1)} %bitcast.15, f32[256,128]{1,0:T(8,128)} %bitcast.19, f32[2,128]{1,0:T(2,128)} %scales_any.3, ...), custom_call_target="tpu_custom_call" | custom-call | tf_op jit(solution)/shard_map/attend_leaving/pallas_call | solution.py:433
  10.5 0.4 %collective-permute-start = (bf16[2,272,128]{2,1,0:T(8,128)(2,1)S(1)}, bf16[2,272,128]{2,1,0:T(8,128)(2,1)S(1)}, u32[]{:S(2)}, u32[]{:S(2)}) collective-permute-start(bf16[2,272,128]{2,1,0:T(8,128)(2,1)S(1)} %get-tuple-element.36), channel_id=1, source_target_pairs={{0,4},{4,0},{8,12},{12,8},{1,5},{5,1},{9,13},{13,9},{2,6},{6,2},{1... | collective-permute-start | bytes 417800 | tf_op jit(solution)/shard_map/ppermute | solution.py:48
  10.9 1.5 %place.3 = (bf16[512,128]{1,0:T(8,128)(2,1)S(1)}, bf16[512,128]{1,0:T(8,128)(2,1)S(1)}, bf16[1024,128]{1,0:T(8,128)(2,1)S(1)}) custom-call(s32[128]{0:T(128)} %owner_any.3, bf16[4096,128]{1,0:T(8,128)(2,1)} %bitcast.16, f32[256,128]{1,0:T(8,128)} %bitcast.20, f32[2,128]{1,0:T(2,128)} %scales_any.3), custom_call_target="tpu_custom_call" | custom-call | tf_op jit(solution)/shard_map/place/pallas_call | solution.py:403
  12.5 2.7 %attend_staying.1.keep_ref = f32[2,136,256]{2,1,0:T(8,128)S(1)} custom-call(bf16[2048,256]{1,0:T(8,128)(2,1)S(1)} %get-tuple-element.31.keys_ref, bf16[128,2048]{1,0:T(8,128)(2,1)S(1)} %get-tuple-element.32.turned_ref, bf16[1024,256]{1,0:T(8,128)(2,1)S(1)} %get-tuple-element.33.asked_ref, f32[136,256]{1,0:T(8,128)S(1)} %get-tuple-element.34.own_ref), custom_call_target="tpu_custom_call" | custom-call | tf_op jit(solution)/shard_map/attend_staying/pallas_call | solution.py:461
  15.2 1.7 %collective-permute-start.4 = (bf16[512,128]{1,0:T(8,128)(2,1)S(1)}, bf16[512,128]{1,0:T(8,128)(2,1)S(1)}, u32[]{:S(2)}, u32[]{:S(2)}) collective-permute-start(bf16[512,128]{1,0:T(8,128)(2,1)S(1)} %get-tuple-element.42), channel_id=1, source_target_pairs={{0,8},{4,0},{8,12},{12,4},{1,9},{5,1},{9,13},{13,5},{2,10},{6,2},{... | collective-permute-start | bytes 393224 | tf_op jit(solution)/shard_map/ppermute | solution.py:53
  16.9 1.3 %collective-permute-start.5 = (bf16[512,128]{1,0:T(8,128)(2,1)S(1)}, bf16[512,128]{1,0:T(8,128)(2,1)S(1)}, u32[]{:S(2)}, u32[]{:S(2)}) collective-permute-start(bf16[512,128]{1,0:T(8,128)(2,1)S(1)} %get-tuple-element.43), channel_id=1, source_target_pairs={{0,8},{4,0},{8,12},{12,4},{1,9},{5,1},{9,13},{13,5},{2,10},{6,2},{... | collective-permute-start | bytes 393224 | tf_op jit(solution)/shard_map/ppermute | solution.py:53
  18.3 1.9 %collective-permute-done.got_ref = bf16[2,272,128]{2,1,0:T(8,128)(2,1)S(1)} collective-permute-done((bf16[2,272,128]{2,1,0:T(8,128)(2,1)S(1)}, bf16[2,272,128]{2,1,0:T(8,128)(2,1)S(1)}, u32[]{:S(2)}, u32[]{:S(2)}) %collective-permute-start) | collective-permute-done | bytes 139296 | tf_op jit(solution)/shard_map/ppermute | solution.py:48
  20.1 0.1 join.1
  20.2 0.5 %collective-permute-start.1 = (bf16[1,272,128]{2,1,0:T(8,128)(2,1)S(1)}, bf16[1,272,128]{2,1,0:T(8,128)(2,1)S(1)}, u32[]{:S(2)}, u32[]{:S(2)}) collective-permute-start(bf16[1,272,128]{2,1,0:T(8,128)(2,1)S(1)} %get-tuple-element.38), channel_id=1, source_target_pairs={{0,12},{4,8},{8,4},{12,0},{1,13},{5,9},{9,5},{13,1},{2,14},{6,10},... | collective-permute-start | bytes 208904 | tf_op jit(solution)/shard_map/ppermute | solution.py:48
  20.7 0.0 collective-permute-done.2.refs_0_
  20.7 0.8 %settle.1._ = bf16[4096,128]{1,0:T(8,128)(2,1)} custom-call(bf16[1024,128]{1,0:T(8,128)(2,1)S(1)} %collective-permute-done.2.refs_0_, bf16[1024,128]{1,0:T(8,128)(2,1)S(1)} %get-tuple-element.40.refs_1_), custom_call_target="tpu_custom_call" | custom-call | tf_op jit(solution)/shard_map/settle/pallas_call | solution.py:483
  21.6 1.4 %collective-permute-done.4.refs_1_ = bf16[512,128]{1,0:T(8,128)(2,1)S(1)} collective-permute-done((bf16[512,128]{1,0:T(8,128)(2,1)S(1)}, bf16[512,128]{1,0:T(8,128)(2,1)S(1)}, u32[]{:S(2)}, u32[]{:S(2)}) %collective-permute-start.4) | collective-permute-done | bytes 131104 | tf_op jit(solution)/shard_map/ppermute | solution.py:53
  22.9 3.1 %collective-permute-done.5.refs_2_ = bf16[512,128]{1,0:T(8,128)(2,1)S(1)} collective-permute-done((bf16[512,128]{1,0:T(8,128)(2,1)S(1)}, bf16[512,128]{1,0:T(8,128)(2,1)S(1)}, u32[]{:S(2)}, u32[]{:S(2)}) %collective-permute-start.5) | collective-permute-done | bytes 131104 | tf_op jit(solution)/shard_map/ppermute | solution.py:53
  26.0 5.2 %collective-permute-done.1.got_ref = bf16[1,272,128]{2,1,0:T(8,128)(2,1)S(1)} collective-permute-done((bf16[1,272,128]{2,1,0:T(8,128)(2,1)S(1)}, bf16[1,272,128]{2,1,0:T(8,128)(2,1)S(1)}, u32[]{:S(2)}, u32[]{:S(2)}) %collective-permute-start.1) | collective-permute-done | bytes 69664 | tf_op jit(solution)/shard_map/ppermute | solution.py:48
  31.2 0.0 collective-permute-done.3.refs_0_
  31.2 0.9 %finish.1 = (bf16[256,128]{1,0:T(8,128)(2,1)}, bf16[4096,128]{1,0:T(8,128)(2,1)}) custom-call(f32[1,136,256]{2,1,0:T(8,128)S(1)} %get-tuple-element.37.keep_ref, bf16[1,272,128]{2,1,0:T(8,128)(2,1)S(1)} %collective-permute-done.1.got_ref, bf16[4096,128]{1,0:T(8,128)(2,1)} %settle.1._, ...), custom_call_target="tpu_custom_call", output_to_operand_aliasing={{1}: (2, {})} | custom-call | tf_op jit(solution)/shard_map/finish/pallas_call | solution.py:492
Async XLA Ops:
  2.2 18.5 %collective-permute-start.2 = (bf16[1024,128]{1,0:T(8,128)(2,1)S(1)}, bf16[1024,128]{1,0:T(8,128)(2,1)S(1)}, u32[]{:S(2)}, u32[]{:S(2)}) collective-permute-start(bf16[1024,128]{1,0:T(8,128)(2,1)S(1)} %get-tuple-element.39), channel_id=1, source_target_pairs={{0,4},{4,12},{8,0},{12,8},{1,5},{5,13},{9,1},{13,9},{2,6},{6,14},{... | collective-permute-start | bytes 786440 | tf_op jit(solution)/shard_map/ppermute | solution.py:53
  2.3 28.9 %collective-permute-start.3 = (bf16[1024,128]{1,0:T(8,128)(2,1)S(1)}, bf16[1024,128]{1,0:T(8,128)(2,1)S(1)}, u32[]{:S(2)}, u32[]{:S(2)}) collective-permute-start(bf16[1024,128]{1,0:T(8,128)(2,1)S(1)} %get-tuple-element.41), channel_id=1, source_target_pairs={{0,12},{4,8},{8,4},{12,0},{1,13},{5,9},{9,5},{13,1},{2,14},{6,10},... | collective-permute-start | bytes 786440 | tf_op jit(solution)/shard_map/ppermute | solution.py:53
  10.5 9.6 %collective-permute-start = (bf16[2,272,128]{2,1,0:T(8,128)(2,1)S(1)}, bf16[2,272,128]{2,1,0:T(8,128)(2,1)S(1)}, u32[]{:S(2)}, u32[]{:S(2)}) collective-permute-start(bf16[2,272,128]{2,1,0:T(8,128)(2,1)S(1)} %get-tuple-element.36), channel_id=1, source_target_pairs={{0,4},{4,0},{8,12},{12,8},{1,5},{5,1},{9,13},{13,9},{2,6},{6,2},{1... | collective-permute-start | bytes 417800 | tf_op jit(solution)/shard_map/ppermute | solution.py:48
  15.2 7.8 %collective-permute-start.4 = (bf16[512,128]{1,0:T(8,128)(2,1)S(1)}, bf16[512,128]{1,0:T(8,128)(2,1)S(1)}, u32[]{:S(2)}, u32[]{:S(2)}) collective-permute-start(bf16[512,128]{1,0:T(8,128)(2,1)S(1)} %get-tuple-element.42), channel_id=1, source_target_pairs={{0,8},{4,0},{8,12},{12,4},{1,9},{5,1},{9,13},{13,5},{2,10},{6,2},{... | collective-permute-start | bytes 393224 | tf_op jit(solution)/shard_map/ppermute | solution.py:53
  16.9 9.1 %collective-permute-start.5 = (bf16[512,128]{1,0:T(8,128)(2,1)S(1)}, bf16[512,128]{1,0:T(8,128)(2,1)S(1)}, u32[]{:S(2)}, u32[]{:S(2)}) collective-permute-start(bf16[512,128]{1,0:T(8,128)(2,1)S(1)} %get-tuple-element.43), channel_id=1, source_target_pairs={{0,8},{4,0},{8,12},{12,4},{1,9},{5,1},{9,13},{13,5},{2,10},{6,2},{... | collective-permute-start | bytes 393224 | tf_op jit(solution)/shard_map/ppermute | solution.py:53
  20.2 11.0 %collective-permute-start.1 = (bf16[1,272,128]{2,1,0:T(8,128)(2,1)S(1)}, bf16[1,272,128]{2,1,0:T(8,128)(2,1)S(1)}, u32[]{:S(2)}, u32[]{:S(2)}) collective-permute-start(bf16[1,272,128]{2,1,0:T(8,128)(2,1)S(1)} %get-tuple-element.38), channel_id=1, source_target_pairs={{0,12},{4,8},{8,4},{12,0},{1,13},{5,9},{9,5},{13,1},{2,14},{6,10},... | collective-permute-start | bytes 208904 | tf_op jit(solution)/shard_map/ppermute | solution.py:48

commit v32 on v28

--- a/solution.py
+++ b/solution.py
@@ -463,7 +463,6 @@
     send, late_deltas = lax.optimization_barrier((send, late_deltas))
     passed = exchange(send, k)
     *sent, mine = place(behind + own, late_deltas)
-    got = got_ahead[1:] + [hand(message, k) for message, (k, _, _) in zip(sent, behind)]
     keep = pl.pallas_call(
         second_kernel,
         out_shape=staying(senders),
@@ -472,6 +471,8 @@
         compiler_params=roomy,
         name="attend_staying",
     )(*common)
+    sent, keep = lax.optimization_barrier((sent, keep))
+    got = got_ahead[1:] + [hand(message, partner) for message, (partner, _, _) in zip(sent, behind)]
     while count > 1:
         send, keep = pl.pallas_call(
             join_kernel,

time: 32.2 us -> 32.2 us (level)
  no operation moved by 1% of the time
where the time goes in v32:
time: 32.2 us; the launch traced here: 32 us
  Pallas kernels  12.8 us (40%)
  waiting for transfers between devices  11.9 us (37%)
  starting transfers between devices  6.56 us (20%)
  between operations  0.68 us (2%)
    ppermute x2, waiting for transfers between devices, exchange(): lax.ppermute(message, 'seq', [(i, i ^ k ^ (last and i < count // 2)) for...  8.79 us
    pallas_call x1, Pallas kernels, per_device(): pl.pallas_call(first_kernel, out_shape=[leaving(senders), jax.ShapeDtypeS...  5.23 us
    ppermute x4, starting transfers between devices, hand(): lax.ppermute(message, 'seq', [(i, partner(i, k, count)) for i in range(co...  3.37 us
    ppermute x2, starting transfers between devices, exchange(): lax.ppermute(message, 'seq', [(i, i ^ k ^ (last and i < count // 2)) for...  3.2 us
    ppermute x4, waiting for transfers between devices, hand(): lax.ppermute(message, 'seq', [(i, partner(i, k, count)) for i in range(co...  3.14 us
    pallas_call x2, Pallas kernels, place(): pl.pallas_call(functools.partial(place_kernel, plan), out_shape=[jax.Shap...  3.09 us
    pallas_call x1, Pallas kernels, per_device(): pl.pallas_call(second_kernel, out_shape=staying(senders), in_specs=[VMEM]...  2.71 us
    pallas_call x1, Pallas kernels, per_device(): pl.pallas_call(functools.partial(finish_kernel, ahead[1:] + behind), out_...  0.88 us
  transfers between devices with their start and end apart: 6, of which 4 were waited for; matrix products, arithmetic and copies ran while one was open for 0% of the time, Pallas kernels for 32%

profile of v32, /device:TPU:24, one launch (start us, length us, event | category | flops | bytes accessed | tf_op | source)
XLA Modules:
  0.0 32.0 jit_solution(11361887074769354747)
XLA Ops:
  0.6 1.6 %place.2 = (bf16[1024,128]{1,0:T(8,128)(2,1)S(1)}, bf16[1024,128]{1,0:T(8,128)(2,1)S(1)}) custom-call(s32[128]{0:T(128)} %owner_any.3, bf16[4096,128]{1,0:T(8,128)(2,1)} %bitcast.14, f32[256,128]{1,0:T(8,128)} %bitcast.18, f32[2,128]{1,0:T(2,128)} %scales_any.3), custom_call_target="tpu_custom_call" | custom-call | tf_op jit(solution)/shard_map/place/pallas_call | solution.py:408
  2.2 0.5 %collective-permute-start.2 = (bf16[1024,128]{1,0:T(8,128)(2,1)S(1)}, bf16[1024,128]{1,0:T(8,128)(2,1)S(1)}, u32[]{:S(2)}, u32[]{:S(2)}) collective-permute-start(bf16[1024,128]{1,0:T(8,128)(2,1)S(1)} %get-tuple-element.39), channel_id=1, source_target_pairs={{0,4},{4,12},{8,0},{12,8},{1,5},{5,13},{9,1},{13,9},{2,6},{6,14},{... | collective-permute-start | bytes 786440 | tf_op jit(solution)/shard_map/ppermute | solution.py:54
  2.7 1.3 %collective-permute-start.3 = (bf16[1024,128]{1,0:T(8,128)(2,1)S(1)}, bf16[1024,128]{1,0:T(8,128)(2,1)S(1)}, u32[]{:S(2)}, u32[]{:S(2)}) collective-permute-start(bf16[1024,128]{1,0:T(8,128)(2,1)S(1)} %get-tuple-element.41), channel_id=1, source_target_pairs={{0,12},{4,8},{8,4},{12,0},{1,13},{5,9},{9,5},{13,1},{2,14},{6,10},... | collective-permute-start | bytes 786440 | tf_op jit(solution)/shard_map/ppermute | solution.py:54
  4.1 5.2 %attend_leaving.1 = (bf16[2,272,128]{2,1,0:T(8,128)(2,1)S(1)}, bf16[2048,256]{1,0:T(8,128)(2,1)S(1)}, bf16[128,2048]{1,0:T(8,128)(2,1)S(1)}, bf16[1024,256]{1,0:T(8,128)(2,1)S(1)}, f32[136,256]{1,0:T(8,128)S(1)}) custom-call(bf16[4096,128]{1,0:T(8,128)(2,1)} %bitcast.15, f32[256,128]{1,0:T(8,128)} %bitcast.19, f32[2,128]{1,0:T(2,128)} %scales_any.3, ...), custom_call_target="tpu_custom_call" | custom-call | tf_op jit(solution)/shard_map/attend_leaving/pallas_call | solution.py:438
  9.3 1.8 %collective-permute-start = (bf16[2,272,128]{2,1,0:T(8,128)(2,1)S(1)}, bf16[2,272,128]{2,1,0:T(8,128)(2,1)S(1)}, u32[]{:S(2)}, u32[]{:S(2)}) collective-permute-start(bf16[2,272,128]{2,1,0:T(8,128)(2,1)S(1)} %get-tuple-element.36), channel_id=1, source_target_pairs={{0,4},{4,0},{8,12},{12,8},{1,5},{5,1},{9,13},{13,9},{2,6},{6,2},{1... | collective-permute-start | bytes 417800 | tf_op jit(solution)/shard_map/ppermute | solution.py:49
  11.1 1.5 %place.3 = (bf16[512,128]{1,0:T(8,128)(2,1)S(1)}, bf16[512,128]{1,0:T(8,128)(2,1)S(1)}, bf16[1024,128]{1,0:T(8,128)(2,1)S(1)}) custom-call(s32[128]{0:T(128)} %owner_any.3, bf16[4096,128]{1,0:T(8,128)(2,1)} %bitcast.16, f32[256,128]{1,0:T(8,128)} %bitcast.20, f32[2,128]{1,0:T(2,128)} %scales_any.3), custom_call_target="tpu_custom_call" | custom-call | tf_op jit(solution)/shard_map/place/pallas_call | solution.py:408
  12.6 2.7 %attend_staying.1.keep_ref = f32[2,136,256]{2,1,0:T(8,128)S(1)} custom-call(bf16[2048,256]{1,0:T(8,128)(2,1)S(1)} %get-tuple-element.31.keys_ref, bf16[128,2048]{1,0:T(8,128)(2,1)S(1)} %get-tuple-element.32.turned_ref, bf16[1024,256]{1,0:T(8,128)(2,1)S(1)} %get-tuple-element.33.asked_ref, f32[136,256]{1,0:T(8,128)S(1)} %get-tuple-element.34.own_ref), custom_call_target="tpu_custom_call" | custom-call | tf_op jit(solution)/shard_map/attend_staying/pallas_call | solution.py:466
  15.3 1.4 %collective-permute-start.4 = (bf16[512,128]{1,0:T(8,128)(2,1)S(1)}, bf16[512,128]{1,0:T(8,128)(2,1)S(1)}, u32[]{:S(2)}, u32[]{:S(2)}) collective-permute-start(bf16[512,128]{1,0:T(8,128)(2,1)S(1)} %get-tuple-element.42), channel_id=1, source_target_pairs={{0,8},{4,0},{8,12},{12,4},{1,9},{5,1},{9,13},{13,5},{2,10},{6,2},{... | collective-permute-start | bytes 393224 | tf_op jit(solution)/shard_map/ppermute | solution.py:54
  16.7 0.1 collective-permute-start.5
  16.8 3.1 %collective-permute-done.got_ref = bf16[2,272,128]{2,1,0:T(8,128)(2,1)S(1)} collective-permute-done((bf16[2,272,128]{2,1,0:T(8,128)(2,1)S(1)}, bf16[2,272,128]{2,1,0:T(8,128)(2,1)S(1)}, u32[]{:S(2)}, u32[]{:S(2)}) %collective-permute-start) | collective-permute-done | bytes 139296 | tf_op jit(solution)/shard_map/ppermute | solution.py:49
  20.0 0.1 join.1
  20.0 1.4 %collective-permute-start.1 = (bf16[1,272,128]{2,1,0:T(8,128)(2,1)S(1)}, bf16[1,272,128]{2,1,0:T(8,128)(2,1)S(1)}, u32[]{:S(2)}, u32[]{:S(2)}) collective-permute-start(bf16[1,272,128]{2,1,0:T(8,128)(2,1)S(1)} %get-tuple-element.38), channel_id=1, source_target_pairs={{0,8},{4,12},{8,4},{12,0},{1,9},{5,13},{9,5},{13,1},{2,10},{6,14},... | collective-permute-start | bytes 208904 | tf_op jit(solution)/shard_map/ppermute | solution.py:49
  21.5 0.0 collective-permute-done.2.refs_0_
  21.5 0.8 %settle.1._ = bf16[4096,128]{1,0:T(8,128)(2,1)} custom-call(bf16[1024,128]{1,0:T(8,128)(2,1)S(1)} %collective-permute-done.2.refs_0_, bf16[1024,128]{1,0:T(8,128)(2,1)S(1)} %get-tuple-element.40.refs_1_), custom_call_target="tpu_custom_call" | custom-call | tf_op jit(solution)/shard_map/settle/pallas_call | solution.py:488
  22.3 0.5 %collective-permute-done.4.refs_1_ = bf16[512,128]{1,0:T(8,128)(2,1)S(1)} collective-permute-done((bf16[512,128]{1,0:T(8,128)(2,1)S(1)}, bf16[512,128]{1,0:T(8,128)(2,1)S(1)}, u32[]{:S(2)}, u32[]{:S(2)}) %collective-permute-start.4) | collective-permute-done | bytes 131104 | tf_op jit(solution)/shard_map/ppermute | solution.py:54
  22.8 2.7 %collective-permute-done.5.refs_2_ = bf16[512,128]{1,0:T(8,128)(2,1)S(1)} collective-permute-done((bf16[512,128]{1,0:T(8,128)(2,1)S(1)}, bf16[512,128]{1,0:T(8,128)(2,1)S(1)}, u32[]{:S(2)}, u32[]{:S(2)}) %collective-permute-start.5) | collective-permute-done | bytes 131104 | tf_op jit(solution)/shard_map/ppermute | solution.py:54
  25.4 5.6 %collective-permute-done.1.got_ref = bf16[1,272,128]{2,1,0:T(8,128)(2,1)S(1)} collective-permute-done((bf16[1,272,128]{2,1,0:T(8,128)(2,1)S(1)}, bf16[1,272,128]{2,1,0:T(8,128)(2,1)S(1)}, u32[]{:S(2)}, u32[]{:S(2)}) %collective-permute-start.1) | collective-permute-done | bytes 69664 | tf_op jit(solution)/shard_map/ppermute | solution.py:49
  31.1 0.0 collective-permute-done.3.refs_0_
  31.1 0.9 %finish.1 = (bf16[256,128]{1,0:T(8,128)(2,1)}, bf16[4096,128]{1,0:T(8,128)(2,1)}) custom-call(f32[1,136,256]{2,1,0:T(8,128)S(1)} %get-tuple-element.37.keep_ref, bf16[1,272,128]{2,1,0:T(8,128)(2,1)S(1)} %collective-permute-done.1.got_ref, bf16[4096,128]{1,0:T(8,128)(2,1)} %settle.1._, ...), custom_call_target="tpu_custom_call", output_to_operand_aliasing={{1}: (2, {})} | custom-call | tf_op jit(solution)/shard_map/finish/pallas_call | solution.py:497
Async XLA Ops:
  2.2 19.3 %collective-permute-start.2 = (bf16[1024,128]{1,0:T(8,128)(2,1)S(1)}, bf16[1024,128]{1,0:T(8,128)(2,1)S(1)}, u32[]{:S(2)}, u32[]{:S(2)}) collective-permute-start(bf16[1024,128]{1,0:T(8,128)(2,1)S(1)} %get-tuple-element.39), channel_id=1, source_target_pairs={{0,4},{4,12},{8,0},{12,8},{1,5},{5,13},{9,1},{13,9},{2,6},{6,14},{... | collective-permute-start | bytes 786440 | tf_op jit(solution)/shard_map/ppermute | solution.py:54
  2.7 28.4 %collective-permute-start.3 = (bf16[1024,128]{1,0:T(8,128)(2,1)S(1)}, bf16[1024,128]{1,0:T(8,128)(2,1)S(1)}, u32[]{:S(2)}, u32[]{:S(2)}) collective-permute-start(bf16[1024,128]{1,0:T(8,128)(2,1)S(1)} %get-tuple-element.41), channel_id=1, source_target_pairs={{0,12},{4,8},{8,4},{12,0},{1,13},{5,9},{9,5},{13,1},{2,14},{6,10},... | collective-permute-start | bytes 786440 | tf_op jit(solution)/shard_map/ppermute | solution.py:54
  9.3 10.7 %collective-permute-start = (bf16[2,272,128]{2,1,0:T(8,128)(2,1)S(1)}, bf16[2,272,128]{2,1,0:T(8,128)(2,1)S(1)}, u32[]{:S(2)}, u32[]{:S(2)}) collective-permute-start(bf16[2,272,128]{2,1,0:T(8,128)(2,1)S(1)} %get-tuple-element.36), channel_id=1, source_target_pairs={{0,4},{4,0},{8,12},{12,8},{1,5},{5,1},{9,13},{13,9},{2,6},{6,2},{1... | collective-permute-start | bytes 417800 | tf_op jit(solution)/shard_map/ppermute | solution.py:49
  15.3 7.5 %collective-permute-start.4 = (bf16[512,128]{1,0:T(8,128)(2,1)S(1)}, bf16[512,128]{1,0:T(8,128)(2,1)S(1)}, u32[]{:S(2)}, u32[]{:S(2)}) collective-permute-start(bf16[512,128]{1,0:T(8,128)(2,1)S(1)} %get-tuple-element.42), channel_id=1, source_target_pairs={{0,8},{4,0},{8,12},{12,4},{1,9},{5,1},{9,13},{13,5},{2,10},{6,2},{... | collective-permute-start | bytes 393224 | tf_op jit(solution)/shard_map/ppermute | solution.py:54
  16.7 8.7 %collective-permute-start.5 = (bf16[512,128]{1,0:T(8,128)(2,1)S(1)}, bf16[512,128]{1,0:T(8,128)(2,1)S(1)}, u32[]{:S(2)}, u32[]{:S(2)}) collective-permute-start(bf16[512,128]{1,0:T(8,128)(2,1)S(1)} %get-tuple-element.43), channel_id=1, source_target_pairs={{0,8},{4,0},{8,12},{12,4},{1,9},{5,1},{9,13},{13,5},{2,10},{6,2},{... | collective-permute-start | bytes 393224 | tf_op jit(solution)/shard_map/ppermute | solution.py:54
  20.0 11.0 %collective-permute-start.1 = (bf16[1,272,128]{2,1,0:T(8,128)(2,1)S(1)}, bf16[1,272,128]{2,1,0:T(8,128)(2,1)S(1)}, u32[]{:S(2)}, u32[]{:S(2)}) collective-permute-start(bf16[1,272,128]{2,1,0:T(8,128)(2,1)S(1)} %get-tuple-element.38), channel_id=1, source_target_pairs={{0,8},{4,12},{8,4},{12,0},{1,9},{5,13},{9,5},{13,1},{2,10},{6,14},... | collective-permute-start | bytes 208904 | tf_op jit(solution)/shard_map/ppermute | solution.py:49

commit v33 on v32

--- a/solution.py
+++ b/solution.py
@@ -484,7 +484,7 @@
         )(keep, passed)
         k, count = 2 * k + 1, count // 2
         passed = exchange(send, k)
-    settled = ahead[:1] + own
+    settled = ahead[:1] + behind + own
     pages = pl.pallas_call(
         functools.partial(settle_kernel, settled),
         out_shape=whole,
@@ -493,20 +493,20 @@
         scratch_shapes=[pltpu.SemaphoreType.DMA((len(settled),))],
         compiler_params=small,
         name="settle",
-    )(got_ahead[0], mine)
+    )(got_ahead[0], *got[len(ahead) - 1 :], mine)
     attended, pages = pl.pallas_call(
-        functools.partial(finish_kernel, ahead[1:] + behind),
+        functools.partial(finish_kernel, ahead[1:]),
         out_shape=[jax.ShapeDtypeStruct((width, HD), jnp.bfloat16), whole],
-        in_specs=[VMEM] * 2 + [HBM] + [ANY] * len(got),
+        in_specs=[VMEM] * 2 + [HBM] + [ANY] * len(ahead[1:]),
         out_specs=[HBM, HBM],
         scratch_shapes=[
             pltpu.VMEM((width, HD), jnp.bfloat16),
-            pltpu.SemaphoreType.DMA((len(got) + 1,)),
+            pltpu.SemaphoreType.DMA((len(ahead),)),
         ],
         input_output_aliases={2: 1},
         compiler_params=small,
         name="finish",
-    )(keep, passed, pages, *got)
+    )(keep, passed, pages, *got_ahead[1:])
     pages = pages.reshape(blocks, tokens // blocks, 2, HD)
     attended = (
         attended.reshape(rows_dev, GQ, steps, HD).transpose(0, 2, 1, 3).reshape(rows_dev, steps, GQ * HD)

time: 32.2 us -> 32.1 us (level)
    ppermute x2, waiting for transfers between devices: 8.79 us -> 7.87 us  [exchange(): lax.ppermute(message, 'seq', [(i, i ^ k ^ (last and i < count // 2)) for...]
    ppermute x4, waiting for transfers between devices: 3.14 us -> 3.96 us  [hand(): lax.ppermute(message, 'seq', [(i, partner(i, k, count)) for i in range(co...]
  transfers between devices with their start and end apart: 6 -> 6, of which waited for: 4 -> 4; matrix products, arithmetic and copies ran while one was open for 0% -> 0% of each run, Pallas kernels for 32% -> 33%
where the time goes in v33:
time: 32.1 us; the launch traced here: 31.9 us
  Pallas kernels  12.8 us (40%)
  waiting for transfers between devices  11.8 us (37%)
  starting transfers between devices  6.56 us (20%)
  between operations  0.68 us (2%)
    ppermute x2, waiting for transfers between devices, exchange(): lax.ppermute(message, 'seq', [(i, i ^ k ^ (last and i < count // 2)) for...  7.87 us
    pallas_call x1, Pallas kernels, per_device(): pl.pallas_call(first_kernel, out_shape=[leaving(senders), jax.ShapeDtypeS...  5.23 us
    ppermute x4, waiting for transfers between devices, hand(): lax.ppermute(message, 'seq', [(i, partner(i, k, count)) for i in range(co...  3.96 us
    ppermute x4, starting transfers between devices, hand(): lax.ppermute(message, 'seq', [(i, partner(i, k, count)) for i in range(co...  3.37 us
    ppermute x2, starting transfers between devices, exchange(): lax.ppermute(message, 'seq', [(i, i ^ k ^ (last and i < count // 2)) for...  3.2 us
    pallas_call x2, Pallas kernels, place(): pl.pallas_call(functools.partial(place_kernel, plan), out_shape=[jax.Shap...  3.09 us
    pallas_call x1, Pallas kernels, per_device(): pl.pallas_call(second_kernel, out_shape=staying(senders), in_specs=[VMEM]...  2.71 us
    pallas_call x1, Pallas kernels, per_device(): pl.pallas_call(functools.partial(settle_kernel, settled), out_shape=whole...  0.91 us
  transfers between devices with their start and end apart: 6, of which 4 were waited for; matrix products, arithmetic and copies ran while one was open for 0% of the time, Pallas kernels for 33%

profile of v33, /device:TPU:24, one launch (start us, length us, event | category | flops | bytes accessed | tf_op | source)
XLA Modules:
  0.0 31.9 jit_solution(6009430615589193145)
XLA Ops:
  0.6 1.6 %place.2 = (bf16[1024,128]{1,0:T(8,128)(2,1)S(1)}, bf16[1024,128]{1,0:T(8,128)(2,1)S(1)}) custom-call(s32[128]{0:T(128)} %owner_any.3, bf16[4096,128]{1,0:T(8,128)(2,1)} %bitcast.14, f32[256,128]{1,0:T(8,128)} %bitcast.18, f32[2,128]{1,0:T(2,128)} %scales_any.3), custom_call_target="tpu_custom_call" | custom-call | tf_op jit(solution)/shard_map/place/pallas_call | solution.py:408
  2.2 0.5 %collective-permute-start.2 = (bf16[1024,128]{1,0:T(8,128)(2,1)S(1)}, bf16[1024,128]{1,0:T(8,128)(2,1)S(1)}, u32[]{:S(2)}, u32[]{:S(2)}) collective-permute-start(bf16[1024,128]{1,0:T(8,128)(2,1)S(1)} %get-tuple-element.39), channel_id=1, source_target_pairs={{0,4},{4,12},{8,0},{12,8},{1,5},{5,13},{9,1},{13,9},{2,6},{6,14},{... | collective-permute-start | bytes 786440 | tf_op jit(solution)/shard_map/ppermute | solution.py:54
  2.7 1.3 %collective-permute-start.5 = (bf16[1024,128]{1,0:T(8,128)(2,1)S(1)}, bf16[1024,128]{1,0:T(8,128)(2,1)S(1)}, u32[]{:S(2)}, u32[]{:S(2)}) collective-permute-start(bf16[1024,128]{1,0:T(8,128)(2,1)S(1)} %get-tuple-element.43), channel_id=1, source_target_pairs={{0,12},{4,8},{8,4},{12,0},{1,13},{5,9},{9,5},{13,1},{2,14},{6,10},... | collective-permute-start | bytes 786440 | tf_op jit(solution)/shard_map/ppermute | solution.py:54
  4.1 5.2 %attend_leaving.1 = (bf16[2,272,128]{2,1,0:T(8,128)(2,1)S(1)}, bf16[2048,256]{1,0:T(8,128)(2,1)S(1)}, bf16[128,2048]{1,0:T(8,128)(2,1)S(1)}, bf16[1024,256]{1,0:T(8,128)(2,1)S(1)}, f32[136,256]{1,0:T(8,128)S(1)}) custom-call(bf16[4096,128]{1,0:T(8,128)(2,1)} %bitcast.15, f32[256,128]{1,0:T(8,128)} %bitcast.19, f32[2,128]{1,0:T(2,128)} %scales_any.3, ...), custom_call_target="tpu_custom_call" | custom-call | tf_op jit(solution)/shard_map/attend_leaving/pallas_call | solution.py:438
  9.3 1.8 %collective-permute-start = (bf16[2,272,128]{2,1,0:T(8,128)(2,1)S(1)}, bf16[2,272,128]{2,1,0:T(8,128)(2,1)S(1)}, u32[]{:S(2)}, u32[]{:S(2)}) collective-permute-start(bf16[2,272,128]{2,1,0:T(8,128)(2,1)S(1)} %get-tuple-element.36), channel_id=1, source_target_pairs={{0,4},{4,0},{8,12},{12,8},{1,5},{5,1},{9,13},{13,9},{2,6},{6,2},{1... | collective-permute-start | bytes 417800 | tf_op jit(solution)/shard_map/ppermute | solution.py:49
  11.1 1.5 %place.3 = (bf16[512,128]{1,0:T(8,128)(2,1)S(1)}, bf16[512,128]{1,0:T(8,128)(2,1)S(1)}, bf16[1024,128]{1,0:T(8,128)(2,1)S(1)}) custom-call(s32[128]{0:T(128)} %owner_any.3, bf16[4096,128]{1,0:T(8,128)(2,1)} %bitcast.16, f32[256,128]{1,0:T(8,128)} %bitcast.20, f32[2,128]{1,0:T(2,128)} %scales_any.3), custom_call_target="tpu_custom_call" | custom-call | tf_op jit(solution)/shard_map/place/pallas_call | solution.py:408
  12.6 2.7 %attend_staying.1.keep_ref = f32[2,136,256]{2,1,0:T(8,128)S(1)} custom-call(bf16[2048,256]{1,0:T(8,128)(2,1)S(1)} %get-tuple-element.31.keys_ref, bf16[128,2048]{1,0:T(8,128)(2,1)S(1)} %get-tuple-element.32.turned_ref, bf16[1024,256]{1,0:T(8,128)(2,1)S(1)} %get-tuple-element.33.asked_ref, f32[136,256]{1,0:T(8,128)S(1)} %get-tuple-element.34.own_ref), custom_call_target="tpu_custom_call" | custom-call | tf_op jit(solution)/shard_map/attend_staying/pallas_call | solution.py:466
  15.3 1.4 %collective-permute-start.3 = (bf16[512,128]{1,0:T(8,128)(2,1)S(1)}, bf16[512,128]{1,0:T(8,128)(2,1)S(1)}, u32[]{:S(2)}, u32[]{:S(2)}) collective-permute-start(bf16[512,128]{1,0:T(8,128)(2,1)S(1)} %get-tuple-element.40), channel_id=1, source_target_pairs={{0,8},{4,0},{8,12},{12,4},{1,9},{5,1},{9,13},{13,5},{2,10},{6,2},{... | collective-permute-start | bytes 393224 | tf_op jit(solution)/shard_map/ppermute | solution.py:54
  16.7 0.1 collective-permute-start.4
  16.8 3.1 %collective-permute-done.got_ref = bf16[2,272,128]{2,1,0:T(8,128)(2,1)S(1)} collective-permute-done((bf16[2,272,128]{2,1,0:T(8,128)(2,1)S(1)}, bf16[2,272,128]{2,1,0:T(8,128)(2,1)S(1)}, u32[]{:S(2)}, u32[]{:S(2)}) %collective-permute-start) | collective-permute-done | bytes 139296 | tf_op jit(solution)/shard_map/ppermute | solution.py:49
  20.0 0.1 join.1
  20.0 1.4 %collective-permute-start.1 = (bf16[1,272,128]{2,1,0:T(8,128)(2,1)S(1)}, bf16[1,272,128]{2,1,0:T(8,128)(2,1)S(1)}, u32[]{:S(2)}, u32[]{:S(2)}) collective-permute-start(bf16[1,272,128]{2,1,0:T(8,128)(2,1)S(1)} %get-tuple-element.38), channel_id=1, source_target_pairs={{0,8},{4,12},{8,4},{12,0},{1,9},{5,13},{9,5},{13,1},{2,10},{6,14},... | collective-permute-start | bytes 208904 | tf_op jit(solution)/shard_map/ppermute | solution.py:49
  21.5 1.3 %collective-permute-done.3.refs_1_ = bf16[512,128]{1,0:T(8,128)(2,1)S(1)} collective-permute-done((bf16[512,128]{1,0:T(8,128)(2,1)S(1)}, bf16[512,128]{1,0:T(8,128)(2,1)S(1)}, u32[]{:S(2)}, u32[]{:S(2)}) %collective-permute-start.3) | collective-permute-done | bytes 131104 | tf_op jit(solution)/shard_map/ppermute | solution.py:54
  22.8 2.7 %collective-permute-done.4.refs_2_ = bf16[512,128]{1,0:T(8,128)(2,1)S(1)} collective-permute-done((bf16[512,128]{1,0:T(8,128)(2,1)S(1)}, bf16[512,128]{1,0:T(8,128)(2,1)S(1)}, u32[]{:S(2)}, u32[]{:S(2)}) %collective-permute-start.4) | collective-permute-done | bytes 131104 | tf_op jit(solution)/shard_map/ppermute | solution.py:54
  25.4 0.0 collective-permute-done.2.refs_0_
  25.4 0.9 %settle.1._ = bf16[4096,128]{1,0:T(8,128)(2,1)} custom-call(bf16[1024,128]{1,0:T(8,128)(2,1)S(1)} %collective-permute-done.2.refs_0_, bf16[512,128]{1,0:T(8,128)(2,1)S(1)} %collective-permute-done.3.refs_1_, bf16[512,128]{1,0:T(8,128)(2,1)S(1)} %collective-permute-done.4.refs_2_, bf16[1024,128]{1,0:T(8,128)(2,1)S(1)} %get-tuple-element.42.refs_3_), custom_call_target="tpu_custom_call" | custom-call | tf_op jit(solution)/shard_map/settle/pallas_call | solution.py:488
  26.4 4.7 %collective-permute-done.1.got_ref = bf16[1,272,128]{2,1,0:T(8,128)(2,1)S(1)} collective-permute-done((bf16[1,272,128]{2,1,0:T(8,128)(2,1)S(1)}, bf16[1,272,128]{2,1,0:T(8,128)(2,1)S(1)}, u32[]{:S(2)}, u32[]{:S(2)}) %collective-permute-start.1) | collective-permute-done | bytes 69664 | tf_op jit(solution)/shard_map/ppermute | solution.py:49
  31.1 0.0 collective-permute-done.5.refs_0_
  31.1 0.8 %finish.1 = (bf16[256,128]{1,0:T(8,128)(2,1)}, bf16[4096,128]{1,0:T(8,128)(2,1)}) custom-call(f32[1,136,256]{2,1,0:T(8,128)S(1)} %get-tuple-element.37.keep_ref, bf16[1,272,128]{2,1,0:T(8,128)(2,1)S(1)} %collective-permute-done.1.got_ref, bf16[4096,128]{1,0:T(8,128)(2,1)} %settle.1._, ...), custom_call_target="tpu_custom_call", output_to_operand_aliasing={{1}: (2, {})} | custom-call | tf_op jit(solution)/shard_map/finish/pallas_call | solution.py:497
Async XLA Ops:
  2.2 23.2 %collective-permute-start.2 = (bf16[1024,128]{1,0:T(8,128)(2,1)S(1)}, bf16[1024,128]{1,0:T(8,128)(2,1)S(1)}, u32[]{:S(2)}, u32[]{:S(2)}) collective-permute-start(bf16[1024,128]{1,0:T(8,128)(2,1)S(1)} %get-tuple-element.39), channel_id=1, source_target_pairs={{0,4},{4,12},{8,0},{12,8},{1,5},{5,13},{9,1},{13,9},{2,6},{6,14},{... | collective-permute-start | bytes 786440 | tf_op jit(solution)/shard_map/ppermute | solution.py:54
  2.7 28.4 %collective-permute-start.5 = (bf16[1024,128]{1,0:T(8,128)(2,1)S(1)}, bf16[1024,128]{1,0:T(8,128)(2,1)S(1)}, u32[]{:S(2)}, u32[]{:S(2)}) collective-permute-start(bf16[1024,128]{1,0:T(8,128)(2,1)S(1)} %get-tuple-element.43), channel_id=1, source_target_pairs={{0,12},{4,8},{8,4},{12,0},{1,13},{5,9},{9,5},{13,1},{2,14},{6,10},... | collective-permute-start | bytes 786440 | tf_op jit(solution)/shard_map/ppermute | solution.py:54
  9.3 10.7 %collective-permute-start = (bf16[2,272,128]{2,1,0:T(8,128)(2,1)S(1)}, bf16[2,272,128]{2,1,0:T(8,128)(2,1)S(1)}, u32[]{:S(2)}, u32[]{:S(2)}) collective-permute-start(bf16[2,272,128]{2,1,0:T(8,128)(2,1)S(1)} %get-tuple-element.36), channel_id=1, source_target_pairs={{0,4},{4,0},{8,12},{12,8},{1,5},{5,1},{9,13},{13,9},{2,6},{6,2},{1... | collective-permute-start | bytes 417800 | tf_op jit(solution)/shard_map/ppermute | solution.py:49
  15.3 7.5 %collective-permute-start.3 = (bf16[512,128]{1,0:T(8,128)(2,1)S(1)}, bf16[512,128]{1,0:T(8,128)(2,1)S(1)}, u32[]{:S(2)}, u32[]{:S(2)}) collective-permute-start(bf16[512,128]{1,0:T(8,128)(2,1)S(1)} %get-tuple-element.40), channel_id=1, source_target_pairs={{0,8},{4,0},{8,12},{12,4},{1,9},{5,1},{9,13},{13,5},{2,10},{6,2},{... | collective-permute-start | bytes 393224 | tf_op jit(solution)/shard_map/ppermute | solution.py:54
  16.7 8.7 %collective-permute-start.4 = (bf16[512,128]{1,0:T(8,128)(2,1)S(1)}, bf16[512,128]{1,0:T(8,128)(2,1)S(1)}, u32[]{:S(2)}, u32[]{:S(2)}) collective-permute-start(bf16[512,128]{1,0:T(8,128)(2,1)S(1)} %get-tuple-element.41), channel_id=1, source_target_pairs={{0,8},{4,0},{8,12},{12,4},{1,9},{5,1},{9,13},{13,5},{2,10},{6,2},{... | collective-permute-start | bytes 393224 | tf_op jit(solution)/shard_map/ppermute | solution.py:54
  20.0 11.0 %collective-permute-start.1 = (bf16[1,272,128]{2,1,0:T(8,128)(2,1)S(1)}, bf16[1,272,128]{2,1,0:T(8,128)(2,1)S(1)}, u32[]{:S(2)}, u32[]{:S(2)}) collective-permute-start(bf16[1,272,128]{2,1,0:T(8,128)(2,1)S(1)} %get-tuple-element.38), channel_id=1, source_target_pairs={{0,8},{4,12},{8,4},{12,0},{1,9},{5,13},{9,5},{13,1},{2,10},{6,14},... | collective-permute-start | bytes 208904 | tf_op jit(solution)/shard_map/ppermute | solution.py:49

commit v34 on v33

--- a/solution.py
+++ b/solution.py
@@ -45,8 +45,7 @@
 
 def exchange(message, k):
     count = lax.axis_size("seq")
-    last = k == count - 1
-    return lax.ppermute(message, "seq", [(i, i ^ k ^ (last and i < count // 2)) for i in range(count)])
+    return lax.ppermute(message, "seq", [(i, i ^ k) for i in range(count)])
 
 
 def hand(message, k):
@@ -192,8 +191,6 @@
 
 def attend(parity, width, keys_ref, turned_ref, asked_ref, store):
     me = lax.axis_index("seq")
-    far = lax.axis_size("seq") // 2
-    lower = 1 - me // far
     asked = asked_ref.shape[0]
 
     def partial_of(here):
@@ -208,8 +205,7 @@
 
     if width % HD == 0:
         for index in range(asked // width // 2):
-            place = 2 * index + parity
-            there = (me ^ difference(place) ^ (lower if place >= far else 0)) * width
+            there = (me ^ difference(2 * index + parity)) * width
             store(index, partial_of(asked_ref[pl.ds(pl.multiple_of(there, width), width), :]))
         return
     tile = min(2 * HD, asked)
@@ -221,7 +217,6 @@
         for part in range(parts):
             lanes = slice(part * width, (part + 1) * width)
             apart = (tile_index * parts + part) ^ me
-            apart = apart ^ (apart // far * lower)
             place = apart ^ (apart >> 1)
 
             @pl.when(place % 2 == parity)

time: 32.1 us -> 32.2 us (level)
  the two profiles are of different devices: /device:TPU:24 before, /device:TPU:16 now
where the time goes in v34:
time: 32.2 us; the launch traced here: 32 us
  Pallas kernels  12.8 us (40%)
  waiting for transfers between devices  11.4 us (35%)
  starting transfers between devices  7.09 us (22%)
  between operations  0.68 us (2%)
    ppermute x4, starting transfers between devices, hand(): lax.ppermute(message, 'seq', [(i, partner(i, k, count)) for i in range(co...  6.17 us
    ppermute x2, waiting for transfers between devices, exchange(): return lax.ppermute(message, 'seq', [(i, i ^ k) for i in range(count)])  6.12 us
    ppermute x4, waiting for transfers between devices, hand(): lax.ppermute(message, 'seq', [(i, partner(i, k, count)) for i in range(co...  5.29 us
    pallas_call x1, Pallas kernels, per_device(): pl.pallas_call(first_kernel, out_shape=[leaving(senders), jax.ShapeDtypeS...  5.23 us
    pallas_call x2, Pallas kernels, place(): pl.pallas_call(functools.partial(place_kernel, plan), out_shape=[jax.Shap...  3.09 us
    pallas_call x1, Pallas kernels, per_device(): pl.pallas_call(second_kernel, out_shape=staying(senders), in_specs=[VMEM]...  2.71 us
    ppermute x2, starting transfers between devices, exchange(): return lax.ppermute(message, 'seq', [(i, i ^ k) for i in range(count)])  0.92 us
    pallas_call x1, Pallas kernels, per_device(): pl.pallas_call(functools.partial(settle_kernel, settled), out_shape=whole...  0.91 us
  transfers between devices with their start and end apart: 6, of which 4 were waited for; matrix products, arithmetic and copies ran while one was open for 0% of the time, Pallas kernels for 33%

profile of v34, /device:TPU:16, one launch (start us, length us, event | category | flops | bytes accessed | tf_op | source)
XLA Modules:
  0.0 32.0 jit_solution(15928563930470820376)
XLA Ops:
  0.6 1.6 %place.2 = (bf16[1024,128]{1,0:T(8,128)(2,1)S(1)}, bf16[1024,128]{1,0:T(8,128)(2,1)S(1)}) custom-call(s32[128]{0:T(128)} %owner_any.3, bf16[4096,128]{1,0:T(8,128)(2,1)} %bitcast.14, f32[256,128]{1,0:T(8,128)} %bitcast.18, f32[2,128]{1,0:T(2,128)} %scales_any.3), custom_call_target="tpu_custom_call" | custom-call | tf_op jit(solution)/shard_map/place/pallas_call | solution.py:403
  2.2 0.1 collective-permute-start.2
  2.3 3.0 %collective-permute-start.5 = (bf16[1024,128]{1,0:T(8,128)(2,1)S(1)}, bf16[1024,128]{1,0:T(8,128)(2,1)S(1)}, u32[]{:S(2)}, u32[]{:S(2)}) collective-permute-start(bf16[1024,128]{1,0:T(8,128)(2,1)S(1)} %get-tuple-element.43), channel_id=1, source_target_pairs={{0,12},{4,8},{8,4},{12,0},{1,13},{5,9},{9,5},{13,1},{2,14},{6,10},... | collective-permute-start | bytes 786440 | tf_op jit(solution)/shard_map/ppermute | solution.py:53
  5.3 5.2 %attend_leaving.1 = (bf16[2,272,128]{2,1,0:T(8,128)(2,1)S(1)}, bf16[2048,256]{1,0:T(8,128)(2,1)S(1)}, bf16[128,2048]{1,0:T(8,128)(2,1)S(1)}, bf16[1024,256]{1,0:T(8,128)(2,1)S(1)}, f32[136,256]{1,0:T(8,128)S(1)}) custom-call(bf16[4096,128]{1,0:T(8,128)(2,1)} %bitcast.15, f32[256,128]{1,0:T(8,128)} %bitcast.19, f32[2,128]{1,0:T(2,128)} %scales_any.3, ...), custom_call_target="tpu_custom_call" | custom-call | tf_op jit(solution)/shard_map/attend_leaving/pallas_call | solution.py:433
  10.5 0.4 %collective-permute-start = (bf16[2,272,128]{2,1,0:T(8,128)(2,1)S(1)}, bf16[2,272,128]{2,1,0:T(8,128)(2,1)S(1)}, u32[]{:S(2)}, u32[]{:S(2)}) collective-permute-start(bf16[2,272,128]{2,1,0:T(8,128)(2,1)S(1)} %get-tuple-element.36), channel_id=1, source_target_pairs={{0,4},{4,0},{8,12},{12,8},{1,5},{5,1},{9,13},{13,9},{2,6},{6,2},{1... | collective-permute-start | bytes 417800 | tf_op jit(solution)/shard_map/ppermute | solution.py:48
  10.9 1.5 %place.3 = (bf16[512,128]{1,0:T(8,128)(2,1)S(1)}, bf16[512,128]{1,0:T(8,128)(2,1)S(1)}, bf16[1024,128]{1,0:T(8,128)(2,1)S(1)}) custom-call(s32[128]{0:T(128)} %owner_any.3, bf16[4096,128]{1,0:T(8,128)(2,1)} %bitcast.16, f32[256,128]{1,0:T(8,128)} %bitcast.20, f32[2,128]{1,0:T(2,128)} %scales_any.3), custom_call_target="tpu_custom_call" | custom-call | tf_op jit(solution)/shard_map/place/pallas_call | solution.py:403
  12.5 2.7 %attend_staying.1.keep_ref = f32[2,136,256]{2,1,0:T(8,128)S(1)} custom-call(bf16[2048,256]{1,0:T(8,128)(2,1)S(1)} %get-tuple-element.31.keys_ref, bf16[128,2048]{1,0:T(8,128)(2,1)S(1)} %get-tuple-element.32.turned_ref, bf16[1024,256]{1,0:T(8,128)(2,1)S(1)} %get-tuple-element.33.asked_ref, f32[136,256]{1,0:T(8,128)S(1)} %get-tuple-element.34.own_ref), custom_call_target="tpu_custom_call" | custom-call | tf_op jit(solution)/shard_map/attend_staying/pallas_call | solution.py:461
  15.2 1.7 %collective-permute-start.3 = (bf16[512,128]{1,0:T(8,128)(2,1)S(1)}, bf16[512,128]{1,0:T(8,128)(2,1)S(1)}, u32[]{:S(2)}, u32[]{:S(2)}) collective-permute-start(bf16[512,128]{1,0:T(8,128)(2,1)S(1)} %get-tuple-element.40), channel_id=1, source_target_pairs={{0,8},{4,0},{8,12},{12,4},{1,9},{5,1},{9,13},{13,5},{2,10},{6,2},{... | collective-permute-start | bytes 393224 | tf_op jit(solution)/shard_map/ppermute | solution.py:53
  16.9 1.3 %collective-permute-start.4 = (bf16[512,128]{1,0:T(8,128)(2,1)S(1)}, bf16[512,128]{1,0:T(8,128)(2,1)S(1)}, u32[]{:S(2)}, u32[]{:S(2)}) collective-permute-start(bf16[512,128]{1,0:T(8,128)(2,1)S(1)} %get-tuple-element.41), channel_id=1, source_target_pairs={{0,8},{4,0},{8,12},{12,4},{1,9},{5,1},{9,13},{13,5},{2,10},{6,2},{... | collective-permute-start | bytes 393224 | tf_op jit(solution)/shard_map/ppermute | solution.py:53
  18.3 1.9 %collective-permute-done.got_ref = bf16[2,272,128]{2,1,0:T(8,128)(2,1)S(1)} collective-permute-done((bf16[2,272,128]{2,1,0:T(8,128)(2,1)S(1)}, bf16[2,272,128]{2,1,0:T(8,128)(2,1)S(1)}, u32[]{:S(2)}, u32[]{:S(2)}) %collective-permute-start) | collective-permute-done | bytes 139296 | tf_op jit(solution)/shard_map/ppermute | solution.py:48
  20.1 0.1 join.1
  20.2 0.5 %collective-permute-start.1 = (bf16[1,272,128]{2,1,0:T(8,128)(2,1)S(1)}, bf16[1,272,128]{2,1,0:T(8,128)(2,1)S(1)}, u32[]{:S(2)}, u32[]{:S(2)}) collective-permute-start(bf16[1,272,128]{2,1,0:T(8,128)(2,1)S(1)} %get-tuple-element.38), channel_id=1, source_target_pairs={{0,12},{4,8},{8,4},{12,0},{1,13},{5,9},{9,5},{13,1},{2,14},{6,10},... | collective-permute-start | bytes 208904 | tf_op jit(solution)/shard_map/ppermute | solution.py:48
  20.7 2.2 %collective-permute-done.3.refs_1_ = bf16[512,128]{1,0:T(8,128)(2,1)S(1)} collective-permute-done((bf16[512,128]{1,0:T(8,128)(2,1)S(1)}, bf16[512,128]{1,0:T(8,128)(2,1)S(1)}, u32[]{:S(2)}, u32[]{:S(2)}) %collective-permute-start.3) | collective-permute-done | bytes 131104 | tf_op jit(solution)/shard_map/ppermute | solution.py:53
  22.9 3.1 %collective-permute-done.4.refs_2_ = bf16[512,128]{1,0:T(8,128)(2,1)S(1)} collective-permute-done((bf16[512,128]{1,0:T(8,128)(2,1)S(1)}, bf16[512,128]{1,0:T(8,128)(2,1)S(1)}, u32[]{:S(2)}, u32[]{:S(2)}) %collective-permute-start.4) | collective-permute-done | bytes 131104 | tf_op jit(solution)/shard_map/ppermute | solution.py:53
  26.0 0.0 collective-permute-done.2.refs_0_
  26.0 0.9 %settle.1._ = bf16[4096,128]{1,0:T(8,128)(2,1)} custom-call(bf16[1024,128]{1,0:T(8,128)(2,1)S(1)} %collective-permute-done.2.refs_0_, bf16[512,128]{1,0:T(8,128)(2,1)S(1)} %collective-permute-done.3.refs_1_, bf16[512,128]{1,0:T(8,128)(2,1)S(1)} %collective-permute-done.4.refs_2_, bf16[1024,128]{1,0:T(8,128)(2,1)S(1)} %get-tuple-element.42.refs_3_), custom_call_target="tpu_custom_call" | custom-call | tf_op jit(solution)/shard_map/settle/pallas_call | solution.py:483
  26.9 4.3 %collective-permute-done.1.got_ref = bf16[1,272,128]{2,1,0:T(8,128)(2,1)S(1)} collective-permute-done((bf16[1,272,128]{2,1,0:T(8,128)(2,1)S(1)}, bf16[1,272,128]{2,1,0:T(8,128)(2,1)S(1)}, u32[]{:S(2)}, u32[]{:S(2)}) %collective-permute-start.1) | collective-permute-done | bytes 69664 | tf_op jit(solution)/shard_map/ppermute | solution.py:48
  31.2 0.0 collective-permute-done.5.refs_0_
  31.2 0.8 %finish.1 = (bf16[256,128]{1,0:T(8,128)(2,1)}, bf16[4096,128]{1,0:T(8,128)(2,1)}) custom-call(f32[1,136,256]{2,1,0:T(8,128)S(1)} %get-tuple-element.37.keep_ref, bf16[1,272,128]{2,1,0:T(8,128)(2,1)S(1)} %collective-permute-done.1.got_ref, bf16[4096,128]{1,0:T(8,128)(2,1)} %settle.1._, ...), custom_call_target="tpu_custom_call", output_to_operand_aliasing={{1}: (2, {})} | custom-call | tf_op jit(solution)/shard_map/finish/pallas_call | solution.py:492
Async XLA Ops:
  2.2 23.8 %collective-permute-start.2 = (bf16[1024,128]{1,0:T(8,128)(2,1)S(1)}, bf16[1024,128]{1,0:T(8,128)(2,1)S(1)}, u32[]{:S(2)}, u32[]{:S(2)}) collective-permute-start(bf16[1024,128]{1,0:T(8,128)(2,1)S(1)} %get-tuple-element.39), channel_id=1, source_target_pairs={{0,4},{4,12},{8,0},{12,8},{1,5},{5,13},{9,1},{13,9},{2,6},{6,14},{... | collective-permute-start | bytes 786440 | tf_op jit(solution)/shard_map/ppermute | solution.py:53
  2.3 28.9 %collective-permute-start.5 = (bf16[1024,128]{1,0:T(8,128)(2,1)S(1)}, bf16[1024,128]{1,0:T(8,128)(2,1)S(1)}, u32[]{:S(2)}, u32[]{:S(2)}) collective-permute-start(bf16[1024,128]{1,0:T(8,128)(2,1)S(1)} %get-tuple-element.43), channel_id=1, source_target_pairs={{0,12},{4,8},{8,4},{12,0},{1,13},{5,9},{9,5},{13,1},{2,14},{6,10},... | collective-permute-start | bytes 786440 | tf_op jit(solution)/shard_map/ppermute | solution.py:53
  10.5 9.6 %collective-permute-start = (bf16[2,272,128]{2,1,0:T(8,128)(2,1)S(1)}, bf16[2,272,128]{2,1,0:T(8,128)(2,1)S(1)}, u32[]{:S(2)}, u32[]{:S(2)}) collective-permute-start(bf16[2,272,128]{2,1,0:T(8,128)(2,1)S(1)} %get-tuple-element.36), channel_id=1, source_target_pairs={{0,4},{4,0},{8,12},{12,8},{1,5},{5,1},{9,13},{13,9},{2,6},{6,2},{1... | collective-permute-start | bytes 417800 | tf_op jit(solution)/shard_map/ppermute | solution.py:48
  15.2 7.8 %collective-permute-start.3 = (bf16[512,128]{1,0:T(8,128)(2,1)S(1)}, bf16[512,128]{1,0:T(8,128)(2,1)S(1)}, u32[]{:S(2)}, u32[]{:S(2)}) collective-permute-start(bf16[512,128]{1,0:T(8,128)(2,1)S(1)} %get-tuple-element.40), channel_id=1, source_target_pairs={{0,8},{4,0},{8,12},{12,4},{1,9},{5,1},{9,13},{13,5},{2,10},{6,2},{... | collective-permute-start | bytes 393224 | tf_op jit(solution)/shard_map/ppermute | solution.py:53
  16.9 9.1 %collective-permute-start.4 = (bf16[512,128]{1,0:T(8,128)(2,1)S(1)}, bf16[512,128]{1,0:T(8,128)(2,1)S(1)}, u32[]{:S(2)}, u32[]{:S(2)}) collective-permute-start(bf16[512,128]{1,0:T(8,128)(2,1)S(1)} %get-tuple-element.41), channel_id=1, source_target_pairs={{0,8},{4,0},{8,12},{12,4},{1,9},{5,1},{9,13},{13,5},{2,10},{6,2},{... | collective-permute-start | bytes 393224 | tf_op jit(solution)/shard_map/ppermute | solution.py:53
  20.2 11.0 %collective-permute-start.1 = (bf16[1,272,128]{2,1,0:T(8,128)(2,1)S(1)}, bf16[1,272,128]{2,1,0:T(8,128)(2,1)S(1)}, u32[]{:S(2)}, u32[]{:S(2)}) collective-permute-start(bf16[1,272,128]{2,1,0:T(8,128)(2,1)S(1)} %get-tuple-element.38), channel_id=1, source_target_pairs={{0,12},{4,8},{8,4},{12,0},{1,13},{5,9},{9,5},{13,1},{2,14},{6,10},... | collective-permute-start | bytes 208904 | tf_op jit(solution)/shard_map/ppermute | solution.py:48
